TPU v7x, 512 devices: a whole 4x8x8 slice. The times are simulated.
512 devices in a mesh: dp: 32 (over x, z), sx: 8 (over y), sy: 2 (over core).
Axes of the slice: x: 4, y: 8, z: 8, core: 2. Of those that a mesh axis runs over, the one named last changes fastest.
Arguments:
- features: bfloat16 [32, 128, 16, 8, 128], P('dp', None, 'sx', 'sy'), may hold values from -6 to 6
- cotangent: bfloat16 [32, 128, 16, 8, 128], P('dp', None, 'sx', 'sy'), may hold values from -6 to 6
- weights: bfloat16 [27, 128, 128], replicated, may hold values from -0.109375 to 0.109375
- conv_bias: float32 [128], replicated, may hold values from -3 to 3
- error_state: float32 [32, 8, 2, 128, 3456], P('dp', 'sx', 'sy'), may hold values from -96 to 96
- warm_factor: float32 [4, 3456], replicated, may hold values from -6 to 6
Outputs:
- activation: bfloat16 [32, 128, 16, 8, 128], P('dp', None, 'sx', 'sy')
- input_grad: bfloat16 [32, 128, 16, 8, 128], P('dp', None, 'sx', 'sy')
- bias_grad: float32 [128], replicated
- factor_p: float32 [4, 128], replicated
- factor_q: float32 [4, 3456], replicated
- new_error: float32 [32, 8, 2, 128, 3456], P('dp', 'sx', 'sy')
All inputs are finite; a program needn't handle non-finite values.
Results may differ from a plain program's by a relative error of at most 0.006.
Values may be sent and summed in bfloat16 or wider, within the bound.
No kernel may reach another device: no remote copies, remote signals or barrier semaphores. Data moves between devices by JAX's collectives and lax.ppermute only.
A program may use at most 64 MiB of HBM per device.

v0:
```python
import functools

import jax
import jax.numpy as jnp
from jax import lax
from jax.sharding import Mesh
from jax.sharding import PartitionSpec as P

DP = ("dp_0", "dp_1")
DP_SX_SY = ("dp_0", "dp_1", "sx", "sy")


tap_offsets = tuple(
    ((first, second, third) for first in range(3) for second in range(3) for third in range(3))
)


def with_halo(block, sides, width):
    for axis, dim in sides:
        count = lax.axis_size(axis)
        forward = [(i, i + 1) for i in range(count - 1)]
        backward = [(target, source) for source, target in forward]
        low = lax.ppermute(
            lax.slice_in_dim(block, block.shape[dim] - width, None, axis=dim), axis, forward
        )
        high = lax.ppermute(lax.slice_in_dim(block, 0, width, axis=dim), axis, backward)
        block = jnp.concatenate([low, block, high], axis=dim)
    return block


def one_axis_at_a_time(x, axes):
    return functools.reduce(lax.psum, axes, x)


def orthonormal(rows):
    result = []
    for column in range(rows.shape[0]):
        vector = rows[column]
        for basis in result:
            vector = vector - jnp.sum(basis * vector) * basis
        vector = vector / jnp.sqrt(jnp.sum(vector * vector) + 1e-06)
        result.append(vector)
    return jnp.stack(result)


def shards(features, cotangent, weights, conv_bias, error_state, warm_factor):
    inputs = features[0]
    channels, extent_x, extent_y, extent_z = inputs.shape
    padded = with_halo(inputs, (("sx", 1), ("sy", 2)), 1)
    padded = jnp.pad(padded, ((0, 0), (0, 0), (0, 0), (1, 1)))
    total = jnp.zeros((channels, extent_x * extent_y * extent_z), jnp.float32)
    for tap_index, (shift_x, shift_y, shift_z) in enumerate(tap_offsets):
        window = padded[
            :,
            shift_x : shift_x + extent_x,
            shift_y : shift_y + extent_y,
            shift_z : shift_z + extent_z,
        ].reshape(channels, -1)
        total = total + jnp.dot(weights[tap_index], window, preferred_element_type=jnp.float32)
    pre = total + conv_bias[:, None]
    activation = jax.nn.silu(pre).astype(jnp.bfloat16)
    sigma = jax.nn.sigmoid(pre)
    upstream = cotangent[0].reshape(channels, -1).astype(jnp.float32)
    grad_pre = (upstream * sigma * (1.0 + pre * (1.0 - sigma))).astype(jnp.bfloat16)
    grad_cube = grad_pre.reshape(channels, extent_x, extent_y, extent_z)
    partial_list = []
    for tap_index, (shift_x, shift_y, shift_z) in enumerate(tap_offsets):
        window = padded[
            :,
            shift_x : shift_x + extent_x,
            shift_y : shift_y + extent_y,
            shift_z : shift_z + extent_z,
        ].reshape(channels, -1)
        partial_list.append(
            lax.dot_general(
                grad_pre, window, (((1,), (1,)), ((), ())), preferred_element_type=jnp.float32
            )
        )
    merged = jnp.stack(partial_list, axis=1).reshape(channels, -1) + error_state[0, 0, 0]
    grad_padded = with_halo(grad_cube, (("sx", 1), ("sy", 2)), 1)
    grad_padded = jnp.pad(grad_padded, ((0, 0), (0, 0), (0, 0), (1, 1)))
    back = jnp.zeros((channels, extent_x * extent_y * extent_z), jnp.float32)
    for tap_index, (shift_x, shift_y, shift_z) in enumerate(tap_offsets):
        window = grad_padded[
            :,
            2 - shift_x : 2 - shift_x + extent_x,
            2 - shift_y : 2 - shift_y + extent_y,
            2 - shift_z : 2 - shift_z + extent_z,
        ].reshape(channels, -1)
        back = back + lax.dot_general(
            weights[tap_index], window, (((0,), (0,)), ((), ())), preferred_element_type=jnp.float32
        )
    input_grad = back.reshape(channels, extent_x, extent_y, extent_z)
    devices_count = lax.axis_size(DP) * lax.axis_size("sx") * lax.axis_size("sy")
    bias_local = jnp.sum(grad_pre.astype(jnp.float32), axis=1)
    p_local = lax.dot_general(
        warm_factor,
        merged,
        (((1,), (1,)), ((), ())),
        precision=lax.Precision.HIGHEST,
        preferred_element_type=jnp.float32,
    )
    bias_sum = one_axis_at_a_time(bias_local, DP_SX_SY)
    p_sum = one_axis_at_a_time(p_local, DP_SX_SY)
    factor_p = orthonormal(p_sum)
    q_local = jnp.dot(
        factor_p, merged, precision=lax.Precision.HIGHEST, preferred_element_type=jnp.float32
    )
    factor_q = one_axis_at_a_time(q_local, DP_SX_SY) / devices_count
    new_error = merged - lax.dot_general(
        factor_p,
        q_local,
        (((0,), (0,)), ((), ())),
        precision=lax.Precision.HIGHEST,
        preferred_element_type=jnp.float32,
    )
    bias_grad = bias_sum / devices_count
    return (
        activation.reshape(1, channels, extent_x, extent_y, extent_z),
        input_grad.astype(jnp.bfloat16)[None],
        bias_grad,
        factor_p,
        factor_q,
        new_error[None, None, None],
    )


def solution(mesh):
    torus = Mesh(
        mesh.devices.reshape(4, 8, mesh.shape["sx"], mesh.shape["sy"]), ("dp_0", "dp_1", "sx", "sy")
    )
    in_specs = (
        P(DP, None, "sx", "sy", None),
        P(DP, None, "sx", "sy", None),
        P(),
        P(),
        P(DP, "sx", "sy", None, None),
        P(),
    )
    out_specs = (
        P(DP, None, "sx", "sy", None),
        P(DP, None, "sx", "sy", None),
        P(),
        P(),
        P(),
        P(DP, "sx", "sy", None, None),
    )
    return jax.shard_map(
        shards, mesh=torus, in_specs=in_specs, out_specs=out_specs, check_vma=False
    )
```

profile of v0, /device:TPU:1, one launch (start us, length us, event | category | flops | bytes accessed | tf_op | source)
XLA Modules:
  0.0 277.9 jit_solution(8099095123667609711)
XLA Ops:
  0.7 1.1 fusion.203
  1.8 4.0 %collective-permute-start = (bf16[128,1,4,128]{3,2,1,0:T(4,128)(2,1)S(1)}, bf16[128,1,4,128]{3,2,1,0:T(4,128)(2,1)S(1)}, u32[]{:S(2)}, u32[]{:S(2)}) collective-permute-start(bf16[128,1,4,128]{3,2,1,0:T(4,128)(2,1)S(1)} %get-tuple-element.99), channel_id=1, source_target_pairs={{0,2},{2,4},{4,6},{6,8},{8,10},{10,12},{12,14},{1,3},{3,5},{5,7},{... | collective-permute-start | bytes 393224 | tf_op jit(solution)/shard_map/ppermute | solution.py:23
  5.8 1.3 collective-permute-start.1
  7.8 3.8 %collective-permute-done.1 = bf16[128,1,4,128]{3,2,1,0:T(4,128)(2,1)S(1)} collective-permute-done((bf16[128,1,4,128]{3,2,1,0:T(4,128)(2,1)S(1)}, bf16[128,1,4,128]{3,2,1,0:T(4,128)(2,1)S(1)}, u32[]{:S(2)}, u32[]{:S(2)}) %collective-permute-start.1) | collective-permute-done | bytes 131104 | tf_op jit(solution)/shard_map/ppermute | solution.py:26
  11.6 1.4 pad_maximum_fusion.1
  13.3 1.3 collective-permute-start.2
  14.6 7.2 %collective-permute-start.3 = (bf16[128,4,1,128]{3,2,1,0:T(2,128)(2,1)S(1)}, bf16[128,4,1,128]{3,2,1,0:T(2,128)(2,1)S(1)}, u32[]{:S(2)}, u32[]{:S(2)}) collective-permute-start(bf16[128,4,1,128]{3,2,1,0:T(2,128)(2,1)S(1)} %get-tuple-element.92), channel_id=1, source_target_pairs={{1,0},{3,2},{5,4},{7,6},{9,8},{11,10},{13,12},{15,14},{17,16},{19,... | collective-permute-start | bytes 393224 | tf_op jit(solution)/shard_map/ppermute | solution.py:26
  25.2 3.3 %select_maximum_fusion = bf16[128,4,6,130]{3,2,1,0:T(8,128)(2,1)S(1)} fusion(bf16[128,4,1,128]{3,2,1,0:T(2,128)(2,1)S(1)} %collective-permute-done.3, bf16[128,4,1,128]{3,2,1,0:T(2,128)(2,1)S(1)} %collective-permute-done.2, bf16[128,1,4,128]{3,2,1,0:T(4,128)(2,1)S(1)} %collective-permute-done.1, bf16[128,2,4,128]{3,2,1,0:T(4,128)(2,1)S(1)} %bitcast.554, ...), kind=kLoop, calls=%fused_computation.7 | loop fusion | flops 7188480 | bytes 1585152 | tf_op jit(solution)/shard_map/concatenate | solution.py:27
  28.5 3.9 %fusion.197 = (bf16[128,2,4,128]{3,2,1,0:T(4,128)(2,1)}, bf16[128,2,4,128]{3,2,1,0:T(4,128)(2,1)}, bf16[128,2,4,128]{3,2,1,0:T(4,128)(2,1)}, bf16[128,2,4,128]{3...) fusion(bf16[128,4,6,130]{3,2,1,0:T(8,128)(2,1)S(1)} %select_max, ...), kind=kLoop, calls=%fused_computation.324 | loop fusion | bytes 9437184 | tf_op jit(solution)/shard_map/slice | solution.py:53
  32.7 1.0 fusion.101
  35.0 1.1 fusion.110
  36.2 1.1 fusion.116
  37.5 1.1 fusion.120
  38.7 1.1 fusion.126
  41.0 1.1 reshape.228
  43.2 1.1 reshape.240
  44.3 1.1 fusion.98
  45.3 3.3 %pad_maximum_fusion.4 = (bf16[128,2,4,128]{3,2,1,0:T(4,128)(2,1)}, bf16[128,2,4,128]{3,2,1,0:T(4,128)(2,1)}, bf16[128,2,4,128]{3,2,1,0:T(4,128)(2,1)}, bf16[128,...) fusion(bf16[128,4,1,128]{3,2,1,0:T(2,128)(2,1)} %copy-done.29, bf16[128,1,4,128]{3,2,1,0:T(4,128)(2,1)} %copy-done.24, ...), kind=kLoop, calls=%fused_computation.155 | loop fusion | flops 4194304 | bytes 1966080 | tf_op jit(solution)/shard_map/concatenate | solution.py:27
  48.7 1.8 reshape.235
  50.5 2.0 fusion.113
  52.5 1.8 reshape.232
  54.3 2.0 fusion.123
  56.3 2.8 %pad_maximum_fusion.8 = (bf16[128,2,4,128]{3,2,1,0:T(4,128)(2,1)}, bf16[128,2,4,128]{3,2,1,0:T(4,128)(2,1)}, bf16[128,2,4,128]{3,2,1,0:T(4,128)(2,1)}) fusion(bf16[128,4,1,128]{3,2,1,0:T(2,128)(2,1)} %copy-done.28, bf16[128,1,4,128]{3,2,1,0:T(4,128)(2,1)} %copy-done.24, bf16[128,2,4,128]{3,2,1,0:T(4,128)(2,1)S(1)} %bitcast.556, ...), kind=kLoop, calls=%fused_computation.159 | loop fusion | flops 3145728 | bytes 1441792 | tf_op jit(solution)/shard_map/concatenate | solution.py:27
  59.1 1.1 reshape.238
  61.3 1.8 reshape.229
  63.2 2.0 fusion.132
  65.2 1.8 reshape.242
  67.0 1.8 reshape.243
  68.8 1.8 reshape.244
  70.6 1.9 reshape.245
  72.5 1.8 reshape.246
  74.3 1.8 reshape.247
  76.1 1.8 reshape.248
  78.0 1.8 reshape.249
  79.8 1.8 reshape.250
  82.5 1.1 reshape.252
  83.7 1.9 reshape.253
  85.6 1.8 reshape.254
  87.4 3.5 %convolution_add_fusion.15 = f32[128,1024]{0,1:T(8,128)S(1)} fusion(bf16[128,1024]{1,0:T(8,128)(2,1)} %reshape.241, f32[1024,128]{1,0:T(8,128)} %fusion.98, f32[1024,128]{1,0:T(8,128)} %fusion.101, f32[1024,128]{1,0:T(8,128)} %fusion.104, f32[1024,128]{1,0:T(8,128)} %fusion.107, f32[1024,128]{1,0:T(8,128)} %fusion.110, f32[1024,128]{1,0:T(8,128)} %fusion.113, ...), kind=kOutput, calls=%fused_computation.78 | convolution fusion | flops 35258368 | bytes 7634944 | tf_op jit(solution)/shard_map/dot_general | solution.py:59
  95.3 1.2 convert_reduce_fusion
  102.9 1.2 copy-done.25
  104.1 2.0 copy.14
  106.0 3.1 %convolution_bitcast_fusion.50 = f32[4,128]{1,0:T(4,128)S(1)} fusion(f32[4,3456]{1,0:T(4,128)S(1)} %copy-done, f32[128,3456]{1,0:T(8,128)S(1)} %copy.14, f32[1,1,1,128,3456]{4,3,2,1,0:T(8,128)} %param.10), kind=kOutput, calls=%fused_computation.136 | convolution fusion | flops 21676032 | bytes 3596288 | tf_op jit(solution)/shard_map/dot_general | solution.py:96
  109.1 6.0 %psum.88 = f32[4,128]{1,0:T(4,128)S(1)} all-reduce(f32[4,128]{1,0:T(4,128)S(1)} %convolution_bitcast_fusion.50), channel_id=1, replica_groups=mesh['dp_0'=4,'dp_1'=8,'sx'=8,'sy'=2] {'dp_0'}, use_global_device_ids=true, to_apply=%region_5.6 | all-reduce | flops 512 | bytes 4096 | tf_op jit(solution)/shard_map/psum | solution.py:32
  115.1 18.8 %psum.89 = f32[4,128]{1,0:T(4,128)S(1)} all-reduce(f32[4,128]{1,0:T(4,128)S(1)} %psum.88), channel_id=1, replica_groups=mesh['dp_0'=4,'dp_1'=8,'sx'=8,'sy'=2] {'dp_1'}, use_global_device_ids=true, to_apply=%region_6.7 | all-reduce | flops 512 | bytes 4096 | tf_op jit(solution)/shard_map/psum | solution.py:32
  133.9 14.4 %psum.90 = f32[4,128]{1,0:T(4,128)S(1)} all-reduce(f32[4,128]{1,0:T(4,128)S(1)} %psum.89), channel_id=1, replica_groups=mesh['dp_0'=4,'dp_1'=8,'sx'=8,'sy'=2] {'sx'}, use_global_device_ids=true, to_apply=%region_7.8 | all-reduce | flops 512 | bytes 4096 | tf_op jit(solution)/shard_map/psum | solution.py:32
  148.3 10.8 %psum.91 = f32[4,128]{1,0:T(4,128)S(1)} all-reduce(f32[4,128]{1,0:T(4,128)S(1)} %psum.90), channel_id=1, replica_groups=mesh['dp_0'=4,'dp_1'=8,'sx'=8,'sy'=2] {'sy'}, use_global_device_ids=true, to_apply=%region_8.9 | all-reduce | flops 512 | bytes 4096 | tf_op jit(solution)/shard_map/psum | solution.py:32
  161.0 1.3 fusion.192
  162.9 1.9 multiply_reduce_fusion.4
  164.8 1.9 multiply_reduce_fusion.2
  167.4 1.9 multiply_reduce_fusion.1
  169.3 1.9 multiply_reduce_fusion
  171.8 3.9 %subtract_divide_fusion = (f32[1,128]{1,0:T(1,128)S(1)}, f32[1,128]{1,0:T(1,128)S(1)}, f32[1,128]{1,0:T(1,128)S(1)}) fusion(f32[1,128]{1,0:T(1,128)S(1)} %get-tuple-element.35, f32[]{:T(128)S(6)} %sqrt.15, f32[]{:T(128)} %get-tuple-element.28, f32[]{:T(128)} %get-tuple-element.15, f32[]{:T(128)} %get-tuple-element.12, f32[4,128]{1,0:T(4,128)S(1)} %psum.91, ...), kind=kLoop, calls=%fused_computation.308 | loop fusion | flops 1920 | bytes 3620 | tf_op jit(solution)/shard_map/div | solution.py:41
  175.7 2.6 fusion.195
  178.3 11.4 %all-reduce.4 = (f32[128]{0:T(128)S(1)}, f32[4,3456]{1,0:T(4,128)S(1)}) all-reduce(f32[128]{0:T(128)S(1)} %get-tuple-element.36, f32[4,3456]{1,0:T(4,128)S(1)} %fusion.195), channel_id=1, replica_groups=mesh['dp_0'=4,'dp_1'=8,'sx'=8,'sy'=2] {'dp_0'}, use_global_device_ids=true, to_apply=%region_1.2 | all-reduce | flops 13952 | bytes 111616 | tf_op jit(solution)/shard_map/psum | solution.py:32
  189.7 20.5 %all-reduce.3 = (f32[128]{0:T(128)S(1)}, f32[4,3456]{1,0:T(4,128)S(1)}) all-reduce(f32[128]{0:T(128)S(1)} %get-tuple-element.21, f32[4,3456]{1,0:T(4,128)S(1)} %get-tuple-element.22), channel_id=1, replica_groups=mesh['dp_0'=4,'dp_1'=8,'sx'=8,'sy'=2] {'dp_1'}, use_global_device_ids=true, to_apply=%region_2.3 | all-reduce | flops 13952 | bytes 111616 | tf_op jit(solution)/shard_map/psum | solution.py:32
  210.2 20.6 %all-reduce.2 = (f32[128]{0:T(128)S(1)}, f32[4,3456]{1,0:T(4,128)S(1)}) all-reduce(f32[128]{0:T(128)S(1)} %get-tuple-element.19, f32[4,3456]{1,0:T(4,128)S(1)} %get-tuple-element.20), channel_id=1, replica_groups=mesh['dp_0'=4,'dp_1'=8,'sx'=8,'sy'=2] {'sx'}, use_global_device_ids=true, to_apply=%region_3.4 | all-reduce | flops 13952 | bytes 111616 | tf_op jit(solution)/shard_map/psum | solution.py:32
  230.8 21.1 %all-reduce.5 = (f32[128]{0:T(128)S(1)}, f32[4,3456]{1,0:T(4,128)S(1)}) all-reduce(f32[128]{0:T(128)S(1)} %get-tuple-element.17, f32[4,3456]{1,0:T(4,128)S(1)} %get-tuple-element.18), channel_id=1, replica_groups=mesh['dp_0'=4,'dp_1'=8,'sx'=8,'sy'=2] {'sy'}, use_global_device_ids=true, to_apply=%region_4.5 | all-reduce | flops 13952 | bytes 111616 | tf_op jit(solution)/shard_map/psum | solution.py:32
  252.5 3.5 %collective-permute-start.4 = (bf16[128,1,4,128]{0,3,2,1:T(8,128)(2,1)S(1)}, bf16[128,1,4,128]{0,3,2,1:T(8,128)(2,1)S(1)}, u32[]{:S(2)}, u32[]{:S(2)}) collective-permute-start(bf16[128,1,4,128]{0,3,2,1:T(8,128)(2,1)S(1)} %get-tuple-element.97), channel_id=1, source_target_pairs={{0,2},{2,4},{4,6},{6,8},{8,10},{10,12},{12,14},{1,3},{3,5},{5,7},{... | collective-permute-start | bytes 393224 | tf_op jit(solution)/shard_map/ppermute | solution.py:23
  256.0 1.3 collective-permute-start.5
  257.3 4.5 %fusion = f32[1,1,1,128,3456]{4,3,2,1,0:T(8,128)} fusion(f32[4,128]{1,0:T(4,128)S(1)} %pad_maximum_fusion.19, f32[4,3456]{1,0:T(4,128)S(1)} %fusion.195, f32[128,3456]{1,0:T(8,128)S(1)} %copy.14, f32[1,1,1,128,3456]{4,3,2,1,0:T(8,128)} %param.10), kind=kOutput, calls=%fused_computation.3 | convolution fusion | flops 22118400 | bytes 5365760 | tf_op jit(solution)/shard_map/dot_general | solution.py:110
  262.6 1.3 collective-permute-start.6
  263.9 3.5 %collective-permute-start.7 = (bf16[128,4,1,128]{0,3,2,1:T(8,128)(2,1)S(1)}, bf16[128,4,1,128]{0,3,2,1:T(8,128)(2,1)S(1)}, u32[]{:S(2)}, u32[]{:S(2)}) collective-permute-start(bf16[128,4,1,128]{0,3,2,1:T(8,128)(2,1)S(1)} %get-tuple-element.89), channel_id=1, source_target_pairs={{1,0},{3,2},{5,4},{7,6},{9,8},{11,10},{13,12},{15,14},{17,16},{19,... | collective-permute-start | bytes 393224 | tf_op jit(solution)/shard_map/ppermute | solution.py:26
  267.9 1.8 copy.15
  (168 shorter events, 32.0 us)
Async XLA Ops:
  0.6 105.4 %copy-start = (f32[4,3456]{1,0:T(4,128)S(1)}, f32[4,3456]{1,0:T(4,128)}, u32[]{:S(2)}) copy-start(f32[4,3456]{1,0:T(4,128)} %param.11) | copy-start | bytes 165892
  0.6 21.2 %copy-start.1 = (bf16[1,128,2,4,128]{4,3,2,1,0:T(4,128)(2,1)S(1)}, bf16[1,128,2,4,128]{4,3,2,1,0:T(4,128)(2,1)}, u32[]{:S(2)}) copy-start(bf16[1,128,2,4,128]{4,3,2,1,0:T(4,128)(2,1)} %param.6) | copy-start | bytes 786436
  0.7 22.1 %copy-start.31 = (bf16[1,128,2,4,128]{4,3,2,1,0:T(4,128)(2,1)S(1)}, bf16[1,128,2,4,128]{4,3,2,1,0:T(4,128)(2,1)}, u32[]{:S(2)}) copy-start(bf16[1,128,2,4,128]{4,3,2,1,0:T(4,128)(2,1)} %param.7) | copy-start | bytes 786436
  1.8 6.0 %collective-permute-start = (bf16[128,1,4,128]{3,2,1,0:T(4,128)(2,1)S(1)}, bf16[128,1,4,128]{3,2,1,0:T(4,128)(2,1)S(1)}, u32[]{:S(2)}, u32[]{:S(2)}) collective-permute-start(bf16[128,1,4,128]{3,2,1,0:T(4,128)(2,1)S(1)} %get-tuple-element.99), channel_id=1, source_target_pairs={{0,2},{2,4},{4,6},{6,8},{8,10},{10,12},{12,14},{1,3},{3,5},{5,7},{... | collective-permute-start | bytes 393224 | tf_op jit(solution)/shard_map/ppermute | solution.py:23
  5.8 5.7 %collective-permute-start.1 = (bf16[128,1,4,128]{3,2,1,0:T(4,128)(2,1)S(1)}, bf16[128,1,4,128]{3,2,1,0:T(4,128)(2,1)S(1)}, u32[]{:S(2)}, u32[]{:S(2)}) collective-permute-start(bf16[128,1,4,128]{3,2,1,0:T(4,128)(2,1)S(1)} %get-tuple-element.100), channel_id=1, source_target_pairs={{2,0},{4,2},{6,4},{8,6},{10,8},{12,10},{14,12},{3,1},{5,3},{7,5},{... | collective-permute-start | bytes 393224 | tf_op jit(solution)/shard_map/ppermute | solution.py:26
  11.5 12.2 %copy-start.24 = (bf16[128,1,4,128]{3,2,1,0:T(4,128)(2,1)}, bf16[128,1,4,128]{3,2,1,0:T(4,128)(2,1)S(1)}, u32[]{:S(2)}) copy-start(bf16[128,1,4,128]{3,2,1,0:T(4,128)(2,1)S(1)} %collective-permute-done.1) | copy-start | bytes 393220
  13.3 10.4 %collective-permute-start.2 = (bf16[128,4,1,128]{3,2,1,0:T(2,128)(2,1)S(1)}, bf16[128,4,1,128]{3,2,1,0:T(2,128)(2,1)S(1)}, u32[]{:S(2)}, u32[]{:S(2)}) collective-permute-start(bf16[128,4,1,128]{3,2,1,0:T(2,128)(2,1)S(1)} %get-tuple-element.91), channel_id=1, source_target_pairs={{0,1},{2,3},{4,5},{6,7},{8,9},{10,11},{12,13},{14,15},{16,17},{18,... | collective-permute-start | bytes 393224 | tf_op jit(solution)/shard_map/ppermute | solution.py:23
  14.6 9.1 %collective-permute-start.3 = (bf16[128,4,1,128]{3,2,1,0:T(2,128)(2,1)S(1)}, bf16[128,4,1,128]{3,2,1,0:T(2,128)(2,1)S(1)}, u32[]{:S(2)}, u32[]{:S(2)}) collective-permute-start(bf16[128,4,1,128]{3,2,1,0:T(2,128)(2,1)S(1)} %get-tuple-element.92), channel_id=1, source_target_pairs={{1,0},{3,2},{5,4},{7,6},{9,8},{11,10},{13,12},{15,14},{17,16},{19,... | collective-permute-start | bytes 393224 | tf_op jit(solution)/shard_map/ppermute | solution.py:26
  23.7 0.7 copy-start.28
  24.4 0.7 copy-start.29
  28.5 4.2 %copy-start.2 = (bf16[27,128,128]{2,1,0:T(8,128)(2,1)S(1)}, bf16[27,128,128]{2,1,0:T(8,128)(2,1)}, u32[]{:S(2)}) copy-start(bf16[27,128,128]{2,1,0:T(8,128)(2,1)} %param.8) | copy-start | bytes 2654212
  42.1 1.1 copy-start.6
  60.3 10.4 %copy-start.4 = (bf16[128,1024]{1,0:T(8,128)(2,1)}, bf16[128,1024]{1,0:T(8,128)(2,1)S(1)}, u32[]{:S(2)}) copy-start(bf16[128,1024]{1,0:T(8,128)(2,1)S(1)} %reshape.238) | copy-start | bytes 786436
  70.6 11.0 %copy-start.26 = (bf16[128,2,4,128]{3,2,1,0:T(4,128)(2,1)S(1)}, bf16[128,2,4,128]{3,2,1,0:T(4,128)(2,1)}, u32[]{:S(2)}) copy-start(bf16[128,2,4,128]{3,2,1,0:T(4,128)(2,1)} %get-tuple-element.40) | copy-start | bytes 786436
  83.7 10.8 %copy-start.10 = (bf16[128,1024]{1,0:T(8,128)(2,1)}, bf16[128,1024]{1,0:T(8,128)(2,1)S(1)}, u32[]{:S(2)}) copy-start(bf16[128,1024]{1,0:T(8,128)(2,1)S(1)} %reshape.252) | copy-start | bytes 786436
  87.4 3.5 %copy-start.22 = (bf16[128,1024]{1,0:T(8,128)(2,1)S(1)}, bf16[128,1024]{1,0:T(8,128)(2,1)}, u32[]{:S(2)}) copy-start(bf16[128,1024]{1,0:T(8,128)(2,1)} %reshape.242) | copy-start | bytes 786436
  87.4 3.8 %copy-start.21 = (bf16[128,1024]{1,0:T(8,128)(2,1)S(1)}, bf16[128,1024]{1,0:T(8,128)(2,1)}, u32[]{:S(2)}) copy-start(bf16[128,1024]{1,0:T(8,128)(2,1)} %reshape.243) | copy-start | bytes 786436
  90.9 1.0 copy-start.20
  90.9 1.2 copy-start.19
  91.2 1.2 copy-start.17
  91.9 1.0 copy-start.18
  92.1 1.0 copy-start.16
  92.4 1.0 copy-start.15
  92.8 1.0 copy-start.14
  93.1 1.0 copy-start.13
  93.8 1.0 copy-start.12
  94.1 1.0 copy-start.27
  94.1 1.1 copy-start.30
  94.1 1.1 copy-start.33
  95.3 1.2 copy-start.7
  95.3 1.4 copy-start.9
  96.4 0.9 copy-start.8
  96.7 1.6 copy-start.3
  97.4 1.6 copy-start.5
  98.3 1.4 copy-start.23
  100.8 1.4 copy-start.11
  102.8 1.2 copy-start.25
  175.7 81.6 %copy-start.32 = (f32[4,128]{1,0:T(4,128)}, f32[4,128]{1,0:T(4,128)S(1)}, u32[]{:S(2)}) copy-start(f32[4,128]{1,0:T(4,128)S(1)} %pad_maximum_fusion.19) | copy-start | bytes 6148
  252.5 9.3 %collective-permute-start.4 = (bf16[128,1,4,128]{0,3,2,1:T(8,128)(2,1)S(1)}, bf16[128,1,4,128]{0,3,2,1:T(8,128)(2,1)S(1)}, u32[]{:S(2)}, u32[]{:S(2)}) collective-permute-start(bf16[128,1,4,128]{0,3,2,1:T(8,128)(2,1)S(1)} %get-tuple-element.97), channel_id=1, source_target_pairs={{0,2},{2,4},{4,6},{6,8},{8,10},{10,12},{12,14},{1,3},{3,5},{5,7},{... | collective-permute-start | bytes 393224 | tf_op jit(solution)/shard_map/ppermute | solution.py:23
  256.0 6.5 %collective-permute-start.5 = (bf16[128,1,4,128]{0,3,2,1:T(8,128)(2,1)S(1)}, bf16[128,1,4,128]{0,3,2,1:T(8,128)(2,1)S(1)}, u32[]{:S(2)}, u32[]{:S(2)}) collective-permute-start(bf16[128,1,4,128]{0,3,2,1:T(8,128)(2,1)S(1)} %get-tuple-element.98), channel_id=1, source_target_pairs={{2,0},{4,2},{6,4},{8,6},{10,8},{12,10},{14,12},{3,1},{5,3},{7,5},{... | collective-permute-start | bytes 393224 | tf_op jit(solution)/shard_map/ppermute | solution.py:26
  262.6 7.2 %collective-permute-start.6 = (bf16[128,4,1,128]{0,3,2,1:T(8,128)(2,1)S(1)}, bf16[128,4,1,128]{0,3,2,1:T(8,128)(2,1)S(1)}, u32[]{:S(2)}, u32[]{:S(2)}) collective-permute-start(bf16[128,4,1,128]{0,3,2,1:T(8,128)(2,1)S(1)} %get-tuple-element.88), channel_id=1, source_target_pairs={{0,1},{2,3},{4,5},{6,7},{8,9},{10,11},{12,13},{14,15},{16,17},{18,... | collective-permute-start | bytes 393224 | tf_op jit(solution)/shard_map/ppermute | solution.py:23
  263.9 5.9 %collective-permute-start.7 = (bf16[128,4,1,128]{0,3,2,1:T(8,128)(2,1)S(1)}, bf16[128,4,1,128]{0,3,2,1:T(8,128)(2,1)S(1)}, u32[]{:S(2)}, u32[]{:S(2)}) collective-permute-start(bf16[128,4,1,128]{0,3,2,1:T(8,128)(2,1)S(1)} %get-tuple-element.89), channel_id=1, source_target_pairs={{1,0},{3,2},{5,4},{7,6},{9,8},{11,10},{13,12},{15,14},{17,16},{19,... | collective-permute-start | bytes 393224 | tf_op jit(solution)/shard_map/ppermute | solution.py:26
where the time goes:
time: 280 us; the launch traced here: 278 us
  blocking collectives  123 us (44%)
  local copies, waits for them, and re-layouts  48.9 us (17%)
  matrix products  46.2 us (16%)
  other arithmetic  26.4 us (9%)
  starting transfers between devices  23.4 us (8%)
  waiting for transfers between devices  5.15 us (2%)
  between operations  4.34 us (2%)
    psum x8, blocking collectives, one_axis_at_a_time(): return functools.reduce(lax.psum, axes, x)  123 us
    reshape x27, local copies, waits for them, and re-layouts, shards(): window = padded[:, shift_x:shift_x + extent_x, shift_y:shift_y + extent_y...  33.1 us
    dot_general x27, matrix products, shards(): jnp.dot(weights[tap_index], window, preferred_element_type=jnp.float32)  24.3 us
    ppermute x4, starting transfers between devices, with_halo(): lax.ppermute(lax.slice_in_dim(block, 0, width, axis=dim), axis, backward)  13.3 us
    concatenate x7, other arithmetic, with_halo(): block = jnp.concatenate([low, block, high], axis=dim)  11.3 us
    ppermute x4, starting transfers between devices, with_halo(): lax.ppermute(lax.slice_in_dim(block, block.shape[dim] - width, None, axis...  10.1 us
    reduce_sum x5, other arithmetic, orthonormal(): vector = vector - jnp.sum(basis * vector) * basis  7.56 us
    unnamed x70, local copies, waits for them, and re-layouts  6.5 us
  transfers between devices with their start and end apart: 8, of which 3 were waited for; matrix products, arithmetic and copies ran while one was open for 3% of the time, Pallas kernels for 0%

commit v1 on v0

v1 whole, which is shorter than its diff:
```python
import jax
import jax.numpy as jnp
from jax import lax
from jax.experimental import pallas as pl
from jax.experimental.pallas import tpu as pltpu
from jax.sharding import Mesh
from jax.sharding import PartitionSpec as P

DP = ("dp_0", "dp_1")
ALL_AXES = ("dp_0", "dp_1", "sx", "sy")
C = 128
CX = 2
CY = 4
CZ = 128
PX = CX + 2
PY = CY + 2
TAPS = 27
K = TAPS * C
RANK = 4
GROUP = 3 * C
F32 = jnp.float32
BF16 = jnp.bfloat16
NT = (((1,), (1,)), ((), ()))
NN = (((1,), (0,)), ((), ()))
TN = (((0,), (0,)), ((), ()))
HIGHEST = lax.Precision.HIGHEST
VMEM = pl.BlockSpec(memory_space=pltpu.VMEM)
SMEM = pl.BlockSpec(memory_space=pltpu.SMEM)
PARAMS = pltpu.CompilerParams(vmem_limit_bytes=48 * 1024 * 1024)


def fill_planes(side, planes, own, low, high, across):
    lane = lax.broadcasted_iota(jnp.int32, (C, CZ), 1)
    zero = jnp.zeros((C, CZ), F32)

    def put(xp, yp, block):
        where = pl.ds((xp * PY + yp) * CZ, CZ)
        wide = block.astype(F32)
        before = jnp.where(lane == 0, zero, pltpu.roll(wide, 1, 1))
        after = jnp.where(lane == CZ - 1, zero, pltpu.roll(wide, CZ - 1, 1))
        planes[pl.ds(0, C), where] = before.astype(BF16)
        planes[pl.ds(C, C), where] = block
        planes[pl.ds(2 * C, C), where] = after.astype(BF16)

    first = side == 0
    for xp in range(PX):
        source = low if xp == 0 else high if xp == PX - 1 else own.at[xp - 1]
        for y in range(CY):
            put(xp, y + 1, source[y])
        edge = across[xp]
        nothing = jnp.zeros_like(edge)
        put(xp, 0, jnp.where(first, nothing, edge))
        put(xp, PY - 1, jnp.where(first, edge, nothing))


def window(planes, x, a, b):
    return planes[:, pl.ds(((x + a) * PY + b) * CZ, CY * CZ)]


def convolve(planes, lhs, x):
    total = None
    for a in range(3):
        for b in range(3):
            part = lax.dot_general(
                lhs[:, pl.ds((3 * a + b) * GROUP, GROUP)],
                window(planes, x, a, b),
                NN,
                preferred_element_type=F32,
            )
            total = part if total is None else total + part
    return total


def forward_kernel(
    side, own, low, high, across, upstream, lhs, bias, error, warm, act, grad, merged, sums, planes
):
    fill_planes(side[0], planes, own, low, high, across)
    grads = []
    bias_sum = jnp.zeros((C, CZ), F32)
    for x in range(CX):
        pre = convolve(planes, lhs, x) + bias[...]
        sigma = jax.nn.sigmoid(pre)
        active = (pre * sigma).astype(BF16)
        slope = sigma * (1.0 + pre * (1.0 - sigma))
        pieces = []
        for y in range(CY):
            span = slice(y * CZ, (y + 1) * CZ)
            act[x, y] = active[:, span]
            piece = (upstream[x, y].astype(F32) * slope[:, span]).astype(BF16)
            grad[x, y] = piece
            bias_sum = bias_sum + piece.astype(F32)
            pieces.append(piece)
        grads.append(jnp.concatenate(pieces, axis=1))
    for a in range(3):
        for b in range(3):
            span = pl.ds((3 * a + b) * GROUP, GROUP)
            part = error[:, span]
            for x in range(CX):
                part = part + lax.dot_general(
                    grads[x], window(planes, x, a, b), NT, preferred_element_type=F32
                )
            merged[:, span] = part
    local = lax.dot_general(
        warm[...], merged[...], NT, precision=HIGHEST, preferred_element_type=F32
    )
    sums[pl.ds(0, RANK), :] = local
    row = lax.dot_general(
        jnp.ones((8, CZ), F32), bias_sum, NT, precision=HIGHEST, preferred_element_type=F32
    )
    sums[pl.ds(RANK, RANK), :] = row[:RANK]


def project_kernel(sums, merged, factor_p, local_q, new_error):
    rows = []
    for r in range(RANK):
        vector = sums[pl.ds(r, 1), :]
        for basis in rows:
            vector = vector - jnp.sum(basis * vector) * basis
        vector = vector / jnp.sqrt(jnp.sum(vector * vector) + 1e-06)
        rows.append(vector)
        factor_p[pl.ds(r, 1), :] = vector
    basis = factor_p[...]
    q = lax.dot_general(basis, merged[...], NN, precision=HIGHEST, preferred_element_type=F32)
    local_q[...] = q
    new_error[...] = merged[...] - lax.dot_general(
        basis, q, TN, precision=HIGHEST, preferred_element_type=F32
    )


def backward_kernel(side, own, low, high, across, lhs, out, planes):
    fill_planes(side[0], planes, own, low, high, across)
    for x in range(CX):
        total = convolve(planes, lhs, x).astype(BF16)
        for y in range(CY):
            out[x, y] = total[:, y * CZ : (y + 1) * CZ]


def exchange(own, first):
    count = lax.axis_size("sx")
    up = [(i, i + 1) for i in range(count - 1)]
    down = [(i + 1, i) for i in range(count - 1)]
    low = lax.ppermute(own[CX - 1], "sx", up)
    high = lax.ppermute(own[0], "sx", down)
    slabs = jnp.concatenate([low[None], own, high[None]], axis=0)
    edge = jnp.where(first, slabs[:, CY - 1], slabs[:, 0])
    across = lax.ppermute(edge, "sy", [(0, 1), (1, 0)])
    return low, high, across


def reduce_all(x, axes):
    for axis in axes:
        x = lax.psum(x, axis)
    return x


def shards(features, cotangent, weights, conv_bias, error_state, warm_factor):
    side = lax.axis_index("sy").astype(jnp.int32)
    first = side == 0
    side = side.reshape(1)
    inputs = jnp.transpose(features[0], (1, 2, 0, 3))
    upstream = jnp.transpose(cotangent[0], (1, 2, 0, 3))
    lhs = jnp.transpose(weights, (1, 0, 2)).reshape(C, K)
    lhs_back = jnp.transpose(weights[::-1], (2, 0, 1)).reshape(C, K)
    low, high, across = exchange(inputs, first)
    block = jax.ShapeDtypeStruct((CX, CY, C, CZ), BF16)
    planes = pltpu.VMEM((GROUP, PX * PY * CZ), BF16)
    act, grad, merged, sums = pl.pallas_call(
        forward_kernel,
        out_shape=(
            block,
            block,
            jax.ShapeDtypeStruct((C, K), F32),
            jax.ShapeDtypeStruct((2 * RANK, C), F32),
        ),
        in_specs=[SMEM] + [VMEM] * 9,
        out_specs=(VMEM,) * 4,
        scratch_shapes=[planes],
        compiler_params=PARAMS,
        name="forward",
    )(
        side, inputs, low, high, across, upstream, lhs, conv_bias[:, None],
        error_state[0, 0, 0], warm_factor,
    )
    sums = reduce_all(sums, ("sy", "dp_0", "dp_1", "sx"))
    factor_p, local_q, new_error = pl.pallas_call(
        project_kernel,
        out_shape=(
            jax.ShapeDtypeStruct((RANK, C), F32),
            jax.ShapeDtypeStruct((RANK, K), F32),
            jax.ShapeDtypeStruct((C, K), F32),
        ),
        in_specs=[VMEM] * 2,
        out_specs=(VMEM,) * 3,
        compiler_params=PARAMS,
        name="project",
    )(sums, merged)
    g_low, g_high, g_across = exchange(grad, first)
    input_grad = pl.pallas_call(
        backward_kernel,
        out_shape=block,
        in_specs=[SMEM] + [VMEM] * 5,
        out_specs=VMEM,
        scratch_shapes=[planes],
        compiler_params=PARAMS,
        name="backward",
    )(side, grad, g_low, g_high, g_across, lhs_back)
    devices = 1
    for axis in ALL_AXES:
        devices = devices * lax.axis_size(axis)
    factor_q = reduce_all(local_q, ("sy", "dp_0", "dp_1", "sx")) / devices
    bias_grad = sums[RANK] / devices
    return (
        jnp.transpose(act, (2, 0, 1, 3))[None],
        jnp.transpose(input_grad, (2, 0, 1, 3))[None],
        bias_grad,
        factor_p,
        factor_q,
        new_error[None, None, None],
    )


def solution(mesh):
    torus = Mesh(mesh.devices.reshape(4, 8, mesh.shape["sx"], mesh.shape["sy"]), ALL_AXES)
    split = P(DP, None, "sx", "sy", None)
    state = P(DP, "sx", "sy", None, None)
    return jax.shard_map(
        shards,
        mesh=torus,
        in_specs=(split, split, P(), P(), state, P()),
        out_specs=(split, split, P(), P(), P(), state),
        check_vma=False,
    )
```

time: 280 us -> 178 us (0.64)
  matrix products: 46.2 us -> 0 us
  local copies, waits for them, and re-layouts: 48.9 us -> 14 us
  other arithmetic: 26.4 us -> 1.22 us
  Pallas kernels: 0 us -> 11.4 us
  blocking collectives: 123 us -> 112 us
  starting transfers between devices: 23.4 us -> 34.2 us
  between operations: 4.34 us -> 0.86 us
    dot_general x84 -> x0, matrix products: 46.2 us -> none  [the longest x27 24.3 us: shards(): jnp.dot(weights[tap_index], window, preferred_element_type=jnp.float32)]
    reshape x28 -> x2, local copies, waits for them, and re-layouts: 35 us -> 3.14 us  [the longest x1 1.57 us: shards(): lhs = jnp.transpose(weights, (1, 0, 2)).reshape(C, K)]
    psum x8, blocking collectives: 123 us -> 112 us  [reduce_all(): x = lax.psum(x, axis)]
    pallas_call x0 -> x3, Pallas kernels: none -> 11.4 us  [the longest x1 5.35 us: shards(): pl.pallas_call(forward_kernel, out_shape=(block, block, jax.ShapeDtypeStr...]
    concatenate x7 -> x0, other arithmetic: 11.3 us -> none  [with_halo(): block = jnp.concatenate([low, block, high], axis=dim)]
    ppermute x8 -> x6, starting transfers between devices: 23.4 us -> 34.2 us  [the longest x2 26.3 us: exchange(): across = lax.ppermute(edge, 'sy', [(0, 1), (1, 0)])]
    reduce_sum x7 -> x0, other arithmetic: 10 us -> none  [the longest x5 7.56 us: orthonormal(): vector = vector - jnp.sum(basis * vector) * basis]
    slice x6 -> x0, local copies, waits for them, and re-layouts: 6.4 us -> none  [the longest x1 3.87 us: shards(): padded[:, shift_x:shift_x + extent_x, shift_y:shift_y + extent_y, shift_z...]
  transfers between devices with their start and end apart: 8 -> 6, of which waited for: 3 -> 2; matrix products, arithmetic and copies ran while one was open for 3% -> 5% of each run, Pallas kernels for 0% -> 3%
where the time goes in v1:
time: 178 us; the launch traced here: 177 us
  blocking collectives  112 us (63%)
  starting transfers between devices  34.2 us (19%)
  local copies, waits for them, and re-layouts  14 us (8%)
  Pallas kernels  11.4 us (6%)
  waiting for transfers between devices  3.86 us (2%)
    psum x8, blocking collectives, reduce_all(): x = lax.psum(x, axis)  112 us
    ppermute x2, starting transfers between devices, exchange(): across = lax.ppermute(edge, 'sy', [(0, 1), (1, 0)])  26.3 us
    unnamed x19, local copies, waits for them, and re-layouts  8.76 us
    pallas_call x1, Pallas kernels, shards(): pl.pallas_call(forward_kernel, out_shape=(block, block, jax.ShapeDtypeStr...  5.35 us
    ppermute x2, starting transfers between devices, exchange(): low = lax.ppermute(own[CX - 1], 'sx', up)  5.33 us
    pallas_call x1, Pallas kernels, shards(): pl.pallas_call(project_kernel, out_shape=(jax.ShapeDtypeStruct((RANK, C),...  4.53 us
  transfers between devices with their start and end apart: 6, of which 2 were waited for; matrix products, arithmetic and copies ran while one was open for 5% of the time, Pallas kernels for 3%

profile of v1, /device:TPU:1, one launch (start us, length us, event | category | flops | bytes accessed | tf_op | source)
XLA Modules:
  0.0 177.1 jit_solution(11166372804015000452)
XLA Ops:
  0.6 0.0 copy-start.4
  0.6 1.1 copy.41
  1.7 4.0 %collective-permute-start = (bf16[4,128,128]{2,1,0:T(8,128)(2,1)S(1)}, bf16[4,128,128]{2,1,0:T(8,128)(2,1)S(1)}, u32[]{:S(2)}, u32[]{:S(2)}) collective-permute-start(bf16[4,128,128]{2,1,0:T(8,128)(2,1)S(1)} %get-tuple-element.35), channel_id=1, source_target_pairs={{0,2},{2,4},{4,6},{6,8},{8,10},{10,12},{12,14},{1,3},{3,5},{5,7},{... | collective-permute-start | bytes 393224 | tf_op jit(solution)/shard_map/ppermute | solution.py:142
  5.8 1.3 collective-permute-start.1
  7.1 1.0 copy.39
  8.1 0.0 collective-permute-done.low
  8.1 3.4 %collective-permute-done.1.high = bf16[4,128,128]{2,1,0:T(8,128)(2,1)S(1)} collective-permute-done((bf16[4,128,128]{2,1,0:T(8,128)(2,1)S(1)}, bf16[4,128,128]{2,1,0:T(8,128)(2,1)S(1)}, u32[]{:S(2)}, u32[]{:S(2)}) %collective-permute-start.1) | collective-permute-done | bytes 131104 | tf_op jit(solution)/shard_map/ppermute | solution.py:143
  11.5 7.2 %collective-permute-start.2 = (bf16[4,128,128]{2,1,0:T(8,128)(2,1)S(1)}, bf16[4,128,128]{2,1,0:T(8,128)(2,1)S(1)}, u32[]{:S(2)}, u32[]{:S(2)}) collective-permute-start(bf16[4,128,128]{2,1,0:T(8,128)(2,1)S(1)} %fusion.3), channel_id=1, source_target_pairs={{0,1},{1,0},{2,3},{3,2},{4,5},{5,4},{6,7},{7,6},{8,9},{9,8},{10,11... | collective-permute-start | bytes 393224 | tf_op jit(solution)/shard_map/ppermute | solution.py:146
  18.7 0.0 copy-done.4
  18.7 1.6 copy.26
  20.4 0.0 copy-start.5
  20.4 0.0 copy-start.6
  20.4 1.0 rev.3
  21.4 0.0 copy-start.3
  21.4 1.6 copy.27.lhs
  23.0 0.0 copy-done.5
  23.0 0.0 copy-done.6
  23.0 0.1 copy.28.bias
  23.1 1.6 copy.30.lhs
  24.7 0.0 collective-permute-done.2.across
  24.7 0.0 copy-done.3
  24.7 0.0 copy-start.2
  24.7 1.5 copy-done.2
  26.2 5.3 %forward.1 = (bf16[2,4,128,128]{3,2,1,0:T(8,128)(2,1)S(1)}, bf16[2,4,128,128]{3,2,1,0:T(8,128)(2,1)S(1)}, f32[128,3456]{1,0:T(8,128)S(1)}, f32[8,128]{1,0:T(8,128)S(1)}) custom-call(s32[1]{0:T(128)} %bitcast.side, bf16[2,4,128,128]{3,2,1,0:T(8,128)(2,1)S(1)} %bitcast.50, bf16[4,128,128]{2,1,0:T(8,128)(2,1)S(1)} %collective-permute-done.low, ...), custom_call_target="tpu_custom_call" | custom-call | tf_op jit(solution)/shard_map/forward/pallas_call | solution.py:167
  31.6 0.0 copy-start
  31.6 1.2 copy-done
  32.8 1.3 collective-permute-start.3
  34.1 1.3 collective-permute-start.4
  35.4 2.5 %psum.56 = f32[8,128]{1,0:T(8,128)S(1)} all-reduce(f32[8,128]{1,0:T(8,128)S(1)} %get-tuple-element.15), channel_id=1, replica_groups=mesh['dp_0'=4,'dp_1'=8,'sx'=8,'sy'=2] {'sy'}, use_global_device_ids=true, to_apply=%region_0.1 | all-reduce | flops 1024 | bytes 8192 | tf_op jit(solution)/shard_map/psum | solution.py:152
  37.9 7.2 %psum.57 = f32[8,128]{1,0:T(8,128)S(1)} all-reduce(f32[8,128]{1,0:T(8,128)S(1)} %psum.56), channel_id=1, replica_groups=mesh['dp_0'=4,'dp_1'=8,'sx'=8,'sy'=2] {'dp_0'}, use_global_device_ids=true, to_apply=%region_1.2 | all-reduce | flops 1024 | bytes 8192 | tf_op jit(solution)/shard_map/psum | solution.py:152
  45.1 19.4 %psum.58 = f32[8,128]{1,0:T(8,128)S(1)} all-reduce(f32[8,128]{1,0:T(8,128)S(1)} %psum.57), channel_id=1, replica_groups=mesh['dp_0'=4,'dp_1'=8,'sx'=8,'sy'=2] {'dp_1'}, use_global_device_ids=true, to_apply=%region_2.3 | all-reduce | flops 1024 | bytes 8192 | tf_op jit(solution)/shard_map/psum | solution.py:152
  64.5 15.6 %psum.59.sums = f32[8,128]{1,0:T(8,128)S(1)} all-reduce(f32[8,128]{1,0:T(8,128)S(1)} %psum.58), channel_id=1, replica_groups=mesh['dp_0'=4,'dp_1'=8,'sx'=8,'sy'=2] {'sx'}, use_global_device_ids=true, to_apply=%region_3.4 | all-reduce | flops 1024 | bytes 8192 | tf_op jit(solution)/shard_map/psum | solution.py:152
  80.1 0.0 copy-start.1
  80.1 1.5 copy-done.1
  81.6 4.5 %project.1 = (f32[4,128]{1,0:T(4,128)}, f32[4,3456]{1,0:T(4,128)S(1)}, f32[128,3456]{1,0:T(8,128)}) custom-call(f32[8,128]{1,0:T(8,128)S(1)} %psum.59.sums, f32[128,3456]{1,0:T(8,128)S(1)} %copy-done.1), custom_call_target="tpu_custom_call" | custom-call | tf_op jit(solution)/shard_map/project/pallas_call | solution.py:185
  86.1 13.0 %psum.60 = f32[4,3456]{1,0:T(4,128)S(1)} all-reduce(f32[4,3456]{1,0:T(4,128)S(1)} %get-tuple-element.18), channel_id=1, replica_groups=mesh['dp_0'=4,'dp_1'=8,'sx'=8,'sy'=2] {'sy'}, use_global_device_ids=true, to_apply=%region_4.5 | all-reduce | flops 13824 | bytes 110592 | tf_op jit(solution)/shard_map/psum | solution.py:152
  99.1 11.7 %psum.61 = f32[4,3456]{1,0:T(4,128)S(1)} all-reduce(f32[4,3456]{1,0:T(4,128)S(1)} %psum.60), channel_id=1, replica_groups=mesh['dp_0'=4,'dp_1'=8,'sx'=8,'sy'=2] {'dp_0'}, use_global_device_ids=true, to_apply=%region_5.6 | all-reduce | flops 13824 | bytes 110592 | tf_op jit(solution)/shard_map/psum | solution.py:152
  110.8 20.5 %psum.62 = f32[4,3456]{1,0:T(4,128)S(1)} all-reduce(f32[4,3456]{1,0:T(4,128)S(1)} %psum.61), channel_id=1, replica_groups=mesh['dp_0'=4,'dp_1'=8,'sx'=8,'sy'=2] {'dp_1'}, use_global_device_ids=true, to_apply=%region_6.7 | all-reduce | flops 13824 | bytes 110592 | tf_op jit(solution)/shard_map/psum | solution.py:152
  131.4 21.7 %psum.63 = f32[4,3456]{1,0:T(4,128)S(1)} all-reduce(f32[4,3456]{1,0:T(4,128)S(1)} %psum.62), channel_id=1, replica_groups=mesh['dp_0'=4,'dp_1'=8,'sx'=8,'sy'=2] {'sx'}, use_global_device_ids=true, to_apply=%region_7.8 | all-reduce | flops 13824 | bytes 110592 | tf_op jit(solution)/shard_map/psum | solution.py:152
  153.0 0.6 broadcast_multiply_fusion
  153.7 0.9 copy.31
  154.6 0.0 collective-permute-done.3.low
  154.6 0.0 collective-permute-done.4.high
  154.6 19.1 %collective-permute-start.5 = (bf16[4,128,128]{2,1,0:T(8,128)(2,1)S(1)}, bf16[4,128,128]{2,1,0:T(8,128)(2,1)S(1)}, u32[]{:S(2)}, u32[]{:S(2)}) collective-permute-start(bf16[4,128,128]{2,1,0:T(8,128)(2,1)S(1)} %fusion.1), channel_id=1, source_target_pairs={{0,1},{1,0},{2,3},{3,2},{4,5},{5,4},{6,7},{7,6},{8,9},{9,8},{10,11... | collective-permute-start | bytes 393224 | tf_op jit(solution)/shard_map/ppermute | solution.py:146
  173.7 0.5 multiply_bitcast_fusion
  174.2 0.4 collective-permute-done.5.across
  174.7 1.5 backward.1
  176.2 0.9 copy.32
  (5 shorter events, 0.1 us)
Async XLA Ops:
  0.6 18.1 %copy-start.4 = (bf16[27,128,128]{2,1,0:T(8,128)(2,1)S(1)}, bf16[27,128,128]{2,1,0:T(8,128)(2,1)}, u32[]{:S(2)}) copy-start(bf16[27,128,128]{2,1,0:T(8,128)(2,1)} %param.8) | copy-start | bytes 2654212
  1.7 6.3 %collective-permute-start = (bf16[4,128,128]{2,1,0:T(8,128)(2,1)S(1)}, bf16[4,128,128]{2,1,0:T(8,128)(2,1)S(1)}, u32[]{:S(2)}, u32[]{:S(2)}) collective-permute-start(bf16[4,128,128]{2,1,0:T(8,128)(2,1)S(1)} %get-tuple-element.35), channel_id=1, source_target_pairs={{0,2},{2,4},{4,6},{6,8},{8,10},{10,12},{12,14},{1,3},{3,5},{5,7},{... | collective-permute-start | bytes 393224 | tf_op jit(solution)/shard_map/ppermute | solution.py:142
  5.8 5.7 %collective-permute-start.1 = (bf16[4,128,128]{2,1,0:T(8,128)(2,1)S(1)}, bf16[4,128,128]{2,1,0:T(8,128)(2,1)S(1)}, u32[]{:S(2)}, u32[]{:S(2)}) collective-permute-start(bf16[4,128,128]{2,1,0:T(8,128)(2,1)S(1)} %get-tuple-element.34), channel_id=1, source_target_pairs={{2,0},{4,2},{6,4},{8,6},{10,8},{12,10},{14,12},{3,1},{5,3},{7,5},{... | collective-permute-start | bytes 393224 | tf_op jit(solution)/shard_map/ppermute | solution.py:143
  11.5 13.2 %collective-permute-start.2 = (bf16[4,128,128]{2,1,0:T(8,128)(2,1)S(1)}, bf16[4,128,128]{2,1,0:T(8,128)(2,1)S(1)}, u32[]{:S(2)}, u32[]{:S(2)}) collective-permute-start(bf16[4,128,128]{2,1,0:T(8,128)(2,1)S(1)} %fusion.3), channel_id=1, source_target_pairs={{0,1},{1,0},{2,3},{3,2},{4,5},{5,4},{6,7},{7,6},{8,9},{9,8},{10,11... | collective-permute-start | bytes 393224 | tf_op jit(solution)/shard_map/ppermute | solution.py:146
  20.4 2.6 %copy-start.5 = (bf16[1,128,2,4,128]{4,3,2,1,0:T(4,128)(2,1)S(1)}, bf16[1,128,2,4,128]{4,3,2,1,0:T(4,128)(2,1)}, u32[]{:S(2)}) copy-start(bf16[1,128,2,4,128]{4,3,2,1,0:T(4,128)(2,1)} %param.7) | copy-start | bytes 786436
  20.4 2.6 %copy-start.6 = (f32[128]{0:T(128)S(1)}, f32[128]{0:T(128)}, u32[]{:S(2)}) copy-start(f32[128]{0:T(128)} %param.9) | copy-start | bytes 1540
  21.4 3.3 %copy-start.3 = (f32[4,3456]{1,0:T(4,128)S(1)}, f32[4,3456]{1,0:T(4,128)}, u32[]{:S(2)}) copy-start(f32[4,3456]{1,0:T(4,128)} %warm.1) | copy-start | bytes 165892
  24.7 1.5 copy-start.2
  31.6 1.2 copy-start
  32.8 121.7 %collective-permute-start.3 = (bf16[4,128,128]{2,1,0:T(8,128)(2,1)S(1)}, bf16[4,128,128]{2,1,0:T(8,128)(2,1)S(1)}, u32[]{:S(2)}, u32[]{:S(2)}) collective-permute-start(bf16[4,128,128]{2,1,0:T(8,128)(2,1)S(1)} %get-tuple-element.33), channel_id=1, source_target_pairs={{0,2},{2,4},{4,6},{6,8},{8,10},{10,12},{12,14},{1,3},{3,5},{5,7},{... | collective-permute-start | bytes 393224 | tf_op jit(solution)/shard_map/ppermute | solution.py:142
  34.1 120.4 %collective-permute-start.4 = (bf16[4,128,128]{2,1,0:T(8,128)(2,1)S(1)}, bf16[4,128,128]{2,1,0:T(8,128)(2,1)S(1)}, u32[]{:S(2)}, u32[]{:S(2)}) collective-permute-start(bf16[4,128,128]{2,1,0:T(8,128)(2,1)S(1)} %get-tuple-element.32), channel_id=1, source_target_pairs={{2,0},{4,2},{6,4},{8,6},{10,8},{12,10},{14,12},{3,1},{5,3},{7,5},{... | collective-permute-start | bytes 393224 | tf_op jit(solution)/shard_map/ppermute | solution.py:143
  80.1 1.5 copy-start.1
  154.6 20.1 %collective-permute-start.5 = (bf16[4,128,128]{2,1,0:T(8,128)(2,1)S(1)}, bf16[4,128,128]{2,1,0:T(8,128)(2,1)S(1)}, u32[]{:S(2)}, u32[]{:S(2)}) collective-permute-start(bf16[4,128,128]{2,1,0:T(8,128)(2,1)S(1)} %fusion.1), channel_id=1, source_target_pairs={{0,1},{1,0},{2,3},{3,2},{4,5},{5,4},{6,7},{7,6},{8,9},{9,8},{10,11... | collective-permute-start | bytes 393224 | tf_op jit(solution)/shard_map/ppermute | solution.py:146

commit v2 on v1

--- a/solution.py
+++ b/solution.py
@@ -1,3 +1,5 @@
+import functools
+
 import jax
 import jax.numpy as jnp
 from jax import lax
@@ -7,6 +9,7 @@
 from jax.sharding import PartitionSpec as P
 
 DP = ("dp_0", "dp_1")
+BLOCK = ("sx", "sy")
 ALL_AXES = ("dp_0", "dp_1", "sx", "sy")
 C = 128
 CX = 2
@@ -71,26 +74,26 @@
     return total
 
 
-def forward_kernel(
-    side, own, low, high, across, upstream, lhs, bias, error, warm, act, grad, merged, sums, planes
-):
+def forward_kernel(side, own, low, high, across, upstream, lhs, bias, act, grad, planes):
     fill_planes(side[0], planes, own, low, high, across)
-    grads = []
-    bias_sum = jnp.zeros((C, CZ), F32)
     for x in range(CX):
         pre = convolve(planes, lhs, x) + bias[...]
         sigma = jax.nn.sigmoid(pre)
         active = (pre * sigma).astype(BF16)
         slope = sigma * (1.0 + pre * (1.0 - sigma))
-        pieces = []
         for y in range(CY):
             span = slice(y * CZ, (y + 1) * CZ)
             act[x, y] = active[:, span]
-            piece = (upstream[x, y].astype(F32) * slope[:, span]).astype(BF16)
-            grad[x, y] = piece
-            bias_sum = bias_sum + piece.astype(F32)
-            pieces.append(piece)
-        grads.append(jnp.concatenate(pieces, axis=1))
+            grad[x, y] = (upstream[x, y].astype(F32) * slope[:, span]).astype(BF16)
+
+
+def gradient_kernel(grad, planes, error, warm, merged, sums):
+    grads = []
+    bias_sum = jnp.zeros((C, CZ), F32)
+    for x in range(CX):
+        grads.append(jnp.concatenate([grad[x, y] for y in range(CY)], axis=1))
+        for y in range(CY):
+            bias_sum = bias_sum + grad[x, y].astype(F32)
     for a in range(3):
         for b in range(3):
             span = pl.ds((3 * a + b) * GROUP, GROUP)
@@ -103,17 +106,30 @@
     local = lax.dot_general(
         warm[...], merged[...], NT, precision=HIGHEST, preferred_element_type=F32
     )
-    sums[pl.ds(0, RANK), :] = local
     row = lax.dot_general(
         jnp.ones((8, CZ), F32), bias_sum, NT, precision=HIGHEST, preferred_element_type=F32
     )
-    sums[pl.ds(RANK, RANK), :] = row[:RANK]
-
-
-def project_kernel(sums, merged, factor_p, local_q, new_error):
+    both = jnp.concatenate([local, row[:RANK]], axis=0)
+    for copy in range(sums.shape[0]):
+        sums[copy] = both
+
+
+def fold_kernel(parts, copies):
+    total = parts[0]
+    for source in range(1, parts.shape[0]):
+        total = total + parts[source]
+    for copy in range(copies.shape[0]):
+        copies[copy] = total
+
+
+def project_kernel(parts, merged, factor_p, bias_grad, blocks, new_error, *, devices):
+    sums = parts[0]
+    for source in range(1, parts.shape[0]):
+        sums = sums + parts[source]
+    bias_grad[...] = sums[RANK : RANK + 1] / devices
     rows = []
     for r in range(RANK):
-        vector = sums[pl.ds(r, 1), :]
+        vector = sums[r : r + 1]
         for basis in rows:
             vector = vector - jnp.sum(basis * vector) * basis
         vector = vector / jnp.sqrt(jnp.sum(vector * vector) + 1e-06)
@@ -121,10 +137,19 @@
         factor_p[pl.ds(r, 1), :] = vector
     basis = factor_p[...]
     q = lax.dot_general(basis, merged[...], NN, precision=HIGHEST, preferred_element_type=F32)
-    local_q[...] = q
+    for block in range(blocks.shape[0]):
+        if block < TAPS:
+            blocks[block] = q[:, block * C : (block + 1) * C]
+        else:
+            blocks[block] = jnp.zeros((RANK, C), F32)
     new_error[...] = merged[...] - lax.dot_general(
         basis, q, TN, precision=HIGHEST, preferred_element_type=F32
     )
+
+
+def finish_kernel(blocks, factor_q, *, devices):
+    for tap in range(TAPS):
+        factor_q[:, pl.ds(tap * C, C)] = blocks[tap] / devices
 
 
 def backward_kernel(side, own, low, high, across, lhs, out, planes):
@@ -147,72 +172,99 @@
     return low, high, across
 
 
-def reduce_all(x, axes):
+def size_of(axes):
+    count = 1
     for axis in axes:
-        x = lax.psum(x, axis)
-    return x
+        count = count * lax.axis_size(axis)
+    return count
+
+
+def swap(x, axes):
+    return lax.all_to_all(x, axes, 0, 0, tiled=True)
+
+
+def call(kernel, name, shapes, args, scalars=0, scratch=()):
+    return pl.pallas_call(
+        kernel,
+        out_shape=shapes,
+        in_specs=[SMEM] * scalars + [VMEM] * (len(args) - scalars),
+        out_specs=jax.tree.map(lambda _: VMEM, shapes),
+        scratch_shapes=list(scratch),
+        compiler_params=PARAMS,
+        name=name,
+    )(*args)
+
+
+def fold(parts, count):
+    shape = jax.ShapeDtypeStruct((count,) + parts.shape[1:], F32)
+    return call(fold_kernel, "fold", shape, (parts,))
 
 
 def shards(features, cotangent, weights, conv_bias, error_state, warm_factor):
     side = lax.axis_index("sy").astype(jnp.int32)
     first = side == 0
     side = side.reshape(1)
+    chips, columns = size_of(DP), size_of(BLOCK)
+    devices = chips * columns
     inputs = jnp.transpose(features[0], (1, 2, 0, 3))
     upstream = jnp.transpose(cotangent[0], (1, 2, 0, 3))
     lhs = jnp.transpose(weights, (1, 0, 2)).reshape(C, K)
     lhs_back = jnp.transpose(weights[::-1], (2, 0, 1)).reshape(C, K)
     low, high, across = exchange(inputs, first)
     block = jax.ShapeDtypeStruct((CX, CY, C, CZ), BF16)
-    planes = pltpu.VMEM((GROUP, PX * PY * CZ), BF16)
-    act, grad, merged, sums = pl.pallas_call(
+    plane_shape = (GROUP, PX * PY * CZ)
+    act, grad, planes = call(
         forward_kernel,
-        out_shape=(
-            block,
-            block,
+        "forward",
+        (block, block, jax.ShapeDtypeStruct(plane_shape, BF16)),
+        (side, inputs, low, high, across, upstream, lhs, conv_bias[:, None]),
+        scalars=1,
+    )
+    g_low, g_high, g_across = exchange(grad, first)
+    merged, sums = call(
+        gradient_kernel,
+        "gradient",
+        (
             jax.ShapeDtypeStruct((C, K), F32),
-            jax.ShapeDtypeStruct((2 * RANK, C), F32),
+            jax.ShapeDtypeStruct((chips, 2 * RANK, C), F32),
         ),
-        in_specs=[SMEM] + [VMEM] * 9,
-        out_specs=(VMEM,) * 4,
-        scratch_shapes=[planes],
-        compiler_params=PARAMS,
-        name="forward",
-    )(
-        side, inputs, low, high, across, upstream, lhs, conv_bias[:, None],
-        error_state[0, 0, 0], warm_factor,
-    )
-    sums = reduce_all(sums, ("sy", "dp_0", "dp_1", "sx"))
-    factor_p, local_q, new_error = pl.pallas_call(
-        project_kernel,
-        out_shape=(
+        (grad, planes, error_state[0, 0, 0], warm_factor),
+    )
+    parts = swap(fold(swap(sums, DP), columns), BLOCK)
+    padded = -(-TAPS // columns) * columns
+    factor_p, bias_grad, blocks, new_error = call(
+        functools.partial(project_kernel, devices=devices),
+        "project",
+        (
             jax.ShapeDtypeStruct((RANK, C), F32),
-            jax.ShapeDtypeStruct((RANK, K), F32),
+            jax.ShapeDtypeStruct((1, C), F32),
+            jax.ShapeDtypeStruct((padded, RANK, C), F32),
             jax.ShapeDtypeStruct((C, K), F32),
         ),
-        in_specs=[VMEM] * 2,
-        out_specs=(VMEM,) * 3,
-        compiler_params=PARAMS,
-        name="project",
-    )(sums, merged)
-    g_low, g_high, g_across = exchange(grad, first)
-    input_grad = pl.pallas_call(
+        (parts, merged),
+    )
+    input_grad = call(
         backward_kernel,
-        out_shape=block,
-        in_specs=[SMEM] + [VMEM] * 5,
-        out_specs=VMEM,
-        scratch_shapes=[planes],
-        compiler_params=PARAMS,
-        name="backward",
-    )(side, grad, g_low, g_high, g_across, lhs_back)
-    devices = 1
-    for axis in ALL_AXES:
-        devices = devices * lax.axis_size(axis)
-    factor_q = reduce_all(local_q, ("sy", "dp_0", "dp_1", "sx")) / devices
-    bias_grad = sums[RANK] / devices
+        "backward",
+        block,
+        (side, grad, g_low, g_high, g_across, lhs_back),
+        scalars=1,
+        scratch=[pltpu.VMEM(plane_shape, BF16)],
+    )
+    width = padded // columns * RANK
+    mine = fold(swap(blocks, BLOCK).reshape(columns, width, C), chips)
+    mine = fold(swap(mine, DP), columns)
+    blocks = swap(mine, BLOCK).reshape(padded, RANK, C)
+    factor_q = call(
+        functools.partial(finish_kernel, devices=devices),
+        "finish",
+        jax.ShapeDtypeStruct((RANK, K), F32),
+        (blocks,),
+    )
     return (
         jnp.transpose(act, (2, 0, 1, 3))[None],
         jnp.transpose(input_grad, (2, 0, 1, 3))[None],
-        bias_grad,
+        bias_grad[0],
         factor_p,
         factor_q,
         new_error[None, None, None],

time: 178 us -> 119 us (0.67)
  blocking collectives: 112 us -> 35.6 us
  waiting for transfers between devices: 3.86 us -> 17.2 us
  Pallas kernels: 11.4 us -> 16.3 us
    psum x8 -> x0, blocking collectives: 112 us -> none  [reduce_all(): x = lax.psum(x, axis)]
    all_to_all x0 -> x2, blocking collectives: none -> 35.6 us  [swap(): return lax.all_to_all(x, axes, 0, 0, tiled=True)]
    ppermute x2, starting transfers between devices: 26.3 us -> 9.28 us  [exchange(): across = lax.ppermute(edge, 'sy', [(0, 1), (1, 0)])]
    all_to_all x0 -> x3, starting transfers between devices: none -> 14.8 us  [swap(): return lax.all_to_all(x, axes, 0, 0, tiled=True)]
    all_to_all x0 -> x3, waiting for transfers between devices: none -> 13.8 us  [swap(): return lax.all_to_all(x, axes, 0, 0, tiled=True)]
    pallas_call x3 -> x8, Pallas kernels: 11.4 us -> 16.3 us  [call(): pl.pallas_call(kernel, out_shape=shapes, in_specs=[SMEM] * scalars + [VME...]
    ppermute x2, starting transfers between devices: 5.33 us -> 7.34 us  [exchange(): low = lax.ppermute(own[CX - 1], 'sx', up)]
    unnamed x19 -> x29, local copies, waits for them, and re-layouts: 8.76 us -> 9.64 us
  transfers between devices with their start and end apart: 6 -> 9, of which waited for: 2 -> 4; matrix products, arithmetic and copies ran while one was open for 5% -> 7% of each run, Pallas kernels for 3% -> 2%
where the time goes in v2:
time: 119 us; the launch traced here: 118 us
  blocking collectives  35.6 us (30%)
  starting transfers between devices  34 us (29%)
  waiting for transfers between devices  17.2 us (14%)
  Pallas kernels  16.3 us (14%)
  local copies, waits for them, and re-layouts  13.6 us (11%)
    all_to_all x2, blocking collectives, swap(): return lax.all_to_all(x, axes, 0, 0, tiled=True)  35.6 us
    pallas_call x8, Pallas kernels, call(): pl.pallas_call(kernel, out_shape=shapes, in_specs=[SMEM] * scalars + [VME...  16.3 us
    all_to_all x3, starting transfers between devices, swap(): return lax.all_to_all(x, axes, 0, 0, tiled=True)  14.8 us
    all_to_all x3, waiting for transfers between devices, swap(): return lax.all_to_all(x, axes, 0, 0, tiled=True)  13.8 us
    unnamed x29, local copies, waits for them, and re-layouts  9.64 us
    ppermute x2, starting transfers between devices, exchange(): across = lax.ppermute(edge, 'sy', [(0, 1), (1, 0)])  9.28 us
    ppermute x2, starting transfers between devices, exchange(): low = lax.ppermute(own[CX - 1], 'sx', up)  7.34 us
    ppermute x2, waiting for transfers between devices, exchange(): high = lax.ppermute(own[0], 'sx', down)  3.39 us
  transfers between devices with their start and end apart: 9, of which 4 were waited for; matrix products, arithmetic and copies ran while one was open for 7% of the time, Pallas kernels for 2%

profile of v2, /device:TPU:1, one launch (start us, length us, event | category | flops | bytes accessed | tf_op | source)
XLA Modules:
  0.0 118.4 jit_solution(9560672995290192385)
XLA Ops:
  0.6 0.0 copy-start.9
  0.6 1.1 copy.41
  1.7 4.0 %collective-permute-start = (bf16[4,128,128]{2,1,0:T(8,128)(2,1)S(1)}, bf16[4,128,128]{2,1,0:T(8,128)(2,1)S(1)}, u32[]{:S(2)}, u32[]{:S(2)}) collective-permute-start(bf16[4,128,128]{2,1,0:T(8,128)(2,1)S(1)} %get-tuple-element.39), channel_id=1, source_target_pairs={{0,2},{2,4},{4,6},{6,8},{8,10},{10,12},{12,14},{1,3},{3,5},{5,7},{... | collective-permute-start | bytes 393224 | tf_op jit(solution)/shard_map/ppermute | solution.py:167
  5.8 1.3 %collective-permute-start.1 = (bf16[4,128,128]{2,1,0:T(8,128)(2,1)S(1)}, bf16[4,128,128]{2,1,0:T(8,128)(2,1)S(1)}, u32[]{:S(2)}, u32[]{:S(2)}) collective-permute-start(bf16[4,128,128]{2,1,0:T(8,128)(2,1)S(1)} %get-tuple-element.38), channel_id=1, source_target_pairs={{2,0},{4,2},{6,4},{8,6},{10,8},{12,10},{14,12},{3,1},{5,3},{7,5},{... | collective-permute-start | bytes 393224 | tf_op jit(solution)/shard_map/ppermute | solution.py:168
  7.1 1.0 copy.39
  8.1 0.0 collective-permute-done.low
  8.1 0.0 copy-start.2
  8.1 3.4 %collective-permute-done.1.high = bf16[4,128,128]{2,1,0:T(8,128)(2,1)S(1)} collective-permute-done((bf16[4,128,128]{2,1,0:T(8,128)(2,1)S(1)}, bf16[4,128,128]{2,1,0:T(8,128)(2,1)S(1)}, u32[]{:S(2)}, u32[]{:S(2)}) %collective-permute-start.1) | collective-permute-done | bytes 131104 | tf_op jit(solution)/shard_map/ppermute | solution.py:168
  11.5 0.0 copy-start.4
  11.5 0.7 fusion.3
  12.2 0.0 copy-start.11
  12.2 7.3 %collective-permute-start.2 = (bf16[4,128,128]{2,1,0:T(8,128)(2,1)}, bf16[4,128,128]{2,1,0:T(8,128)(2,1)}, u32[]{:S(2)}, u32[]{:S(2)}) collective-permute-start(bf16[4,128,128]{2,1,0:T(8,128)(2,1)} %fusion.3), channel_id=1, source_target_pairs={{0,1},{1,0},{2,3},{3,2},{4,5},{5,4},{6,7},{7,6},{8,9},{9,8},{10,11... | collective-permute-start | bytes 393224 | tf_op jit(solution)/shard_map/ppermute | solution.py:171
  19.5 0.0 copy-done.9
  19.5 1.6 %copy.26 = bf16[27,128,128]{1,2,0:T(8,128)(2,1)} copy(bf16[27,128,128]{2,1,0:T(8,128)(2,1)S(1)} %copy-done.9) | data formatting | bytes 1769472 | tf_op args[2]
  21.2 0.0 copy-start.1
  21.2 1.7 %copy.27.lhs = bf16[128,3456]{1,0:T(8,128)(2,1)S(1)} copy(bf16[128,3456]{0,1:T(8,128)(2,1)} %bitcast.62) | data formatting | bytes 1769472 | tf_op jit(solution)/shard_map/reshape | solution.py:211
  22.9 0.0 copy-done.2
  22.9 0.0 copy-done.4
  22.9 1.0 copy.40
  23.9 0.0 copy-done.11
  23.9 0.1 copy.28.bias
  24.0 0.0 collective-permute-done.2.across
  24.0 0.0 copy-start.3
  24.0 0.9 copy-done.3
  24.9 0.0 copy-start.5
  24.9 0.9 copy-done.5
  25.8 2.6 %forward.1 = (bf16[2,4,128,128]{3,2,1,0:T(8,128)(2,1)S(1)}, bf16[2,4,128,128]{3,2,1,0:T(8,128)(2,1)S(1)}, bf16[384,3072]{1,0:T(8,128)(2,1)S(1)}) custom-call(s32[1]{0:T(128)} %bitcast.side, bf16[2,4,128,128]{3,2,1,0:T(8,128)(2,1)S(1)} %bitcast.51, bf16[4,128,128]{2,1,0:T(8,128)(2,1)S(1)} %copy-done.3, bf16[4,128,128]{2,1,0:T(8,128)(2,1)S(1)} %copy-done.5, ...), custom_call_target="tpu_custom_call" | custom-call | tf_op jit(solution)/shard_map/forward/pallas_call | solution.py:187
  28.4 0.0 copy-start
  28.4 1.4 %copy-done = bf16[384,3072]{1,0:T(8,128)(2,1)} copy-done((bf16[384,3072]{1,0:T(8,128)(2,1)}, bf16[384,3072]{1,0:T(8,128)(2,1)S(1)}, u32[]{:S(2)}) %copy-start) | copy-done | bytes 2359320
  29.9 0.0 copy-start.6
  29.9 0.0 copy-done.1
  29.9 0.0 copy-start.8
  29.9 0.9 copy-done.8
  30.7 5.6 %gradient.1 = (f32[128,3456]{1,0:T(8,128)S(1)}, f32[32,8,128]{2,1,0:T(8,128)S(1)}) custom-call(bf16[2,4,128,128]{3,2,1,0:T(8,128)(2,1)S(1)} %get-tuple-element.16.own.grad, bf16[384,3072]{1,0:T(8,128)(2,1)} %copy-done, f32[128,3456]{1,0:T(8,128)S(1)} %bitcast.52, f32[4,3456]{1,0:T(4,128)S(1)} %copy-done.8), custom_call_target="tpu_custom_call" | custom-call | tf_op jit(solution)/shard_map/gradient/pallas_call | solution.py:187
  36.4 0.0 copy-done.6
  36.4 18.7 %all_to_all.25.parts = f32[32,8,128]{2,1,0:T(8,128)S(1)} all-to-all(f32[32,8,128]{2,1,0:T(8,128)S(1)} %get-tuple-element.18), channel_id=1, replica_groups=mesh['dp_0'=4,'dp_1'=8,'sx'=8,'sy'=2] {'dp_0','dp_1'}, dimensions={0} | all-to-all | bytes 262144 | tf_op jit(solution)/shard_map/all_to_all | solution.py:183
  55.1 17.0 %all_to_all.26.parts = f32[16,8,128]{2,1,0:T(8,128)S(1)} all-to-all(f32[16,8,128]{2,1,0:T(8,128)S(1)} %fold.3), channel_id=1, replica_groups=mesh['dp_0'=4,'dp_1'=8,'sx'=8,'sy'=2] {'sx','sy'}, dimensions={0} | all-to-all | bytes 131072 | tf_op jit(solution)/shard_map/all_to_all | solution.py:183
  72.1 0.0 copy-start.10
  72.1 4.6 %project.1 = (f32[4,128]{1,0:T(4,128)}, f32[1,128]{1,0:T(1,128)}, f32[32,4,128]{2,1,0:T(4,128)}, f32[128,3456]{1,0:T(8,128)}) custom-call(f32[16,8,128]{2,1,0:T(8,128)S(1)} %all_to_all.26.parts, f32[128,3456]{1,0:T(8,128)S(1)} %get-tuple-element.19.merged), custom_call_target="tpu_custom_call" | custom-call | tf_op jit(solution)/shard_map/project/pallas_call | solution.py:187
  76.6 3.5 %all-to-all-start.2 = ((f32[32,4,128]{2,1,0:T(4,128)}), f32[32,4,128]{2,1,0:T(4,128)S(1)}, u32[]{:S(2)}, u32[]{:S(2)}) async-start(f32[32,4,128]{2,1,0:T(4,128)} %get-tuple-element.22), calls=%async_computation.2 | async-start | bytes 131072 | tf_op jit(solution)/shard_map/all_to_all | solution.py:183
  80.1 3.3 %collective-permute-start.3 = (bf16[4,128,128]{2,1,0:T(8,128)(2,1)S(1)}, bf16[4,128,128]{2,1,0:T(8,128)(2,1)S(1)}, u32[]{:S(2)}, u32[]{:S(2)}) collective-permute-start(bf16[4,128,128]{2,1,0:T(8,128)(2,1)S(1)} %get-tuple-element.37), channel_id=1, source_target_pairs={{0,2},{2,4},{4,6},{6,8},{8,10},{10,12},{12,14},{1,3},{3,5},{5,7},{... | collective-permute-start | bytes 393224 | tf_op jit(solution)/shard_map/ppermute | solution.py:167
  83.4 1.3 %collective-permute-start.4 = (bf16[4,128,128]{2,1,0:T(8,128)(2,1)S(1)}, bf16[4,128,128]{2,1,0:T(8,128)(2,1)S(1)}, u32[]{:S(2)}, u32[]{:S(2)}) collective-permute-start(bf16[4,128,128]{2,1,0:T(8,128)(2,1)S(1)} %get-tuple-element.36), channel_id=1, source_target_pairs={{2,0},{4,2},{6,4},{8,6},{10,8},{12,10},{14,12},{3,1},{5,3},{7,5},{... | collective-permute-start | bytes 393224 | tf_op jit(solution)/shard_map/ppermute | solution.py:168
  84.7 3.3 %all-to-all-done.2 = f32[32,4,128]{2,1,0:T(4,128)S(1)} async-done(((f32[32,4,128]{2,1,0:T(4,128)}), f32[32,4,128]{2,1,0:T(4,128)S(1)}, u32[]{:S(2)}, u32[]{:S(2)}) %all-to-all-start.2) | async-done | bytes 65568 | tf_op jit(solution)/shard_map/all_to_all | solution.py:183
  88.0 0.7 fold.4
  88.7 3.9 %all-to-all-start.3 = ((f32[32,8,128]{2,1,0:T(8,128)}), f32[32,8,128]{2,1,0:T(8,128)S(1)}, u32[]{:S(2)}, u32[]{:S(2)}) async-start(f32[32,8,128]{2,1,0:T(8,128)} %fold.4), calls=%async_computation.3 | async-start | bytes 262144 | tf_op jit(solution)/shard_map/all_to_all | solution.py:183
  92.6 0.0 collective-permute-done.3.low
  92.6 0.0 collective-permute-done.4.high
  92.6 2.0 %collective-permute-start.5 = (bf16[4,128,128]{2,1,0:T(8,128)(2,1)S(1)}, bf16[4,128,128]{2,1,0:T(8,128)(2,1)S(1)}, u32[]{:S(2)}, u32[]{:S(2)}) collective-permute-start(bf16[4,128,128]{2,1,0:T(8,128)(2,1)S(1)} %fusion.1), channel_id=1, source_target_pairs={{0,1},{1,0},{2,3},{3,2},{4,5},{5,4},{6,7},{7,6},{8,9},{9,8},{10,11... | collective-permute-start | bytes 393224 | tf_op jit(solution)/shard_map/ppermute | solution.py:171
  94.6 7.2 %all-to-all-done.3.parts = f32[32,8,128]{2,1,0:T(8,128)S(1)} async-done(((f32[32,8,128]{2,1,0:T(8,128)}), f32[32,8,128]{2,1,0:T(8,128)S(1)}, u32[]{:S(2)}, u32[]{:S(2)}) %all-to-all-start.3) | async-done | bytes 131104 | tf_op jit(solution)/shard_map/all_to_all | solution.py:183
  101.8 0.7 fold.5
  102.5 7.5 %all-to-all-start.4 = ((f32[16,8,128]{2,1,0:T(8,128)}), f32[16,8,128]{2,1,0:T(8,128)S(1)}, u32[]{:S(2)}, u32[]{:S(2)}) async-start(f32[16,8,128]{2,1,0:T(8,128)} %fold.5), calls=%async_computation.4 | async-start | bytes 131072 | tf_op jit(solution)/shard_map/all_to_all | solution.py:183
  109.9 0.0 copy-done.10
  109.9 0.0 copy-start.7
  110.0 0.1 rev.3
  110.0 1.0 copy.30.lhs
  111.1 0.0 copy-done.7
  111.1 0.9 copy.31
  112.0 0.0 collective-permute-done.5.across
  112.0 1.5 %backward.1 = bf16[2,4,128,128]{3,2,1,0:T(8,128)(2,1)S(1)} custom-call(s32[1]{0:T(128)} %bitcast.side, bf16[2,4,128,128]{3,2,1,0:T(8,128)(2,1)S(1)} %get-tuple-element.16.own.grad, bf16[4,128,128]{2,1,0:T(8,128)(2,1)S(1)} %collective-permute-done.3.low, bf16[4,128,128]{2,1,0:T(8,128)(2,1)S(1)} %collective-permute-done.4.high, ...), custom_call_target="tpu_custom_call" | custom-call | tf_op jit(solution)/shard_map/backward/pallas_call | solution.py:187
  113.5 0.9 copy.32
  114.4 3.3 %all-to-all-done.4 = f32[16,8,128]{2,1,0:T(8,128)S(1)} async-done(((f32[16,8,128]{2,1,0:T(8,128)}), f32[16,8,128]{2,1,0:T(8,128)S(1)}, u32[]{:S(2)}, u32[]{:S(2)}) %all-to-all-start.4) | async-done | bytes 65568 | tf_op jit(solution)/shard_map/all_to_all | solution.py:183
  117.7 0.6 finish.1
  (4 shorter events, 0.1 us)
Async XLA Ops:
  0.6 18.9 %copy-start.9 = (bf16[27,128,128]{2,1,0:T(8,128)(2,1)S(1)}, bf16[27,128,128]{2,1,0:T(8,128)(2,1)}, u32[]{:S(2)}) copy-start(bf16[27,128,128]{2,1,0:T(8,128)(2,1)} %param.8) | copy-start | bytes 2654212
  1.7 6.3 %collective-permute-start = (bf16[4,128,128]{2,1,0:T(8,128)(2,1)S(1)}, bf16[4,128,128]{2,1,0:T(8,128)(2,1)S(1)}, u32[]{:S(2)}, u32[]{:S(2)}) collective-permute-start(bf16[4,128,128]{2,1,0:T(8,128)(2,1)S(1)} %get-tuple-element.39), channel_id=1, source_target_pairs={{0,2},{2,4},{4,6},{6,8},{8,10},{10,12},{12,14},{1,3},{3,5},{5,7},{... | collective-permute-start | bytes 393224 | tf_op jit(solution)/shard_map/ppermute | solution.py:167
  5.8 5.7 %collective-permute-start.1 = (bf16[4,128,128]{2,1,0:T(8,128)(2,1)S(1)}, bf16[4,128,128]{2,1,0:T(8,128)(2,1)S(1)}, u32[]{:S(2)}, u32[]{:S(2)}) collective-permute-start(bf16[4,128,128]{2,1,0:T(8,128)(2,1)S(1)} %get-tuple-element.38), channel_id=1, source_target_pairs={{2,0},{4,2},{6,4},{8,6},{10,8},{12,10},{14,12},{3,1},{5,3},{7,5},{... | collective-permute-start | bytes 393224 | tf_op jit(solution)/shard_map/ppermute | solution.py:168
  8.1 14.8 %copy-start.2 = (bf16[4,128,128]{2,1,0:T(8,128)(2,1)}, bf16[4,128,128]{2,1,0:T(8,128)(2,1)S(1)}, u32[]{:S(2)}) copy-start(bf16[4,128,128]{2,1,0:T(8,128)(2,1)S(1)} %collective-permute-done.low) | copy-start | bytes 393220
  11.5 11.4 %copy-start.4 = (bf16[4,128,128]{2,1,0:T(8,128)(2,1)}, bf16[4,128,128]{2,1,0:T(8,128)(2,1)S(1)}, u32[]{:S(2)}) copy-start(bf16[4,128,128]{2,1,0:T(8,128)(2,1)S(1)} %collective-permute-done.1.high) | copy-start | bytes 393220
  12.2 11.7 %copy-start.11 = (f32[128]{0:T(128)S(1)}, f32[128]{0:T(128)}, u32[]{:S(2)}) copy-start(f32[128]{0:T(128)} %param.9) | copy-start | bytes 1540
  12.2 11.8 %collective-permute-start.2 = (bf16[4,128,128]{2,1,0:T(8,128)(2,1)}, bf16[4,128,128]{2,1,0:T(8,128)(2,1)}, u32[]{:S(2)}, u32[]{:S(2)}) collective-permute-start(bf16[4,128,128]{2,1,0:T(8,128)(2,1)} %fusion.3), channel_id=1, source_target_pairs={{0,1},{1,0},{2,3},{3,2},{4,5},{5,4},{6,7},{7,6},{8,9},{9,8},{10,11... | collective-permute-start | bytes 393224 | tf_op jit(solution)/shard_map/ppermute | solution.py:171
  21.2 8.7 %copy-start.1 = (f32[1,1,1,128,3456]{4,3,2,1,0:T(8,128)S(1)}, f32[1,1,1,128,3456]{4,3,2,1,0:T(8,128)}, u32[]{:S(2)}) copy-start(f32[1,1,1,128,3456]{4,3,2,1,0:T(8,128)} %param.10) | copy-start | bytes 5308420
  24.0 0.9 copy-start.3
  24.9 0.9 copy-start.5
  28.4 1.4 %copy-start = (bf16[384,3072]{1,0:T(8,128)(2,1)}, bf16[384,3072]{1,0:T(8,128)(2,1)S(1)}, u32[]{:S(2)}) copy-start(bf16[384,3072]{1,0:T(8,128)(2,1)S(1)} %get-tuple-element.17.planes) | copy-start | bytes 7077892
  29.9 6.5 %copy-start.6 = (bf16[2,4,128,128]{3,2,1,0:T(8,128)(2,1)}, bf16[2,4,128,128]{3,2,1,0:T(8,128)(2,1)S(1)}, u32[]{:S(2)}) copy-start(bf16[2,4,128,128]{3,2,1,0:T(8,128)(2,1)S(1)} %get-tuple-element.15) | copy-start | bytes 786436
  29.9 0.9 copy-start.8
  72.1 37.9 %copy-start.10 = (bf16[27,128,128]{2,1,0:T(8,128)(2,1)S(1)}, bf16[27,128,128]{2,1,0:T(8,128)(2,1)}, u32[]{:S(2)}) copy-start(bf16[27,128,128]{2,1,0:T(8,128)(2,1)} %param.8) | copy-start | bytes 2654212
  76.6 11.4 %all-to-all-start.2 = ((f32[32,4,128]{2,1,0:T(4,128)}), f32[32,4,128]{2,1,0:T(4,128)S(1)}, u32[]{:S(2)}, u32[]{:S(2)}) async-start(f32[32,4,128]{2,1,0:T(4,128)} %get-tuple-element.22), calls=%async_computation.2 | async-start | bytes 131072 | tf_op jit(solution)/shard_map/all_to_all | solution.py:183
  80.1 12.5 %collective-permute-start.3 = (bf16[4,128,128]{2,1,0:T(8,128)(2,1)S(1)}, bf16[4,128,128]{2,1,0:T(8,128)(2,1)S(1)}, u32[]{:S(2)}, u32[]{:S(2)}) collective-permute-start(bf16[4,128,128]{2,1,0:T(8,128)(2,1)S(1)} %get-tuple-element.37), channel_id=1, source_target_pairs={{0,2},{2,4},{4,6},{6,8},{8,10},{10,12},{12,14},{1,3},{3,5},{5,7},{... | collective-permute-start | bytes 393224 | tf_op jit(solution)/shard_map/ppermute | solution.py:167
  83.4 9.2 %collective-permute-start.4 = (bf16[4,128,128]{2,1,0:T(8,128)(2,1)S(1)}, bf16[4,128,128]{2,1,0:T(8,128)(2,1)S(1)}, u32[]{:S(2)}, u32[]{:S(2)}) collective-permute-start(bf16[4,128,128]{2,1,0:T(8,128)(2,1)S(1)} %get-tuple-element.36), channel_id=1, source_target_pairs={{2,0},{4,2},{6,4},{8,6},{10,8},{12,10},{14,12},{3,1},{5,3},{7,5},{... | collective-permute-start | bytes 393224 | tf_op jit(solution)/shard_map/ppermute | solution.py:168
  88.7 13.1 %all-to-all-start.3 = ((f32[32,8,128]{2,1,0:T(8,128)}), f32[32,8,128]{2,1,0:T(8,128)S(1)}, u32[]{:S(2)}, u32[]{:S(2)}) async-start(f32[32,8,128]{2,1,0:T(8,128)} %fold.4), calls=%async_computation.3 | async-start | bytes 262144 | tf_op jit(solution)/shard_map/all_to_all | solution.py:183
  92.6 19.3 %collective-permute-start.5 = (bf16[4,128,128]{2,1,0:T(8,128)(2,1)S(1)}, bf16[4,128,128]{2,1,0:T(8,128)(2,1)S(1)}, u32[]{:S(2)}, u32[]{:S(2)}) collective-permute-start(bf16[4,128,128]{2,1,0:T(8,128)(2,1)S(1)} %fusion.1), channel_id=1, source_target_pairs={{0,1},{1,0},{2,3},{3,2},{4,5},{5,4},{6,7},{7,6},{8,9},{9,8},{10,11... | collective-permute-start | bytes 393224 | tf_op jit(solution)/shard_map/ppermute | solution.py:171
  102.5 15.3 %all-to-all-start.4 = ((f32[16,8,128]{2,1,0:T(8,128)}), f32[16,8,128]{2,1,0:T(8,128)S(1)}, u32[]{:S(2)}, u32[]{:S(2)}) async-start(f32[16,8,128]{2,1,0:T(8,128)} %fold.5), calls=%async_computation.4 | async-start | bytes 131072 | tf_op jit(solution)/shard_map/all_to_all | solution.py:183
  109.9 1.1 copy-start.7

commit v3 on v2

v3 whole, which is shorter than its diff:
```python
import functools

import jax
import jax.numpy as jnp
from jax import lax
from jax.experimental import pallas as pl
from jax.experimental.pallas import tpu as pltpu
from jax.sharding import Mesh
from jax.sharding import PartitionSpec as P

DP = ("dp_0", "dp_1")
BLOCK = ("sx", "sy")
ALL_AXES = ("dp_0", "dp_1", "sx", "sy")
C = 128
CX = 2
CY = 4
CZ = 128
PX = CX + 2
PY = CY + 2
TAPS = 27
K = TAPS * C
RANK = 4
GROUP = 3 * C
EXTRA = 4 * RANK
F32 = jnp.float32
BF16 = jnp.bfloat16
NT = (((1,), (1,)), ((), ()))
NN = (((1,), (0,)), ((), ()))
TN = (((0,), (0,)), ((), ()))
HIGHEST = lax.Precision.HIGHEST
VMEM = pl.BlockSpec(memory_space=pltpu.VMEM)
MIB = 1024 * 1024


def fill_planes(planes, low, own_0, own_1, high, across):
    lane = lax.broadcasted_iota(jnp.int32, (C, CZ), 1)
    zero = jnp.zeros((C, CZ), F32)

    def put(xp, yp, block):
        where = pl.ds((xp * PY + yp) * CZ, CZ)
        wide = block.astype(F32)
        before = jnp.where(lane == 0, zero, pltpu.roll(wide, 1, 1))
        after = jnp.where(lane == CZ - 1, zero, pltpu.roll(wide, CZ - 1, 1))
        planes[pl.ds(0, C), where] = before.astype(BF16)
        planes[pl.ds(C, C), where] = block
        planes[pl.ds(2 * C, C), where] = after.astype(BF16)

    first = lax.axis_index("sy") == 0
    for xp, source in enumerate((low, own_0, own_1, high)):
        for y in range(CY):
            put(xp, y + 1, source[y])
        edge = across[xp]
        nothing = jnp.zeros_like(edge)
        put(xp, 0, jnp.where(first, nothing, edge))
        put(xp, PY - 1, jnp.where(first, edge, nothing))


def window(planes, x, a, b):
    return planes[:, pl.ds(((x + a) * PY + b) * CZ, CY * CZ)]


def convolve(planes, lhs, x):
    total = None
    for a in range(3):
        for b in range(3):
            part = lax.dot_general(
                lhs[:, pl.ds((3 * a + b) * GROUP, GROUP)],
                window(planes, x, a, b),
                NN,
                preferred_element_type=F32,
            )
            total = part if total is None else total + part
    return total


def pieces(x):
    first = x.astype(BF16).astype(F32)
    rest = x - first
    second = rest.astype(BF16).astype(F32)
    third = (rest - second).astype(BF16).astype(F32)
    return first, second, third


def prepare_kernel(weights, warm, error, bias, lhs, base, bias_plane):
    bias_plane[...] = jnp.transpose(jnp.broadcast_to(bias[...], (C, C)))
    for tap in range(TAPS):
        lhs[pl.ds(0, C), pl.ds(tap * C, C)] = weights[tap]
    rows = warm[...]
    first, second, third = pieces(rows)
    stacked = jnp.concatenate([first, second, third, jnp.zeros_like(rows)], axis=0)
    lhs[pl.ds(C, EXTRA), :] = stacked.astype(BF16)
    base[...] = lax.dot_general(rows, error[...], NT, precision=HIGHEST, preferred_element_type=F32)


def forward_kernel(
    low, own_0, own_1, high, across, upstream, lhs, bias, base,
    act, grad_0, grad_1, sums, planes,
):
    fill_planes(planes, low, own_0, own_1, high, across)
    joint = jnp.zeros((EXTRA, C), F32)
    for x, grad in enumerate((grad_0, grad_1)):
        total = convolve(planes, lhs, x)
        pre = total[:C] + bias[:, :1]
        sigma = jax.nn.sigmoid(pre)
        active = (pre * sigma).astype(BF16)
        slope = sigma * (1.0 + pre * (1.0 - sigma))
        grads = []
        for y in range(CY):
            span = slice(y * CZ, (y + 1) * CZ)
            act[x, y] = active[:, span]
            piece = (upstream[x, y].astype(F32) * slope[:, span]).astype(BF16)
            grad[y] = piece
            grads.append(piece)
        field = total[C : C + RANK] + total[C + RANK : C + 2 * RANK]
        field = field + total[C + 2 * RANK : C + 3 * RANK]
        first, second, third = pieces(field)
        stacked = jnp.concatenate([first, second, third, jnp.ones_like(field)], axis=0)
        joint = joint + lax.dot_general(
            stacked.astype(BF16), jnp.concatenate(grads, axis=1), NT, preferred_element_type=F32
        )
    local = joint[:RANK] + joint[RANK : 2 * RANK] + joint[2 * RANK : 3 * RANK] + base[...]
    both = jnp.concatenate([local, joint[3 * RANK :]], axis=0)
    for copy in range(sums.shape[0]):
        sums[copy] = both


def gradient_kernel(
    low, own_0, own_1, high, across, grad_0, grad_1, error, merged, upper, lower, planes
):
    fill_planes(planes, low, own_0, own_1, high, across)
    grads = []
    for grad in (grad_0, grad_1):
        grads.append(jnp.concatenate([grad[y] for y in range(CY)], axis=1))
    for a in range(3):
        for b in range(3):
            span = pl.ds((3 * a + b) * GROUP, GROUP)
            part = error[:, span]
            for x in range(CX):
                part = part + lax.dot_general(
                    grads[x], window(planes, x, a, b), NT, preferred_element_type=F32
                )
            merged[:, span] = part
            rounded = part.astype(BF16)
            upper[:, span] = rounded
            lower[:, span] = (part - rounded.astype(F32)).astype(BF16)


def fold_kernel(parts, copies):
    total = parts[0]
    for source in range(1, parts.shape[0]):
        total = total + parts[source]
    for copy in range(copies.shape[0]):
        copies[copy] = total


def project_kernel(parts, upper, lower, factor_p, bias_grad, blocks, *, devices):
    sums = parts[0]
    for source in range(1, parts.shape[0]):
        sums = sums + parts[source]
    bias_grad[...] = sums[RANK : RANK + 1] / devices
    rows = []
    for r in range(RANK):
        vector = sums[r : r + 1]
        for basis in rows:
            vector = vector - jnp.sum(basis * vector) * basis
        vector = vector / jnp.sqrt(jnp.sum(vector * vector) + 1e-06)
        rows.append(vector)
        factor_p[pl.ds(r, 1), :] = vector
    basis = jnp.concatenate(rows, axis=0)
    first, second, third = pieces(basis)
    stacked = jnp.concatenate([first, second, third, jnp.zeros_like(basis)], axis=0).astype(BF16)
    q = lax.dot_general(stacked, upper[...], NN, preferred_element_type=F32)
    q = q + lax.dot_general(stacked, lower[...], NN, preferred_element_type=F32)
    q = q[:RANK] + q[RANK : 2 * RANK] + q[2 * RANK : 3 * RANK]
    for block in range(blocks.shape[0]):
        if block < TAPS:
            blocks[block] = q[:, block * C : (block + 1) * C]
        else:
            blocks[block] = jnp.zeros((RANK, C), F32)


def residual_kernel(basis, blocks, merged, new_error):
    for tap in range(TAPS):
        span = pl.ds(tap * C, C)
        new_error[:, span] = merged[:, span] - lax.dot_general(
            basis[...], blocks[tap], TN, precision=HIGHEST, preferred_element_type=F32
        )


def finish_kernel(blocks, factor_q, *, devices):
    for tap in range(TAPS):
        factor_q[:, pl.ds(tap * C, C)] = blocks[tap] / devices


def backward_kernel(low, own_0, own_1, high, across, weights, out, planes):
    fill_planes(planes, low, own_0, own_1, high, across)
    totals = [None] * CX
    for pair in range(9):
        taps = [TAPS - 1 - 3 * pair - c for c in range(3)]
        stack = jnp.concatenate([weights[tap] for tap in taps], axis=0)
        for x in range(CX):
            part = lax.dot_general(
                stack, window(planes, x, pair // 3, pair % 3), TN, preferred_element_type=F32
            )
            totals[x] = part if totals[x] is None else totals[x] + part
    for x in range(CX):
        total = totals[x].astype(BF16)
        for y in range(CY):
            out[x, y] = total[:, y * CZ : (y + 1) * CZ]


def edge_kernel(low, own_0, own_1, high, edge):
    first = lax.axis_index("sy") == 0
    for xp, source in enumerate((low, own_0, own_1, high)):
        edge[xp] = jnp.where(first, source[CY - 1], source[0])


def exchange_x(own_0, own_1):
    count = lax.axis_size("sx")
    up = [(i, i + 1) for i in range(count - 1)]
    down = [(i + 1, i) for i in range(count - 1)]
    return lax.ppermute(own_1, "sx", up), lax.ppermute(own_0, "sx", down)


def exchange_y(low, own_0, own_1, high):
    slab = jax.ShapeDtypeStruct((PX, C, CZ), BF16)
    edge = call(edge_kernel, "edge", 2, slab, (low, own_0, own_1, high))
    return lax.ppermute(edge, "sy", [(0, 1), (1, 0)])


tie = lax.optimization_barrier


def size_of(axes):
    count = 1
    for axis in axes:
        count = count * lax.axis_size(axis)
    return count


def swap(x, axes):
    return lax.all_to_all(x, axes, 0, 0, tiled=True)


def call(kernel, name, room, shapes, args, scratch=()):
    return pl.pallas_call(
        kernel,
        out_shape=shapes,
        in_specs=[VMEM] * len(args),
        out_specs=jax.tree.map(lambda _: VMEM, shapes),
        scratch_shapes=list(scratch),
        compiler_params=pltpu.CompilerParams(vmem_limit_bytes=room * MIB),
        name=name,
    )(*args)


def fold(parts, count):
    shape = jax.ShapeDtypeStruct((count,) + parts.shape[1:], F32)
    return call(fold_kernel, "fold", 2, shape, (parts,))


def f32(*shape):
    return jax.ShapeDtypeStruct(shape, F32)


def bf16(*shape):
    return jax.ShapeDtypeStruct(shape, BF16)


def shards(features, cotangent, weights, conv_bias, error_state, warm_factor):
    chips, columns = size_of(DP), size_of(BLOCK)
    devices = chips * columns
    padded = -(-TAPS // columns) * columns
    planes = pltpu.VMEM((GROUP, PX * PY * CZ), BF16)
    error = error_state[0, 0, 0]
    own_0 = jnp.transpose(features[0, :, 0], (1, 0, 2))
    own_1 = jnp.transpose(features[0, :, 1], (1, 0, 2))
    low, high = exchange_x(own_0, own_1)
    upstream = jnp.transpose(cotangent[0], (1, 2, 0, 3))
    lhs, base, bias = call(
        prepare_kernel,
        "prepare",
        8,
        (bf16(C + EXTRA, K), f32(RANK, C), f32(C, C)),
        (weights, warm_factor, error, conv_bias[None]),
    )
    low, high, lhs, base, bias, upstream = tie((low, high, lhs, base, bias, upstream))
    across = exchange_y(low, own_0, own_1, high)
    block = (low, own_0, own_1, high, across)
    act, grad_0, grad_1, sums = call(
        forward_kernel,
        "forward",
        10,
        (bf16(CX, CY, C, CZ), bf16(CY, C, CZ), bf16(CY, C, CZ), f32(chips, 2 * RANK, C)),
        (*block, upstream, lhs, bias, base),
        [planes],
    )
    parts = swap(sums, DP)
    g_low, g_high = exchange_x(grad_0, grad_1)
    merged, upper, lower = call(
        gradient_kernel,
        "gradient",
        14,
        (f32(C, K), bf16(C, K), bf16(C, K)),
        (*block, grad_0, grad_1, error),
        [planes],
    )
    parts, g_low, g_high, upper = tie((parts, g_low, g_high, upper))
    parts = swap(fold(parts, columns), BLOCK)
    g_across = exchange_y(g_low, grad_0, grad_1, g_high)
    input_grad = call(
        backward_kernel,
        "backward",
        8,
        bf16(CX, CY, C, CZ),
        (g_low, grad_0, grad_1, g_high, g_across, weights),
        [planes],
    )
    activation = jnp.transpose(act, (2, 0, 1, 3))[None]
    input_grad = jnp.transpose(input_grad, (2, 0, 1, 3))[None]
    parts, input_grad, activation = tie((parts, input_grad, activation))
    factor_p, bias_grad, blocks = call(
        functools.partial(project_kernel, devices=devices),
        "project",
        6,
        (f32(RANK, C), f32(1, C), f32(padded, RANK, C)),
        (parts, upper, lower),
    )
    new_error = call(
        residual_kernel, "residual", 6, f32(C, K), (factor_p, blocks, merged)
    )
    width = padded // columns * RANK
    mine, new_error = tie((swap(blocks, BLOCK), new_error))
    mine = fold(mine.reshape(columns, width, C), chips)
    mine = fold(swap(mine, DP), columns)
    blocks = swap(mine, BLOCK).reshape(padded, RANK, C)
    factor_q = call(
        functools.partial(finish_kernel, devices=devices), "finish", 2, f32(RANK, K), (blocks,)
    )
    return (
        activation,
        input_grad,
        bias_grad[0],
        factor_p,
        factor_q,
        new_error[None, None, None],
    )


def solution(mesh):
    torus = Mesh(mesh.devices.reshape(4, 8, mesh.shape["sx"], mesh.shape["sy"]), ALL_AXES)
    split = P(DP, None, "sx", "sy", None)
    state = P(DP, "sx", "sy", None, None)
    return jax.shard_map(
        shards,
        mesh=torus,
        in_specs=(split, split, P(), P(), state, P()),
        out_specs=(split, split, P(), P(), P(), state),
        check_vma=False,
    )
```

time: 119 us -> 121 us (1.017)
  blocking collectives: 35.6 us -> 18.4 us
  starting transfers between devices: 34 us -> 49.5 us
  local copies, waits for them, and re-layouts: 13.6 us -> 20.3 us
  waiting for transfers between devices: 17.2 us -> 14.7 us
    all_to_all x2 -> x1, blocking collectives: 35.6 us -> 18.4 us  [swap(): return lax.all_to_all(x, axes, 0, 0, tiled=True)]
    all_to_all x3 -> x4, starting transfers between devices: 14.8 us -> 29.6 us  [swap(): return lax.all_to_all(x, axes, 0, 0, tiled=True)]
    unnamed x29 -> x51, local copies, waits for them, and re-layouts: 9.64 us -> 19.2 us
    reshape x2 -> x0, local copies, waits for them, and re-layouts: 2.7 us -> none  [the longest x1 1.7 us: shards(): lhs = jnp.transpose(weights, (1, 0, 2)).reshape(C, K)]
    ppermute x6, waiting for transfers between devices: 3.4 us -> 0.99 us  [the longest x2 0.97 us: exchange_y(): return lax.ppermute(edge, 'sy', [(0, 1), (1, 0)])]
    all_to_all x3 -> x4, waiting for transfers between devices: 13.8 us -> 13.7 us  [swap(): return lax.all_to_all(x, axes, 0, 0, tiled=True)]
    pallas_call x8 -> x12, Pallas kernels: 16.3 us -> 16.5 us  [call(): pl.pallas_call(kernel, out_shape=shapes, in_specs=[VMEM] * len(args), out...]
  transfers between devices with their start and end apart: 9 -> 10, of which waited for: 4 -> 4; matrix products, arithmetic and copies ran while one was open for 7% -> 2% of each run, Pallas kernels for 2% -> 9%
where the time goes in v3:
time: 121 us; the launch traced here: 120 us
  starting transfers between devices  49.5 us (41%)
  local copies, waits for them, and re-layouts  20.3 us (17%)
  blocking collectives  18.4 us (15%)
  Pallas kernels  16.5 us (14%)
  waiting for transfers between devices  14.7 us (12%)
    all_to_all x4, starting transfers between devices, swap(): return lax.all_to_all(x, axes, 0, 0, tiled=True)  29.6 us
    unnamed x51, local copies, waits for them, and re-layouts  19.2 us
    all_to_all x1, blocking collectives, swap(): return lax.all_to_all(x, axes, 0, 0, tiled=True)  18.4 us
    pallas_call x12, Pallas kernels, call(): pl.pallas_call(kernel, out_shape=shapes, in_specs=[VMEM] * len(args), out...  16.5 us
    all_to_all x4, waiting for transfers between devices, swap(): return lax.all_to_all(x, axes, 0, 0, tiled=True)  13.7 us
    ppermute x4, starting transfers between devices, exchange_x(): return (lax.ppermute(own_1, 'sx', up), lax.ppermute(own_0, 'sx', down))  10.9 us
    ppermute x2, starting transfers between devices, exchange_y(): return lax.ppermute(edge, 'sy', [(0, 1), (1, 0)])  9 us
  transfers between devices with their start and end apart: 10, of which 4 were waited for; matrix products, arithmetic and copies ran while one was open for 2% of the time, Pallas kernels for 9%

profile of v3, /device:TPU:1, one launch (start us, length us, event | category | flops | bytes accessed | tf_op | source)
XLA Modules:
  0.0 120.1 jit_solution(13013937512135717914)
XLA Ops:
  0.6 0.0 copy-start.2
  0.6 1.1 fusion
  1.8 4.0 %collective-permute-start = (bf16[4,128,128]{2,1,0:T(8,128)(2,1)S(1)}, bf16[4,128,128]{2,1,0:T(8,128)(2,1)S(1)}, u32[]{:S(2)}, u32[]{:S(2)}) collective-permute-start(bf16[4,128,128]{2,1,0:T(8,128)(2,1)S(1)} %bitcast.29), channel_id=1, source_target_pairs={{0,2},{2,4},{4,6},{6,8},{8,10},{10,12},{12,14},{1,3},{3,5},{5,7},{... | collective-permute-start | bytes 393224 | tf_op jit(solution)/shard_map/ppermute | solution.py:222
  5.9 1.3 %collective-permute-start.1 = (bf16[4,128,128]{2,1,0:T(8,128)(2,1)S(1)}, bf16[4,128,128]{2,1,0:T(8,128)(2,1)S(1)}, u32[]{:S(2)}, u32[]{:S(2)}) collective-permute-start(bf16[4,128,128]{2,1,0:T(8,128)(2,1)S(1)} %bitcast.33), channel_id=1, source_target_pairs={{2,0},{4,2},{6,4},{8,6},{10,8},{12,10},{14,12},{3,1},{5,3},{7,5},{... | collective-permute-start | bytes 393224 | tf_op jit(solution)/shard_map/ppermute | solution.py:222
  7.2 1.0 copy.22
  8.2 0.0 copy-done.2
  8.2 0.0 copy-start
  8.2 1.5 %copy-done = f32[1,1,1,128,3456]{4,3,2,1,0:T(8,128)S(1)} copy-done((f32[1,1,1,128,3456]{4,3,2,1,0:T(8,128)S(1)}, f32[1,1,1,128,3456]{4,3,2,1,0:T(8,128)}, u32[]{:S(2)}) %copy-start) | copy-done | bytes 1769496
  9.7 0.8 copy-done.20
  10.5 0.7 copy-done.22
  11.1 1.7 %prepare.1 = (bf16[144,3456]{1,0:T(8,128)(2,1)S(1)}, f32[4,128]{1,0:T(4,128)S(1)}, f32[128,128]{1,0:T(8,128)S(1)}) custom-call(bf16[27,128,128]{2,1,0:T(8,128)(2,1)S(1)} %copy-done.2, f32[4,3456]{1,0:T(4,128)S(1)} %copy-done.20, f32[128,3456]{1,0:T(8,128)S(1)} %bitcast.27, f32[1,128]{1,0:T(1,128)S(1)} %bitcast.42), custom_call_target="tpu_custom_call" | custom-call | tf_op jit(solution)/shard_map/prepare/pallas_call | solution.py:246
  12.8 0.0 collective-permute-done.low
  12.8 0.0 collective-permute-done.1.high
  12.9 6.2 %collective-permute-start.2 = (bf16[4,128,128]{2,1,0:T(8,128)(2,1)S(1)}, bf16[4,128,128]{2,1,0:T(8,128)(2,1)S(1)}, u32[]{:S(2)}, u32[]{:S(2)}) collective-permute-start(bf16[4,128,128]{2,1,0:T(8,128)(2,1)S(1)} %edge.2), channel_id=1, source_target_pairs={{0,1},{1,0},{2,3},{3,2},{4,5},{5,4},{6,7},{7,6},{8,9},{9,8},{10,11... | collective-permute-start | bytes 393224 | tf_op jit(solution)/shard_map/ppermute | solution.py:228
  19.1 1.0 collective-permute-done.2.across
  20.0 2.0 %forward.1 = (bf16[2,4,128,128]{3,2,1,0:T(8,128)(2,1)S(1)}, bf16[4,128,128]{2,1,0:T(8,128)(2,1)S(1)}, bf16[4,128,128]{2,1,0:T(8,128)(2,1)S(1)}, f32[32,8,128]{2,1,0:T(8,128)S(1)}) custom-call(bf16[4,128,128]{2,1,0:T(8,128)(2,1)S(1)} %collective-permute-done.low, bf16[4,128,128]{2,1,0:T(8,128)(2,1)S(1)} %bitcast.35, bf16[4,128,128]{2,1,0:T(8,128)(2,1)S(1)} %bitcast.31, ...), custom_call_target="tpu_custom_call" | custom-call | tf_op jit(solution)/shard_map/forward/pallas_call | solution.py:246
  22.1 0.0 copy-done.15
  22.1 0.0 copy-start.17
  22.1 0.7 copy-done.17
  22.8 0.6 copy-done.19
  23.4 9.8 %all-to-all-start = ((f32[32,8,128]{2,1,0:T(8,128)}), f32[32,8,128]{2,1,0:T(8,128)}, u32[]{:S(2)}, u32[]{:S(2)}) async-start(f32[32,8,128]{2,1,0:T(8,128)} %copy-done.19), calls=%async_computation | async-start | bytes 262144 | tf_op jit(solution)/shard_map/all_to_all | solution.py:242
  33.3 4.3 %collective-permute-start.3 = (bf16[4,128,128]{2,1,0:T(8,128)(2,1)S(1)}, bf16[4,128,128]{2,1,0:T(8,128)(2,1)S(1)}, u32[]{:S(2)}, u32[]{:S(2)}) collective-permute-start(bf16[4,128,128]{2,1,0:T(8,128)(2,1)S(1)} %get-tuple-element.44.grad_1.own_1), channel_id=1, source_target_pairs={{0,2},{2,4},{4,6},{6,8},{8,10},{10,12},{12,14},{1,3},{3,5},{5,7},{... | collective-permute-start | bytes 393224 | tf_op jit(solution)/shard_map/ppermute | solution.py:222
  37.6 1.3 %collective-permute-start.4 = (bf16[4,128,128]{2,1,0:T(8,128)(2,1)S(1)}, bf16[4,128,128]{2,1,0:T(8,128)(2,1)S(1)}, u32[]{:S(2)}, u32[]{:S(2)}) collective-permute-start(bf16[4,128,128]{2,1,0:T(8,128)(2,1)S(1)} %get-tuple-element.45.grad_0.own_0), channel_id=1, source_target_pairs={{2,0},{4,2},{6,4},{8,6},{10,8},{12,10},{14,12},{3,1},{5,3},{7,5},{... | collective-permute-start | bytes 393224 | tf_op jit(solution)/shard_map/ppermute | solution.py:222
  38.9 0.0 copy-done.1
  38.9 0.0 copy-start.16
  38.9 0.9 copy-done.16
  39.8 2.4 %gradient.1 = (f32[128,3456]{1,0:T(8,128)S(1)}, bf16[128,3456]{1,0:T(8,128)(2,1)S(1)}, bf16[128,3456]{1,0:T(8,128)(2,1)S(1)}) custom-call(bf16[4,128,128]{2,1,0:T(8,128)(2,1)S(1)} %collective-permute-done.low, bf16[4,128,128]{2,1,0:T(8,128)(2,1)S(1)} %bitcast.36, bf16[4,128,128]{2,1,0:T(8,128)(2,1)S(1)} %bitcast.32, ...), custom_call_target="tpu_custom_call" | custom-call | tf_op jit(solution)/shard_map/gradient/pallas_call | solution.py:246
  42.1 0.0 copy-start.3
  42.2 1.2 copy-done.3
  43.4 0.9 copy-done.5
  44.3 0.9 copy-done.7
  45.2 0.0 collective-permute-done.3.low
  45.2 0.7 copy-done.9
  45.9 0.0 collective-permute-done.4.high
  45.9 0.6 copy-done.12
  46.5 0.0 all-to-all-done.parts
  46.5 0.9 copy-done.10
  47.4 0.9 copy-done.13
  48.4 2.8 %collective-permute-start.5 = (bf16[4,128,128]{2,1,0:T(8,128)(2,1)S(1)}, bf16[4,128,128]{2,1,0:T(8,128)(2,1)S(1)}, u32[]{:S(2)}, u32[]{:S(2)}) collective-permute-start(bf16[4,128,128]{2,1,0:T(8,128)(2,1)S(1)} %edge.3), channel_id=1, source_target_pairs={{0,1},{1,0},{2,3},{3,2},{4,5},{5,4},{6,7},{7,6},{8,9},{9,8},{10,11... | collective-permute-start | bytes 393224 | tf_op jit(solution)/shard_map/ppermute | solution.py:228
  51.2 1.6 %fold.3 = f32[16,8,128]{2,1,0:T(8,128)} custom-call(f32[32,8,128]{2,1,0:T(8,128)} %all-to-all-done.parts), custom_call_target="tpu_custom_call" | custom-call | tf_op jit(solution)/shard_map/fold/pallas_call | solution.py:246
  52.8 10.7 %all-to-all-start.1 = ((f32[16,8,128]{2,1,0:T(8,128)}), f32[16,8,128]{2,1,0:T(8,128)S(1)}, u32[]{:S(2)}, u32[]{:S(2)}) async-start(f32[16,8,128]{2,1,0:T(8,128)} %fold.3), calls=%async_computation.1 | async-start | bytes 131072 | tf_op jit(solution)/shard_map/all_to_all | solution.py:242
  63.5 0.0 collective-permute-done.5.across
  63.5 0.0 copy-start.11
  63.5 1.0 copy-done.11
  64.5 0.9 copy-done.14
  65.4 1.6 %backward.1 = bf16[2,4,128,128]{3,2,1,0:T(8,128)(2,1)S(1)} custom-call(bf16[4,128,128]{2,1,0:T(8,128)(2,1)S(1)} %copy-done.11, bf16[4,128,128]{2,1,0:T(8,128)(2,1)S(1)} %get-tuple-element.45.grad_0.own_0, bf16[4,128,128]{2,1,0:T(8,128)(2,1)S(1)} %get-tuple-element.44.grad_1.own_1, bf16[4,128,128]{2,1,0:T(8,128)(2,1)S(1)} %copy-done.14, ...), custom_call_target="tpu_custom_call" | custom-call | tf_op jit(solution)/shard_map/backward/pallas_call | solution.py:246
  67.1 4.2 %all-to-all-done.1.parts = f32[16,8,128]{2,1,0:T(8,128)S(1)} async-done(((f32[16,8,128]{2,1,0:T(8,128)}), f32[16,8,128]{2,1,0:T(8,128)S(1)}, u32[]{:S(2)}, u32[]{:S(2)}) %all-to-all-start.1) | async-done | bytes 65568 | tf_op jit(solution)/shard_map/all_to_all | solution.py:242
  71.3 1.2 copy-done.6
  72.5 1.2 copy-done.8
  73.6 2.1 %project.1 = (f32[4,128]{1,0:T(4,128)}, f32[1,128]{1,0:T(1,128)}, f32[32,4,128]{2,1,0:T(4,128)}) custom-call(f32[16,8,128]{2,1,0:T(8,128)S(1)} %all-to-all-done.1.parts, bf16[128,3456]{1,0:T(8,128)(2,1)S(1)} %copy-done.6, bf16[128,3456]{1,0:T(8,128)(2,1)S(1)} %copy-done.8), custom_call_target="tpu_custom_call" | custom-call | tf_op jit(solution)/shard_map/project/pallas_call | solution.py:246
  75.8 3.5 %all-to-all-start.2 = ((f32[32,4,128]{2,1,0:T(4,128)}), f32[32,4,128]{2,1,0:T(4,128)S(1)}, u32[]{:S(2)}, u32[]{:S(2)}) async-start(f32[32,4,128]{2,1,0:T(4,128)} %get-tuple-element.58.blocks), calls=%async_computation.2 | async-start | bytes 131072 | tf_op jit(solution)/shard_map/all_to_all | solution.py:242
  79.2 0.0 copy-done.4
  79.2 0.0 copy-start.21
  79.2 0.7 copy-done.21
  79.9 3.7 %residual.1 = f32[128,3456]{1,0:T(8,128)} custom-call(f32[4,128]{1,0:T(4,128)S(1)} %copy-done.21, f32[32,4,128]{2,1,0:T(4,128)} %get-tuple-element.58.blocks, f32[128,3456]{1,0:T(8,128)S(1)} %copy-done.4), custom_call_target="tpu_custom_call" | custom-call | tf_op jit(solution)/shard_map/residual/pallas_call | solution.py:246
  83.6 3.5 %all-to-all-done.2 = f32[32,4,128]{2,1,0:T(4,128)S(1)} async-done(((f32[32,4,128]{2,1,0:T(4,128)}), f32[32,4,128]{2,1,0:T(4,128)S(1)}, u32[]{:S(2)}, u32[]{:S(2)}) %all-to-all-start.2) | async-done | bytes 65568 | tf_op jit(solution)/shard_map/all_to_all | solution.py:242
  87.1 18.4 %all_to_all.25.parts = f32[32,8,128]{2,1,0:T(8,128)S(1)} all-to-all(f32[32,8,128]{2,1,0:T(8,128)S(1)} %fold.4), channel_id=1, replica_groups=mesh['dp_0'=4,'dp_1'=8,'sx'=8,'sy'=2] {'dp_0','dp_1'}, dimensions={0} | all-to-all | bytes 262144 | tf_op jit(solution)/shard_map/all_to_all | solution.py:242
  105.5 0.7 fold.5
  106.1 5.6 %all-to-all-start.4 = ((f32[16,8,128]{2,1,0:T(8,128)}), f32[16,8,128]{2,1,0:T(8,128)S(1)}, u32[]{:S(2)}, u32[]{:S(2)}) async-start(f32[16,8,128]{2,1,0:T(8,128)} %fold.5), calls=%async_computation.4 | async-start | bytes 131072 | tf_op jit(solution)/shard_map/all_to_all | solution.py:242
  111.7 0.0 copy-done.18
  111.7 0.9 copy.15
  112.6 0.9 copy.16
  113.5 6.0 %all-to-all-done.4 = f32[16,8,128]{2,1,0:T(8,128)S(1)} async-done(((f32[16,8,128]{2,1,0:T(8,128)}), f32[16,8,128]{2,1,0:T(8,128)S(1)}, u32[]{:S(2)}, u32[]{:S(2)}) %all-to-all-start.4) | async-done | bytes 65568 | tf_op jit(solution)/shard_map/all_to_all | solution.py:242
  119.5 0.6 finish.1
  (21 shorter events, 0.2 us)
Async XLA Ops:
  0.6 7.5 %copy-start.2 = (bf16[27,128,128]{2,1,0:T(8,128)(2,1)S(1)}, bf16[27,128,128]{2,1,0:T(8,128)(2,1)}, u32[]{:S(2)}) copy-start(bf16[27,128,128]{2,1,0:T(8,128)(2,1)} %weights.3) | copy-start | bytes 2654212
  1.8 11.0 %collective-permute-start = (bf16[4,128,128]{2,1,0:T(8,128)(2,1)S(1)}, bf16[4,128,128]{2,1,0:T(8,128)(2,1)S(1)}, u32[]{:S(2)}, u32[]{:S(2)}) collective-permute-start(bf16[4,128,128]{2,1,0:T(8,128)(2,1)S(1)} %bitcast.29), channel_id=1, source_target_pairs={{0,2},{2,4},{4,6},{6,8},{8,10},{10,12},{12,14},{1,3},{3,5},{5,7},{... | collective-permute-start | bytes 393224 | tf_op jit(solution)/shard_map/ppermute | solution.py:222
  5.9 6.9 %collective-permute-start.1 = (bf16[4,128,128]{2,1,0:T(8,128)(2,1)S(1)}, bf16[4,128,128]{2,1,0:T(8,128)(2,1)S(1)}, u32[]{:S(2)}, u32[]{:S(2)}) collective-permute-start(bf16[4,128,128]{2,1,0:T(8,128)(2,1)S(1)} %bitcast.33), channel_id=1, source_target_pairs={{2,0},{4,2},{6,4},{8,6},{10,8},{12,10},{14,12},{3,1},{5,3},{7,5},{... | collective-permute-start | bytes 393224 | tf_op jit(solution)/shard_map/ppermute | solution.py:222
  8.2 1.5 %copy-start = (f32[1,1,1,128,3456]{4,3,2,1,0:T(8,128)S(1)}, f32[1,1,1,128,3456]{4,3,2,1,0:T(8,128)}, u32[]{:S(2)}) copy-start(f32[1,1,1,128,3456]{4,3,2,1,0:T(8,128)} %param.10) | copy-start | bytes 5308420
  9.7 0.8 copy-start.20
  10.5 0.7 copy-start.22
  12.8 26.1 %copy-start.1 = (f32[1,1,1,128,3456]{4,3,2,1,0:T(8,128)S(1)}, f32[1,1,1,128,3456]{4,3,2,1,0:T(8,128)}, u32[]{:S(2)}) copy-start(f32[1,1,1,128,3456]{4,3,2,1,0:T(8,128)} %param.10) | copy-start | bytes 5308420
  12.9 7.2 %collective-permute-start.2 = (bf16[4,128,128]{2,1,0:T(8,128)(2,1)S(1)}, bf16[4,128,128]{2,1,0:T(8,128)(2,1)S(1)}, u32[]{:S(2)}, u32[]{:S(2)}) collective-permute-start(bf16[4,128,128]{2,1,0:T(8,128)(2,1)S(1)} %edge.2), channel_id=1, source_target_pairs={{0,1},{1,0},{2,3},{3,2},{4,5},{5,4},{6,7},{7,6},{8,9},{9,8},{10,11... | collective-permute-start | bytes 393224 | tf_op jit(solution)/shard_map/ppermute | solution.py:228
  20.0 2.1 %copy-start.15 = (bf16[4,128,128]{2,1,0:T(8,128)(2,1)}, bf16[4,128,128]{2,1,0:T(8,128)(2,1)S(1)}, u32[]{:S(2)}) copy-start(bf16[4,128,128]{2,1,0:T(8,128)(2,1)S(1)} %collective-permute-done.2.across) | copy-start | bytes 393220
  22.1 0.7 copy-start.17
  22.8 0.6 copy-start.19
  23.4 23.1 %all-to-all-start = ((f32[32,8,128]{2,1,0:T(8,128)}), f32[32,8,128]{2,1,0:T(8,128)}, u32[]{:S(2)}, u32[]{:S(2)}) async-start(f32[32,8,128]{2,1,0:T(8,128)} %copy-done.19), calls=%async_computation | async-start | bytes 262144 | tf_op jit(solution)/shard_map/all_to_all | solution.py:242
  33.3 11.9 %collective-permute-start.3 = (bf16[4,128,128]{2,1,0:T(8,128)(2,1)S(1)}, bf16[4,128,128]{2,1,0:T(8,128)(2,1)S(1)}, u32[]{:S(2)}, u32[]{:S(2)}) collective-permute-start(bf16[4,128,128]{2,1,0:T(8,128)(2,1)S(1)} %get-tuple-element.44.grad_1.own_1), channel_id=1, source_target_pairs={{0,2},{2,4},{4,6},{6,8},{8,10},{10,12},{12,14},{1,3},{3,5},{5,7},{... | collective-permute-start | bytes 393224 | tf_op jit(solution)/shard_map/ppermute | solution.py:222
  37.6 8.3 %collective-permute-start.4 = (bf16[4,128,128]{2,1,0:T(8,128)(2,1)S(1)}, bf16[4,128,128]{2,1,0:T(8,128)(2,1)S(1)}, u32[]{:S(2)}, u32[]{:S(2)}) collective-permute-start(bf16[4,128,128]{2,1,0:T(8,128)(2,1)S(1)} %get-tuple-element.45.grad_0.own_0), channel_id=1, source_target_pairs={{2,0},{4,2},{6,4},{8,6},{10,8},{12,10},{14,12},{3,1},{5,3},{7,5},{... | collective-permute-start | bytes 393224 | tf_op jit(solution)/shard_map/ppermute | solution.py:222
  38.9 0.9 copy-start.16
  42.1 1.2 %copy-start.3 = (f32[128,3456]{1,0:T(8,128)}, f32[128,3456]{1,0:T(8,128)S(1)}, u32[]{:S(2)}) copy-start(f32[128,3456]{1,0:T(8,128)S(1)} %get-tuple-element.59.merged) | copy-start | bytes 5308420
  43.3 0.9 copy-start.5
  44.3 0.9 copy-start.7
  45.2 0.7 copy-start.9
  45.9 0.7 copy-start.12
  46.5 0.9 copy-start.10
  47.4 0.9 copy-start.13
  48.4 15.1 %collective-permute-start.5 = (bf16[4,128,128]{2,1,0:T(8,128)(2,1)S(1)}, bf16[4,128,128]{2,1,0:T(8,128)(2,1)S(1)}, u32[]{:S(2)}, u32[]{:S(2)}) collective-permute-start(bf16[4,128,128]{2,1,0:T(8,128)(2,1)S(1)} %edge.3), channel_id=1, source_target_pairs={{0,1},{1,0},{2,3},{3,2},{4,5},{5,4},{6,7},{7,6},{8,9},{9,8},{10,11... | collective-permute-start | bytes 393224 | tf_op jit(solution)/shard_map/ppermute | solution.py:228
  52.8 18.5 %all-to-all-start.1 = ((f32[16,8,128]{2,1,0:T(8,128)}), f32[16,8,128]{2,1,0:T(8,128)S(1)}, u32[]{:S(2)}, u32[]{:S(2)}) async-start(f32[16,8,128]{2,1,0:T(8,128)} %fold.3), calls=%async_computation.1 | async-start | bytes 131072 | tf_op jit(solution)/shard_map/all_to_all | solution.py:242
  63.5 15.7 %copy-start.4 = (f32[128,3456]{1,0:T(8,128)S(1)}, f32[128,3456]{1,0:T(8,128)}, u32[]{:S(2)}) copy-start(f32[128,3456]{1,0:T(8,128)} %copy-done.3) | copy-start | bytes 5308420
  63.5 1.0 copy-start.11
  64.5 0.9 copy-start.14
  71.3 1.2 copy-start.6
  72.5 1.2 copy-start.8
  75.8 11.3 %all-to-all-start.2 = ((f32[32,4,128]{2,1,0:T(4,128)}), f32[32,4,128]{2,1,0:T(4,128)S(1)}, u32[]{:S(2)}, u32[]{:S(2)}) async-start(f32[32,4,128]{2,1,0:T(4,128)} %get-tuple-element.58.blocks), calls=%async_computation.2 | async-start | bytes 131072 | tf_op jit(solution)/shard_map/all_to_all | solution.py:242
  79.2 0.7 copy-start.21
  79.9 31.8 %copy-start.18 = (bf16[2,4,128,128]{3,2,1,0:T(8,128)(2,1)S(1)}, bf16[2,4,128,128]{3,2,1,0:T(8,128)(2,1)}, u32[]{:S(2)}) copy-start(bf16[2,4,128,128]{3,2,1,0:T(8,128)(2,1)} %copy-done.17) | copy-start | bytes 786436
  106.1 13.4 %all-to-all-start.4 = ((f32[16,8,128]{2,1,0:T(8,128)}), f32[16,8,128]{2,1,0:T(8,128)S(1)}, u32[]{:S(2)}, u32[]{:S(2)}) async-start(f32[16,8,128]{2,1,0:T(8,128)} %fold.5), calls=%async_computation.4 | async-start | bytes 131072 | tf_op jit(solution)/shard_map/all_to_all | solution.py:242

commit v4 on v3

--- a/solution.py
+++ b/solution.py
@@ -29,6 +29,7 @@
 TN = (((0,), (0,)), ((), ()))
 HIGHEST = lax.Precision.HIGHEST
 VMEM = pl.BlockSpec(memory_space=pltpu.VMEM)
+HBM = pl.BlockSpec(memory_space=pltpu.HBM)
 MIB = 1024 * 1024
 
 
@@ -124,25 +125,33 @@
         sums[copy] = both
 
 
-def gradient_kernel(
-    low, own_0, own_1, high, across, grad_0, grad_1, error, merged, upper, lower, planes
-):
+def gradient_kernel(wait, block, upper_out, lower_out, planes, upper, lower, sem):
+    low, own_0, own_1, high, across, grad_0, grad_1, error = block
+    wait(0, 1, 2, 3, 4)
     fill_planes(planes, low, own_0, own_1, high, across)
+    wait(5, 6)
     grads = []
     for grad in (grad_0, grad_1):
         grads.append(jnp.concatenate([grad[y] for y in range(CY)], axis=1))
-    for a in range(3):
-        for b in range(3):
-            span = pl.ds((3 * a + b) * GROUP, GROUP)
-            part = error[:, span]
-            for x in range(CX):
-                part = part + lax.dot_general(
-                    grads[x], window(planes, x, a, b), NT, preferred_element_type=F32
-                )
-            merged[:, span] = part
-            rounded = part.astype(BF16)
-            upper[:, span] = rounded
-            lower[:, span] = (part - rounded.astype(F32)).astype(BF16)
+    wait(7)
+    leaving = []
+    for pair in range(9):
+        span = pl.ds(pair * GROUP, GROUP)
+        part = error[:, span]
+        for x in range(CX):
+            part = part + lax.dot_general(
+                grads[x], window(planes, x, pair // 3, pair % 3), NT, preferred_element_type=F32
+            )
+        rounded = part.astype(BF16)
+        upper[:, span] = rounded
+        lower[:, span] = (part - rounded.astype(F32)).astype(BF16)
+        for side, (held, out) in enumerate(((upper, upper_out), (lower, lower_out))):
+            leaving.append(
+                pltpu.make_async_copy(held.at[:, span], out.at[:, span], sem.at[2 * pair + side])
+            )
+            leaving[-1].start()
+    for transfer in leaving:
+        transfer.wait()
 
 
 def fold_kernel(parts, copies):
@@ -153,7 +162,8 @@
         copies[copy] = total
 
 
-def project_kernel(parts, upper, lower, factor_p, bias_grad, blocks, *, devices):
+def project_kernel(wait, held, parts, factor_p, bias_grad, blocks, *, devices):
+    upper, lower = held
     sums = parts[0]
     for source in range(1, parts.shape[0]):
         sums = sums + parts[source]
@@ -169,6 +179,7 @@
     basis = jnp.concatenate(rows, axis=0)
     first, second, third = pieces(basis)
     stacked = jnp.concatenate([first, second, third, jnp.zeros_like(basis)], axis=0).astype(BF16)
+    wait(0, 1)
     q = lax.dot_general(stacked, upper[...], NN, preferred_element_type=F32)
     q = q + lax.dot_general(stacked, lower[...], NN, preferred_element_type=F32)
     q = q[:RANK] + q[RANK : 2 * RANK] + q[2 * RANK : 3 * RANK]
@@ -179,12 +190,21 @@
             blocks[block] = jnp.zeros((RANK, C), F32)
 
 
-def residual_kernel(basis, blocks, merged, new_error):
-    for tap in range(TAPS):
-        span = pl.ds(tap * C, C)
-        new_error[:, span] = merged[:, span] - lax.dot_general(
-            basis[...], blocks[tap], TN, precision=HIGHEST, preferred_element_type=F32
+def residual_kernel(wait, held, out, new_error, sem):
+    basis, blocks, upper, lower = held
+    wait(0, 1, 2, 3)
+    leaving = []
+    for pair in range(9):
+        span = pl.ds(pair * GROUP, GROUP)
+        rows = jnp.concatenate([blocks[3 * pair + c] for c in range(3)], axis=1)
+        merged = upper[:, span].astype(F32) + lower[:, span].astype(F32)
+        new_error[:, span] = merged - lax.dot_general(
+            basis[...], rows, TN, precision=HIGHEST, preferred_element_type=F32
         )
+        leaving.append(pltpu.make_async_copy(new_error.at[:, span], out.at[:, span], sem.at[pair]))
+        leaving[-1].start()
+    for transfer in leaving:
+        transfer.wait()
 
 
 def finish_kernel(blocks, factor_q, *, devices):
@@ -192,8 +212,11 @@
         factor_q[:, pl.ds(tap * C, C)] = blocks[tap] / devices
 
 
-def backward_kernel(low, own_0, own_1, high, across, weights, out, planes):
+def backward_kernel(wait, held, out, planes):
+    low, own_0, own_1, high, across, weights = held
+    wait(0, 1, 2, 3, 4)
     fill_planes(planes, low, own_0, own_1, high, across)
+    wait(5)
     totals = [None] * CX
     for pair in range(9):
         taps = [TAPS - 1 - 3 * pair - c for c in range(3)]
@@ -242,16 +265,52 @@
     return lax.all_to_all(x, axes, 0, 0, tiled=True)
 
 
-def call(kernel, name, room, shapes, args, scratch=()):
+def call(kernel, name, room, shapes, args, scratch=(), outs=VMEM):
     return pl.pallas_call(
         kernel,
         out_shape=shapes,
         in_specs=[VMEM] * len(args),
-        out_specs=jax.tree.map(lambda _: VMEM, shapes),
+        out_specs=jax.tree.map(lambda _: outs, shapes),
         scratch_shapes=list(scratch),
         compiler_params=pltpu.CompilerParams(vmem_limit_bytes=room * MIB),
         name=name,
     )(*args)
+
+
+def fetch_and_call(kernel, name, room, shapes, args, scratch=(), outs=VMEM, near=()):
+    count = len(args)
+
+    def body(*refs):
+        close, refs = refs[: len(near)], refs[len(near) :]
+        sources, rest = refs[:count], refs[count:]
+        results = len(jax.tree.leaves(shapes))
+        held, sem = rest[results : results + count], rest[results + count]
+        copies = [
+            pltpu.make_async_copy(source, target, sem.at[k])
+            for k, (source, target) in enumerate(zip(sources, held))
+        ]
+        for copy in copies:
+            copy.start()
+
+        def wait(*which):
+            for k in which:
+                copies[k].wait()
+
+        kernel(wait, held, *close, *rest[:results], *rest[results + count + 1 :])
+
+    return pl.pallas_call(
+        body,
+        out_shape=shapes,
+        in_specs=[VMEM] * len(near) + [HBM] * count,
+        out_specs=jax.tree.map(lambda _: outs, shapes),
+        scratch_shapes=[
+            *(pltpu.VMEM(arg.shape, arg.dtype) for arg in args),
+            pltpu.SemaphoreType.DMA((count,)),
+            *scratch,
+        ],
+        compiler_params=pltpu.CompilerParams(vmem_limit_bytes=room * MIB),
+        name=name,
+    )(*near, *args)
 
 
 def fold(parts, count):
@@ -296,44 +355,52 @@
         [planes],
     )
     parts = swap(sums, DP)
-    g_low, g_high = exchange_x(grad_0, grad_1)
-    merged, upper, lower = call(
+    upper, lower = fetch_and_call(
         gradient_kernel,
         "gradient",
-        14,
-        (f32(C, K), bf16(C, K), bf16(C, K)),
+        60,
+        (bf16(C, K), bf16(C, K)),
         (*block, grad_0, grad_1, error),
-        [planes],
-    )
-    parts, g_low, g_high, upper = tie((parts, g_low, g_high, upper))
+        [planes, pltpu.VMEM((C, K), BF16), pltpu.VMEM((C, K), BF16), pltpu.SemaphoreType.DMA((18,))],
+        HBM,
+    )
+    parts, upper, lower, near_0, near_1 = tie((parts, upper, lower, grad_0, grad_1))
     parts = swap(fold(parts, columns), BLOCK)
-    g_across = exchange_y(g_low, grad_0, grad_1, g_high)
-    input_grad = call(
+    g_low, g_high = exchange_x(near_0, near_1)
+    factor_p, bias_grad, blocks = fetch_and_call(
+        functools.partial(project_kernel, devices=devices),
+        "project",
+        60,
+        (f32(RANK, C), f32(1, C), f32(padded, RANK, C)),
+        (upper, lower),
+        near=(parts,),
+    )
+    new_error = fetch_and_call(
+        residual_kernel,
+        "residual",
+        60,
+        f32(C, K),
+        (factor_p, blocks, upper, lower),
+        [pltpu.VMEM((C, K), F32), pltpu.SemaphoreType.DMA((9,))],
+        HBM,
+    )
+    width = padded // columns * RANK
+    mine = swap(blocks, BLOCK)
+    mine, new_error, g_low, g_high = tie((mine, new_error, g_low, g_high))
+    mine = swap(fold(mine.reshape(columns, width, C), chips), DP)
+    g_across = exchange_y(g_low, near_0, near_1, g_high)
+    mine, g_across, act = tie((mine, g_across, act))
+    blocks = swap(fold(mine, columns), BLOCK).reshape(padded, RANK, C)
+    input_grad = fetch_and_call(
         backward_kernel,
         "backward",
-        8,
+        60,
         bf16(CX, CY, C, CZ),
-        (g_low, grad_0, grad_1, g_high, g_across, weights),
+        (g_low, near_0, near_1, g_high, g_across, weights),
         [planes],
     )
     activation = jnp.transpose(act, (2, 0, 1, 3))[None]
     input_grad = jnp.transpose(input_grad, (2, 0, 1, 3))[None]
-    parts, input_grad, activation = tie((parts, input_grad, activation))
-    factor_p, bias_grad, blocks = call(
-        functools.partial(project_kernel, devices=devices),
-        "project",
-        6,
-        (f32(RANK, C), f32(1, C), f32(padded, RANK, C)),
-        (parts, upper, lower),
-    )
-    new_error = call(
-        residual_kernel, "residual", 6, f32(C, K), (factor_p, blocks, merged)
-    )
-    width = padded // columns * RANK
-    mine, new_error = tie((swap(blocks, BLOCK), new_error))
-    mine = fold(mine.reshape(columns, width, C), chips)
-    mine = fold(swap(mine, DP), columns)
-    blocks = swap(mine, BLOCK).reshape(padded, RANK, C)
     factor_q = call(
         functools.partial(finish_kernel, devices=devices), "finish", 2, f32(RANK, K), (blocks,)
     )

time: 121 us -> 110 us (0.909)
  blocking collectives: 18.4 us -> 0 us
  local copies, waits for them, and re-layouts: 20.3 us -> 9.85 us
  Pallas kernels: 16.5 us -> 23.1 us
  starting transfers between devices: 49.5 us -> 55.5 us
  waiting for transfers between devices: 14.7 us -> 20.1 us
    all_to_all x1 -> x0, blocking collectives: 18.4 us -> none  [swap(): return lax.all_to_all(x, axes, 0, 0, tiled=True)]
    pallas_call x0 -> x4, Pallas kernels: none -> 16 us  [fetch_and_call(): pl.pallas_call(body, out_shape=shapes, in_specs=[VMEM] * len(near) + [HBM...]
    unnamed x51 -> x39, local copies, waits for them, and re-layouts: 19.2 us -> 8.71 us
    pallas_call x12 -> x8, Pallas kernels: 16.5 us -> 7.08 us  [call(): pl.pallas_call(kernel, out_shape=shapes, in_specs=[VMEM] * len(args), out...]
    all_to_all x4 -> x5, starting transfers between devices: 29.6 us -> 37.1 us  [swap(): return lax.all_to_all(x, axes, 0, 0, tiled=True)]
    all_to_all x4 -> x5, waiting for transfers between devices: 13.7 us -> 18.1 us  [swap(): return lax.all_to_all(x, axes, 0, 0, tiled=True)]
  transfers between devices with their start and end apart: 10 -> 11, of which waited for: 4 -> 7; matrix products, arithmetic and copies ran while one was open for 2% -> 3% of each run, Pallas kernels for 9% -> 16%
where the time goes in v4:
time: 110 us; the launch traced here: 109 us
  starting transfers between devices  55.5 us (50%)
  Pallas kernels  23.1 us (21%)
  waiting for transfers between devices  20.1 us (18%)
  local copies, waits for them, and re-layouts  9.85 us (9%)
    all_to_all x5, starting transfers between devices, swap(): return lax.all_to_all(x, axes, 0, 0, tiled=True)  37.1 us
    all_to_all x5, waiting for transfers between devices, swap(): return lax.all_to_all(x, axes, 0, 0, tiled=True)  18.1 us
    pallas_call x4, Pallas kernels, fetch_and_call(): pl.pallas_call(body, out_shape=shapes, in_specs=[VMEM] * len(near) + [HBM...  16 us
    ppermute x4, starting transfers between devices, exchange_x(): return (lax.ppermute(own_1, 'sx', up), lax.ppermute(own_0, 'sx', down))  9.92 us
    unnamed x39, local copies, waits for them, and re-layouts  8.71 us
    ppermute x2, starting transfers between devices, exchange_y(): return lax.ppermute(edge, 'sy', [(0, 1), (1, 0)])  8.4 us
    pallas_call x8, Pallas kernels, call(): pl.pallas_call(kernel, out_shape=shapes, in_specs=[VMEM] * len(args), out...  7.08 us
  transfers between devices with their start and end apart: 11, of which 7 were waited for; matrix products, arithmetic and copies ran while one was open for 3% of the time, Pallas kernels for 16%

profile of v4, /device:TPU:1, one launch (start us, length us, event | category | flops | bytes accessed | tf_op | source)
XLA Modules:
  0.0 109.4 jit_solution(17200172547292618140)
XLA Ops:
  0.6 0.0 copy-start.1
  0.6 1.1 %fusion = (bf16[1,128,1,4,128]{4,3,2,1,0:T(4,128)(2,1)S(1)}, bf16[1,128,1,4,128]{4,3,2,1,0:T(4,128)(2,1)S(1)}) fusion(bf16[1,128,2,4,128]{4,3,2,1,0:T(4,128)(2,1)} %param.6), kind=kLoop, calls=%fused_computation.3 | loop fusion | bytes 524288 | tf_op jit(solution)/shard_map/slice | solution.py:335
  1.8 0.0 copy-start.2
  1.8 4.0 %collective-permute-start = (bf16[4,128,128]{2,1,0:T(8,128)(2,1)S(1)}, bf16[4,128,128]{2,1,0:T(8,128)(2,1)S(1)}, u32[]{:S(2)}, u32[]{:S(2)}) collective-permute-start(bf16[4,128,128]{2,1,0:T(8,128)(2,1)S(1)} %bitcast.29), channel_id=1, source_target_pairs={{0,2},{2,4},{4,6},{6,8},{8,10},{10,12},{12,14},{1,3},{3,5},{5,7},{... | collective-permute-start | bytes 393224 | tf_op jit(solution)/shard_map/ppermute | solution.py:245
  5.9 0.0 copy-start.3
  5.9 1.3 %collective-permute-start.1 = (bf16[4,128,128]{2,1,0:T(8,128)(2,1)S(1)}, bf16[4,128,128]{2,1,0:T(8,128)(2,1)S(1)}, u32[]{:S(2)}, u32[]{:S(2)}) collective-permute-start(bf16[4,128,128]{2,1,0:T(8,128)(2,1)S(1)} %bitcast.33), channel_id=1, source_target_pairs={{2,0},{4,2},{6,4},{8,6},{10,8},{12,10},{14,12},{3,1},{5,3},{7,5},{... | collective-permute-start | bytes 393224 | tf_op jit(solution)/shard_map/ppermute | solution.py:245
  7.2 1.0 copy.22
  8.2 0.0 copy-done.1
  8.2 0.0 copy-start
  8.2 1.5 %copy-done = f32[1,1,1,128,3456]{4,3,2,1,0:T(8,128)S(1)} copy-done((f32[1,1,1,128,3456]{4,3,2,1,0:T(8,128)S(1)}, f32[1,1,1,128,3456]{4,3,2,1,0:T(8,128)}, u32[]{:S(2)}) %copy-start) | copy-done | bytes 1769496
  9.7 0.0 copy-start.13
  9.7 0.8 copy-done.13
  10.5 0.0 copy-start.14
  10.5 0.7 copy-done.14
  11.2 1.7 %prepare.1 = (bf16[144,3456]{1,0:T(8,128)(2,1)S(1)}, f32[4,128]{1,0:T(4,128)S(1)}, f32[128,128]{1,0:T(8,128)S(1)}) custom-call(bf16[27,128,128]{2,1,0:T(8,128)(2,1)S(1)} %copy-done.1, f32[4,3456]{1,0:T(4,128)S(1)} %copy-done.13, f32[128,3456]{1,0:T(8,128)S(1)} %bitcast.28, f32[1,128]{1,0:T(1,128)S(1)} %bitcast.41), custom_call_target="tpu_custom_call" | custom-call | tf_op jit(solution)/shard_map/prepare/pallas_call | solution.py:269
  12.8 0.0 collective-permute-done.low.refs_0_
  12.8 0.0 copy-start.8
  12.8 0.0 collective-permute-done.1.high.refs_3_
  12.9 0.0 copy-start.9
  12.9 6.0 %collective-permute-start.2 = (bf16[4,128,128]{2,1,0:T(8,128)(2,1)S(1)}, bf16[4,128,128]{2,1,0:T(8,128)(2,1)S(1)}, u32[]{:S(2)}, u32[]{:S(2)}) collective-permute-start(bf16[4,128,128]{2,1,0:T(8,128)(2,1)S(1)} %edge.2), channel_id=1, source_target_pairs={{0,1},{1,0},{2,3},{3,2},{4,5},{5,4},{6,7},{7,6},{8,9},{9,8},{10,11... | collective-permute-start | bytes 393224 | tf_op jit(solution)/shard_map/ppermute | solution.py:251
  19.0 1.0 collective-permute-done.2.across.refs_4_
  19.9 0.0 copy-done.2
  19.9 0.0 copy-done.3
  19.9 0.0 copy-start.12
  19.9 2.7 %forward.1 = (bf16[2,4,128,128]{3,2,1,0:T(8,128)(2,1)S(1)}, bf16[4,128,128]{2,1,0:T(8,128)(2,1)S(1)}, bf16[4,128,128]{2,1,0:T(8,128)(2,1)S(1)}, f32[32,8,128]{2,1,0:T(8,128)}) custom-call(bf16[4,128,128]{2,1,0:T(8,128)(2,1)S(1)} %collective-permute-done.low.refs_0_, bf16[4,128,128]{2,1,0:T(8,128)(2,1)S(1)} %bitcast.35, bf16[4,128,128]{2,1,0:T(8,128)(2,1)S(1)} %bitcast.31, ...), custom_call_target="tpu_custom_call" | custom-call | tf_op jit(solution)/shard_map/forward/pallas_call | solution.py:269
  22.6 0.6 copy-done.4
  23.3 0.7 copy-done.6
  23.9 9.8 %all-to-all-start = ((f32[32,8,128]{2,1,0:T(8,128)}), f32[32,8,128]{2,1,0:T(8,128)S(1)}, u32[]{:S(2)}, u32[]{:S(2)}) async-start(f32[32,8,128]{2,1,0:T(8,128)} %get-tuple-element.45), calls=%async_computation | async-start | bytes 262144 | tf_op jit(solution)/shard_map/all_to_all | solution.py:265
  33.8 0.0 copy-done.8
  33.8 0.0 copy-done.9
  33.8 0.0 copy-done.12
  33.8 5.0 %gradient.1 = (bf16[128,3456]{1,0:T(8,128)(2,1)}, bf16[128,3456]{1,0:T(8,128)(2,1)}) custom-call(bf16[4,128,128]{2,1,0:T(8,128)(2,1)} %copy-done.8, bf16[4,128,128]{2,1,0:T(8,128)(2,1)} %bitcast.36, bf16[4,128,128]{2,1,0:T(8,128)(2,1)} %bitcast.32, bf16[4,128,128]{2,1,0:T(8,128)(2,1)} %copy-done.9, bf16[4,128,128]{2,1,0:T(8,128)(2,1)} %copy-done.12, ...), custom_call_target="tpu_custom_call" | custom-call | tf_op jit(solution)/shard_map/gradient/pallas_call | solution.py:301
  38.8 4.1 %all-to-all-done.parts = f32[32,8,128]{2,1,0:T(8,128)S(1)} async-done(((f32[32,8,128]{2,1,0:T(8,128)}), f32[32,8,128]{2,1,0:T(8,128)S(1)}, u32[]{:S(2)}, u32[]{:S(2)}) %all-to-all-start) | async-done | bytes 131104 | tf_op jit(solution)/shard_map/all_to_all | solution.py:265
  42.9 0.7 fold.3
  43.6 11.5 %all-to-all-start.1 = ((f32[16,8,128]{2,1,0:T(8,128)}), f32[16,8,128]{2,1,0:T(8,128)S(1)}, u32[]{:S(2)}, u32[]{:S(2)}) async-start(f32[16,8,128]{2,1,0:T(8,128)} %fold.3), calls=%async_computation.1 | async-start | bytes 131072 | tf_op jit(solution)/shard_map/all_to_all | solution.py:265
  55.1 0.0 copy-done.7
  55.1 3.3 %collective-permute-start.3 = (bf16[4,128,128]{2,1,0:T(8,128)(2,1)S(1)}, bf16[4,128,128]{2,1,0:T(8,128)(2,1)S(1)}, u32[]{:S(2)}, u32[]{:S(2)}) collective-permute-start(bf16[4,128,128]{2,1,0:T(8,128)(2,1)S(1)} %copy-done.7), channel_id=1, source_target_pairs={{0,2},{2,4},{4,6},{6,8},{8,10},{10,12},{12,14},{1,3},{3,5},{5,7},{... | collective-permute-start | bytes 393224 | tf_op jit(solution)/shard_map/ppermute | solution.py:245
  58.4 0.0 copy-done.5
  58.4 1.3 %collective-permute-start.4 = (bf16[4,128,128]{2,1,0:T(8,128)(2,1)S(1)}, bf16[4,128,128]{2,1,0:T(8,128)(2,1)S(1)}, u32[]{:S(2)}, u32[]{:S(2)}) collective-permute-start(bf16[4,128,128]{2,1,0:T(8,128)(2,1)S(1)} %copy-done.5), channel_id=1, source_target_pairs={{2,0},{4,2},{6,4},{8,6},{10,8},{12,10},{14,12},{3,1},{5,3},{7,5},{... | collective-permute-start | bytes 393224 | tf_op jit(solution)/shard_map/ppermute | solution.py:245
  59.7 3.2 %all-to-all-done.1.refs_0_ = f32[16,8,128]{2,1,0:T(8,128)S(1)} async-done(((f32[16,8,128]{2,1,0:T(8,128)}), f32[16,8,128]{2,1,0:T(8,128)S(1)}, u32[]{:S(2)}, u32[]{:S(2)}) %all-to-all-start.1) | async-done | bytes 65568 | tf_op jit(solution)/shard_map/all_to_all | solution.py:265
  62.9 0.6 copy-done.15
  63.6 3.3 %project.1 = (f32[4,128]{1,0:T(4,128)}, f32[1,128]{1,0:T(1,128)}, f32[32,4,128]{2,1,0:T(4,128)}) custom-call(f32[16,8,128]{2,1,0:T(8,128)} %copy-done.15, bf16[128,3456]{1,0:T(8,128)(2,1)} %get-tuple-element.51.refs_1_.refs_2_, bf16[128,3456]{1,0:T(8,128)(2,1)} %get-tuple-element.52.refs_2_.refs_3_), custom_call_target="tpu_custom_call" | custom-call | tf_op jit(solution)/shard_map/project/pallas_call | solution.py:301
  66.8 6.5 %all-to-all-start.2 = ((f32[32,4,128]{2,1,0:T(4,128)}), f32[32,4,128]{2,1,0:T(4,128)S(1)}, u32[]{:S(2)}, u32[]{:S(2)}) async-start(f32[32,4,128]{2,1,0:T(4,128)} %get-tuple-element.53.refs_1_), calls=%async_computation.2 | async-start | bytes 131072 | tf_op jit(solution)/shard_map/all_to_all | solution.py:265
  73.3 3.9 %residual.1 = f32[128,3456]{1,0:T(8,128)} custom-call(f32[4,128]{1,0:T(4,128)} %get-tuple-element.69.refs_0_, f32[32,4,128]{2,1,0:T(4,128)} %get-tuple-element.53.refs_1_, bf16[128,3456]{1,0:T(8,128)(2,1)} %get-tuple-element.51.refs_1_.refs_2_, bf16[128,3456]{1,0:T(8,128)(2,1)} %get-tuple-element.52.refs_2_.refs_3_), custom_call_target="tpu_custom_call" | custom-call | tf_op jit(solution)/shard_map/residual/pallas_call | solution.py:301
  77.2 0.0 collective-permute-done.3.low.refs_0_
  77.2 0.0 copy-start.10
  77.2 0.0 collective-permute-done.4.high.refs_3_
  77.2 0.0 copy-start.11
  77.2 3.9 %all-to-all-done.2 = f32[32,4,128]{2,1,0:T(4,128)S(1)} async-done(((f32[32,4,128]{2,1,0:T(4,128)}), f32[32,4,128]{2,1,0:T(4,128)S(1)}, u32[]{:S(2)}, u32[]{:S(2)}) %all-to-all-start.2) | async-done | bytes 65568 | tf_op jit(solution)/shard_map/all_to_all | solution.py:265
  81.1 0.7 fold.4
  81.8 3.9 %all-to-all-start.3 = ((f32[32,8,128]{2,1,0:T(8,128)}), f32[32,8,128]{2,1,0:T(8,128)S(1)}, u32[]{:S(2)}, u32[]{:S(2)}) async-start(f32[32,8,128]{2,1,0:T(8,128)} %fold.4), calls=%async_computation.3 | async-start | bytes 262144 | tf_op jit(solution)/shard_map/all_to_all | solution.py:265
  85.8 2.4 %collective-permute-start.5 = (bf16[4,128,128]{2,1,0:T(8,128)(2,1)S(1)}, bf16[4,128,128]{2,1,0:T(8,128)(2,1)S(1)}, u32[]{:S(2)}, u32[]{:S(2)}) collective-permute-start(bf16[4,128,128]{2,1,0:T(8,128)(2,1)S(1)} %edge.3), channel_id=1, source_target_pairs={{0,1},{1,0},{2,3},{3,2},{4,5},{5,4},{6,7},{7,6},{8,9},{9,8},{10,11... | collective-permute-start | bytes 393224 | tf_op jit(solution)/shard_map/ppermute | solution.py:251
  88.2 1.0 collective-permute-done.5.refs_4_
  89.1 5.8 %all-to-all-done.3.parts = f32[32,8,128]{2,1,0:T(8,128)S(1)} async-done(((f32[32,8,128]{2,1,0:T(8,128)}), f32[32,8,128]{2,1,0:T(8,128)S(1)}, u32[]{:S(2)}, u32[]{:S(2)}) %all-to-all-start.3) | async-done | bytes 131104 | tf_op jit(solution)/shard_map/all_to_all | solution.py:265
  94.9 0.7 fold.5
  95.6 5.4 %all-to-all-start.4 = ((f32[16,8,128]{2,1,0:T(8,128)}), f32[16,8,128]{2,1,0:T(8,128)S(1)}, u32[]{:S(2)}, u32[]{:S(2)}) async-start(f32[16,8,128]{2,1,0:T(8,128)} %fold.5), calls=%async_computation.4 | async-start | bytes 131072 | tf_op jit(solution)/shard_map/all_to_all | solution.py:265
  101.0 0.0 copy-done.10
  101.0 0.0 copy-done.11
  101.0 0.0 copy-done.16
  101.0 3.9 %backward.1 = bf16[2,4,128,128]{3,2,1,0:T(8,128)(2,1)} custom-call(bf16[4,128,128]{2,1,0:T(8,128)(2,1)} %copy-done.10, bf16[4,128,128]{2,1,0:T(8,128)(2,1)} %copy-done.4, bf16[4,128,128]{2,1,0:T(8,128)(2,1)} %copy-done.6, bf16[4,128,128]{2,1,0:T(8,128)(2,1)} %copy-done.11, bf16[4,128,128]{2,1,0:T(8,128)(2,1)} %copy-done.16, bf16[27,128,128]{2,1,0:T(8,128)(2,1)} %refs_5_.1), custom_call_target="tpu_custom_call" | custom-call | tf_op jit(solution)/shard_map/backward/pallas_call | solution.py:301
  104.9 0.9 copy.15
  105.8 1.9 %copy.16 = bf16[1,128,2,4,128]{4,3,2,1,0:T(4,128)(2,1)} copy(bf16[1,128,2,4,128]{4,1,3,2,0:T(8,128)(2,1)} %bitcast.43) | data formatting | bytes 524288
  107.7 1.1 %all-to-all-done.4 = f32[16,8,128]{2,1,0:T(8,128)S(1)} async-done(((f32[16,8,128]{2,1,0:T(8,128)}), f32[16,8,128]{2,1,0:T(8,128)S(1)}, u32[]{:S(2)}, u32[]{:S(2)}) %all-to-all-start.4) | async-done | bytes 65568 | tf_op jit(solution)/shard_map/all_to_all | solution.py:265
  108.8 0.6 finish.1
  (10 shorter events, 0.1 us)
Async XLA Ops:
  0.6 7.6 %copy-start.1 = (bf16[27,128,128]{2,1,0:T(8,128)(2,1)S(1)}, bf16[27,128,128]{2,1,0:T(8,128)(2,1)}, u32[]{:S(2)}) copy-start(bf16[27,128,128]{2,1,0:T(8,128)(2,1)} %refs_5_.1) | copy-start | bytes 2654212
  1.8 18.1 %copy-start.2 = (bf16[1,128,1,4,128]{4,1,3,2,0:T(8,128)(2,1)}, bf16[1,128,1,4,128]{4,1,3,2,0:T(8,128)(2,1)S(1)}, u32[]{:S(2)}) copy-start(bf16[1,128,1,4,128]{4,1,3,2,0:T(8,128)(2,1)S(1)} %copy.24) | copy-start | bytes 393220
  1.8 11.0 %collective-permute-start = (bf16[4,128,128]{2,1,0:T(8,128)(2,1)S(1)}, bf16[4,128,128]{2,1,0:T(8,128)(2,1)S(1)}, u32[]{:S(2)}, u32[]{:S(2)}) collective-permute-start(bf16[4,128,128]{2,1,0:T(8,128)(2,1)S(1)} %bitcast.29), channel_id=1, source_target_pairs={{0,2},{2,4},{4,6},{6,8},{8,10},{10,12},{12,14},{1,3},{3,5},{5,7},{... | collective-permute-start | bytes 393224 | tf_op jit(solution)/shard_map/ppermute | solution.py:245
  5.9 14.0 %copy-start.3 = (bf16[1,128,1,4,128]{4,1,3,2,0:T(8,128)(2,1)}, bf16[1,128,1,4,128]{4,1,3,2,0:T(8,128)(2,1)S(1)}, u32[]{:S(2)}) copy-start(bf16[1,128,1,4,128]{4,1,3,2,0:T(8,128)(2,1)S(1)} %copy.23) | copy-start | bytes 393220
  5.9 6.9 %collective-permute-start.1 = (bf16[4,128,128]{2,1,0:T(8,128)(2,1)S(1)}, bf16[4,128,128]{2,1,0:T(8,128)(2,1)S(1)}, u32[]{:S(2)}, u32[]{:S(2)}) collective-permute-start(bf16[4,128,128]{2,1,0:T(8,128)(2,1)S(1)} %bitcast.33), channel_id=1, source_target_pairs={{2,0},{4,2},{6,4},{8,6},{10,8},{12,10},{14,12},{3,1},{5,3},{7,5},{... | collective-permute-start | bytes 393224 | tf_op jit(solution)/shard_map/ppermute | solution.py:245
  8.2 1.5 %copy-start = (f32[1,1,1,128,3456]{4,3,2,1,0:T(8,128)S(1)}, f32[1,1,1,128,3456]{4,3,2,1,0:T(8,128)}, u32[]{:S(2)}) copy-start(f32[1,1,1,128,3456]{4,3,2,1,0:T(8,128)} %param.10) | copy-start | bytes 5308420
  9.7 0.8 copy-start.13
  10.5 0.7 copy-start.14
  12.8 21.0 %copy-start.8 = (bf16[4,128,128]{2,1,0:T(8,128)(2,1)}, bf16[4,128,128]{2,1,0:T(8,128)(2,1)S(1)}, u32[]{:S(2)}) copy-start(bf16[4,128,128]{2,1,0:T(8,128)(2,1)S(1)} %collective-permute-done.low.refs_0_) | copy-start | bytes 393220
  12.9 20.9 %copy-start.9 = (bf16[4,128,128]{2,1,0:T(8,128)(2,1)}, bf16[4,128,128]{2,1,0:T(8,128)(2,1)S(1)}, u32[]{:S(2)}) copy-start(bf16[4,128,128]{2,1,0:T(8,128)(2,1)S(1)} %collective-permute-done.1.high.refs_3_) | copy-start | bytes 393220
  12.9 7.0 %collective-permute-start.2 = (bf16[4,128,128]{2,1,0:T(8,128)(2,1)S(1)}, bf16[4,128,128]{2,1,0:T(8,128)(2,1)S(1)}, u32[]{:S(2)}, u32[]{:S(2)}) collective-permute-start(bf16[4,128,128]{2,1,0:T(8,128)(2,1)S(1)} %edge.2), channel_id=1, source_target_pairs={{0,1},{1,0},{2,3},{3,2},{4,5},{5,4},{6,7},{7,6},{8,9},{9,8},{10,11... | collective-permute-start | bytes 393224 | tf_op jit(solution)/shard_map/ppermute | solution.py:251
  19.9 13.9 %copy-start.12 = (bf16[4,128,128]{2,1,0:T(8,128)(2,1)}, bf16[4,128,128]{2,1,0:T(8,128)(2,1)S(1)}, u32[]{:S(2)}) copy-start(bf16[4,128,128]{2,1,0:T(8,128)(2,1)S(1)} %collective-permute-done.2.across.refs_4_) | copy-start | bytes 393220
  22.6 0.6 copy-start.4
  23.3 0.7 copy-start.6
  23.9 31.2 %copy-start.7 = (bf16[4,128,128]{2,1,0:T(8,128)(2,1)S(1)}, bf16[4,128,128]{2,1,0:T(8,128)(2,1)}, u32[]{:S(2)}) copy-start(bf16[4,128,128]{2,1,0:T(8,128)(2,1)} %copy-done.6) | copy-start | bytes 393220
  23.9 34.5 %copy-start.5 = (bf16[4,128,128]{2,1,0:T(8,128)(2,1)S(1)}, bf16[4,128,128]{2,1,0:T(8,128)(2,1)}, u32[]{:S(2)}) copy-start(bf16[4,128,128]{2,1,0:T(8,128)(2,1)} %copy-done.4) | copy-start | bytes 393220
  23.9 19.0 %all-to-all-start = ((f32[32,8,128]{2,1,0:T(8,128)}), f32[32,8,128]{2,1,0:T(8,128)S(1)}, u32[]{:S(2)}, u32[]{:S(2)}) async-start(f32[32,8,128]{2,1,0:T(8,128)} %get-tuple-element.45), calls=%async_computation | async-start | bytes 262144 | tf_op jit(solution)/shard_map/all_to_all | solution.py:265
  43.6 19.3 %all-to-all-start.1 = ((f32[16,8,128]{2,1,0:T(8,128)}), f32[16,8,128]{2,1,0:T(8,128)S(1)}, u32[]{:S(2)}, u32[]{:S(2)}) async-start(f32[16,8,128]{2,1,0:T(8,128)} %fold.3), calls=%async_computation.1 | async-start | bytes 131072 | tf_op jit(solution)/shard_map/all_to_all | solution.py:265
  55.1 22.1 %collective-permute-start.3 = (bf16[4,128,128]{2,1,0:T(8,128)(2,1)S(1)}, bf16[4,128,128]{2,1,0:T(8,128)(2,1)S(1)}, u32[]{:S(2)}, u32[]{:S(2)}) collective-permute-start(bf16[4,128,128]{2,1,0:T(8,128)(2,1)S(1)} %copy-done.7), channel_id=1, source_target_pairs={{0,2},{2,4},{4,6},{6,8},{8,10},{10,12},{12,14},{1,3},{3,5},{5,7},{... | collective-permute-start | bytes 393224 | tf_op jit(solution)/shard_map/ppermute | solution.py:245
  58.4 18.8 %collective-permute-start.4 = (bf16[4,128,128]{2,1,0:T(8,128)(2,1)S(1)}, bf16[4,128,128]{2,1,0:T(8,128)(2,1)S(1)}, u32[]{:S(2)}, u32[]{:S(2)}) collective-permute-start(bf16[4,128,128]{2,1,0:T(8,128)(2,1)S(1)} %copy-done.5), channel_id=1, source_target_pairs={{2,0},{4,2},{6,4},{8,6},{10,8},{12,10},{14,12},{3,1},{5,3},{7,5},{... | collective-permute-start | bytes 393224 | tf_op jit(solution)/shard_map/ppermute | solution.py:245
  62.9 0.6 copy-start.15
  66.8 14.3 %all-to-all-start.2 = ((f32[32,4,128]{2,1,0:T(4,128)}), f32[32,4,128]{2,1,0:T(4,128)S(1)}, u32[]{:S(2)}, u32[]{:S(2)}) async-start(f32[32,4,128]{2,1,0:T(4,128)} %get-tuple-element.53.refs_1_), calls=%async_computation.2 | async-start | bytes 131072 | tf_op jit(solution)/shard_map/all_to_all | solution.py:265
  77.2 23.7 %copy-start.10 = (bf16[4,128,128]{2,1,0:T(8,128)(2,1)}, bf16[4,128,128]{2,1,0:T(8,128)(2,1)S(1)}, u32[]{:S(2)}) copy-start(bf16[4,128,128]{2,1,0:T(8,128)(2,1)S(1)} %collective-permute-done.3.low.refs_0_) | copy-start | bytes 393220
  77.2 23.7 %copy-start.11 = (bf16[4,128,128]{2,1,0:T(8,128)(2,1)}, bf16[4,128,128]{2,1,0:T(8,128)(2,1)S(1)}, u32[]{:S(2)}) copy-start(bf16[4,128,128]{2,1,0:T(8,128)(2,1)S(1)} %collective-permute-done.4.high.refs_3_) | copy-start | bytes 393220
  81.8 13.1 %all-to-all-start.3 = ((f32[32,8,128]{2,1,0:T(8,128)}), f32[32,8,128]{2,1,0:T(8,128)S(1)}, u32[]{:S(2)}, u32[]{:S(2)}) async-start(f32[32,8,128]{2,1,0:T(8,128)} %fold.4), calls=%async_computation.3 | async-start | bytes 262144 | tf_op jit(solution)/shard_map/all_to_all | solution.py:265
  85.8 3.3 %collective-permute-start.5 = (bf16[4,128,128]{2,1,0:T(8,128)(2,1)S(1)}, bf16[4,128,128]{2,1,0:T(8,128)(2,1)S(1)}, u32[]{:S(2)}, u32[]{:S(2)}) collective-permute-start(bf16[4,128,128]{2,1,0:T(8,128)(2,1)S(1)} %edge.3), channel_id=1, source_target_pairs={{0,1},{1,0},{2,3},{3,2},{4,5},{5,4},{6,7},{7,6},{8,9},{9,8},{10,11... | collective-permute-start | bytes 393224 | tf_op jit(solution)/shard_map/ppermute | solution.py:251
  89.1 11.8 %copy-start.16 = (bf16[4,128,128]{2,1,0:T(8,128)(2,1)}, bf16[4,128,128]{2,1,0:T(8,128)(2,1)S(1)}, u32[]{:S(2)}) copy-start(bf16[4,128,128]{2,1,0:T(8,128)(2,1)S(1)} %collective-permute-done.5.refs_4_) | copy-start | bytes 393220
  95.6 13.2 %all-to-all-start.4 = ((f32[16,8,128]{2,1,0:T(8,128)}), f32[16,8,128]{2,1,0:T(8,128)S(1)}, u32[]{:S(2)}, u32[]{:S(2)}) async-start(f32[16,8,128]{2,1,0:T(8,128)} %fold.5), calls=%async_computation.4 | async-start | bytes 131072 | tf_op jit(solution)/shard_map/all_to_all | solution.py:265

commit v5 on v4

--- a/solution.py
+++ b/solution.py
@@ -95,9 +95,10 @@
 
 def forward_kernel(
     low, own_0, own_1, high, across, upstream, lhs, bias, base,
-    act, grad_0, grad_1, sums, planes,
+    act, grad_0, grad_1, edges, sums, planes,
 ):
     fill_planes(planes, low, own_0, own_1, high, across)
+    first_core = lax.axis_index("sy") == 0
     joint = jnp.zeros((EXTRA, C), F32)
     for x, grad in enumerate((grad_0, grad_1)):
         total = convolve(planes, lhs, x)
@@ -106,12 +107,13 @@
         active = (pre * sigma).astype(BF16)
         slope = sigma * (1.0 + pre * (1.0 - sigma))
         grads = []
+        act[:, x] = active.reshape(C, CY, CZ)
         for y in range(CY):
             span = slice(y * CZ, (y + 1) * CZ)
-            act[x, y] = active[:, span]
             piece = (upstream[x, y].astype(F32) * slope[:, span]).astype(BF16)
             grad[y] = piece
             grads.append(piece)
+        edges[x] = jnp.where(first_core, grads[CY - 1], grads[0])
         field = total[C : C + RANK] + total[C + RANK : C + 2 * RANK]
         field = field + total[C + 2 * RANK : C + 3 * RANK]
         first, second, third = pieces(field)
@@ -168,15 +170,15 @@
     for source in range(1, parts.shape[0]):
         sums = sums + parts[source]
     bias_grad[...] = sums[RANK : RANK + 1] / devices
-    rows = []
+    rows = sums[:RANK]
+    done = []
     for r in range(RANK):
-        vector = sums[r : r + 1]
-        for basis in rows:
-            vector = vector - jnp.sum(basis * vector) * basis
-        vector = vector / jnp.sqrt(jnp.sum(vector * vector) + 1e-06)
-        rows.append(vector)
-        factor_p[pl.ds(r, 1), :] = vector
-    basis = jnp.concatenate(rows, axis=0)
+        vector = rows[r : r + 1]
+        vector = vector / jnp.sqrt(jnp.sum(vector * vector, axis=1, keepdims=True) + 1e-06)
+        done.append(vector)
+        rows = rows - jnp.sum(rows * vector, axis=1, keepdims=True) * vector
+    basis = jnp.concatenate(done, axis=0)
+    factor_p[...] = basis
     first, second, third = pieces(basis)
     stacked = jnp.concatenate([first, second, third, jnp.zeros_like(basis)], axis=0).astype(BF16)
     wait(0, 1)
@@ -213,8 +215,9 @@
 
 
 def backward_kernel(wait, held, out, planes):
-    low, own_0, own_1, high, across, weights = held
+    low, own_0, own_1, high, middle, weights = held
     wait(0, 1, 2, 3, 4)
+    across = (low[CY], middle[0], middle[1], high[CY])
     fill_planes(planes, low, own_0, own_1, high, across)
     wait(5)
     totals = [None] * CX
@@ -227,15 +230,24 @@
             )
             totals[x] = part if totals[x] is None else totals[x] + part
     for x in range(CX):
-        total = totals[x].astype(BF16)
+        out[:, x] = totals[x].astype(BF16).reshape(C, CY, CZ)
+
+
+def pack_kernel(own_0, own_1, middle, down, up):
+    for own, row, out in ((own_0, 0, down), (own_1, 1, up)):
         for y in range(CY):
-            out[x, y] = total[:, y * CZ : (y + 1) * CZ]
+            out[y] = own[y]
+        out[CY] = middle[row]
 
 
 def edge_kernel(low, own_0, own_1, high, edge):
     first = lax.axis_index("sy") == 0
     for xp, source in enumerate((low, own_0, own_1, high)):
         edge[xp] = jnp.where(first, source[CY - 1], source[0])
+
+
+def swap_cores(edge):
+    return lax.ppermute(edge, "sy", [(0, 1), (1, 0)])
 
 
 def exchange_x(own_0, own_1):
@@ -248,7 +260,7 @@
 def exchange_y(low, own_0, own_1, high):
     slab = jax.ShapeDtypeStruct((PX, C, CZ), BF16)
     edge = call(edge_kernel, "edge", 2, slab, (low, own_0, own_1, high))
-    return lax.ppermute(edge, "sy", [(0, 1), (1, 0)])
+    return swap_cores(edge)
 
 
 tie = lax.optimization_barrier
@@ -346,11 +358,17 @@
     low, high, lhs, base, bias, upstream = tie((low, high, lhs, base, bias, upstream))
     across = exchange_y(low, own_0, own_1, high)
     block = (low, own_0, own_1, high, across)
-    act, grad_0, grad_1, sums = call(
+    act, grad_0, grad_1, edges, sums = call(
         forward_kernel,
         "forward",
         10,
-        (bf16(CX, CY, C, CZ), bf16(CY, C, CZ), bf16(CY, C, CZ), f32(chips, 2 * RANK, C)),
+        (
+            bf16(C, CX, CY, CZ),
+            bf16(CY, C, CZ),
+            bf16(CY, C, CZ),
+            bf16(CX, C, CZ),
+            f32(chips, 2 * RANK, C),
+        ),
         (*block, upstream, lhs, bias, base),
         [planes],
     )
@@ -364,9 +382,9 @@
         [planes, pltpu.VMEM((C, K), BF16), pltpu.VMEM((C, K), BF16), pltpu.SemaphoreType.DMA((18,))],
         HBM,
     )
-    parts, upper, lower, near_0, near_1 = tie((parts, upper, lower, grad_0, grad_1))
+    parts, upper, lower, edges = tie((parts, upper, lower, edges))
     parts = swap(fold(parts, columns), BLOCK)
-    g_low, g_high = exchange_x(near_0, near_1)
+    middle = swap_cores(edges)
     factor_p, bias_grad, blocks = fetch_and_call(
         functools.partial(project_kernel, devices=devices),
         "project",
@@ -386,27 +404,32 @@
     )
     width = padded // columns * RANK
     mine = swap(blocks, BLOCK)
-    mine, new_error, g_low, g_high = tie((mine, new_error, g_low, g_high))
+    mine, new_error, middle, near_0, near_1 = tie((mine, new_error, middle, grad_0, grad_1))
     mine = swap(fold(mine.reshape(columns, width, C), chips), DP)
-    g_across = exchange_y(g_low, near_0, near_1, g_high)
-    mine, g_across, act = tie((mine, g_across, act))
+    down, up = call(
+        pack_kernel,
+        "pack",
+        4,
+        (bf16(CY + 1, C, CZ), bf16(CY + 1, C, CZ)),
+        (near_0, near_1, middle),
+    )
+    g_low, g_high = exchange_x(down, up)
+    mine, g_low, g_high = tie((mine, g_low, g_high))
     blocks = swap(fold(mine, columns), BLOCK).reshape(padded, RANK, C)
     input_grad = fetch_and_call(
         backward_kernel,
         "backward",
         60,
-        bf16(CX, CY, C, CZ),
-        (g_low, near_0, near_1, g_high, g_across, weights),
+        bf16(C, CX, CY, CZ),
+        (g_low, near_0, near_1, g_high, middle, weights),
         [planes],
     )
-    activation = jnp.transpose(act, (2, 0, 1, 3))[None]
-    input_grad = jnp.transpose(input_grad, (2, 0, 1, 3))[None]
     factor_q = call(
         functools.partial(finish_kernel, devices=devices), "finish", 2, f32(RANK, K), (blocks,)
     )
     return (
-        activation,
-        input_grad,
+        act[None],
+        input_grad[None],
         bias_grad[0],
         factor_p,
         factor_q,

time: 110 us -> 109 us (level)
  blocking collectives: 0 us -> 19.2 us
  starting transfers between devices: 55.5 us -> 42.2 us
  waiting for transfers between devices: 20.1 us -> 16.3 us
  local copies, waits for them, and re-layouts: 9.85 us -> 6.45 us
    all_to_all x0 -> x1, blocking collectives: none -> 19.2 us  [swap(): return lax.all_to_all(x, axes, 0, 0, tiled=True)]
    all_to_all x5 -> x4, starting transfers between devices: 37.1 us -> 25.3 us  [swap(): return lax.all_to_all(x, axes, 0, 0, tiled=True)]
    all_to_all x5 -> x4, waiting for transfers between devices: 18.1 us -> 9.9 us  [swap(): return lax.all_to_all(x, axes, 0, 0, tiled=True)]
    ppermute x4, waiting for transfers between devices: 0.02 us -> 5.46 us  [exchange_x(): return (lax.ppermute(own_1, 'sx', up), lax.ppermute(own_0, 'sx', down))]
    unnamed x39 -> x35, local copies, waits for them, and re-layouts: 8.71 us -> 5.31 us
    ppermute x4, starting transfers between devices: 9.92 us -> 8.76 us  [exchange_x(): return (lax.ppermute(own_1, 'sx', up), lax.ppermute(own_0, 'sx', down))]
  transfers between devices with their start and end apart: 11 -> 10, of which waited for: 7 -> 7; matrix products, arithmetic and copies ran while one was open for 3% -> 1% of each run, Pallas kernels for 16% -> 13%
where the time goes in v5:
time: 109 us; the launch traced here: 108 us
  starting transfers between devices  42.2 us (39%)
  Pallas kernels  22.7 us (21%)
  blocking collectives  19.2 us (18%)
  waiting for transfers between devices  16.3 us (15%)
  local copies, waits for them, and re-layouts  6.45 us (6%)
    all_to_all x4, starting transfers between devices, swap(): return lax.all_to_all(x, axes, 0, 0, tiled=True)  25.3 us
    all_to_all x1, blocking collectives, swap(): return lax.all_to_all(x, axes, 0, 0, tiled=True)  19.2 us
    pallas_call x4, Pallas kernels, fetch_and_call(): pl.pallas_call(body, out_shape=shapes, in_specs=[VMEM] * len(near) + [HBM...  16.1 us
    all_to_all x4, waiting for transfers between devices, swap(): return lax.all_to_all(x, axes, 0, 0, tiled=True)  9.9 us
    ppermute x4, starting transfers between devices, exchange_x(): return (lax.ppermute(own_1, 'sx', up), lax.ppermute(own_0, 'sx', down))  8.76 us
    ppermute x2, starting transfers between devices, swap_cores(): return lax.ppermute(edge, 'sy', [(0, 1), (1, 0)])  8.17 us
    pallas_call x8, Pallas kernels, call(): pl.pallas_call(kernel, out_shape=shapes, in_specs=[VMEM] * len(args), out...  6.59 us
    ppermute x4, waiting for transfers between devices, exchange_x(): return (lax.ppermute(own_1, 'sx', up), lax.ppermute(own_0, 'sx', down))  5.46 us
  transfers between devices with their start and end apart: 10, of which 7 were waited for; matrix products, arithmetic and copies ran while one was open for 1% of the time, Pallas kernels for 13%

profile of v5, /device:TPU:1, one launch (start us, length us, event | category | flops | bytes accessed | tf_op | source)
XLA Modules:
  0.0 107.8 jit_solution(14528448853948298392)
XLA Ops:
  0.6 0.0 copy-start.1
  0.6 1.1 %fusion = (bf16[1,128,1,4,128]{4,3,2,1,0:T(4,128)(2,1)S(1)}, bf16[1,128,1,4,128]{4,3,2,1,0:T(4,128)(2,1)S(1)}) fusion(bf16[1,128,2,4,128]{4,3,2,1,0:T(4,128)(2,1)} %param.6), kind=kLoop, calls=%fused_computation.3 | loop fusion | bytes 524288 | tf_op jit(solution)/shard_map/slice | solution.py:347
  1.8 0.0 copy-start.2
  1.8 4.0 %collective-permute-start = (bf16[4,128,128]{2,1,0:T(8,128)(2,1)S(1)}, bf16[4,128,128]{2,1,0:T(8,128)(2,1)S(1)}, u32[]{:S(2)}, u32[]{:S(2)}) collective-permute-start(bf16[4,128,128]{2,1,0:T(8,128)(2,1)S(1)} %bitcast.25), channel_id=1, source_target_pairs={{0,2},{2,4},{4,6},{6,8},{8,10},{10,12},{12,14},{1,3},{3,5},{5,7},{... | collective-permute-start | bytes 393224 | tf_op jit(solution)/shard_map/ppermute | solution.py:257
  5.9 0.0 copy-start.3
  5.9 1.3 %collective-permute-start.1 = (bf16[4,128,128]{2,1,0:T(8,128)(2,1)S(1)}, bf16[4,128,128]{2,1,0:T(8,128)(2,1)S(1)}, u32[]{:S(2)}, u32[]{:S(2)}) collective-permute-start(bf16[4,128,128]{2,1,0:T(8,128)(2,1)S(1)} %bitcast.29), channel_id=1, source_target_pairs={{2,0},{4,2},{6,4},{8,6},{10,8},{12,10},{14,12},{3,1},{5,3},{7,5},{... | collective-permute-start | bytes 393224 | tf_op jit(solution)/shard_map/ppermute | solution.py:257
  7.2 1.0 copy.20
  8.2 0.0 copy-done.1
  8.2 0.0 copy-start
  8.2 1.5 %copy-done = f32[1,1,1,128,3456]{4,3,2,1,0:T(8,128)S(1)} copy-done((f32[1,1,1,128,3456]{4,3,2,1,0:T(8,128)S(1)}, f32[1,1,1,128,3456]{4,3,2,1,0:T(8,128)}, u32[]{:S(2)}) %copy-start) | copy-done | bytes 1769496
  9.7 0.0 copy-start.12
  9.7 0.8 copy-done.12
  10.5 0.0 copy-start.13
  10.5 0.7 copy-done.13
  11.2 1.7 %prepare.1 = (bf16[144,3456]{1,0:T(8,128)(2,1)S(1)}, f32[4,128]{1,0:T(4,128)S(1)}, f32[128,128]{1,0:T(8,128)S(1)}) custom-call(bf16[27,128,128]{2,1,0:T(8,128)(2,1)S(1)} %copy-done.1, f32[4,3456]{1,0:T(4,128)S(1)} %copy-done.12, f32[128,3456]{1,0:T(8,128)S(1)} %bitcast.24, f32[1,128]{1,0:T(1,128)S(1)} %bitcast.36), custom_call_target="tpu_custom_call" | custom-call | tf_op jit(solution)/shard_map/prepare/pallas_call | solution.py:281
  12.8 0.0 collective-permute-done.low.refs_0_
  12.8 0.0 copy-start.4
  12.8 0.0 collective-permute-done.1.high.refs_3_
  12.9 0.0 copy-start.5
  12.9 6.0 %collective-permute-start.2 = (bf16[4,128,128]{2,1,0:T(8,128)(2,1)S(1)}, bf16[4,128,128]{2,1,0:T(8,128)(2,1)S(1)}, u32[]{:S(2)}, u32[]{:S(2)}) collective-permute-start(bf16[4,128,128]{2,1,0:T(8,128)(2,1)S(1)} %edge.1), channel_id=1, source_target_pairs={{0,1},{1,0},{2,3},{3,2},{4,5},{5,4},{6,7},{7,6},{8,9},{9,8},{10,11... | collective-permute-start | bytes 393224 | tf_op jit(solution)/shard_map/ppermute | solution.py:250
  19.0 1.0 collective-permute-done.2.across.refs_4_
  19.9 0.0 copy-done.2
  19.9 0.0 copy-done.3
  19.9 0.0 copy-start.10
  19.9 2.8 %forward.1 = (bf16[128,2,4,128]{3,2,1,0:T(4,128)(2,1)}, bf16[4,128,128]{2,1,0:T(8,128)(2,1)S(1)}, bf16[4,128,128]{2,1,0:T(8,128)(2,1)S(1)}, bf16[2,128,128]{2,1,0:T(8,128)(2,1)S(1)}, f32[32,8,128]{2,1,0:T(8,128)}) custom-call(bf16[4,128,128]{2,1,0:T(8,128)(2,1)S(1)} %collective-permute-done.low.refs_0_, bf16[4,128,128]{2,1,0:T(8,128)(2,1)S(1)} %bitcast.31, ...), custom_call_target="tpu_custom_call" | custom-call | tf_op jit(solution)/shard_map/forward/pallas_call | solution.py:281
  22.8 0.0 copy-start.6
  22.8 0.6 copy-done.6
  23.4 0.0 copy-start.8
  23.4 0.6 copy-done.8
  24.1 9.7 %all-to-all-start = ((f32[32,8,128]{2,1,0:T(8,128)}), f32[32,8,128]{2,1,0:T(8,128)S(1)}, u32[]{:S(2)}, u32[]{:S(2)}) async-start(f32[32,8,128]{2,1,0:T(8,128)} %get-tuple-element.49), calls=%async_computation | async-start | bytes 262144 | tf_op jit(solution)/shard_map/all_to_all | solution.py:277
  33.8 0.0 copy-done.4
  33.8 0.0 copy-done.5
  33.8 0.0 copy-done.10
  33.8 5.0 %gradient.1 = (bf16[128,3456]{1,0:T(8,128)(2,1)}, bf16[128,3456]{1,0:T(8,128)(2,1)}) custom-call(bf16[4,128,128]{2,1,0:T(8,128)(2,1)} %copy-done.4, bf16[4,128,128]{2,1,0:T(8,128)(2,1)} %bitcast.32, bf16[4,128,128]{2,1,0:T(8,128)(2,1)} %bitcast.28, bf16[4,128,128]{2,1,0:T(8,128)(2,1)} %copy-done.5, bf16[4,128,128]{2,1,0:T(8,128)(2,1)} %copy-done.10, ...), custom_call_target="tpu_custom_call" | custom-call | tf_op jit(solution)/shard_map/gradient/pallas_call | solution.py:313
  38.8 4.1 %all-to-all-done.parts = f32[32,8,128]{2,1,0:T(8,128)S(1)} async-done(((f32[32,8,128]{2,1,0:T(8,128)}), f32[32,8,128]{2,1,0:T(8,128)S(1)}, u32[]{:S(2)}, u32[]{:S(2)}) %all-to-all-start) | async-done | bytes 131104 | tf_op jit(solution)/shard_map/all_to_all | solution.py:277
  43.0 19.2 %all_to_all.25.refs_0_ = f32[16,8,128]{2,1,0:T(8,128)} all-to-all(f32[16,8,128]{2,1,0:T(8,128)S(1)} %fold.3), channel_id=1, replica_groups=mesh['dp_0'=4,'dp_1'=8,'sx'=8,'sy'=2] {'sx','sy'}, dimensions={0} | all-to-all | bytes 131072 | tf_op jit(solution)/shard_map/all_to_all | solution.py:277
  62.2 3.3 %project.1 = (f32[4,128]{1,0:T(4,128)}, f32[1,128]{1,0:T(1,128)}, f32[32,4,128]{2,1,0:T(4,128)}) custom-call(f32[16,8,128]{2,1,0:T(8,128)} %all_to_all.25.refs_0_, bf16[128,3456]{1,0:T(8,128)(2,1)} %get-tuple-element.56.refs_1_.refs_2_, bf16[128,3456]{1,0:T(8,128)(2,1)} %get-tuple-element.57.refs_2_.refs_3_), custom_call_target="tpu_custom_call" | custom-call | tf_op jit(solution)/shard_map/project/pallas_call | solution.py:313
  65.4 3.5 %all-to-all-start.2 = ((f32[32,4,128]{2,1,0:T(4,128)}), f32[32,4,128]{2,1,0:T(4,128)S(1)}, u32[]{:S(2)}, u32[]{:S(2)}) async-start(f32[32,4,128]{2,1,0:T(4,128)} %get-tuple-element.58.refs_1_), calls=%async_computation.2 | async-start | bytes 131072 | tf_op jit(solution)/shard_map/all_to_all | solution.py:277
  68.9 2.1 %collective-permute-start.3 = (bf16[2,128,128]{2,1,0:T(8,128)(2,1)S(1)}, bf16[2,128,128]{2,1,0:T(8,128)(2,1)S(1)}, u32[]{:S(2)}, u32[]{:S(2)}) collective-permute-start(bf16[2,128,128]{2,1,0:T(8,128)(2,1)S(1)} %get-tuple-element.60), channel_id=1, source_target_pairs={{0,1},{1,0},{2,3},{3,2},{4,5},{5,4},{6,7},{7,6},{8,9},{9,8},{10,11... | collective-permute-start | bytes 196616 | tf_op jit(solution)/shard_map/ppermute | solution.py:250
  71.0 0.0 copy-start.7
  71.1 0.0 copy-start.9
  71.1 3.9 %residual.1 = f32[128,3456]{1,0:T(8,128)} custom-call(f32[4,128]{1,0:T(4,128)} %get-tuple-element.36.refs_0_, f32[32,4,128]{2,1,0:T(4,128)} %get-tuple-element.58.refs_1_, bf16[128,3456]{1,0:T(8,128)(2,1)} %get-tuple-element.56.refs_1_.refs_2_, bf16[128,3456]{1,0:T(8,128)(2,1)} %get-tuple-element.57.refs_2_.refs_3_), custom_call_target="tpu_custom_call" | custom-call | tf_op jit(solution)/shard_map/residual/pallas_call | solution.py:313
  75.0 0.0 collective-permute-done.3.middle.refs_4_
  75.0 0.0 copy-start.11
  75.0 1.8 %all-to-all-done.2 = f32[32,4,128]{2,1,0:T(4,128)S(1)} async-done(((f32[32,4,128]{2,1,0:T(4,128)}), f32[32,4,128]{2,1,0:T(4,128)S(1)}, u32[]{:S(2)}, u32[]{:S(2)}) %all-to-all-start.2) | async-done | bytes 65568 | tf_op jit(solution)/shard_map/all_to_all | solution.py:277
  76.7 0.7 fold.4
  77.4 3.9 %all-to-all-start.3 = ((f32[32,8,128]{2,1,0:T(8,128)}), f32[32,8,128]{2,1,0:T(8,128)S(1)}, u32[]{:S(2)}, u32[]{:S(2)}) async-start(f32[32,8,128]{2,1,0:T(8,128)} %fold.4), calls=%async_computation.3 | async-start | bytes 262144 | tf_op jit(solution)/shard_map/all_to_all | solution.py:277
  81.4 0.0 copy-done.7
  81.4 0.0 copy-done.9
  81.4 2.1 %collective-permute-start.4 = (bf16[5,128,128]{2,1,0:T(8,128)(2,1)S(1)}, bf16[5,128,128]{2,1,0:T(8,128)(2,1)S(1)}, u32[]{:S(2)}, u32[]{:S(2)}) collective-permute-start(bf16[5,128,128]{2,1,0:T(8,128)(2,1)S(1)} %get-tuple-element.65), channel_id=1, source_target_pairs={{0,2},{2,4},{4,6},{6,8},{8,10},{10,12},{12,14},{1,3},{3,5},{5,7},{... | collective-permute-start | bytes 491528 | tf_op jit(solution)/shard_map/ppermute | solution.py:257
  83.6 1.3 %collective-permute-start.5 = (bf16[5,128,128]{2,1,0:T(8,128)(2,1)S(1)}, bf16[5,128,128]{2,1,0:T(8,128)(2,1)S(1)}, u32[]{:S(2)}, u32[]{:S(2)}) collective-permute-start(bf16[5,128,128]{2,1,0:T(8,128)(2,1)S(1)} %get-tuple-element.66), channel_id=1, source_target_pairs={{2,0},{4,2},{6,4},{8,6},{10,8},{12,10},{14,12},{3,1},{5,3},{7,5},{... | collective-permute-start | bytes 491528 | tf_op jit(solution)/shard_map/ppermute | solution.py:257
  84.9 1.7 %collective-permute-done.4.refs_0_ = bf16[5,128,128]{2,1,0:T(8,128)(2,1)S(1)} collective-permute-done((bf16[5,128,128]{2,1,0:T(8,128)(2,1)S(1)}, bf16[5,128,128]{2,1,0:T(8,128)(2,1)S(1)}, u32[]{:S(2)}, u32[]{:S(2)}) %collective-permute-start.4) | collective-permute-done | bytes 163872 | tf_op jit(solution)/shard_map/ppermute | solution.py:257
  86.5 0.0 copy-start.14
  86.5 3.8 %collective-permute-done.5.refs_3_ = bf16[5,128,128]{2,1,0:T(8,128)(2,1)S(1)} collective-permute-done((bf16[5,128,128]{2,1,0:T(8,128)(2,1)S(1)}, bf16[5,128,128]{2,1,0:T(8,128)(2,1)S(1)}, u32[]{:S(2)}, u32[]{:S(2)}) %collective-permute-start.5) | collective-permute-done | bytes 163872 | tf_op jit(solution)/shard_map/ppermute | solution.py:257
  90.3 0.0 copy-start.15
  90.3 0.2 all-to-all-done.3.parts
  90.5 0.7 fold.5
  91.2 8.1 %all-to-all-start.4 = ((f32[16,8,128]{2,1,0:T(8,128)}), f32[16,8,128]{2,1,0:T(8,128)S(1)}, u32[]{:S(2)}, u32[]{:S(2)}) async-start(f32[16,8,128]{2,1,0:T(8,128)} %fold.5), calls=%async_computation.4 | async-start | bytes 131072 | tf_op jit(solution)/shard_map/all_to_all | solution.py:277
  99.3 0.0 copy-done.11
  99.4 0.0 copy-done.14
  99.4 0.0 copy-done.15
  99.4 3.9 %backward.1 = bf16[128,2,4,128]{3,2,1,0:T(4,128)(2,1)} custom-call(bf16[5,128,128]{2,1,0:T(8,128)(2,1)} %copy-done.14, bf16[4,128,128]{2,1,0:T(8,128)(2,1)} %copy-done.6, bf16[4,128,128]{2,1,0:T(8,128)(2,1)} %copy-done.8, bf16[5,128,128]{2,1,0:T(8,128)(2,1)} %copy-done.15, bf16[2,128,128]{2,1,0:T(8,128)(2,1)} %copy-done.11, bf16[27,128,128]{2,1,0:T(8,128)(2,1)} %refs_5_.1), custom_call_target="tpu_custom_call" | custom-call | tf_op jit(solution)/shard_map/backward/pallas_call | solution.py:313
  103.3 3.8 %all-to-all-done.4 = f32[16,8,128]{2,1,0:T(8,128)S(1)} async-done(((f32[16,8,128]{2,1,0:T(8,128)}), f32[16,8,128]{2,1,0:T(8,128)S(1)}, u32[]{:S(2)}, u32[]{:S(2)}) %all-to-all-start.4) | async-done | bytes 65568 | tf_op jit(solution)/shard_map/all_to_all | solution.py:277
  107.2 0.6 finish.1
  (5 shorter events, 0.1 us)
Async XLA Ops:
  0.6 7.6 %copy-start.1 = (bf16[27,128,128]{2,1,0:T(8,128)(2,1)S(1)}, bf16[27,128,128]{2,1,0:T(8,128)(2,1)}, u32[]{:S(2)}) copy-start(bf16[27,128,128]{2,1,0:T(8,128)(2,1)} %refs_5_.1) | copy-start | bytes 2654212
  1.8 18.1 %copy-start.2 = (bf16[1,128,1,4,128]{4,1,3,2,0:T(8,128)(2,1)}, bf16[1,128,1,4,128]{4,1,3,2,0:T(8,128)(2,1)S(1)}, u32[]{:S(2)}) copy-start(bf16[1,128,1,4,128]{4,1,3,2,0:T(8,128)(2,1)S(1)} %copy.22) | copy-start | bytes 393220
  1.8 11.0 %collective-permute-start = (bf16[4,128,128]{2,1,0:T(8,128)(2,1)S(1)}, bf16[4,128,128]{2,1,0:T(8,128)(2,1)S(1)}, u32[]{:S(2)}, u32[]{:S(2)}) collective-permute-start(bf16[4,128,128]{2,1,0:T(8,128)(2,1)S(1)} %bitcast.25), channel_id=1, source_target_pairs={{0,2},{2,4},{4,6},{6,8},{8,10},{10,12},{12,14},{1,3},{3,5},{5,7},{... | collective-permute-start | bytes 393224 | tf_op jit(solution)/shard_map/ppermute | solution.py:257
  5.9 14.0 %copy-start.3 = (bf16[1,128,1,4,128]{4,1,3,2,0:T(8,128)(2,1)}, bf16[1,128,1,4,128]{4,1,3,2,0:T(8,128)(2,1)S(1)}, u32[]{:S(2)}) copy-start(bf16[1,128,1,4,128]{4,1,3,2,0:T(8,128)(2,1)S(1)} %copy.21) | copy-start | bytes 393220
  5.9 6.9 %collective-permute-start.1 = (bf16[4,128,128]{2,1,0:T(8,128)(2,1)S(1)}, bf16[4,128,128]{2,1,0:T(8,128)(2,1)S(1)}, u32[]{:S(2)}, u32[]{:S(2)}) collective-permute-start(bf16[4,128,128]{2,1,0:T(8,128)(2,1)S(1)} %bitcast.29), channel_id=1, source_target_pairs={{2,0},{4,2},{6,4},{8,6},{10,8},{12,10},{14,12},{3,1},{5,3},{7,5},{... | collective-permute-start | bytes 393224 | tf_op jit(solution)/shard_map/ppermute | solution.py:257
  8.2 1.5 %copy-start = (f32[1,1,1,128,3456]{4,3,2,1,0:T(8,128)S(1)}, f32[1,1,1,128,3456]{4,3,2,1,0:T(8,128)}, u32[]{:S(2)}) copy-start(f32[1,1,1,128,3456]{4,3,2,1,0:T(8,128)} %param.10) | copy-start | bytes 5308420
  9.7 0.8 copy-start.12
  10.5 0.7 copy-start.13
  12.8 20.9 %copy-start.4 = (bf16[4,128,128]{2,1,0:T(8,128)(2,1)}, bf16[4,128,128]{2,1,0:T(8,128)(2,1)S(1)}, u32[]{:S(2)}) copy-start(bf16[4,128,128]{2,1,0:T(8,128)(2,1)S(1)} %collective-permute-done.low.refs_0_) | copy-start | bytes 393220
  12.9 20.9 %copy-start.5 = (bf16[4,128,128]{2,1,0:T(8,128)(2,1)}, bf16[4,128,128]{2,1,0:T(8,128)(2,1)S(1)}, u32[]{:S(2)}) copy-start(bf16[4,128,128]{2,1,0:T(8,128)(2,1)S(1)} %collective-permute-done.1.high.refs_3_) | copy-start | bytes 393220
  12.9 7.0 %collective-permute-start.2 = (bf16[4,128,128]{2,1,0:T(8,128)(2,1)S(1)}, bf16[4,128,128]{2,1,0:T(8,128)(2,1)S(1)}, u32[]{:S(2)}, u32[]{:S(2)}) collective-permute-start(bf16[4,128,128]{2,1,0:T(8,128)(2,1)S(1)} %edge.1), channel_id=1, source_target_pairs={{0,1},{1,0},{2,3},{3,2},{4,5},{5,4},{6,7},{7,6},{8,9},{9,8},{10,11... | collective-permute-start | bytes 393224 | tf_op jit(solution)/shard_map/ppermute | solution.py:250
  19.9 13.9 %copy-start.10 = (bf16[4,128,128]{2,1,0:T(8,128)(2,1)}, bf16[4,128,128]{2,1,0:T(8,128)(2,1)S(1)}, u32[]{:S(2)}) copy-start(bf16[4,128,128]{2,1,0:T(8,128)(2,1)S(1)} %collective-permute-done.2.across.refs_4_) | copy-start | bytes 393220
  22.8 0.6 copy-start.6
  23.4 0.7 copy-start.8
  24.1 18.9 %all-to-all-start = ((f32[32,8,128]{2,1,0:T(8,128)}), f32[32,8,128]{2,1,0:T(8,128)S(1)}, u32[]{:S(2)}, u32[]{:S(2)}) async-start(f32[32,8,128]{2,1,0:T(8,128)} %get-tuple-element.49), calls=%async_computation | async-start | bytes 262144 | tf_op jit(solution)/shard_map/all_to_all | solution.py:277
  65.4 11.3 %all-to-all-start.2 = ((f32[32,4,128]{2,1,0:T(4,128)}), f32[32,4,128]{2,1,0:T(4,128)S(1)}, u32[]{:S(2)}, u32[]{:S(2)}) async-start(f32[32,4,128]{2,1,0:T(4,128)} %get-tuple-element.58.refs_1_), calls=%async_computation.2 | async-start | bytes 131072 | tf_op jit(solution)/shard_map/all_to_all | solution.py:277
  68.9 6.1 %collective-permute-start.3 = (bf16[2,128,128]{2,1,0:T(8,128)(2,1)S(1)}, bf16[2,128,128]{2,1,0:T(8,128)(2,1)S(1)}, u32[]{:S(2)}, u32[]{:S(2)}) collective-permute-start(bf16[2,128,128]{2,1,0:T(8,128)(2,1)S(1)} %get-tuple-element.60), channel_id=1, source_target_pairs={{0,1},{1,0},{2,3},{3,2},{4,5},{5,4},{6,7},{7,6},{8,9},{9,8},{10,11... | collective-permute-start | bytes 196616 | tf_op jit(solution)/shard_map/ppermute | solution.py:250
  71.0 10.3 %copy-start.7 = (bf16[4,128,128]{2,1,0:T(8,128)(2,1)S(1)}, bf16[4,128,128]{2,1,0:T(8,128)(2,1)}, u32[]{:S(2)}) copy-start(bf16[4,128,128]{2,1,0:T(8,128)(2,1)} %copy-done.6) | copy-start | bytes 393220
  71.1 10.3 %copy-start.9 = (bf16[4,128,128]{2,1,0:T(8,128)(2,1)S(1)}, bf16[4,128,128]{2,1,0:T(8,128)(2,1)}, u32[]{:S(2)}) copy-start(bf16[4,128,128]{2,1,0:T(8,128)(2,1)} %copy-done.8) | copy-start | bytes 393220
  75.0 24.4 %copy-start.11 = (bf16[2,128,128]{2,1,0:T(8,128)(2,1)}, bf16[2,128,128]{2,1,0:T(8,128)(2,1)S(1)}, u32[]{:S(2)}) copy-start(bf16[2,128,128]{2,1,0:T(8,128)(2,1)S(1)} %collective-permute-done.3.middle.refs_4_) | copy-start | bytes 196612
  77.4 13.1 %all-to-all-start.3 = ((f32[32,8,128]{2,1,0:T(8,128)}), f32[32,8,128]{2,1,0:T(8,128)S(1)}, u32[]{:S(2)}, u32[]{:S(2)}) async-start(f32[32,8,128]{2,1,0:T(8,128)} %fold.4), calls=%async_computation.3 | async-start | bytes 262144 | tf_op jit(solution)/shard_map/all_to_all | solution.py:277
  81.4 5.1 %collective-permute-start.4 = (bf16[5,128,128]{2,1,0:T(8,128)(2,1)S(1)}, bf16[5,128,128]{2,1,0:T(8,128)(2,1)S(1)}, u32[]{:S(2)}, u32[]{:S(2)}) collective-permute-start(bf16[5,128,128]{2,1,0:T(8,128)(2,1)S(1)} %get-tuple-element.65), channel_id=1, source_target_pairs={{0,2},{2,4},{4,6},{6,8},{8,10},{10,12},{12,14},{1,3},{3,5},{5,7},{... | collective-permute-start | bytes 491528 | tf_op jit(solution)/shard_map/ppermute | solution.py:257
  83.6 6.8 %collective-permute-start.5 = (bf16[5,128,128]{2,1,0:T(8,128)(2,1)S(1)}, bf16[5,128,128]{2,1,0:T(8,128)(2,1)S(1)}, u32[]{:S(2)}, u32[]{:S(2)}) collective-permute-start(bf16[5,128,128]{2,1,0:T(8,128)(2,1)S(1)} %get-tuple-element.66), channel_id=1, source_target_pairs={{2,0},{4,2},{6,4},{8,6},{10,8},{12,10},{14,12},{3,1},{5,3},{7,5},{... | collective-permute-start | bytes 491528 | tf_op jit(solution)/shard_map/ppermute | solution.py:257
  86.5 12.8 %copy-start.14 = (bf16[5,128,128]{2,1,0:T(8,128)(2,1)}, bf16[5,128,128]{2,1,0:T(8,128)(2,1)S(1)}, u32[]{:S(2)}) copy-start(bf16[5,128,128]{2,1,0:T(8,128)(2,1)S(1)} %collective-permute-done.4.refs_0_) | copy-start | bytes 491524
  90.3 9.0 %copy-start.15 = (bf16[5,128,128]{2,1,0:T(8,128)(2,1)}, bf16[5,128,128]{2,1,0:T(8,128)(2,1)S(1)}, u32[]{:S(2)}) copy-start(bf16[5,128,128]{2,1,0:T(8,128)(2,1)S(1)} %collective-permute-done.5.refs_3_) | copy-start | bytes 491524
  91.2 15.9 %all-to-all-start.4 = ((f32[16,8,128]{2,1,0:T(8,128)}), f32[16,8,128]{2,1,0:T(8,128)S(1)}, u32[]{:S(2)}, u32[]{:S(2)}) async-start(f32[16,8,128]{2,1,0:T(8,128)} %fold.5), calls=%async_computation.4 | async-start | bytes 131072 | tf_op jit(solution)/shard_map/all_to_all | solution.py:277

commit v6 on v5

--- a/solution.py
+++ b/solution.py
@@ -33,11 +33,29 @@
 MIB = 1024 * 1024
 
 
-def fill_planes(planes, low, own_0, own_1, high, across):
+def is_even():
+    return lax.rem(lax.axis_index("sx"), 2) == 0
+
+
+def rows_of(planes, here_a, here_b, from_a, from_b, across):
+    even = is_even()
+    ascending = (from_b, here_b, here_a, from_a)
+    descending = (from_a, here_a, here_b, from_b)
+    for xp in range(PX):
+        for y in range(CY):
+            yield xp, y + 1, jnp.where(even, ascending[xp][y], descending[xp][y])
+    first = lax.axis_index("sy") == 0
+    for xp in range(PX):
+        edge = across(xp)
+        nothing = jnp.zeros_like(edge)
+        yield xp, 0, jnp.where(first, nothing, edge)
+        yield xp, PY - 1, jnp.where(first, edge, nothing)
+
+
+def fill_planes(planes, *sources):
     lane = lax.broadcasted_iota(jnp.int32, (C, CZ), 1)
     zero = jnp.zeros((C, CZ), F32)
-
-    def put(xp, yp, block):
+    for xp, yp, block in rows_of(planes, *sources):
         where = pl.ds((xp * PY + yp) * CZ, CZ)
         wide = block.astype(F32)
         before = jnp.where(lane == 0, zero, pltpu.roll(wide, 1, 1))
@@ -45,15 +63,6 @@
         planes[pl.ds(0, C), where] = before.astype(BF16)
         planes[pl.ds(C, C), where] = block
         planes[pl.ds(2 * C, C), where] = after.astype(BF16)
-
-    first = lax.axis_index("sy") == 0
-    for xp, source in enumerate((low, own_0, own_1, high)):
-        for y in range(CY):
-            put(xp, y + 1, source[y])
-        edge = across[xp]
-        nothing = jnp.zeros_like(edge)
-        put(xp, 0, jnp.where(first, nothing, edge))
-        put(xp, PY - 1, jnp.where(first, edge, nothing))
 
 
 def window(planes, x, a, b):
@@ -94,25 +103,35 @@
 
 
 def forward_kernel(
-    low, own_0, own_1, high, across, upstream, lhs, bias, base,
-    act, grad_0, grad_1, edges, sums, planes,
+    wait, held, act_out, grad_a_out, grad_b_out, edges_out, sums_out,
+    planes, act, grad_a, grad_b, edges, sums, sem,
 ):
-    fill_planes(planes, low, own_0, own_1, high, across)
+    here_a, here_b, from_a, from_b, across, upstream, lhs, bias, base = held
+    wait(0, 1, 2, 3, 4)
+    fill_planes(planes, here_a, here_b, from_a, from_b, lambda xp: across[xp])
     first_core = lax.axis_index("sy") == 0
+    even = is_even()
     joint = jnp.zeros((EXTRA, C), F32)
-    for x, grad in enumerate((grad_0, grad_1)):
+    wait(6, 7, 5)
+    cube = []
+    leaving = []
+
+    def leave(source, target):
+        leaving.append(pltpu.make_async_copy(source, target, sem.at[len(leaving)]))
+        leaving[-1].start()
+
+    for x in range(CX):
         total = convolve(planes, lhs, x)
         pre = total[:C] + bias[:, :1]
         sigma = jax.nn.sigmoid(pre)
         active = (pre * sigma).astype(BF16)
         slope = sigma * (1.0 + pre * (1.0 - sigma))
+        act[:, x] = active.reshape(C, CY, CZ)
         grads = []
-        act[:, x] = active.reshape(C, CY, CZ)
         for y in range(CY):
             span = slice(y * CZ, (y + 1) * CZ)
-            piece = (upstream[x, y].astype(F32) * slope[:, span]).astype(BF16)
-            grad[y] = piece
-            grads.append(piece)
+            grads.append((upstream[x, y].astype(F32) * slope[:, span]).astype(BF16))
+        cube.append(grads)
         edges[x] = jnp.where(first_core, grads[CY - 1], grads[0])
         field = total[C : C + RANK] + total[C + RANK : C + 2 * RANK]
         field = field + total[C + 2 * RANK : C + 3 * RANK]
@@ -121,20 +140,32 @@
         joint = joint + lax.dot_general(
             stacked.astype(BF16), jnp.concatenate(grads, axis=1), NT, preferred_element_type=F32
         )
+    leave(act, act_out)
+    wait(8)
     local = joint[:RANK] + joint[RANK : 2 * RANK] + joint[2 * RANK : 3 * RANK] + base[...]
     both = jnp.concatenate([local, joint[3 * RANK :]], axis=0)
     for copy in range(sums.shape[0]):
         sums[copy] = both
+    leave(sums, sums_out)
+    for y in range(CY):
+        grad_a[y] = jnp.where(even, cube[1][y], cube[0][y])
+        grad_b[y] = jnp.where(even, cube[0][y], cube[1][y])
+    leave(grad_a, grad_a_out)
+    leave(grad_b, grad_b_out)
+    leave(edges, edges_out)
+    for transfer in leaving:
+        transfer.wait()
 
 
 def gradient_kernel(wait, block, upper_out, lower_out, planes, upper, lower, sem):
-    low, own_0, own_1, high, across, grad_0, grad_1, error = block
+    here_a, here_b, from_a, from_b, across, grad_a, grad_b, error = block
     wait(0, 1, 2, 3, 4)
-    fill_planes(planes, low, own_0, own_1, high, across)
+    fill_planes(planes, here_a, here_b, from_a, from_b, lambda xp: across[xp])
     wait(5, 6)
-    grads = []
-    for grad in (grad_0, grad_1):
-        grads.append(jnp.concatenate([grad[y] for y in range(CY)], axis=1))
+    even = is_even()
+    side_a = jnp.concatenate([grad_a[y] for y in range(CY)], axis=1)
+    side_b = jnp.concatenate([grad_b[y] for y in range(CY)], axis=1)
+    grads = (jnp.where(even, side_b, side_a), jnp.where(even, side_a, side_b))
     wait(7)
     leaving = []
     for pair in range(9):
@@ -194,14 +225,19 @@
 
 def residual_kernel(wait, held, out, new_error, sem):
     basis, blocks, upper, lower = held
-    wait(0, 1, 2, 3)
+    wait(0, 1)
+    b1, b2, b3 = pieces(basis[...])
+    left = jnp.concatenate([b1, b2, b3, b1, b2, b1], axis=0).astype(BF16)
+    q = jnp.concatenate([blocks[tap] for tap in range(TAPS)], axis=1)
+    q1, q2, q3 = pieces(q)
+    right = jnp.concatenate([q1, q1, q1, q2, q2, q3], axis=0).astype(BF16)
+    wait(2, 3)
     leaving = []
     for pair in range(9):
         span = pl.ds(pair * GROUP, GROUP)
-        rows = jnp.concatenate([blocks[3 * pair + c] for c in range(3)], axis=1)
         merged = upper[:, span].astype(F32) + lower[:, span].astype(F32)
         new_error[:, span] = merged - lax.dot_general(
-            basis[...], rows, TN, precision=HIGHEST, preferred_element_type=F32
+            left, right[:, pair * GROUP : (pair + 1) * GROUP], TN, preferred_element_type=F32
         )
         leaving.append(pltpu.make_async_copy(new_error.at[:, span], out.at[:, span], sem.at[pair]))
         leaving[-1].start()
@@ -215,10 +251,17 @@
 
 
 def backward_kernel(wait, held, out, planes):
-    low, own_0, own_1, high, middle, weights = held
+    here_a, here_b, from_a, from_b, middle, weights = held
     wait(0, 1, 2, 3, 4)
-    across = (low[CY], middle[0], middle[1], high[CY])
-    fill_planes(planes, low, own_0, own_1, high, across)
+    even = is_even()
+
+    def across(xp):
+        if 0 < xp < PX - 1:
+            return middle[xp - 1]
+        above = xp > 0
+        return jnp.where(even == above, from_a[CY], from_b[CY])
+
+    fill_planes(planes, here_a, here_b, from_a, from_b, across)
     wait(5)
     totals = [None] * CX
     for pair in range(9):
@@ -233,34 +276,35 @@
         out[:, x] = totals[x].astype(BF16).reshape(C, CY, CZ)
 
 
-def pack_kernel(own_0, own_1, middle, down, up):
-    for own, row, out in ((own_0, 0, down), (own_1, 1, up)):
-        for y in range(CY):
-            out[y] = own[y]
-        out[CY] = middle[row]
-
-
-def edge_kernel(low, own_0, own_1, high, edge):
+def pack_kernel(here_a, here_b, middle, to_a, to_b):
+    even = is_even()
+    for y in range(CY):
+        to_a[y] = here_a[y]
+        to_b[y] = here_b[y]
+    to_a[CY] = jnp.where(even, middle[1], middle[0])
+    to_b[CY] = jnp.where(even, middle[0], middle[1])
+
+
+def edge_kernel(here_a, here_b, from_a, from_b, edge):
     first = lax.axis_index("sy") == 0
-    for xp, source in enumerate((low, own_0, own_1, high)):
-        edge[xp] = jnp.where(first, source[CY - 1], source[0])
+    even = is_even()
+    ascending = (from_b, here_b, here_a, from_a)
+    descending = (from_a, here_a, here_b, from_b)
+    for xp in range(PX):
+        last = jnp.where(even, ascending[xp][CY - 1], descending[xp][CY - 1])
+        start = jnp.where(even, ascending[xp][0], descending[xp][0])
+        edge[xp] = jnp.where(first, last, start)
 
 
 def swap_cores(edge):
     return lax.ppermute(edge, "sy", [(0, 1), (1, 0)])
 
 
-def exchange_x(own_0, own_1):
+def exchange_x(to_a, to_b):
     count = lax.axis_size("sx")
-    up = [(i, i + 1) for i in range(count - 1)]
-    down = [(i + 1, i) for i in range(count - 1)]
-    return lax.ppermute(own_1, "sx", up), lax.ppermute(own_0, "sx", down)
-
-
-def exchange_y(low, own_0, own_1, high):
-    slab = jax.ShapeDtypeStruct((PX, C, CZ), BF16)
-    edge = call(edge_kernel, "edge", 2, slab, (low, own_0, own_1, high))
-    return swap_cores(edge)
+    pairs_a = [(i, i ^ 1) for i in range(count) if i ^ 1 < count]
+    pairs_b = [(i, j) for i in range(1, count - 1) for j in [((i - 1) ^ 1) + 1] if j < count]
+    return lax.ppermute(to_a, "sx", pairs_a), lax.ppermute(to_b, "sx", pairs_b)
 
 
 tie = lax.optimization_barrier
@@ -344,9 +388,12 @@
     padded = -(-TAPS // columns) * columns
     planes = pltpu.VMEM((GROUP, PX * PY * CZ), BF16)
     error = error_state[0, 0, 0]
-    own_0 = jnp.transpose(features[0, :, 0], (1, 0, 2))
-    own_1 = jnp.transpose(features[0, :, 1], (1, 0, 2))
-    low, high = exchange_x(own_0, own_1)
+    shift = jnp.where(is_even(), 1, 0)
+    here_a, here_b = (
+        jnp.transpose(lax.dynamic_index_in_dim(features[0], which, 1, False), (1, 0, 2))
+        for which in (shift, 1 - shift)
+    )
+    from_a, from_b = exchange_x(here_a, here_b)
     upstream = jnp.transpose(cotangent[0], (1, 2, 0, 3))
     lhs, base, bias = call(
         prepare_kernel,
@@ -355,22 +402,24 @@
         (bf16(C + EXTRA, K), f32(RANK, C), f32(C, C)),
         (weights, warm_factor, error, conv_bias[None]),
     )
-    low, high, lhs, base, bias, upstream = tie((low, high, lhs, base, bias, upstream))
-    across = exchange_y(low, own_0, own_1, high)
-    block = (low, own_0, own_1, high, across)
-    act, grad_0, grad_1, edges, sums = call(
+    from_a, from_b, lhs, base, bias, upstream = tie((from_a, from_b, lhs, base, bias, upstream))
+    edge = call(edge_kernel, "edge", 2, bf16(PX, C, CZ), (here_a, here_b, from_a, from_b))
+    block = (here_a, here_b, from_a, from_b, swap_cores(edge))
+    shapes = (
+        bf16(C, CX, CY, CZ),
+        bf16(CY, C, CZ),
+        bf16(CY, C, CZ),
+        bf16(CX, C, CZ),
+        f32(chips, 2 * RANK, C),
+    )
+    act, grad_a, grad_b, edges, sums = fetch_and_call(
         forward_kernel,
         "forward",
-        10,
-        (
-            bf16(C, CX, CY, CZ),
-            bf16(CY, C, CZ),
-            bf16(CY, C, CZ),
-            bf16(CX, C, CZ),
-            f32(chips, 2 * RANK, C),
-        ),
+        60,
+        shapes,
         (*block, upstream, lhs, bias, base),
-        [planes],
+        [planes, *(pltpu.VMEM(s.shape, s.dtype) for s in shapes), pltpu.SemaphoreType.DMA((5,))],
+        HBM,
     )
     parts = swap(sums, DP)
     upper, lower = fetch_and_call(
@@ -378,13 +427,13 @@
         "gradient",
         60,
         (bf16(C, K), bf16(C, K)),
-        (*block, grad_0, grad_1, error),
+        (*block, grad_a, grad_b, error),
         [planes, pltpu.VMEM((C, K), BF16), pltpu.VMEM((C, K), BF16), pltpu.SemaphoreType.DMA((18,))],
         HBM,
     )
     parts, upper, lower, edges = tie((parts, upper, lower, edges))
     parts = swap(fold(parts, columns), BLOCK)
-    middle = swap_cores(edges)
+    parts, middle = tie((parts, swap_cores(edges)))
     factor_p, bias_grad, blocks = fetch_and_call(
         functools.partial(project_kernel, devices=devices),
         "project",
@@ -404,24 +453,23 @@
     )
     width = padded // columns * RANK
     mine = swap(blocks, BLOCK)
-    mine, new_error, middle, near_0, near_1 = tie((mine, new_error, middle, grad_0, grad_1))
+    mine, new_error, middle, near_a, near_b = tie((mine, new_error, middle, grad_a, grad_b))
     mine = swap(fold(mine.reshape(columns, width, C), chips), DP)
-    down, up = call(
+    to_a, to_b = call(
         pack_kernel,
         "pack",
         4,
         (bf16(CY + 1, C, CZ), bf16(CY + 1, C, CZ)),
-        (near_0, near_1, middle),
-    )
-    g_low, g_high = exchange_x(down, up)
-    mine, g_low, g_high = tie((mine, g_low, g_high))
+        (near_a, near_b, middle),
+    )
+    g_from_a, g_from_b = exchange_x(to_a, to_b)
     blocks = swap(fold(mine, columns), BLOCK).reshape(padded, RANK, C)
     input_grad = fetch_and_call(
         backward_kernel,
         "backward",
         60,
         bf16(C, CX, CY, CZ),
-        (g_low, near_0, near_1, g_high, middle, weights),
+        (near_a, near_b, g_from_a, g_from_b, middle, weights),
         [planes],
     )
     factor_q = call(

time: 109 us -> 108 us (level)
  blocking collectives: 19.2 us -> 0 us
  waiting for transfers between devices: 16.3 us -> 24.5 us
  starting transfers between devices: 42.2 us -> 48.3 us
  local copies, waits for them, and re-layouts: 6.45 us -> 9.4 us
  Pallas kernels: 22.7 us -> 24.2 us
    all_to_all x1 -> x0, blocking collectives: 19.2 us -> none  [swap(): return lax.all_to_all(x, axes, 0, 0, tiled=True)]
    all_to_all x4 -> x5, waiting for transfers between devices: 9.9 us -> 22.4 us  [swap(): return lax.all_to_all(x, axes, 0, 0, tiled=True)]
    all_to_all x4 -> x5, starting transfers between devices: 25.3 us -> 32.1 us  [swap(): return lax.all_to_all(x, axes, 0, 0, tiled=True)]
    ppermute x4, waiting for transfers between devices: 5.46 us -> 0.01 us  [the longest x2 0.01 us: exchange_x(): lax.ppermute(to_a, 'sx', pairs_a)]
    pallas_call x4 -> x5, Pallas kernels: 16.1 us -> 19.7 us  [fetch_and_call(): pl.pallas_call(body, out_shape=shapes, in_specs=[VMEM] * len(near) + [HBM...]
    unnamed x35 -> x39, local copies, waits for them, and re-layouts: 5.31 us -> 8.22 us
    pallas_call x8 -> x7, Pallas kernels: 6.59 us -> 4.41 us  [call(): pl.pallas_call(kernel, out_shape=shapes, in_specs=[VMEM] * len(args), out...]
    ppermute x4, starting transfers between devices: 8.76 us -> 7.51 us  [the longest x2 6.17 us: exchange_x(): lax.ppermute(to_a, 'sx', pairs_a)]
  transfers between devices with their start and end apart: 10 -> 11, of which waited for: 7 -> 7; matrix products, arithmetic and copies ran while one was open for 1% -> 2% of each run, Pallas kernels for 13% -> 13%
where the time goes in v6:
time: 108 us; the launch traced here: 107 us
  starting transfers between devices  48.3 us (45%)
  waiting for transfers between devices  24.5 us (23%)
  Pallas kernels  24.2 us (22%)
  local copies, waits for them, and re-layouts  9.4 us (9%)
    all_to_all x5, starting transfers between devices, swap(): return lax.all_to_all(x, axes, 0, 0, tiled=True)  32.1 us
    all_to_all x5, waiting for transfers between devices, swap(): return lax.all_to_all(x, axes, 0, 0, tiled=True)  22.4 us
    pallas_call x5, Pallas kernels, fetch_and_call(): pl.pallas_call(body, out_shape=shapes, in_specs=[VMEM] * len(near) + [HBM...  19.7 us
    ppermute x2, starting transfers between devices, swap_cores(): return lax.ppermute(edge, 'sy', [(0, 1), (1, 0)])  8.69 us
    unnamed x39, local copies, waits for them, and re-layouts  8.22 us
    ppermute x2, starting transfers between devices, exchange_x(): lax.ppermute(to_a, 'sx', pairs_a)  6.17 us
    pallas_call x7, Pallas kernels, call(): pl.pallas_call(kernel, out_shape=shapes, in_specs=[VMEM] * len(args), out...  4.41 us
  transfers between devices with their start and end apart: 11, of which 7 were waited for; matrix products, arithmetic and copies ran while one was open for 2% of the time, Pallas kernels for 13%

profile of v6, /device:TPU:1, one launch (start us, length us, event | category | flops | bytes accessed | tf_op | source)
XLA Modules:
  0.0 107.2 jit_solution(3953272749570287004)
XLA Ops:
  0.6 0.0 copy-start.1
  0.7 1.1 %constant_dynamic-slice_fusion = (bf16[1,128,1,4,128]{4,3,2,1,0:T(4,128)(2,1)S(1)}, bf16[1,128,1,4,128]{4,3,2,1,0:T(4,128)(2,1)S(1)}) fusion(bf16[1,128,2,4,128]{4,3,2,1,0:T(4,128)(2,1)} %param.6, s32[]{:T(128)S(6)} %select_n.10, s32[]{:T(128)S(6)} %select_n.9), kind=kLoop, calls=%fused_computation.3 | loop fusion | bytes 524296 | tf_op jit(solution)/shard_map/jit(dynamic_index_in_dim)/dynamic_slice | solution.py:393
  1.8 0.0 copy-start.2
  1.8 4.0 %collective-permute-start = (bf16[4,128,128]{2,1,0:T(8,128)(2,1)S(1)}, bf16[4,128,128]{2,1,0:T(8,128)(2,1)S(1)}, u32[]{:S(2)}, u32[]{:S(2)}) collective-permute-start(bf16[4,128,128]{2,1,0:T(8,128)(2,1)S(1)} %bitcast.25), channel_id=1, source_target_pairs={{0,2},{2,0},{4,6},{6,4},{8,10},{10,8},{12,14},{14,12},{1,3},{3,1},... | collective-permute-start | bytes 393224 | tf_op jit(solution)/shard_map/ppermute | solution.py:307
  5.9 0.0 copy-start.3
  5.9 0.7 collective-permute-start.1
  6.6 1.7 %copy.18 = bf16[1,128,2,4,128]{4,1,3,2,0:T(8,128)(2,1)} copy(bf16[1,128,2,4,128]{4,3,2,1,0:T(4,128)(2,1)} %param.7) | data formatting | bytes 524288 | tf_op args[1]
  8.3 0.0 copy-done.1
  8.3 0.0 copy-start
  8.3 1.5 %copy-done = f32[1,1,1,128,3456]{4,3,2,1,0:T(8,128)S(1)} copy-done((f32[1,1,1,128,3456]{4,3,2,1,0:T(8,128)S(1)}, f32[1,1,1,128,3456]{4,3,2,1,0:T(8,128)}, u32[]{:S(2)}) %copy-start) | copy-done | bytes 1769496
  9.8 0.0 copy-start.11
  9.8 0.8 copy-done.11
  10.6 0.0 copy-start.13
  10.6 0.7 copy-done.13
  11.2 1.7 %prepare.1 = (bf16[144,3456]{1,0:T(8,128)(2,1)S(1)}, f32[4,128]{1,0:T(4,128)S(1)}, f32[128,128]{1,0:T(8,128)S(1)}) custom-call(bf16[27,128,128]{2,1,0:T(8,128)(2,1)S(1)} %copy-done.1, f32[4,3456]{1,0:T(4,128)S(1)} %copy-done.11, f32[128,3456]{1,0:T(8,128)S(1)} %bitcast.24, f32[1,128]{1,0:T(1,128)S(1)} %bitcast.35), custom_call_target="tpu_custom_call" | custom-call | tf_op jit(solution)/shard_map/prepare/pallas_call | solution.py:325
  12.9 1.0 copy-done.8
  13.9 0.0 collective-permute-done.from_a.refs_2_
  13.9 0.0 collective-permute-done.1.from_b.refs_3_
  13.9 0.0 copy-start.5
  13.9 0.1 edge.1
  14.0 0.0 copy-done.2
  14.0 0.0 copy-done.3
  14.0 6.7 %collective-permute-start.2 = (bf16[4,128,128]{2,1,0:T(8,128)(2,1)S(1)}, bf16[4,128,128]{2,1,0:T(8,128)(2,1)S(1)}, u32[]{:S(2)}, u32[]{:S(2)}) collective-permute-start(bf16[4,128,128]{2,1,0:T(8,128)(2,1)S(1)} %edge.1), channel_id=1, source_target_pairs={{0,1},{1,0},{2,3},{3,2},{4,5},{5,4},{6,7},{7,6},{8,9},{9,8},{10,11... | collective-permute-start | bytes 393224 | tf_op jit(solution)/shard_map/ppermute | solution.py:300
  20.7 0.0 copy-done.10
  20.7 0.0 copy-done.12
  20.7 0.9 collective-permute-done.2.refs_4_
  21.6 0.0 copy-done.4
  21.6 0.0 copy-done.5
  21.6 0.7 copy-done.14
  22.3 4.5 %forward.1 = (bf16[128,2,4,128]{3,2,1,0:T(4,128)(2,1)}, bf16[4,128,128]{2,1,0:T(8,128)(2,1)}, bf16[4,128,128]{2,1,0:T(8,128)(2,1)}, bf16[2,128,128]{2,1,0:T(8,128)(2,1)}, f32[32,8,128]{2,1,0:T(8,128)}) custom-call(bf16[4,128,128]{2,1,0:T(8,128)(2,1)} %bitcast.27, bf16[4,128,128]{2,1,0:T(8,128)(2,1)} %bitcast.31, bf16[4,128,128]{2,1,0:T(8,128)(2,1)} %copy-done.4, ...), custom_call_target="tpu_custom_call" | custom-call | tf_op jit(solution)/shard_map/forward/pallas_call | solution.py:357
  26.8 0.0 copy-start.18
  26.8 9.2 %all-to-all-start = ((f32[32,8,128]{2,1,0:T(8,128)}), f32[32,8,128]{2,1,0:T(8,128)S(1)}, u32[]{:S(2)}, u32[]{:S(2)}) async-start(f32[32,8,128]{2,1,0:T(8,128)} %get-tuple-element.48), calls=%async_computation | async-start | bytes 262144 | tf_op jit(solution)/shard_map/all_to_all | solution.py:321
  36.0 5.0 %gradient.1 = (bf16[128,3456]{1,0:T(8,128)(2,1)}, bf16[128,3456]{1,0:T(8,128)(2,1)}) custom-call(bf16[4,128,128]{2,1,0:T(8,128)(2,1)} %bitcast.28, bf16[4,128,128]{2,1,0:T(8,128)(2,1)} %bitcast.32, bf16[4,128,128]{2,1,0:T(8,128)(2,1)} %copy-done.4, bf16[4,128,128]{2,1,0:T(8,128)(2,1)} %copy-done.5, bf16[4,128,128]{2,1,0:T(8,128)(2,1)} %copy-done.14, ...), custom_call_target="tpu_custom_call" | custom-call | tf_op jit(solution)/shard_map/gradient/pallas_call | solution.py:357
  41.0 4.2 %all-to-all-done.parts = f32[32,8,128]{2,1,0:T(8,128)S(1)} async-done(((f32[32,8,128]{2,1,0:T(8,128)}), f32[32,8,128]{2,1,0:T(8,128)S(1)}, u32[]{:S(2)}, u32[]{:S(2)}) %all-to-all-start) | async-done | bytes 131104 | tf_op jit(solution)/shard_map/all_to_all | solution.py:321
  45.2 0.7 fold.3
  45.9 10.1 %all-to-all-start.1 = ((f32[16,8,128]{2,1,0:T(8,128)}), f32[16,8,128]{2,1,0:T(8,128)S(1)}, u32[]{:S(2)}, u32[]{:S(2)}) async-start(f32[16,8,128]{2,1,0:T(8,128)} %fold.3), calls=%async_computation.1 | async-start | bytes 131072 | tf_op jit(solution)/shard_map/all_to_all | solution.py:321
  56.0 0.0 copy-done.18
  56.0 2.0 %collective-permute-start.3 = (bf16[2,128,128]{2,1,0:T(8,128)(2,1)S(1)}, bf16[2,128,128]{2,1,0:T(8,128)(2,1)S(1)}, u32[]{:S(2)}, u32[]{:S(2)}) collective-permute-start(bf16[2,128,128]{2,1,0:T(8,128)(2,1)S(1)} %copy-done.18), channel_id=1, source_target_pairs={{0,1},{1,0},{2,3},{3,2},{4,5},{5,4},{6,7},{7,6},{8,9},{9,8},{10,11... | collective-permute-start | bytes 196616 | tf_op jit(solution)/shard_map/ppermute | solution.py:300
  58.0 1.1 %collective-permute-done.3.middle.refs_4_ = bf16[2,128,128]{2,1,0:T(8,128)(2,1)S(1)} collective-permute-done((bf16[2,128,128]{2,1,0:T(8,128)(2,1)S(1)}, bf16[2,128,128]{2,1,0:T(8,128)(2,1)S(1)}, u32[]{:S(2)}, u32[]{:S(2)}) %collective-permute-start.3) | collective-permute-done | bytes 65568 | tf_op jit(solution)/shard_map/ppermute | solution.py:300
  59.1 4.7 %all-to-all-done.1.refs_0_ = f32[16,8,128]{2,1,0:T(8,128)S(1)} async-done(((f32[16,8,128]{2,1,0:T(8,128)}), f32[16,8,128]{2,1,0:T(8,128)S(1)}, u32[]{:S(2)}, u32[]{:S(2)}) %all-to-all-start.1) | async-done | bytes 65568 | tf_op jit(solution)/shard_map/all_to_all | solution.py:321
  63.8 0.6 copy-done.15
  64.4 3.3 %project.1 = (f32[4,128]{1,0:T(4,128)}, f32[1,128]{1,0:T(1,128)}, f32[32,4,128]{2,1,0:T(4,128)}) custom-call(f32[16,8,128]{2,1,0:T(8,128)} %copy-done.15, bf16[128,3456]{1,0:T(8,128)(2,1)} %get-tuple-element.57.refs_1_.refs_2_, bf16[128,3456]{1,0:T(8,128)(2,1)} %get-tuple-element.58.refs_2_.refs_3_), custom_call_target="tpu_custom_call" | custom-call | tf_op jit(solution)/shard_map/project/pallas_call | solution.py:357
  67.7 3.5 %all-to-all-start.2 = ((f32[32,4,128]{2,1,0:T(4,128)}), f32[32,4,128]{2,1,0:T(4,128)S(1)}, u32[]{:S(2)}, u32[]{:S(2)}) async-start(f32[32,4,128]{2,1,0:T(4,128)} %get-tuple-element.59.refs_1_), calls=%async_computation.2 | async-start | bytes 131072 | tf_op jit(solution)/shard_map/all_to_all | solution.py:321
  71.2 0.0 copy-start.7
  71.2 3.0 %residual.1 = f32[128,3456]{1,0:T(8,128)} custom-call(f32[4,128]{1,0:T(4,128)} %get-tuple-element.35.refs_0_, f32[32,4,128]{2,1,0:T(4,128)} %get-tuple-element.59.refs_1_, bf16[128,3456]{1,0:T(8,128)(2,1)} %get-tuple-element.57.refs_1_.refs_2_, bf16[128,3456]{1,0:T(8,128)(2,1)} %get-tuple-element.58.refs_2_.refs_3_), custom_call_target="tpu_custom_call" | custom-call | tf_op jit(solution)/shard_map/residual/pallas_call | solution.py:357
  74.2 4.8 %all-to-all-done.2 = f32[32,4,128]{2,1,0:T(4,128)S(1)} async-done(((f32[32,4,128]{2,1,0:T(4,128)}), f32[32,4,128]{2,1,0:T(4,128)S(1)}, u32[]{:S(2)}, u32[]{:S(2)}) %all-to-all-start.2) | async-done | bytes 65568 | tf_op jit(solution)/shard_map/all_to_all | solution.py:321
  79.0 0.7 fold.4
  79.7 3.9 %all-to-all-start.3 = ((f32[32,8,128]{2,1,0:T(8,128)}), f32[32,8,128]{2,1,0:T(8,128)S(1)}, u32[]{:S(2)}, u32[]{:S(2)}) async-start(f32[32,8,128]{2,1,0:T(8,128)} %fold.4), calls=%async_computation.3 | async-start | bytes 262144 | tf_op jit(solution)/shard_map/all_to_all | solution.py:321
  83.6 0.0 copy-done.9
  83.6 0.0 copy-done.6
  83.6 0.0 copy-done.7
  83.7 2.1 %collective-permute-start.4 = (bf16[5,128,128]{2,1,0:T(8,128)(2,1)S(1)}, bf16[5,128,128]{2,1,0:T(8,128)(2,1)S(1)}, u32[]{:S(2)}, u32[]{:S(2)}) collective-permute-start(bf16[5,128,128]{2,1,0:T(8,128)(2,1)S(1)} %get-tuple-element.65), channel_id=1, source_target_pairs={{0,2},{2,0},{4,6},{6,4},{8,10},{10,8},{12,14},{14,12},{1,3},{3,1},... | collective-permute-start | bytes 491528 | tf_op jit(solution)/shard_map/ppermute | solution.py:307
  85.8 0.7 collective-permute-start.5
  86.5 6.3 %all-to-all-done.3.parts = f32[32,8,128]{2,1,0:T(8,128)S(1)} async-done(((f32[32,8,128]{2,1,0:T(8,128)}), f32[32,8,128]{2,1,0:T(8,128)S(1)}, u32[]{:S(2)}, u32[]{:S(2)}) %all-to-all-start.3) | async-done | bytes 131104 | tf_op jit(solution)/shard_map/all_to_all | solution.py:321
  92.7 0.7 fold.5
  93.4 5.4 %all-to-all-start.4 = ((f32[16,8,128]{2,1,0:T(8,128)}), f32[16,8,128]{2,1,0:T(8,128)S(1)}, u32[]{:S(2)}, u32[]{:S(2)}) async-start(f32[16,8,128]{2,1,0:T(8,128)} %fold.5), calls=%async_computation.4 | async-start | bytes 131072 | tf_op jit(solution)/shard_map/all_to_all | solution.py:321
  98.8 0.0 collective-permute-done.4.refs_2_
  98.8 0.0 copy-start.16
  98.8 0.0 collective-permute-done.5.refs_3_
  98.8 0.6 copy-done.16
  99.4 0.7 copy-done.17
  100.1 3.9 %backward.1 = bf16[128,2,4,128]{3,2,1,0:T(4,128)(2,1)} custom-call(bf16[4,128,128]{2,1,0:T(8,128)(2,1)} %get-tuple-element.62.refs_5_.here_a.refs_0_, bf16[4,128,128]{2,1,0:T(8,128)(2,1)} %get-tuple-element.63.refs_6_.here_b.refs_1_, bf16[5,128,128]{2,1,0:T(8,128)(2,1)} %copy-done.16, bf16[5,128,128]{2,1,0:T(8,128)(2,1)} %copy-done.17, ...), custom_call_target="tpu_custom_call" | custom-call | tf_op jit(solution)/shard_map/backward/pallas_call | solution.py:357
  104.0 2.6 %all-to-all-done.4 = f32[16,8,128]{2,1,0:T(8,128)S(1)} async-done(((f32[16,8,128]{2,1,0:T(8,128)}), f32[16,8,128]{2,1,0:T(8,128)S(1)}, u32[]{:S(2)}, u32[]{:S(2)}) %all-to-all-start.4) | async-done | bytes 65568 | tf_op jit(solution)/shard_map/all_to_all | solution.py:321
  106.6 0.6 finish.1
  (12 shorter events, 0.1 us)
Async XLA Ops:
  0.6 7.7 %copy-start.1 = (bf16[27,128,128]{2,1,0:T(8,128)(2,1)S(1)}, bf16[27,128,128]{2,1,0:T(8,128)(2,1)}, u32[]{:S(2)}) copy-start(bf16[27,128,128]{2,1,0:T(8,128)(2,1)} %refs_5_.1) | copy-start | bytes 2654212
  1.8 12.1 %copy-start.2 = (bf16[1,128,1,4,128]{4,1,3,2,0:T(8,128)(2,1)}, bf16[1,128,1,4,128]{4,1,3,2,0:T(8,128)(2,1)S(1)}, u32[]{:S(2)}) copy-start(bf16[1,128,1,4,128]{4,1,3,2,0:T(8,128)(2,1)S(1)} %copy.20) | copy-start | bytes 393220
  1.8 12.0 %collective-permute-start = (bf16[4,128,128]{2,1,0:T(8,128)(2,1)S(1)}, bf16[4,128,128]{2,1,0:T(8,128)(2,1)S(1)}, u32[]{:S(2)}, u32[]{:S(2)}) collective-permute-start(bf16[4,128,128]{2,1,0:T(8,128)(2,1)S(1)} %bitcast.25), channel_id=1, source_target_pairs={{0,2},{2,0},{4,6},{6,4},{8,10},{10,8},{12,14},{14,12},{1,3},{3,1},... | collective-permute-start | bytes 393224 | tf_op jit(solution)/shard_map/ppermute | solution.py:307
  5.9 8.1 %copy-start.3 = (bf16[1,128,1,4,128]{4,1,3,2,0:T(8,128)(2,1)}, bf16[1,128,1,4,128]{4,1,3,2,0:T(8,128)(2,1)S(1)}, u32[]{:S(2)}) copy-start(bf16[1,128,1,4,128]{4,1,3,2,0:T(8,128)(2,1)S(1)} %copy.19) | copy-start | bytes 393220
  5.9 8.0 %collective-permute-start.1 = (bf16[4,128,128]{2,1,0:T(8,128)(2,1)S(1)}, bf16[4,128,128]{2,1,0:T(8,128)(2,1)S(1)}, u32[]{:S(2)}, u32[]{:S(2)}) collective-permute-start(bf16[4,128,128]{2,1,0:T(8,128)(2,1)S(1)} %bitcast.29), channel_id=1, source_target_pairs={{2,4},{4,2},{6,8},{8,6},{10,12},{12,10},{3,5},{5,3},{7,9},{9,7},{1... | collective-permute-start | bytes 393224 | tf_op jit(solution)/shard_map/ppermute | solution.py:307
  8.3 1.5 %copy-start = (f32[1,1,1,128,3456]{4,3,2,1,0:T(8,128)S(1)}, f32[1,1,1,128,3456]{4,3,2,1,0:T(8,128)}, u32[]{:S(2)}) copy-start(f32[1,1,1,128,3456]{4,3,2,1,0:T(8,128)} %param.10) | copy-start | bytes 5308420
  9.8 0.8 copy-start.11
  10.6 0.7 copy-start.13
  12.9 1.0 copy-start.8
  13.9 6.8 %copy-start.10 = (f32[128,128]{1,0:T(8,128)}, f32[128,128]{1,0:T(8,128)S(1)}, u32[]{:S(2)}) copy-start(f32[128,128]{1,0:T(8,128)S(1)} %get-tuple-element.45.refs_7_) | copy-start | bytes 196612
  13.9 6.8 %copy-start.12 = (f32[4,128]{1,0:T(4,128)}, f32[4,128]{1,0:T(4,128)S(1)}, u32[]{:S(2)}) copy-start(f32[4,128]{1,0:T(4,128)S(1)} %get-tuple-element.46.refs_8_) | copy-start | bytes 6148
  13.9 7.8 %copy-start.4 = (bf16[4,128,128]{2,1,0:T(8,128)(2,1)}, bf16[4,128,128]{2,1,0:T(8,128)(2,1)S(1)}, u32[]{:S(2)}) copy-start(bf16[4,128,128]{2,1,0:T(8,128)(2,1)S(1)} %collective-permute-done.from_a.refs_2_) | copy-start | bytes 393220
  13.9 7.7 %copy-start.5 = (bf16[4,128,128]{2,1,0:T(8,128)(2,1)}, bf16[4,128,128]{2,1,0:T(8,128)(2,1)S(1)}, u32[]{:S(2)}) copy-start(bf16[4,128,128]{2,1,0:T(8,128)(2,1)S(1)} %collective-permute-done.1.from_b.refs_3_) | copy-start | bytes 393220
  14.0 7.6 %collective-permute-start.2 = (bf16[4,128,128]{2,1,0:T(8,128)(2,1)S(1)}, bf16[4,128,128]{2,1,0:T(8,128)(2,1)S(1)}, u32[]{:S(2)}, u32[]{:S(2)}) collective-permute-start(bf16[4,128,128]{2,1,0:T(8,128)(2,1)S(1)} %edge.1), channel_id=1, source_target_pairs={{0,1},{1,0},{2,3},{3,2},{4,5},{5,4},{6,7},{7,6},{8,9},{9,8},{10,11... | collective-permute-start | bytes 393224 | tf_op jit(solution)/shard_map/ppermute | solution.py:300
  21.6 0.7 copy-start.14
  26.8 29.2 %copy-start.18 = (bf16[2,128,128]{2,1,0:T(8,128)(2,1)S(1)}, bf16[2,128,128]{2,1,0:T(8,128)(2,1)}, u32[]{:S(2)}) copy-start(bf16[2,128,128]{2,1,0:T(8,128)(2,1)} %get-tuple-element.55) | copy-start | bytes 196612
  26.8 18.4 %all-to-all-start = ((f32[32,8,128]{2,1,0:T(8,128)}), f32[32,8,128]{2,1,0:T(8,128)S(1)}, u32[]{:S(2)}, u32[]{:S(2)}) async-start(f32[32,8,128]{2,1,0:T(8,128)} %get-tuple-element.48), calls=%async_computation | async-start | bytes 262144 | tf_op jit(solution)/shard_map/all_to_all | solution.py:321
  45.9 17.9 %all-to-all-start.1 = ((f32[16,8,128]{2,1,0:T(8,128)}), f32[16,8,128]{2,1,0:T(8,128)S(1)}, u32[]{:S(2)}, u32[]{:S(2)}) async-start(f32[16,8,128]{2,1,0:T(8,128)} %fold.3), calls=%async_computation.1 | async-start | bytes 131072 | tf_op jit(solution)/shard_map/all_to_all | solution.py:321
  56.0 3.1 %collective-permute-start.3 = (bf16[2,128,128]{2,1,0:T(8,128)(2,1)S(1)}, bf16[2,128,128]{2,1,0:T(8,128)(2,1)S(1)}, u32[]{:S(2)}, u32[]{:S(2)}) collective-permute-start(bf16[2,128,128]{2,1,0:T(8,128)(2,1)S(1)} %copy-done.18), channel_id=1, source_target_pairs={{0,1},{1,0},{2,3},{3,2},{4,5},{5,4},{6,7},{7,6},{8,9},{9,8},{10,11... | collective-permute-start | bytes 196616 | tf_op jit(solution)/shard_map/ppermute | solution.py:300
  59.1 24.4 %copy-start.9 = (bf16[2,128,128]{2,1,0:T(8,128)(2,1)}, bf16[2,128,128]{2,1,0:T(8,128)(2,1)S(1)}, u32[]{:S(2)}) copy-start(bf16[2,128,128]{2,1,0:T(8,128)(2,1)S(1)} %collective-permute-done.3.middle.refs_4_) | copy-start | bytes 196612
  63.8 0.6 copy-start.15
  67.7 11.3 %all-to-all-start.2 = ((f32[32,4,128]{2,1,0:T(4,128)}), f32[32,4,128]{2,1,0:T(4,128)S(1)}, u32[]{:S(2)}, u32[]{:S(2)}) async-start(f32[32,4,128]{2,1,0:T(4,128)} %get-tuple-element.59.refs_1_), calls=%async_computation.2 | async-start | bytes 131072 | tf_op jit(solution)/shard_map/all_to_all | solution.py:321
  71.2 12.4 %copy-start.6 = (bf16[4,128,128]{2,1,0:T(8,128)(2,1)S(1)}, bf16[4,128,128]{2,1,0:T(8,128)(2,1)}, u32[]{:S(2)}) copy-start(bf16[4,128,128]{2,1,0:T(8,128)(2,1)} %get-tuple-element.62.refs_5_.here_a.refs_0_) | copy-start | bytes 393220
  71.2 12.4 %copy-start.7 = (bf16[4,128,128]{2,1,0:T(8,128)(2,1)S(1)}, bf16[4,128,128]{2,1,0:T(8,128)(2,1)}, u32[]{:S(2)}) copy-start(bf16[4,128,128]{2,1,0:T(8,128)(2,1)} %get-tuple-element.63.refs_6_.here_b.refs_1_) | copy-start | bytes 393220
  79.7 13.1 %all-to-all-start.3 = ((f32[32,8,128]{2,1,0:T(8,128)}), f32[32,8,128]{2,1,0:T(8,128)S(1)}, u32[]{:S(2)}, u32[]{:S(2)}) async-start(f32[32,8,128]{2,1,0:T(8,128)} %fold.4), calls=%async_computation.3 | async-start | bytes 262144 | tf_op jit(solution)/shard_map/all_to_all | solution.py:321
  83.7 15.1 %collective-permute-start.4 = (bf16[5,128,128]{2,1,0:T(8,128)(2,1)S(1)}, bf16[5,128,128]{2,1,0:T(8,128)(2,1)S(1)}, u32[]{:S(2)}, u32[]{:S(2)}) collective-permute-start(bf16[5,128,128]{2,1,0:T(8,128)(2,1)S(1)} %get-tuple-element.65), channel_id=1, source_target_pairs={{0,2},{2,0},{4,6},{6,4},{8,10},{10,8},{12,14},{14,12},{1,3},{3,1},... | collective-permute-start | bytes 491528 | tf_op jit(solution)/shard_map/ppermute | solution.py:307
  85.8 13.0 %collective-permute-start.5 = (bf16[5,128,128]{2,1,0:T(8,128)(2,1)S(1)}, bf16[5,128,128]{2,1,0:T(8,128)(2,1)S(1)}, u32[]{:S(2)}, u32[]{:S(2)}) collective-permute-start(bf16[5,128,128]{2,1,0:T(8,128)(2,1)S(1)} %get-tuple-element.66), channel_id=1, source_target_pairs={{2,4},{4,2},{6,8},{8,6},{10,12},{12,10},{3,5},{5,3},{7,9},{9,7},{1... | collective-permute-start | bytes 491528 | tf_op jit(solution)/shard_map/ppermute | solution.py:307
  93.4 13.2 %all-to-all-start.4 = ((f32[16,8,128]{2,1,0:T(8,128)}), f32[16,8,128]{2,1,0:T(8,128)S(1)}, u32[]{:S(2)}, u32[]{:S(2)}) async-start(f32[16,8,128]{2,1,0:T(8,128)} %fold.5), calls=%async_computation.4 | async-start | bytes 131072 | tf_op jit(solution)/shard_map/all_to_all | solution.py:321
  98.8 0.7 copy-start.16
  99.4 0.7 copy-start.17

commit v7 on v6

--- a/solution.py
+++ b/solution.py
@@ -69,20 +69,6 @@
     return planes[:, pl.ds(((x + a) * PY + b) * CZ, CY * CZ)]
 
 
-def convolve(planes, lhs, x):
-    total = None
-    for a in range(3):
-        for b in range(3):
-            part = lax.dot_general(
-                lhs[:, pl.ds((3 * a + b) * GROUP, GROUP)],
-                window(planes, x, a, b),
-                NN,
-                preferred_element_type=F32,
-            )
-            total = part if total is None else total + part
-    return total
-
-
 def pieces(x):
     first = x.astype(BF16).astype(F32)
     rest = x - first
@@ -91,82 +77,99 @@
     return first, second, third
 
 
-def prepare_kernel(weights, warm, error, bias, lhs, base, bias_plane):
-    bias_plane[...] = jnp.transpose(jnp.broadcast_to(bias[...], (C, C)))
-    for tap in range(TAPS):
-        lhs[pl.ds(0, C), pl.ds(tap * C, C)] = weights[tap]
+def relayout_kernel(cube, here_a, here_b, edges, edge_a, edge_b):
+    even = is_even()
+    first_core = lax.axis_index("sy") == 0
+    flat = [cube[:, x].reshape(C, CY * CZ) for x in range(CX)]
+    rows = [[flat[x][:, y * CZ : (y + 1) * CZ] for y in range(CY)] for x in range(CX)]
+    for y in range(CY):
+        here_a[y] = jnp.where(even, rows[1][y], rows[0][y])
+        here_b[y] = jnp.where(even, rows[0][y], rows[1][y])
+    border = [jnp.where(first_core, rows[x][CY - 1], rows[x][0]) for x in range(CX)]
+    for x in range(CX):
+        edges[x] = border[x]
+    edge_a[0] = jnp.where(even, border[1], border[0])
+    edge_b[0] = jnp.where(even, border[0], border[1])
+
+
+def base_kernel(warm, error, base):
+    base[...] = lax.dot_general(
+        warm[...], error[...], NT, precision=HIGHEST, preferred_element_type=F32
+    )
+
+
+def rows_across(middle, corner_a, corner_b):
+    even = is_even()
+
+    def across(xp):
+        if 0 < xp < PX - 1:
+            return middle[xp - 1]
+        return jnp.where(even == (xp > 0), corner_a, corner_b)
+
+    return across
+
+
+def forward_kernel(
+    here_a, here_b, from_a, from_b, middle, corner_a, corner_b,
+    upstream, weights, warm, bias, base,
+    act, grad_a, grad_b, edges, sums, planes,
+):
+    across = rows_across(middle, corner_a[0], corner_b[0])
+    fill_planes(planes, here_a, here_b, from_a, from_b, across)
+    first_core = lax.axis_index("sy") == 0
+    even = is_even()
+    offset = jnp.transpose(jnp.broadcast_to(bias[...], (C, C)))[:, :1]
     rows = warm[...]
-    first, second, third = pieces(rows)
-    stacked = jnp.concatenate([first, second, third, jnp.zeros_like(rows)], axis=0)
-    lhs[pl.ds(C, EXTRA), :] = stacked.astype(BF16)
-    base[...] = lax.dot_general(rows, error[...], NT, precision=HIGHEST, preferred_element_type=F32)
-
-
-def forward_kernel(
-    wait, held, act_out, grad_a_out, grad_b_out, edges_out, sums_out,
-    planes, act, grad_a, grad_b, edges, sums, sem,
-):
-    here_a, here_b, from_a, from_b, across, upstream, lhs, bias, base = held
-    wait(0, 1, 2, 3, 4)
-    fill_planes(planes, here_a, here_b, from_a, from_b, lambda xp: across[xp])
-    first_core = lax.axis_index("sy") == 0
-    even = is_even()
+    terms = jnp.concatenate([*pieces(rows), jnp.zeros_like(rows)], axis=0).astype(BF16)
+    totals = [None] * CX
+    for pair in range(9):
+        stack = jnp.concatenate([weights[3 * pair + c] for c in range(3)], axis=1)
+        span = slice(pair * GROUP, (pair + 1) * GROUP)
+        stack = jnp.concatenate([stack, terms[:, span]], axis=0)
+        for x in range(CX):
+            part = lax.dot_general(
+                stack, window(planes, x, pair // 3, pair % 3), NN, preferred_element_type=F32
+            )
+            totals[x] = part if totals[x] is None else totals[x] + part
     joint = jnp.zeros((EXTRA, C), F32)
-    wait(6, 7, 5)
     cube = []
-    leaving = []
-
-    def leave(source, target):
-        leaving.append(pltpu.make_async_copy(source, target, sem.at[len(leaving)]))
-        leaving[-1].start()
-
     for x in range(CX):
-        total = convolve(planes, lhs, x)
-        pre = total[:C] + bias[:, :1]
+        total = totals[x]
+        pre = total[:C] + offset
         sigma = jax.nn.sigmoid(pre)
-        active = (pre * sigma).astype(BF16)
         slope = sigma * (1.0 + pre * (1.0 - sigma))
-        act[:, x] = active.reshape(C, CY, CZ)
-        grads = []
-        for y in range(CY):
-            span = slice(y * CZ, (y + 1) * CZ)
-            grads.append((upstream[x, y].astype(F32) * slope[:, span]).astype(BF16))
+        act[:, x] = (pre * sigma).astype(BF16).reshape(C, CY, CZ)
+        above = upstream[:, x].reshape(C, CY * CZ).astype(F32)
+        gradient = (above * slope).astype(BF16)
+        grads = [gradient[:, y * CZ : (y + 1) * CZ] for y in range(CY)]
         cube.append(grads)
         edges[x] = jnp.where(first_core, grads[CY - 1], grads[0])
         field = total[C : C + RANK] + total[C + RANK : C + 2 * RANK]
         field = field + total[C + 2 * RANK : C + 3 * RANK]
-        first, second, third = pieces(field)
-        stacked = jnp.concatenate([first, second, third, jnp.ones_like(field)], axis=0)
+        stacked = jnp.concatenate([*pieces(field), jnp.ones_like(field)], axis=0)
         joint = joint + lax.dot_general(
-            stacked.astype(BF16), jnp.concatenate(grads, axis=1), NT, preferred_element_type=F32
+            stacked.astype(BF16), gradient, NT, preferred_element_type=F32
         )
-    leave(act, act_out)
-    wait(8)
     local = joint[:RANK] + joint[RANK : 2 * RANK] + joint[2 * RANK : 3 * RANK] + base[...]
     both = jnp.concatenate([local, joint[3 * RANK :]], axis=0)
     for copy in range(sums.shape[0]):
         sums[copy] = both
-    leave(sums, sums_out)
     for y in range(CY):
         grad_a[y] = jnp.where(even, cube[1][y], cube[0][y])
         grad_b[y] = jnp.where(even, cube[0][y], cube[1][y])
-    leave(grad_a, grad_a_out)
-    leave(grad_b, grad_b_out)
-    leave(edges, edges_out)
-    for transfer in leaving:
-        transfer.wait()
 
 
 def gradient_kernel(wait, block, upper_out, lower_out, planes, upper, lower, sem):
-    here_a, here_b, from_a, from_b, across, grad_a, grad_b, error = block
-    wait(0, 1, 2, 3, 4)
-    fill_planes(planes, here_a, here_b, from_a, from_b, lambda xp: across[xp])
-    wait(5, 6)
+    here_a, here_b, from_a, from_b, middle, corner_a, corner_b, grad_a, grad_b, error = block
+    wait(0, 1, 2, 3, 4, 5, 6)
+    across = rows_across(middle, corner_a[0], corner_b[0])
+    fill_planes(planes, here_a, here_b, from_a, from_b, across)
+    wait(7, 8)
     even = is_even()
     side_a = jnp.concatenate([grad_a[y] for y in range(CY)], axis=1)
     side_b = jnp.concatenate([grad_b[y] for y in range(CY)], axis=1)
     grads = (jnp.where(even, side_b, side_a), jnp.where(even, side_a, side_b))
-    wait(7)
+    wait(9)
     leaving = []
     for pair in range(9):
         span = pl.ds(pair * GROUP, GROUP)
@@ -253,14 +256,7 @@
 def backward_kernel(wait, held, out, planes):
     here_a, here_b, from_a, from_b, middle, weights = held
     wait(0, 1, 2, 3, 4)
-    even = is_even()
-
-    def across(xp):
-        if 0 < xp < PX - 1:
-            return middle[xp - 1]
-        above = xp > 0
-        return jnp.where(even == above, from_a[CY], from_b[CY])
-
+    across = rows_across(middle, from_a[CY], from_b[CY])
     fill_planes(planes, here_a, here_b, from_a, from_b, across)
     wait(5)
     totals = [None] * CX
@@ -285,26 +281,28 @@
     to_b[CY] = jnp.where(even, middle[0], middle[1])
 
 
-def edge_kernel(here_a, here_b, from_a, from_b, edge):
-    first = lax.axis_index("sy") == 0
-    even = is_even()
-    ascending = (from_b, here_b, here_a, from_a)
-    descending = (from_a, here_a, here_b, from_b)
-    for xp in range(PX):
-        last = jnp.where(even, ascending[xp][CY - 1], descending[xp][CY - 1])
-        start = jnp.where(even, ascending[xp][0], descending[xp][0])
-        edge[xp] = jnp.where(first, last, start)
-
-
 def swap_cores(edge):
     return lax.ppermute(edge, "sy", [(0, 1), (1, 0)])
 
 
+def pairs_of(count):
+    pairs_a = [(i, i ^ 1) for i in range(count) if i ^ 1 < count]
+    pairs_b = [(i, j) for i in range(1, count) for j in [((i - 1) ^ 1) + 1] if j < count]
+    return pairs_a, pairs_b
+
+
 def exchange_x(to_a, to_b):
-    count = lax.axis_size("sx")
-    pairs_a = [(i, i ^ 1) for i in range(count) if i ^ 1 < count]
-    pairs_b = [(i, j) for i in range(1, count - 1) for j in [((i - 1) ^ 1) + 1] if j < count]
+    pairs_a, pairs_b = pairs_of(lax.axis_size("sx"))
     return lax.ppermute(to_a, "sx", pairs_a), lax.ppermute(to_b, "sx", pairs_b)
+
+
+def exchange_corners(to_a, to_b):
+    cores = lax.axis_size("sy")
+    both = [
+        [(i * cores + c, j * cores + 1 - c) for i, j in pairs for c in range(cores)]
+        for pairs in pairs_of(lax.axis_size("sx"))
+    ]
+    return lax.ppermute(to_a, BLOCK, both[0]), lax.ppermute(to_b, BLOCK, both[1])
 
 
 tie = lax.optimization_barrier
@@ -388,38 +386,32 @@
     padded = -(-TAPS // columns) * columns
     planes = pltpu.VMEM((GROUP, PX * PY * CZ), BF16)
     error = error_state[0, 0, 0]
-    shift = jnp.where(is_even(), 1, 0)
-    here_a, here_b = (
-        jnp.transpose(lax.dynamic_index_in_dim(features[0], which, 1, False), (1, 0, 2))
-        for which in (shift, 1 - shift)
+    here_a, here_b, edges, edge_a, edge_b = call(
+        relayout_kernel,
+        "relayout",
+        4,
+        (bf16(CY, C, CZ), bf16(CY, C, CZ), bf16(CX, C, CZ), bf16(1, C, CZ), bf16(1, C, CZ)),
+        (features[0],),
     )
     from_a, from_b = exchange_x(here_a, here_b)
-    upstream = jnp.transpose(cotangent[0], (1, 2, 0, 3))
-    lhs, base, bias = call(
-        prepare_kernel,
-        "prepare",
-        8,
-        (bf16(C + EXTRA, K), f32(RANK, C), f32(C, C)),
-        (weights, warm_factor, error, conv_bias[None]),
-    )
-    from_a, from_b, lhs, base, bias, upstream = tie((from_a, from_b, lhs, base, bias, upstream))
-    edge = call(edge_kernel, "edge", 2, bf16(PX, C, CZ), (here_a, here_b, from_a, from_b))
-    block = (here_a, here_b, from_a, from_b, swap_cores(edge))
-    shapes = (
-        bf16(C, CX, CY, CZ),
-        bf16(CY, C, CZ),
-        bf16(CY, C, CZ),
-        bf16(CX, C, CZ),
-        f32(chips, 2 * RANK, C),
-    )
-    act, grad_a, grad_b, edges, sums = fetch_and_call(
+    corner_a, corner_b = exchange_corners(edge_a, edge_b)
+    middle = swap_cores(edges)
+    base = call(base_kernel, "base", 4, f32(RANK, C), (warm_factor, error))
+    from_a, from_b, base = tie((from_a, from_b, base))
+    block = (here_a, here_b, from_a, from_b, middle, corner_a, corner_b)
+    act, grad_a, grad_b, edges, sums = call(
         forward_kernel,
         "forward",
-        60,
-        shapes,
-        (*block, upstream, lhs, bias, base),
-        [planes, *(pltpu.VMEM(s.shape, s.dtype) for s in shapes), pltpu.SemaphoreType.DMA((5,))],
-        HBM,
+        12,
+        (
+            bf16(C, CX, CY, CZ),
+            bf16(CY, C, CZ),
+            bf16(CY, C, CZ),
+            bf16(CX, C, CZ),
+            f32(chips, 2 * RANK, C),
+        ),
+        (*block, cotangent[0], weights, warm_factor, conv_bias[None], base),
+        [planes],
     )
     parts = swap(sums, DP)
     upper, lower = fetch_and_call(

time: 108 us -> 109 us (level)
  starting transfers between devices: 48.3 us -> 54.5 us
  local copies, waits for them, and re-layouts: 9.4 us -> 6.55 us
  Pallas kernels: 24.2 us -> 22.6 us
    ppermute x0 -> x2, starting transfers between devices: none -> 5.45 us  [the longest x1 4.79 us: exchange_corners(): lax.ppermute(to_a, BLOCK, both[0])]
    pallas_call x5 -> x4, Pallas kernels: 19.7 us -> 15.3 us  [fetch_and_call(): pl.pallas_call(body, out_shape=shapes, in_specs=[VMEM] * len(near) + [HBM...]
    pallas_call x7 -> x8, Pallas kernels: 4.41 us -> 7.38 us  [call(): pl.pallas_call(kernel, out_shape=shapes, in_specs=[VMEM] * len(args), out...]
    unnamed x39 -> x44, local copies, waits for them, and re-layouts: 8.22 us -> 6.55 us
    dynamic_slice x3 -> x0, local copies, waits for them, and re-layouts: 1.18 us -> none  [shards(): lax.dynamic_index_in_dim(features[0], which, 1, False)]
  transfers between devices with their start and end apart: 11 -> 13, of which waited for: 7 -> 6; matrix products, arithmetic and copies ran while one was open for 2% -> 0% of each run, Pallas kernels for 13% -> 13%
where the time goes in v7:
time: 109 us; the launch traced here: 108 us
  starting transfers between devices  54.5 us (50%)
  waiting for transfers between devices  23.5 us (22%)
  Pallas kernels  22.6 us (21%)
  local copies, waits for them, and re-layouts  6.55 us (6%)
    all_to_all x5, starting transfers between devices, swap(): return lax.all_to_all(x, axes, 0, 0, tiled=True)  32.8 us
    all_to_all x5, waiting for transfers between devices, swap(): return lax.all_to_all(x, axes, 0, 0, tiled=True)  22.3 us
    pallas_call x4, Pallas kernels, fetch_and_call(): pl.pallas_call(body, out_shape=shapes, in_specs=[VMEM] * len(near) + [HBM...  15.3 us
    ppermute x2, starting transfers between devices, swap_cores(): return lax.ppermute(edge, 'sy', [(0, 1), (1, 0)])  8.68 us
    pallas_call x8, Pallas kernels, call(): pl.pallas_call(kernel, out_shape=shapes, in_specs=[VMEM] * len(args), out...  7.38 us
    unnamed x44, local copies, waits for them, and re-layouts  6.55 us
    ppermute x2, starting transfers between devices, exchange_x(): lax.ppermute(to_a, 'sx', pairs_a)  6.17 us
    ppermute x1, starting transfers between devices, exchange_corners(): lax.ppermute(to_a, BLOCK, both[0])  4.79 us
  transfers between devices with their start and end apart: 13, of which 6 were waited for; matrix products, arithmetic and copies ran while one was open for 0% of the time, Pallas kernels for 13%

profile of v7, /device:TPU:1, one launch (start us, length us, event | category | flops | bytes accessed | tf_op | source)
XLA Modules:
  0.0 108.1 jit_solution(13895093908281286051)
XLA Ops:
  0.6 0.0 copy-start.18
  0.6 0.0 copy-start.11
  0.7 0.9 copy-done.11
  1.6 0.2 relayout.1
  1.8 0.0 copy-start.6
  1.8 0.0 copy-start.7
  1.9 4.0 %collective-permute-start = (bf16[4,128,128]{2,1,0:T(8,128)(2,1)S(1)}, bf16[4,128,128]{2,1,0:T(8,128)(2,1)S(1)}, u32[]{:S(2)}, u32[]{:S(2)}) collective-permute-start(bf16[4,128,128]{2,1,0:T(8,128)(2,1)S(1)} %get-tuple-element.37.here_a.refs_0_), channel_id=1, source_target_pairs={{0,2},{2,0},{4,6},{6,4},{8,10},{10,8},{12,14},{14,12},{1,3},{3,1},... | collective-permute-start | bytes 393224 | tf_op jit(solution)/shard_map/ppermute | solution.py:296
  5.9 0.7 collective-permute-start.1
  6.6 6.7 %collective-permute-start.2 = (bf16[2,128,128]{2,1,0:T(8,128)(2,1)S(1)}, bf16[2,128,128]{2,1,0:T(8,128)(2,1)S(1)}, u32[]{:S(2)}, u32[]{:S(2)}) collective-permute-start(bf16[2,128,128]{2,1,0:T(8,128)(2,1)S(1)} %get-tuple-element.41), channel_id=1, source_target_pairs={{0,1},{1,0},{2,3},{3,2},{4,5},{5,4},{6,7},{7,6},{8,9},{9,8},{10,11... | collective-permute-start | bytes 196616 | tf_op jit(solution)/shard_map/ppermute | solution.py:285
  13.3 4.8 %collective-permute-start.3 = (bf16[1,128,128]{2,1,0:T(8,128)(2,1)S(1)}, bf16[1,128,128]{2,1,0:T(8,128)(2,1)S(1)}, u32[]{:S(2)}, u32[]{:S(2)}) collective-permute-start(bf16[1,128,128]{2,1,0:T(8,128)(2,1)S(1)} %get-tuple-element.42), channel_id=1, source_target_pairs={{0,3},{1,2},{2,1},{3,0},{4,7},{5,6},{6,5},{7,4},{8,11},{9,10},{10,... | collective-permute-start | bytes 98312 | tf_op jit(solution)/shard_map/ppermute | solution.py:305
  18.1 0.7 collective-permute-start.4
  18.7 0.0 copy-start
  18.7 1.5 %copy-done = f32[1,1,1,128,3456]{4,3,2,1,0:T(8,128)S(1)} copy-done((f32[1,1,1,128,3456]{4,3,2,1,0:T(8,128)S(1)}, f32[1,1,1,128,3456]{4,3,2,1,0:T(8,128)}, u32[]{:S(2)}) %copy-start) | copy-done | bytes 1769496
  20.2 0.8 copy-done.14
  21.0 1.5 %base.1 = f32[4,128]{1,0:T(4,128)S(1)} custom-call(f32[4,3456]{1,0:T(4,128)S(1)} %copy-done.14, f32[128,3456]{1,0:T(8,128)S(1)} %bitcast.11), custom_call_target="tpu_custom_call" | custom-call | tf_op jit(solution)/shard_map/base/pallas_call | solution.py:323
  22.5 0.0 collective-permute-done.from_a.refs_2_
  22.5 0.0 collective-permute-done.1.from_b.refs_3_
  22.6 0.0 copy-start.9
  22.6 0.0 collective-permute-done.3.corner_a.refs_5_
  22.6 0.0 copy-start.16
  22.6 0.0 collective-permute-done.4.corner_b.refs_6_
  22.6 0.0 copy-start.17
  22.6 0.0 collective-permute-done.2.middle.refs_4_
  22.6 0.0 copy-start.13
  22.6 0.0 copy-done.18
  22.7 0.0 copy-done.12
  22.7 0.0 copy-done.1
  22.7 0.0 copy-done.15
  22.7 3.0 %forward.1 = (bf16[128,2,4,128]{3,2,1,0:T(4,128)(2,1)}, bf16[4,128,128]{2,1,0:T(8,128)(2,1)S(1)}, bf16[4,128,128]{2,1,0:T(8,128)(2,1)S(1)}, bf16[2,128,128]{2,1,0:T(8,128)(2,1)S(1)}, f32[32,8,128]{2,1,0:T(8,128)}) custom-call(bf16[4,128,128]{2,1,0:T(8,128)(2,1)S(1)} %get-tuple-element.37.here_a.refs_0_, ...), custom_call_target="tpu_custom_call" | custom-call | tf_op jit(solution)/shard_map/forward/pallas_call | solution.py:323
  25.6 0.0 copy-done.6
  25.6 0.0 copy-done.7
  25.6 0.7 copy-done.2
  26.3 0.6 copy-done.4
  27.0 10.2 %all-to-all-start = ((f32[32,8,128]{2,1,0:T(8,128)}), f32[32,8,128]{2,1,0:T(8,128)S(1)}, u32[]{:S(2)}, u32[]{:S(2)}) async-start(f32[32,8,128]{2,1,0:T(8,128)} %get-tuple-element.46), calls=%async_computation | async-start | bytes 262144 | tf_op jit(solution)/shard_map/all_to_all | solution.py:319
  37.2 0.0 copy-done.8
  37.2 0.0 copy-done.9
  37.2 0.0 copy-done.16
  37.2 0.0 copy-done.17
  37.2 5.0 %gradient.1 = (bf16[128,3456]{1,0:T(8,128)(2,1)}, bf16[128,3456]{1,0:T(8,128)(2,1)}) custom-call(bf16[4,128,128]{2,1,0:T(8,128)(2,1)} %copy-done.6, bf16[4,128,128]{2,1,0:T(8,128)(2,1)} %copy-done.7, bf16[4,128,128]{2,1,0:T(8,128)(2,1)} %copy-done.8, bf16[4,128,128]{2,1,0:T(8,128)(2,1)} %copy-done.9, bf16[2,128,128]{2,1,0:T(8,128)(2,1)} %copy-done.13, ...), custom_call_target="tpu_custom_call" | custom-call | tf_op jit(solution)/shard_map/gradient/pallas_call | solution.py:355
  42.3 4.1 %all-to-all-done.parts = f32[32,8,128]{2,1,0:T(8,128)S(1)} async-done(((f32[32,8,128]{2,1,0:T(8,128)}), f32[32,8,128]{2,1,0:T(8,128)S(1)}, u32[]{:S(2)}, u32[]{:S(2)}) %all-to-all-start) | async-done | bytes 131104 | tf_op jit(solution)/shard_map/all_to_all | solution.py:319
  46.3 0.7 fold.3
  47.0 9.6 %all-to-all-start.1 = ((f32[16,8,128]{2,1,0:T(8,128)}), f32[16,8,128]{2,1,0:T(8,128)S(1)}, u32[]{:S(2)}, u32[]{:S(2)}) async-start(f32[16,8,128]{2,1,0:T(8,128)} %fold.3), calls=%async_computation.1 | async-start | bytes 131072 | tf_op jit(solution)/shard_map/all_to_all | solution.py:319
  56.6 2.0 %collective-permute-start.5 = (bf16[2,128,128]{2,1,0:T(8,128)(2,1)S(1)}, bf16[2,128,128]{2,1,0:T(8,128)(2,1)S(1)}, u32[]{:S(2)}, u32[]{:S(2)}) collective-permute-start(bf16[2,128,128]{2,1,0:T(8,128)(2,1)S(1)} %get-tuple-element.53), channel_id=1, source_target_pairs={{0,1},{1,0},{2,3},{3,2},{4,5},{5,4},{6,7},{7,6},{8,9},{9,8},{10,11... | collective-permute-start | bytes 196616 | tf_op jit(solution)/shard_map/ppermute | solution.py:285
  58.6 1.1 %collective-permute-done.5.middle.refs_4_ = bf16[2,128,128]{2,1,0:T(8,128)(2,1)S(1)} collective-permute-done((bf16[2,128,128]{2,1,0:T(8,128)(2,1)S(1)}, bf16[2,128,128]{2,1,0:T(8,128)(2,1)S(1)}, u32[]{:S(2)}, u32[]{:S(2)}) %collective-permute-start.5) | collective-permute-done | bytes 65568 | tf_op jit(solution)/shard_map/ppermute | solution.py:285
  59.7 4.7 %all-to-all-done.1.refs_0_ = f32[16,8,128]{2,1,0:T(8,128)S(1)} async-done(((f32[16,8,128]{2,1,0:T(8,128)}), f32[16,8,128]{2,1,0:T(8,128)S(1)}, u32[]{:S(2)}, u32[]{:S(2)}) %all-to-all-start.1) | async-done | bytes 65568 | tf_op jit(solution)/shard_map/all_to_all | solution.py:319
  64.4 0.6 copy-done.19
  65.0 3.3 %project.1 = (f32[4,128]{1,0:T(4,128)}, f32[1,128]{1,0:T(1,128)}, f32[32,4,128]{2,1,0:T(4,128)}) custom-call(f32[16,8,128]{2,1,0:T(8,128)} %copy-done.19, bf16[128,3456]{1,0:T(8,128)(2,1)} %get-tuple-element.55.refs_1_.refs_2_, bf16[128,3456]{1,0:T(8,128)(2,1)} %get-tuple-element.56.refs_2_.refs_3_), custom_call_target="tpu_custom_call" | custom-call | tf_op jit(solution)/shard_map/project/pallas_call | solution.py:355
  68.3 3.4 %all-to-all-start.2 = ((f32[32,4,128]{2,1,0:T(4,128)}), f32[32,4,128]{2,1,0:T(4,128)S(1)}, u32[]{:S(2)}, u32[]{:S(2)}) async-start(f32[32,4,128]{2,1,0:T(4,128)} %get-tuple-element.57.refs_1_), calls=%async_computation.2 | async-start | bytes 131072 | tf_op jit(solution)/shard_map/all_to_all | solution.py:319
  71.7 3.0 %residual.1 = f32[128,3456]{1,0:T(8,128)} custom-call(f32[4,128]{1,0:T(4,128)} %get-tuple-element.34.refs_0_, f32[32,4,128]{2,1,0:T(4,128)} %get-tuple-element.57.refs_1_, bf16[128,3456]{1,0:T(8,128)(2,1)} %get-tuple-element.55.refs_1_.refs_2_, bf16[128,3456]{1,0:T(8,128)(2,1)} %get-tuple-element.56.refs_2_.refs_3_), custom_call_target="tpu_custom_call" | custom-call | tf_op jit(solution)/shard_map/residual/pallas_call | solution.py:355
  74.8 4.8 %all-to-all-done.2 = f32[32,4,128]{2,1,0:T(4,128)S(1)} async-done(((f32[32,4,128]{2,1,0:T(4,128)}), f32[32,4,128]{2,1,0:T(4,128)S(1)}, u32[]{:S(2)}, u32[]{:S(2)}) %all-to-all-start.2) | async-done | bytes 65568 | tf_op jit(solution)/shard_map/all_to_all | solution.py:319
  79.6 0.7 fold.4
  80.2 4.2 %all-to-all-start.3 = ((f32[32,8,128]{2,1,0:T(8,128)}), f32[32,8,128]{2,1,0:T(8,128)S(1)}, u32[]{:S(2)}, u32[]{:S(2)}) async-start(f32[32,8,128]{2,1,0:T(8,128)} %fold.4), calls=%async_computation.3 | async-start | bytes 262144 | tf_op jit(solution)/shard_map/all_to_all | solution.py:319
  84.5 2.1 %collective-permute-start.6 = (bf16[5,128,128]{2,1,0:T(8,128)(2,1)S(1)}, bf16[5,128,128]{2,1,0:T(8,128)(2,1)S(1)}, u32[]{:S(2)}, u32[]{:S(2)}) collective-permute-start(bf16[5,128,128]{2,1,0:T(8,128)(2,1)S(1)} %get-tuple-element.63), channel_id=1, source_target_pairs={{0,2},{2,0},{4,6},{6,4},{8,10},{10,8},{12,14},{14,12},{1,3},{3,1},... | collective-permute-start | bytes 491528 | tf_op jit(solution)/shard_map/ppermute | solution.py:296
  86.7 0.7 collective-permute-start.7
  87.4 6.3 %all-to-all-done.3.parts = f32[32,8,128]{2,1,0:T(8,128)S(1)} async-done(((f32[32,8,128]{2,1,0:T(8,128)}), f32[32,8,128]{2,1,0:T(8,128)S(1)}, u32[]{:S(2)}, u32[]{:S(2)}) %all-to-all-start.3) | async-done | bytes 131104 | tf_op jit(solution)/shard_map/all_to_all | solution.py:319
  93.6 0.7 fold.5
  94.3 5.4 %all-to-all-start.4 = ((f32[16,8,128]{2,1,0:T(8,128)}), f32[16,8,128]{2,1,0:T(8,128)S(1)}, u32[]{:S(2)}, u32[]{:S(2)}) async-start(f32[16,8,128]{2,1,0:T(8,128)} %fold.5), calls=%async_computation.4 | async-start | bytes 131072 | tf_op jit(solution)/shard_map/all_to_all | solution.py:319
  99.7 0.0 collective-permute-done.6.refs_2_
  99.7 0.0 collective-permute-done.7.refs_3_
  99.7 0.7 copy-done.20
  100.3 0.7 copy-done.21
  101.0 3.9 %backward.1 = bf16[128,2,4,128]{3,2,1,0:T(4,128)(2,1)} custom-call(bf16[4,128,128]{2,1,0:T(8,128)(2,1)} %copy-done.2, bf16[4,128,128]{2,1,0:T(8,128)(2,1)} %copy-done.4, bf16[5,128,128]{2,1,0:T(8,128)(2,1)} %copy-done.20, bf16[5,128,128]{2,1,0:T(8,128)(2,1)} %copy-done.21, bf16[2,128,128]{2,1,0:T(8,128)(2,1)} %copy-done.10, bf16[27,128,128]{2,1,0:T(8,128)(2,1)} %refs_5_.1), custom_call_target="tpu_custom_call" | custom-call | tf_op jit(solution)/shard_map/backward/pallas_call | solution.py:355
  104.9 2.6 %all-to-all-done.4 = f32[16,8,128]{2,1,0:T(8,128)S(1)} async-done(((f32[16,8,128]{2,1,0:T(8,128)}), f32[16,8,128]{2,1,0:T(8,128)S(1)}, u32[]{:S(2)}, u32[]{:S(2)}) %all-to-all-start.4) | async-done | bytes 65568 | tf_op jit(solution)/shard_map/all_to_all | solution.py:319
  107.5 0.6 finish.1
  (18 shorter events, 0.1 us)
Async XLA Ops:
  0.6 22.0 %copy-start.18 = (f32[128]{0:T(128)S(1)}, f32[128]{0:T(128)}, u32[]{:S(2)}) copy-start(f32[128]{0:T(128)} %param.9) | copy-start | bytes 1540
  0.6 1.0 copy-start.11
  1.6 21.1 %copy-start.12 = (bf16[1,128,2,4,128]{4,3,2,1,0:T(4,128)(2,1)S(1)}, bf16[1,128,2,4,128]{4,3,2,1,0:T(4,128)(2,1)}, u32[]{:S(2)}) copy-start(bf16[1,128,2,4,128]{4,3,2,1,0:T(4,128)(2,1)} %param.7) | copy-start | bytes 786436
  1.8 23.8 %copy-start.6 = (bf16[4,128,128]{2,1,0:T(8,128)(2,1)}, bf16[4,128,128]{2,1,0:T(8,128)(2,1)S(1)}, u32[]{:S(2)}) copy-start(bf16[4,128,128]{2,1,0:T(8,128)(2,1)S(1)} %get-tuple-element.37.here_a.refs_0_) | copy-start | bytes 393220
  1.8 23.8 %copy-start.7 = (bf16[4,128,128]{2,1,0:T(8,128)(2,1)}, bf16[4,128,128]{2,1,0:T(8,128)(2,1)S(1)}, u32[]{:S(2)}) copy-start(bf16[4,128,128]{2,1,0:T(8,128)(2,1)S(1)} %get-tuple-element.38.here_b.refs_1_) | copy-start | bytes 393220
  1.9 20.7 %collective-permute-start = (bf16[4,128,128]{2,1,0:T(8,128)(2,1)S(1)}, bf16[4,128,128]{2,1,0:T(8,128)(2,1)S(1)}, u32[]{:S(2)}, u32[]{:S(2)}) collective-permute-start(bf16[4,128,128]{2,1,0:T(8,128)(2,1)S(1)} %get-tuple-element.37.here_a.refs_0_), channel_id=1, source_target_pairs={{0,2},{2,0},{4,6},{6,4},{8,10},{10,8},{12,14},{14,12},{1,3},{3,1},... | collective-permute-start | bytes 393224 | tf_op jit(solution)/shard_map/ppermute | solution.py:296
  5.9 16.7 %collective-permute-start.1 = (bf16[4,128,128]{2,1,0:T(8,128)(2,1)S(1)}, bf16[4,128,128]{2,1,0:T(8,128)(2,1)S(1)}, u32[]{:S(2)}, u32[]{:S(2)}) collective-permute-start(bf16[4,128,128]{2,1,0:T(8,128)(2,1)S(1)} %get-tuple-element.38.here_b.refs_1_), channel_id=1, source_target_pairs={{2,4},{4,2},{6,8},{8,6},{10,12},{12,10},{3,5},{5,3},{7,9},{9,7},{1... | collective-permute-start | bytes 393224 | tf_op jit(solution)/shard_map/ppermute | solution.py:296
  6.6 16.1 %collective-permute-start.2 = (bf16[2,128,128]{2,1,0:T(8,128)(2,1)S(1)}, bf16[2,128,128]{2,1,0:T(8,128)(2,1)S(1)}, u32[]{:S(2)}, u32[]{:S(2)}) collective-permute-start(bf16[2,128,128]{2,1,0:T(8,128)(2,1)S(1)} %get-tuple-element.41), channel_id=1, source_target_pairs={{0,1},{1,0},{2,3},{3,2},{4,5},{5,4},{6,7},{7,6},{8,9},{9,8},{10,11... | collective-permute-start | bytes 196616 | tf_op jit(solution)/shard_map/ppermute | solution.py:285
  13.3 9.3 %collective-permute-start.3 = (bf16[1,128,128]{2,1,0:T(8,128)(2,1)S(1)}, bf16[1,128,128]{2,1,0:T(8,128)(2,1)S(1)}, u32[]{:S(2)}, u32[]{:S(2)}) collective-permute-start(bf16[1,128,128]{2,1,0:T(8,128)(2,1)S(1)} %get-tuple-element.42), channel_id=1, source_target_pairs={{0,3},{1,2},{2,1},{3,0},{4,7},{5,6},{6,5},{7,4},{8,11},{9,10},{10,... | collective-permute-start | bytes 98312 | tf_op jit(solution)/shard_map/ppermute | solution.py:305
  18.1 4.6 %collective-permute-start.4 = (bf16[1,128,128]{2,1,0:T(8,128)(2,1)S(1)}, bf16[1,128,128]{2,1,0:T(8,128)(2,1)S(1)}, u32[]{:S(2)}, u32[]{:S(2)}) collective-permute-start(bf16[1,128,128]{2,1,0:T(8,128)(2,1)S(1)} %get-tuple-element.43), channel_id=1, source_target_pairs={{2,5},{3,4},{4,3},{5,2},{6,9},{7,8},{8,7},{9,6},{10,13},{11,12},{1... | collective-permute-start | bytes 98312 | tf_op jit(solution)/shard_map/ppermute | solution.py:305
  18.7 1.5 %copy-start = (f32[1,1,1,128,3456]{4,3,2,1,0:T(8,128)S(1)}, f32[1,1,1,128,3456]{4,3,2,1,0:T(8,128)}, u32[]{:S(2)}) copy-start(f32[1,1,1,128,3456]{4,3,2,1,0:T(8,128)} %param.10) | copy-start | bytes 5308420
  20.2 0.8 copy-start.14
  21.0 1.7 %copy-start.1 = (bf16[27,128,128]{2,1,0:T(8,128)(2,1)S(1)}, bf16[27,128,128]{2,1,0:T(8,128)(2,1)}, u32[]{:S(2)}) copy-start(bf16[27,128,128]{2,1,0:T(8,128)(2,1)} %refs_5_.1) | copy-start | bytes 2654212
  21.0 1.7 %copy-start.15 = (f32[4,3456]{1,0:T(4,128)S(1)}, f32[4,3456]{1,0:T(4,128)}, u32[]{:S(2)}) copy-start(f32[4,3456]{1,0:T(4,128)} %warm.3) | copy-start | bytes 165892
  22.5 14.6 %copy-start.8 = (bf16[4,128,128]{2,1,0:T(8,128)(2,1)}, bf16[4,128,128]{2,1,0:T(8,128)(2,1)S(1)}, u32[]{:S(2)}) copy-start(bf16[4,128,128]{2,1,0:T(8,128)(2,1)S(1)} %collective-permute-done.from_a.refs_2_) | copy-start | bytes 393220
  22.6 14.6 %copy-start.9 = (bf16[4,128,128]{2,1,0:T(8,128)(2,1)}, bf16[4,128,128]{2,1,0:T(8,128)(2,1)S(1)}, u32[]{:S(2)}) copy-start(bf16[4,128,128]{2,1,0:T(8,128)(2,1)S(1)} %collective-permute-done.1.from_b.refs_3_) | copy-start | bytes 393220
  22.6 14.6 %copy-start.16 = (bf16[1,128,128]{2,1,0:T(8,128)(2,1)}, bf16[1,128,128]{2,1,0:T(8,128)(2,1)S(1)}, u32[]{:S(2)}) copy-start(bf16[1,128,128]{2,1,0:T(8,128)(2,1)S(1)} %collective-permute-done.3.corner_a.refs_5_) | copy-start | bytes 98308
  22.6 14.6 %copy-start.17 = (bf16[1,128,128]{2,1,0:T(8,128)(2,1)}, bf16[1,128,128]{2,1,0:T(8,128)(2,1)S(1)}, u32[]{:S(2)}) copy-start(bf16[1,128,128]{2,1,0:T(8,128)(2,1)S(1)} %collective-permute-done.4.corner_b.refs_6_) | copy-start | bytes 98308
  22.6 14.6 %copy-start.13 = (bf16[2,128,128]{2,1,0:T(8,128)(2,1)}, bf16[2,128,128]{2,1,0:T(8,128)(2,1)S(1)}, u32[]{:S(2)}) copy-start(bf16[2,128,128]{2,1,0:T(8,128)(2,1)S(1)} %collective-permute-done.2.middle.refs_4_) | copy-start | bytes 196612
  25.6 0.7 copy-start.2
  26.3 0.6 copy-start.4
  27.0 19.4 %all-to-all-start = ((f32[32,8,128]{2,1,0:T(8,128)}), f32[32,8,128]{2,1,0:T(8,128)S(1)}, u32[]{:S(2)}, u32[]{:S(2)}) async-start(f32[32,8,128]{2,1,0:T(8,128)} %get-tuple-element.46), calls=%async_computation | async-start | bytes 262144 | tf_op jit(solution)/shard_map/all_to_all | solution.py:319
  47.0 17.4 %all-to-all-start.1 = ((f32[16,8,128]{2,1,0:T(8,128)}), f32[16,8,128]{2,1,0:T(8,128)S(1)}, u32[]{:S(2)}, u32[]{:S(2)}) async-start(f32[16,8,128]{2,1,0:T(8,128)} %fold.3), calls=%async_computation.1 | async-start | bytes 131072 | tf_op jit(solution)/shard_map/all_to_all | solution.py:319
  56.6 3.1 %collective-permute-start.5 = (bf16[2,128,128]{2,1,0:T(8,128)(2,1)S(1)}, bf16[2,128,128]{2,1,0:T(8,128)(2,1)S(1)}, u32[]{:S(2)}, u32[]{:S(2)}) collective-permute-start(bf16[2,128,128]{2,1,0:T(8,128)(2,1)S(1)} %get-tuple-element.53), channel_id=1, source_target_pairs={{0,1},{1,0},{2,3},{3,2},{4,5},{5,4},{6,7},{7,6},{8,9},{9,8},{10,11... | collective-permute-start | bytes 196616 | tf_op jit(solution)/shard_map/ppermute | solution.py:285
  59.7 24.8 %copy-start.10 = (bf16[2,128,128]{2,1,0:T(8,128)(2,1)}, bf16[2,128,128]{2,1,0:T(8,128)(2,1)S(1)}, u32[]{:S(2)}) copy-start(bf16[2,128,128]{2,1,0:T(8,128)(2,1)S(1)} %collective-permute-done.5.middle.refs_4_) | copy-start | bytes 196612
  64.4 0.6 copy-start.19
  68.3 11.3 %all-to-all-start.2 = ((f32[32,4,128]{2,1,0:T(4,128)}), f32[32,4,128]{2,1,0:T(4,128)S(1)}, u32[]{:S(2)}, u32[]{:S(2)}) async-start(f32[32,4,128]{2,1,0:T(4,128)} %get-tuple-element.57.refs_1_), calls=%async_computation.2 | async-start | bytes 131072 | tf_op jit(solution)/shard_map/all_to_all | solution.py:319
  71.7 12.8 %copy-start.3 = (bf16[4,128,128]{2,1,0:T(8,128)(2,1)S(1)}, bf16[4,128,128]{2,1,0:T(8,128)(2,1)}, u32[]{:S(2)}) copy-start(bf16[4,128,128]{2,1,0:T(8,128)(2,1)} %copy-done.2) | copy-start | bytes 393220
  71.7 12.8 %copy-start.5 = (bf16[4,128,128]{2,1,0:T(8,128)(2,1)S(1)}, bf16[4,128,128]{2,1,0:T(8,128)(2,1)}, u32[]{:S(2)}) copy-start(bf16[4,128,128]{2,1,0:T(8,128)(2,1)} %copy-done.4) | copy-start | bytes 393220
  80.2 13.4 %all-to-all-start.3 = ((f32[32,8,128]{2,1,0:T(8,128)}), f32[32,8,128]{2,1,0:T(8,128)S(1)}, u32[]{:S(2)}, u32[]{:S(2)}) async-start(f32[32,8,128]{2,1,0:T(8,128)} %fold.4), calls=%async_computation.3 | async-start | bytes 262144 | tf_op jit(solution)/shard_map/all_to_all | solution.py:319
  84.5 15.1 %collective-permute-start.6 = (bf16[5,128,128]{2,1,0:T(8,128)(2,1)S(1)}, bf16[5,128,128]{2,1,0:T(8,128)(2,1)S(1)}, u32[]{:S(2)}, u32[]{:S(2)}) collective-permute-start(bf16[5,128,128]{2,1,0:T(8,128)(2,1)S(1)} %get-tuple-element.63), channel_id=1, source_target_pairs={{0,2},{2,0},{4,6},{6,4},{8,10},{10,8},{12,14},{14,12},{1,3},{3,1},... | collective-permute-start | bytes 491528 | tf_op jit(solution)/shard_map/ppermute | solution.py:296
  86.7 13.0 %collective-permute-start.7 = (bf16[5,128,128]{2,1,0:T(8,128)(2,1)S(1)}, bf16[5,128,128]{2,1,0:T(8,128)(2,1)S(1)}, u32[]{:S(2)}, u32[]{:S(2)}) collective-permute-start(bf16[5,128,128]{2,1,0:T(8,128)(2,1)S(1)} %get-tuple-element.64), channel_id=1, source_target_pairs={{2,4},{4,2},{6,8},{8,6},{10,12},{12,10},{3,5},{5,3},{7,9},{9,7},{1... | collective-permute-start | bytes 491528 | tf_op jit(solution)/shard_map/ppermute | solution.py:296
  94.3 13.2 %all-to-all-start.4 = ((f32[16,8,128]{2,1,0:T(8,128)}), f32[16,8,128]{2,1,0:T(8,128)S(1)}, u32[]{:S(2)}, u32[]{:S(2)}) async-start(f32[16,8,128]{2,1,0:T(8,128)} %fold.5), calls=%async_computation.4 | async-start | bytes 131072 | tf_op jit(solution)/shard_map/all_to_all | solution.py:319
  99.7 0.7 copy-start.20
  100.3 0.7 copy-start.21

commit v8 on v7

--- a/solution.py
+++ b/solution.py
@@ -77,19 +77,23 @@
     return first, second, third
 
 
-def relayout_kernel(cube, here_a, here_b, edges, edge_a, edge_b):
-    even = is_even()
-    first_core = lax.axis_index("sy") == 0
+def relayout_kernel(cube, here_a, here_b):
+    even = is_even()
     flat = [cube[:, x].reshape(C, CY * CZ) for x in range(CX)]
-    rows = [[flat[x][:, y * CZ : (y + 1) * CZ] for y in range(CY)] for x in range(CX)]
     for y in range(CY):
-        here_a[y] = jnp.where(even, rows[1][y], rows[0][y])
-        here_b[y] = jnp.where(even, rows[0][y], rows[1][y])
-    border = [jnp.where(first_core, rows[x][CY - 1], rows[x][0]) for x in range(CX)]
-    for x in range(CX):
-        edges[x] = border[x]
-    edge_a[0] = jnp.where(even, border[1], border[0])
-    edge_b[0] = jnp.where(even, border[0], border[1])
+        low, high = (flat[x][:, y * CZ : (y + 1) * CZ] for x in range(CX))
+        here_a[y] = jnp.where(even, high, low)
+        here_b[y] = jnp.where(even, low, high)
+
+
+def edge_kernel(here_a, here_b, from_a, from_b, edge):
+    first = lax.axis_index("sy") == 0
+    even = is_even()
+    border = [jnp.where(first, plane[CY - 1], plane[0]) for plane in (here_a, here_b, from_a, from_b)]
+    edge[0] = jnp.where(even, border[1], border[0])
+    edge[1] = jnp.where(even, border[0], border[1])
+    edge[2] = border[2]
+    edge[3] = border[3]
 
 
 def base_kernel(warm, error, base):
@@ -110,11 +114,11 @@
 
 
 def forward_kernel(
-    here_a, here_b, from_a, from_b, middle, corner_a, corner_b,
-    upstream, weights, warm, bias, base,
+    here_a, here_b, from_a, from_b, middle, upstream,
+    weights, warm, bias, base,
     act, grad_a, grad_b, edges, sums, planes,
 ):
-    across = rows_across(middle, corner_a[0], corner_b[0])
+    across = rows_across(middle, middle[2], middle[3])
     fill_planes(planes, here_a, here_b, from_a, from_b, across)
     first_core = lax.axis_index("sy") == 0
     even = is_even()
@@ -160,16 +164,16 @@
 
 
 def gradient_kernel(wait, block, upper_out, lower_out, planes, upper, lower, sem):
-    here_a, here_b, from_a, from_b, middle, corner_a, corner_b, grad_a, grad_b, error = block
-    wait(0, 1, 2, 3, 4, 5, 6)
-    across = rows_across(middle, corner_a[0], corner_b[0])
+    here_a, here_b, from_a, from_b, middle, grad_a, grad_b, error = block
+    wait(0, 1, 2, 3, 4)
+    across = rows_across(middle, middle[2], middle[3])
     fill_planes(planes, here_a, here_b, from_a, from_b, across)
-    wait(7, 8)
+    wait(5, 6)
     even = is_even()
     side_a = jnp.concatenate([grad_a[y] for y in range(CY)], axis=1)
     side_b = jnp.concatenate([grad_b[y] for y in range(CY)], axis=1)
     grads = (jnp.where(even, side_b, side_a), jnp.where(even, side_a, side_b))
-    wait(9)
+    wait(7)
     leaving = []
     for pair in range(9):
         span = pl.ds(pair * GROUP, GROUP)
@@ -296,15 +300,6 @@
     return lax.ppermute(to_a, "sx", pairs_a), lax.ppermute(to_b, "sx", pairs_b)
 
 
-def exchange_corners(to_a, to_b):
-    cores = lax.axis_size("sy")
-    both = [
-        [(i * cores + c, j * cores + 1 - c) for i, j in pairs for c in range(cores)]
-        for pairs in pairs_of(lax.axis_size("sx"))
-    ]
-    return lax.ppermute(to_a, BLOCK, both[0]), lax.ppermute(to_b, BLOCK, both[1])
-
-
 tie = lax.optimization_barrier
 
 
@@ -386,19 +381,14 @@
     padded = -(-TAPS // columns) * columns
     planes = pltpu.VMEM((GROUP, PX * PY * CZ), BF16)
     error = error_state[0, 0, 0]
-    here_a, here_b, edges, edge_a, edge_b = call(
-        relayout_kernel,
-        "relayout",
-        4,
-        (bf16(CY, C, CZ), bf16(CY, C, CZ), bf16(CX, C, CZ), bf16(1, C, CZ), bf16(1, C, CZ)),
-        (features[0],),
+    here_a, here_b = call(
+        relayout_kernel, "relayout", 4, (bf16(CY, C, CZ), bf16(CY, C, CZ)), (features[0],)
     )
     from_a, from_b = exchange_x(here_a, here_b)
-    corner_a, corner_b = exchange_corners(edge_a, edge_b)
-    middle = swap_cores(edges)
     base = call(base_kernel, "base", 4, f32(RANK, C), (warm_factor, error))
     from_a, from_b, base = tie((from_a, from_b, base))
-    block = (here_a, here_b, from_a, from_b, middle, corner_a, corner_b)
+    edge = call(edge_kernel, "edge", 2, bf16(PX, C, CZ), (here_a, here_b, from_a, from_b))
+    block = (here_a, here_b, from_a, from_b, swap_cores(edge))
     act, grad_a, grad_b, edges, sums = call(
         forward_kernel,
         "forward",
@@ -429,7 +419,7 @@
     factor_p, bias_grad, blocks = fetch_and_call(
         functools.partial(project_kernel, devices=devices),
         "project",
-        60,
+        53,
         (f32(RANK, C), f32(1, C), f32(padded, RANK, C)),
         (upper, lower),
         near=(parts,),
@@ -459,7 +449,7 @@
     input_grad = fetch_and_call(
         backward_kernel,
         "backward",
-        60,
+        40,
         bf16(C, CX, CY, CZ),
         (near_a, near_b, g_from_a, g_from_b, middle, weights),
         [planes],

time: 109 us -> 104 us (0.954)
  starting transfers between devices: 54.5 us -> 49.9 us
  waiting for transfers between devices: 23.5 us -> 25.9 us
  local copies, waits for them, and re-layouts: 6.55 us -> 4.59 us
    ppermute x2 -> x0, starting transfers between devices: 5.45 us -> none  [the longest x1 4.79 us: exchange_corners(): lax.ppermute(to_a, BLOCK, both[0])]
    unnamed x44 -> x32, local copies, waits for them, and re-layouts: 6.55 us -> 4.59 us
    all_to_all x5, waiting for transfers between devices: 22.3 us -> 23.8 us  [swap(): return lax.all_to_all(x, axes, 0, 0, tiled=True)]
    pallas_call x8 -> x9, Pallas kernels: 7.38 us -> 7.36 us  [call(): pl.pallas_call(kernel, out_shape=shapes, in_specs=[VMEM] * len(args), out...]
  transfers between devices with their start and end apart: 13 -> 11, of which waited for: 6 -> 7; matrix products, arithmetic and copies ran while one was open for 0% -> 0% of each run, Pallas kernels for 13% -> 14%
where the time goes in v8:
time: 104 us; the launch traced here: 103 us
  starting transfers between devices  49.9 us (48%)
  waiting for transfers between devices  25.9 us (25%)
  Pallas kernels  21.7 us (21%)
  local copies, waits for them, and re-layouts  4.59 us (4%)
    all_to_all x5, starting transfers between devices, swap(): return lax.all_to_all(x, axes, 0, 0, tiled=True)  33.3 us
    all_to_all x5, waiting for transfers between devices, swap(): return lax.all_to_all(x, axes, 0, 0, tiled=True)  23.8 us
    pallas_call x4, Pallas kernels, fetch_and_call(): pl.pallas_call(body, out_shape=shapes, in_specs=[VMEM] * len(near) + [HBM...  14.3 us
    ppermute x2, starting transfers between devices, swap_cores(): return lax.ppermute(edge, 'sy', [(0, 1), (1, 0)])  9.08 us
    pallas_call x9, Pallas kernels, call(): pl.pallas_call(kernel, out_shape=shapes, in_specs=[VMEM] * len(args), out...  7.36 us
    ppermute x2, starting transfers between devices, exchange_x(): lax.ppermute(to_a, 'sx', pairs_a)  6.17 us
    unnamed x32, local copies, waits for them, and re-layouts  4.59 us
    ppermute x2, waiting for transfers between devices, swap_cores(): return lax.ppermute(edge, 'sy', [(0, 1), (1, 0)])  2.08 us
  transfers between devices with their start and end apart: 11, of which 7 were waited for; matrix products, arithmetic and copies ran while one was open for 0% of the time, Pallas kernels for 14%

profile of v8, /device:TPU:1, one launch (start us, length us, event | category | flops | bytes accessed | tf_op | source)
XLA Modules:
  0.0 103.0 jit_solution(10546699237088892502)
XLA Ops:
  0.6 0.0 copy-start.15
  0.6 0.0 copy-start.11
  0.7 0.9 copy-done.11
  1.6 0.0 copy-start.12
  1.6 0.2 relayout.1
  1.8 0.0 copy-start.2
  1.8 0.0 copy-start.3
  1.8 4.0 %collective-permute-start = (bf16[4,128,128]{2,1,0:T(8,128)(2,1)S(1)}, bf16[4,128,128]{2,1,0:T(8,128)(2,1)S(1)}, u32[]{:S(2)}, u32[]{:S(2)}) collective-permute-start(bf16[4,128,128]{2,1,0:T(8,128)(2,1)S(1)} %get-tuple-element.34.here_a.refs_0_), channel_id=1, source_target_pairs={{0,2},{2,0},{4,6},{6,4},{8,10},{10,8},{12,14},{14,12},{1,3},{3,1},... | collective-permute-start | bytes 393224 | tf_op jit(solution)/shard_map/ppermute | solution.py:300
  5.9 0.7 collective-permute-start.1
  6.6 0.0 copy-start
  6.6 1.5 %copy-done = f32[1,1,1,128,3456]{4,3,2,1,0:T(8,128)S(1)} copy-done((f32[1,1,1,128,3456]{4,3,2,1,0:T(8,128)S(1)}, f32[1,1,1,128,3456]{4,3,2,1,0:T(8,128)}, u32[]{:S(2)}) %copy-start) | copy-done | bytes 1769496
  8.0 0.0 copy-start.13
  8.0 0.8 copy-done.13
  8.8 0.0 copy-start.1
  8.8 0.0 copy-start.14
  8.9 1.5 %base.1 = f32[4,128]{1,0:T(4,128)S(1)} custom-call(f32[4,3456]{1,0:T(4,128)S(1)} %copy-done.13, f32[128,3456]{1,0:T(8,128)S(1)} %bitcast.11), custom_call_target="tpu_custom_call" | custom-call | tf_op jit(solution)/shard_map/base/pallas_call | solution.py:318
  10.4 0.0 collective-permute-done.from_a.refs_2_
  10.4 0.0 copy-start.4
  10.4 0.0 collective-permute-done.1.from_b.refs_3_
  10.4 0.0 copy-start.5
  10.5 7.1 %collective-permute-start.2 = (bf16[4,128,128]{2,1,0:T(8,128)(2,1)S(1)}, bf16[4,128,128]{2,1,0:T(8,128)(2,1)S(1)}, u32[]{:S(2)}, u32[]{:S(2)}) collective-permute-start(bf16[4,128,128]{2,1,0:T(8,128)(2,1)S(1)} %edge.1), channel_id=1, source_target_pairs={{0,1},{1,0},{2,3},{3,2},{4,5},{5,4},{6,7},{7,6},{8,9},{9,8},{10,11... | collective-permute-start | bytes 393224 | tf_op jit(solution)/shard_map/ppermute | solution.py:289
  17.5 1.0 collective-permute-done.2.middle.refs_4_
  18.5 0.0 copy-start.10
  18.5 0.0 copy-done.15
  18.5 0.0 copy-done.12
  18.5 0.0 copy-done.1
  18.5 0.0 copy-done.14
  18.5 2.9 %forward.1 = (bf16[128,2,4,128]{3,2,1,0:T(4,128)(2,1)}, bf16[4,128,128]{2,1,0:T(8,128)(2,1)S(1)}, bf16[4,128,128]{2,1,0:T(8,128)(2,1)S(1)}, bf16[2,128,128]{2,1,0:T(8,128)(2,1)S(1)}, f32[32,8,128]{2,1,0:T(8,128)}) custom-call(bf16[4,128,128]{2,1,0:T(8,128)(2,1)S(1)} %get-tuple-element.34.here_a.refs_0_, ...), custom_call_target="tpu_custom_call" | custom-call | tf_op jit(solution)/shard_map/forward/pallas_call | solution.py:318
  21.4 0.0 copy-done.2
  21.4 0.0 copy-done.3
  21.4 0.7 copy-done.6
  22.1 0.0 copy-start.8
  22.1 0.7 copy-done.8
  22.8 8.7 %all-to-all-start = ((f32[32,8,128]{2,1,0:T(8,128)}), f32[32,8,128]{2,1,0:T(8,128)S(1)}, u32[]{:S(2)}, u32[]{:S(2)}) async-start(f32[32,8,128]{2,1,0:T(8,128)} %get-tuple-element.40), calls=%async_computation | async-start | bytes 262144 | tf_op jit(solution)/shard_map/all_to_all | solution.py:314
  31.4 0.0 copy-done.4
  31.5 0.0 copy-done.5
  31.5 0.0 copy-done.10
  31.5 5.0 %gradient.1 = (bf16[128,3456]{1,0:T(8,128)(2,1)}, bf16[128,3456]{1,0:T(8,128)(2,1)}) custom-call(bf16[4,128,128]{2,1,0:T(8,128)(2,1)} %copy-done.2, bf16[4,128,128]{2,1,0:T(8,128)(2,1)} %copy-done.3, bf16[4,128,128]{2,1,0:T(8,128)(2,1)} %copy-done.4, bf16[4,128,128]{2,1,0:T(8,128)(2,1)} %copy-done.5, bf16[4,128,128]{2,1,0:T(8,128)(2,1)} %copy-done.10, ...), custom_call_target="tpu_custom_call" | custom-call | tf_op jit(solution)/shard_map/gradient/pallas_call | solution.py:350
  36.5 4.1 %all-to-all-done.parts = f32[32,8,128]{2,1,0:T(8,128)S(1)} async-done(((f32[32,8,128]{2,1,0:T(8,128)}), f32[32,8,128]{2,1,0:T(8,128)S(1)}, u32[]{:S(2)}, u32[]{:S(2)}) %all-to-all-start) | async-done | bytes 131104 | tf_op jit(solution)/shard_map/all_to_all | solution.py:314
  40.6 0.7 fold.3
  41.3 11.8 %all-to-all-start.1 = ((f32[16,8,128]{2,1,0:T(8,128)}), f32[16,8,128]{2,1,0:T(8,128)S(1)}, u32[]{:S(2)}, u32[]{:S(2)}) async-start(f32[16,8,128]{2,1,0:T(8,128)} %fold.3), calls=%async_computation.1 | async-start | bytes 131072 | tf_op jit(solution)/shard_map/all_to_all | solution.py:314
  53.1 2.0 %collective-permute-start.3 = (bf16[2,128,128]{2,1,0:T(8,128)(2,1)S(1)}, bf16[2,128,128]{2,1,0:T(8,128)(2,1)S(1)}, u32[]{:S(2)}, u32[]{:S(2)}) collective-permute-start(bf16[2,128,128]{2,1,0:T(8,128)(2,1)S(1)} %get-tuple-element.47), channel_id=1, source_target_pairs={{0,1},{1,0},{2,3},{3,2},{4,5},{5,4},{6,7},{7,6},{8,9},{9,8},{10,11... | collective-permute-start | bytes 196616 | tf_op jit(solution)/shard_map/ppermute | solution.py:289
  55.1 1.1 %collective-permute-done.3.middle.refs_4_ = bf16[2,128,128]{2,1,0:T(8,128)(2,1)S(1)} collective-permute-done((bf16[2,128,128]{2,1,0:T(8,128)(2,1)S(1)}, bf16[2,128,128]{2,1,0:T(8,128)(2,1)S(1)}, u32[]{:S(2)}, u32[]{:S(2)}) %collective-permute-start.3) | collective-permute-done | bytes 65568 | tf_op jit(solution)/shard_map/ppermute | solution.py:289
  56.2 4.7 %all-to-all-done.1.refs_0_ = f32[16,8,128]{2,1,0:T(8,128)S(1)} async-done(((f32[16,8,128]{2,1,0:T(8,128)}), f32[16,8,128]{2,1,0:T(8,128)S(1)}, u32[]{:S(2)}, u32[]{:S(2)}) %all-to-all-start.1) | async-done | bytes 65568 | tf_op jit(solution)/shard_map/all_to_all | solution.py:314
  60.9 2.4 %project.1 = (f32[4,128]{1,0:T(4,128)}, f32[1,128]{1,0:T(1,128)}, f32[32,4,128]{2,1,0:T(4,128)}) custom-call(f32[16,8,128]{2,1,0:T(8,128)S(1)} %all-to-all-done.1.refs_0_, bf16[128,3456]{1,0:T(8,128)(2,1)} %get-tuple-element.49.refs_1_.refs_2_, bf16[128,3456]{1,0:T(8,128)(2,1)} %get-tuple-element.50.refs_2_.refs_3_), custom_call_target="tpu_custom_call" | custom-call | tf_op jit(solution)/shard_map/project/pallas_call | solution.py:350
  63.4 3.5 %all-to-all-start.2 = ((f32[32,4,128]{2,1,0:T(4,128)}), f32[32,4,128]{2,1,0:T(4,128)S(1)}, u32[]{:S(2)}, u32[]{:S(2)}) async-start(f32[32,4,128]{2,1,0:T(4,128)} %get-tuple-element.51.refs_1_), calls=%async_computation.2 | async-start | bytes 131072 | tf_op jit(solution)/shard_map/all_to_all | solution.py:314
  66.8 0.0 copy-start.7
  66.8 0.0 copy-start.9
  66.8 3.0 %residual.1 = f32[128,3456]{1,0:T(8,128)} custom-call(f32[4,128]{1,0:T(4,128)} %get-tuple-element.31.refs_0_, f32[32,4,128]{2,1,0:T(4,128)} %get-tuple-element.51.refs_1_, bf16[128,3456]{1,0:T(8,128)(2,1)} %get-tuple-element.49.refs_1_.refs_2_, bf16[128,3456]{1,0:T(8,128)(2,1)} %get-tuple-element.50.refs_2_.refs_3_), custom_call_target="tpu_custom_call" | custom-call | tf_op jit(solution)/shard_map/residual/pallas_call | solution.py:350
  69.9 4.8 %all-to-all-done.2 = f32[32,4,128]{2,1,0:T(4,128)S(1)} async-done(((f32[32,4,128]{2,1,0:T(4,128)}), f32[32,4,128]{2,1,0:T(4,128)S(1)}, u32[]{:S(2)}, u32[]{:S(2)}) %all-to-all-start.2) | async-done | bytes 65568 | tf_op jit(solution)/shard_map/all_to_all | solution.py:314
  74.7 0.7 fold.4
  75.3 4.0 %all-to-all-start.3 = ((f32[32,8,128]{2,1,0:T(8,128)}), f32[32,8,128]{2,1,0:T(8,128)S(1)}, u32[]{:S(2)}, u32[]{:S(2)}) async-start(f32[32,8,128]{2,1,0:T(8,128)} %fold.4), calls=%async_computation.3 | async-start | bytes 262144 | tf_op jit(solution)/shard_map/all_to_all | solution.py:314
  79.3 0.0 copy-done.7
  79.3 0.0 copy-done.9
  79.4 2.1 %collective-permute-start.4 = (bf16[5,128,128]{2,1,0:T(8,128)(2,1)S(1)}, bf16[5,128,128]{2,1,0:T(8,128)(2,1)S(1)}, u32[]{:S(2)}, u32[]{:S(2)}) collective-permute-start(bf16[5,128,128]{2,1,0:T(8,128)(2,1)S(1)} %get-tuple-element.57), channel_id=1, source_target_pairs={{0,2},{2,0},{4,6},{6,4},{8,10},{10,8},{12,14},{14,12},{1,3},{3,1},... | collective-permute-start | bytes 491528 | tf_op jit(solution)/shard_map/ppermute | solution.py:300
  81.5 0.7 collective-permute-start.5
  82.2 6.3 %all-to-all-done.3.parts = f32[32,8,128]{2,1,0:T(8,128)S(1)} async-done(((f32[32,8,128]{2,1,0:T(8,128)}), f32[32,8,128]{2,1,0:T(8,128)S(1)}, u32[]{:S(2)}, u32[]{:S(2)}) %all-to-all-start.3) | async-done | bytes 131104 | tf_op jit(solution)/shard_map/all_to_all | solution.py:314
  88.5 0.7 fold.5
  89.1 5.4 %all-to-all-start.4 = ((f32[16,8,128]{2,1,0:T(8,128)}), f32[16,8,128]{2,1,0:T(8,128)S(1)}, u32[]{:S(2)}, u32[]{:S(2)}) async-start(f32[16,8,128]{2,1,0:T(8,128)} %fold.5), calls=%async_computation.4 | async-start | bytes 131072 | tf_op jit(solution)/shard_map/all_to_all | solution.py:314
  94.5 0.0 collective-permute-done.4.refs_2_
  94.5 0.0 collective-permute-done.5.refs_3_
  94.5 3.8 %backward.1 = bf16[128,2,4,128]{3,2,1,0:T(4,128)(2,1)} custom-call(bf16[4,128,128]{2,1,0:T(8,128)(2,1)S(1)} %copy-done.7, bf16[4,128,128]{2,1,0:T(8,128)(2,1)S(1)} %copy-done.9, bf16[5,128,128]{2,1,0:T(8,128)(2,1)S(1)} %collective-permute-done.4.refs_2_, bf16[5,128,128]{2,1,0:T(8,128)(2,1)S(1)} %collective-permute-done.5.refs_3_, ...), custom_call_target="tpu_custom_call" | custom-call | tf_op jit(solution)/shard_map/backward/pallas_call | solution.py:350
  98.4 4.0 %all-to-all-done.4 = f32[16,8,128]{2,1,0:T(8,128)S(1)} async-done(((f32[16,8,128]{2,1,0:T(8,128)}), f32[16,8,128]{2,1,0:T(8,128)S(1)}, u32[]{:S(2)}, u32[]{:S(2)}) %all-to-all-start.4) | async-done | bytes 65568 | tf_op jit(solution)/shard_map/all_to_all | solution.py:314
  102.3 0.6 finish.1
  (3 shorter events, 0.1 us)
Async XLA Ops:
  0.6 17.9 %copy-start.15 = (f32[128]{0:T(128)S(1)}, f32[128]{0:T(128)}, u32[]{:S(2)}) copy-start(f32[128]{0:T(128)} %param.9) | copy-start | bytes 1540
  0.6 1.0 copy-start.11
  1.6 16.9 %copy-start.12 = (bf16[1,128,2,4,128]{4,3,2,1,0:T(4,128)(2,1)S(1)}, bf16[1,128,2,4,128]{4,3,2,1,0:T(4,128)(2,1)}, u32[]{:S(2)}) copy-start(bf16[1,128,2,4,128]{4,3,2,1,0:T(4,128)(2,1)} %param.7) | copy-start | bytes 786436
  1.8 19.6 %copy-start.2 = (bf16[4,128,128]{2,1,0:T(8,128)(2,1)}, bf16[4,128,128]{2,1,0:T(8,128)(2,1)S(1)}, u32[]{:S(2)}) copy-start(bf16[4,128,128]{2,1,0:T(8,128)(2,1)S(1)} %get-tuple-element.34.here_a.refs_0_) | copy-start | bytes 393220
  1.8 19.6 %copy-start.3 = (bf16[4,128,128]{2,1,0:T(8,128)(2,1)}, bf16[4,128,128]{2,1,0:T(8,128)(2,1)S(1)}, u32[]{:S(2)}) copy-start(bf16[4,128,128]{2,1,0:T(8,128)(2,1)S(1)} %get-tuple-element.35.here_b.refs_1_) | copy-start | bytes 393220
  1.8 8.5 %collective-permute-start = (bf16[4,128,128]{2,1,0:T(8,128)(2,1)S(1)}, bf16[4,128,128]{2,1,0:T(8,128)(2,1)S(1)}, u32[]{:S(2)}, u32[]{:S(2)}) collective-permute-start(bf16[4,128,128]{2,1,0:T(8,128)(2,1)S(1)} %get-tuple-element.34.here_a.refs_0_), channel_id=1, source_target_pairs={{0,2},{2,0},{4,6},{6,4},{8,10},{10,8},{12,14},{14,12},{1,3},{3,1},... | collective-permute-start | bytes 393224 | tf_op jit(solution)/shard_map/ppermute | solution.py:300
  5.9 4.5 %collective-permute-start.1 = (bf16[4,128,128]{2,1,0:T(8,128)(2,1)S(1)}, bf16[4,128,128]{2,1,0:T(8,128)(2,1)S(1)}, u32[]{:S(2)}, u32[]{:S(2)}) collective-permute-start(bf16[4,128,128]{2,1,0:T(8,128)(2,1)S(1)} %get-tuple-element.35.here_b.refs_1_), channel_id=1, source_target_pairs={{2,4},{4,2},{6,8},{8,6},{10,12},{12,10},{3,5},{5,3},{7,9},{9,7},{1... | collective-permute-start | bytes 393224 | tf_op jit(solution)/shard_map/ppermute | solution.py:300
  6.6 1.5 %copy-start = (f32[1,1,1,128,3456]{4,3,2,1,0:T(8,128)S(1)}, f32[1,1,1,128,3456]{4,3,2,1,0:T(8,128)}, u32[]{:S(2)}) copy-start(f32[1,1,1,128,3456]{4,3,2,1,0:T(8,128)} %param.10) | copy-start | bytes 5308420
  8.0 0.8 copy-start.13
  8.8 9.7 %copy-start.1 = (bf16[27,128,128]{2,1,0:T(8,128)(2,1)S(1)}, bf16[27,128,128]{2,1,0:T(8,128)(2,1)}, u32[]{:S(2)}) copy-start(bf16[27,128,128]{2,1,0:T(8,128)(2,1)} %refs_5_.1) | copy-start | bytes 2654212
  8.8 9.7 %copy-start.14 = (f32[4,3456]{1,0:T(4,128)S(1)}, f32[4,3456]{1,0:T(4,128)}, u32[]{:S(2)}) copy-start(f32[4,3456]{1,0:T(4,128)} %warm.3) | copy-start | bytes 165892
  10.4 21.1 %copy-start.4 = (bf16[4,128,128]{2,1,0:T(8,128)(2,1)}, bf16[4,128,128]{2,1,0:T(8,128)(2,1)S(1)}, u32[]{:S(2)}) copy-start(bf16[4,128,128]{2,1,0:T(8,128)(2,1)S(1)} %collective-permute-done.from_a.refs_2_) | copy-start | bytes 393220
  10.4 21.0 %copy-start.5 = (bf16[4,128,128]{2,1,0:T(8,128)(2,1)}, bf16[4,128,128]{2,1,0:T(8,128)(2,1)S(1)}, u32[]{:S(2)}) copy-start(bf16[4,128,128]{2,1,0:T(8,128)(2,1)S(1)} %collective-permute-done.1.from_b.refs_3_) | copy-start | bytes 393220
  10.5 8.0 %collective-permute-start.2 = (bf16[4,128,128]{2,1,0:T(8,128)(2,1)S(1)}, bf16[4,128,128]{2,1,0:T(8,128)(2,1)S(1)}, u32[]{:S(2)}, u32[]{:S(2)}) collective-permute-start(bf16[4,128,128]{2,1,0:T(8,128)(2,1)S(1)} %edge.1), channel_id=1, source_target_pairs={{0,1},{1,0},{2,3},{3,2},{4,5},{5,4},{6,7},{7,6},{8,9},{9,8},{10,11... | collective-permute-start | bytes 393224 | tf_op jit(solution)/shard_map/ppermute | solution.py:289
  18.5 13.0 %copy-start.10 = (bf16[4,128,128]{2,1,0:T(8,128)(2,1)}, bf16[4,128,128]{2,1,0:T(8,128)(2,1)S(1)}, u32[]{:S(2)}) copy-start(bf16[4,128,128]{2,1,0:T(8,128)(2,1)S(1)} %collective-permute-done.2.middle.refs_4_) | copy-start | bytes 393220
  21.4 0.7 copy-start.6
  22.1 0.7 copy-start.8
  22.8 17.8 %all-to-all-start = ((f32[32,8,128]{2,1,0:T(8,128)}), f32[32,8,128]{2,1,0:T(8,128)S(1)}, u32[]{:S(2)}, u32[]{:S(2)}) async-start(f32[32,8,128]{2,1,0:T(8,128)} %get-tuple-element.40), calls=%async_computation | async-start | bytes 262144 | tf_op jit(solution)/shard_map/all_to_all | solution.py:314
  41.3 19.6 %all-to-all-start.1 = ((f32[16,8,128]{2,1,0:T(8,128)}), f32[16,8,128]{2,1,0:T(8,128)S(1)}, u32[]{:S(2)}, u32[]{:S(2)}) async-start(f32[16,8,128]{2,1,0:T(8,128)} %fold.3), calls=%async_computation.1 | async-start | bytes 131072 | tf_op jit(solution)/shard_map/all_to_all | solution.py:314
  53.1 3.1 %collective-permute-start.3 = (bf16[2,128,128]{2,1,0:T(8,128)(2,1)S(1)}, bf16[2,128,128]{2,1,0:T(8,128)(2,1)S(1)}, u32[]{:S(2)}, u32[]{:S(2)}) collective-permute-start(bf16[2,128,128]{2,1,0:T(8,128)(2,1)S(1)} %get-tuple-element.47), channel_id=1, source_target_pairs={{0,1},{1,0},{2,3},{3,2},{4,5},{5,4},{6,7},{7,6},{8,9},{9,8},{10,11... | collective-permute-start | bytes 196616 | tf_op jit(solution)/shard_map/ppermute | solution.py:289
  63.4 11.3 %all-to-all-start.2 = ((f32[32,4,128]{2,1,0:T(4,128)}), f32[32,4,128]{2,1,0:T(4,128)S(1)}, u32[]{:S(2)}, u32[]{:S(2)}) async-start(f32[32,4,128]{2,1,0:T(4,128)} %get-tuple-element.51.refs_1_), calls=%async_computation.2 | async-start | bytes 131072 | tf_op jit(solution)/shard_map/all_to_all | solution.py:314
  66.8 12.5 %copy-start.7 = (bf16[4,128,128]{2,1,0:T(8,128)(2,1)S(1)}, bf16[4,128,128]{2,1,0:T(8,128)(2,1)}, u32[]{:S(2)}) copy-start(bf16[4,128,128]{2,1,0:T(8,128)(2,1)} %copy-done.6) | copy-start | bytes 393220
  66.8 12.5 %copy-start.9 = (bf16[4,128,128]{2,1,0:T(8,128)(2,1)S(1)}, bf16[4,128,128]{2,1,0:T(8,128)(2,1)}, u32[]{:S(2)}) copy-start(bf16[4,128,128]{2,1,0:T(8,128)(2,1)} %copy-done.8) | copy-start | bytes 393220
  75.3 13.1 %all-to-all-start.3 = ((f32[32,8,128]{2,1,0:T(8,128)}), f32[32,8,128]{2,1,0:T(8,128)S(1)}, u32[]{:S(2)}, u32[]{:S(2)}) async-start(f32[32,8,128]{2,1,0:T(8,128)} %fold.4), calls=%async_computation.3 | async-start | bytes 262144 | tf_op jit(solution)/shard_map/all_to_all | solution.py:314
  79.4 15.1 %collective-permute-start.4 = (bf16[5,128,128]{2,1,0:T(8,128)(2,1)S(1)}, bf16[5,128,128]{2,1,0:T(8,128)(2,1)S(1)}, u32[]{:S(2)}, u32[]{:S(2)}) collective-permute-start(bf16[5,128,128]{2,1,0:T(8,128)(2,1)S(1)} %get-tuple-element.57), channel_id=1, source_target_pairs={{0,2},{2,0},{4,6},{6,4},{8,10},{10,8},{12,14},{14,12},{1,3},{3,1},... | collective-permute-start | bytes 491528 | tf_op jit(solution)/shard_map/ppermute | solution.py:300
  81.5 13.0 %collective-permute-start.5 = (bf16[5,128,128]{2,1,0:T(8,128)(2,1)S(1)}, bf16[5,128,128]{2,1,0:T(8,128)(2,1)S(1)}, u32[]{:S(2)}, u32[]{:S(2)}) collective-permute-start(bf16[5,128,128]{2,1,0:T(8,128)(2,1)S(1)} %get-tuple-element.58), channel_id=1, source_target_pairs={{2,4},{4,2},{6,8},{8,6},{10,12},{12,10},{3,5},{5,3},{7,9},{9,7},{1... | collective-permute-start | bytes 491528 | tf_op jit(solution)/shard_map/ppermute | solution.py:300
  89.1 13.2 %all-to-all-start.4 = ((f32[16,8,128]{2,1,0:T(8,128)}), f32[16,8,128]{2,1,0:T(8,128)S(1)}, u32[]{:S(2)}, u32[]{:S(2)}) async-start(f32[16,8,128]{2,1,0:T(8,128)} %fold.5), calls=%async_computation.4 | async-start | bytes 131072 | tf_op jit(solution)/shard_map/all_to_all | solution.py:314

commit v9 on v8

--- a/solution.py
+++ b/solution.py
@@ -116,11 +116,10 @@
 def forward_kernel(
     here_a, here_b, from_a, from_b, middle, upstream,
     weights, warm, bias, base,
-    act, grad_a, grad_b, edges, sums, planes,
+    act, grad_a, grad_b, sums, planes,
 ):
     across = rows_across(middle, middle[2], middle[3])
     fill_planes(planes, here_a, here_b, from_a, from_b, across)
-    first_core = lax.axis_index("sy") == 0
     even = is_even()
     offset = jnp.transpose(jnp.broadcast_to(bias[...], (C, C)))[:, :1]
     rows = warm[...]
@@ -147,7 +146,6 @@
         gradient = (above * slope).astype(BF16)
         grads = [gradient[:, y * CZ : (y + 1) * CZ] for y in range(CY)]
         cube.append(grads)
-        edges[x] = jnp.where(first_core, grads[CY - 1], grads[0])
         field = total[C : C + RANK] + total[C + RANK : C + 2 * RANK]
         field = field + total[C + 2 * RANK : C + 3 * RANK]
         stacked = jnp.concatenate([*pieces(field), jnp.ones_like(field)], axis=0)
@@ -260,7 +258,7 @@
 def backward_kernel(wait, held, out, planes):
     here_a, here_b, from_a, from_b, middle, weights = held
     wait(0, 1, 2, 3, 4)
-    across = rows_across(middle, from_a[CY], from_b[CY])
+    across = rows_across(middle, middle[2], middle[3])
     fill_planes(planes, here_a, here_b, from_a, from_b, across)
     wait(5)
     totals = [None] * CX
@@ -276,15 +274,6 @@
         out[:, x] = totals[x].astype(BF16).reshape(C, CY, CZ)
 
 
-def pack_kernel(here_a, here_b, middle, to_a, to_b):
-    even = is_even()
-    for y in range(CY):
-        to_a[y] = here_a[y]
-        to_b[y] = here_b[y]
-    to_a[CY] = jnp.where(even, middle[1], middle[0])
-    to_b[CY] = jnp.where(even, middle[0], middle[1])
-
-
 def swap_cores(edge):
     return lax.ppermute(edge, "sy", [(0, 1), (1, 0)])
 
@@ -389,7 +378,7 @@
     from_a, from_b, base = tie((from_a, from_b, base))
     edge = call(edge_kernel, "edge", 2, bf16(PX, C, CZ), (here_a, here_b, from_a, from_b))
     block = (here_a, here_b, from_a, from_b, swap_cores(edge))
-    act, grad_a, grad_b, edges, sums = call(
+    act, grad_a, grad_b, sums = call(
         forward_kernel,
         "forward",
         12,
@@ -397,7 +386,6 @@
             bf16(C, CX, CY, CZ),
             bf16(CY, C, CZ),
             bf16(CY, C, CZ),
-            bf16(CX, C, CZ),
             f32(chips, 2 * RANK, C),
         ),
         (*block, cotangent[0], weights, warm_factor, conv_bias[None], base),
@@ -413,9 +401,9 @@
         [planes, pltpu.VMEM((C, K), BF16), pltpu.VMEM((C, K), BF16), pltpu.SemaphoreType.DMA((18,))],
         HBM,
     )
-    parts, upper, lower, edges = tie((parts, upper, lower, edges))
+    parts, upper, lower, near_a, near_b = tie((parts, upper, lower, grad_a, grad_b))
     parts = swap(fold(parts, columns), BLOCK)
-    parts, middle = tie((parts, swap_cores(edges)))
+    g_from_a, g_from_b = exchange_x(near_a, near_b)
     factor_p, bias_grad, blocks = fetch_and_call(
         functools.partial(project_kernel, devices=devices),
         "project",
@@ -435,23 +423,18 @@
     )
     width = padded // columns * RANK
     mine = swap(blocks, BLOCK)
-    mine, new_error, middle, near_a, near_b = tie((mine, new_error, middle, grad_a, grad_b))
+    mine, new_error, g_from_a, g_from_b = tie((mine, new_error, g_from_a, g_from_b))
     mine = swap(fold(mine.reshape(columns, width, C), chips), DP)
-    to_a, to_b = call(
-        pack_kernel,
-        "pack",
-        4,
-        (bf16(CY + 1, C, CZ), bf16(CY + 1, C, CZ)),
-        (near_a, near_b, middle),
-    )
-    g_from_a, g_from_b = exchange_x(to_a, to_b)
+    planes_here = (near_a, near_b, g_from_a, g_from_b)
+    middle = swap_cores(call(edge_kernel, "edge", 2, bf16(PX, C, CZ), planes_here))
+    mine, middle = tie((mine, middle))
     blocks = swap(fold(mine, columns), BLOCK).reshape(padded, RANK, C)
     input_grad = fetch_and_call(
         backward_kernel,
         "backward",
         40,
         bf16(C, CX, CY, CZ),
-        (near_a, near_b, g_from_a, g_from_b, middle, weights),
+        (*planes_here, middle, weights),
         [planes],
     )
     factor_q = call(

time: 104 us -> 105 us (level)
  starting transfers between devices: 49.9 us -> 52.5 us
  waiting for transfers between devices: 25.9 us -> 24.4 us
    all_to_all x5, waiting for transfers between devices: 23.8 us -> 22.5 us  [swap(): return lax.all_to_all(x, axes, 0, 0, tiled=True)]
    ppermute x2, starting transfers between devices: 6.17 us -> 7.33 us  [exchange_x(): lax.ppermute(to_a, 'sx', pairs_a)]
    all_to_all x5, starting transfers between devices: 33.3 us -> 34.4 us  [swap(): return lax.all_to_all(x, axes, 0, 0, tiled=True)]
  transfers between devices with their start and end apart: 11 -> 11, of which waited for: 7 -> 7; matrix products, arithmetic and copies ran while one was open for 0% -> 0% of each run, Pallas kernels for 14% -> 15%
where the time goes in v9:
time: 105 us; the launch traced here: 104 us
  starting transfers between devices  52.5 us (50%)
  waiting for transfers between devices  24.4 us (23%)
  Pallas kernels  21.6 us (21%)
  local copies, waits for them, and re-layouts  4.57 us (4%)
    all_to_all x5, starting transfers between devices, swap(): return lax.all_to_all(x, axes, 0, 0, tiled=True)  34.4 us
    all_to_all x5, waiting for transfers between devices, swap(): return lax.all_to_all(x, axes, 0, 0, tiled=True)  22.5 us
    pallas_call x4, Pallas kernels, fetch_and_call(): pl.pallas_call(body, out_shape=shapes, in_specs=[VMEM] * len(near) + [HBM...  14.3 us
    ppermute x2, starting transfers between devices, swap_cores(): return lax.ppermute(edge, 'sy', [(0, 1), (1, 0)])  9.42 us
    pallas_call x9, Pallas kernels, call(): pl.pallas_call(kernel, out_shape=shapes, in_specs=[VMEM] * len(args), out...  7.35 us
    ppermute x2, starting transfers between devices, exchange_x(): lax.ppermute(to_a, 'sx', pairs_a)  7.33 us
    unnamed x32, local copies, waits for them, and re-layouts  4.57 us
  transfers between devices with their start and end apart: 11, of which 7 were waited for; matrix products, arithmetic and copies ran while one was open for 0% of the time, Pallas kernels for 15%

profile of v9, /device:TPU:1, one launch (start us, length us, event | category | flops | bytes accessed | tf_op | source)
XLA Modules:
  0.0 104.0 jit_solution(16372377492766578500)
XLA Ops:
  0.6 0.0 copy-start.15
  0.6 0.0 copy-start.11
  0.7 0.9 copy-done.11
  1.6 0.2 relayout.1
  1.8 0.0 copy-start.6
  1.8 0.0 copy-start.7
  1.8 4.0 %collective-permute-start = (bf16[4,128,128]{2,1,0:T(8,128)(2,1)S(1)}, bf16[4,128,128]{2,1,0:T(8,128)(2,1)S(1)}, u32[]{:S(2)}, u32[]{:S(2)}) collective-permute-start(bf16[4,128,128]{2,1,0:T(8,128)(2,1)S(1)} %get-tuple-element.31.here_a.refs_0_), channel_id=1, source_target_pairs={{0,2},{2,0},{4,6},{6,4},{8,10},{10,8},{12,14},{14,12},{1,3},{3,1},... | collective-permute-start | bytes 393224 | tf_op jit(solution)/shard_map/ppermute | solution.py:289
  5.9 0.7 collective-permute-start.1
  6.6 0.0 copy-start
  6.6 1.5 %copy-done = f32[1,1,1,128,3456]{4,3,2,1,0:T(8,128)S(1)} copy-done((f32[1,1,1,128,3456]{4,3,2,1,0:T(8,128)S(1)}, f32[1,1,1,128,3456]{4,3,2,1,0:T(8,128)}, u32[]{:S(2)}) %copy-start) | copy-done | bytes 1769496
  8.0 0.0 copy-start.13
  8.0 0.8 copy-done.13
  8.8 0.0 copy-start.1
  8.8 0.0 copy-start.14
  8.8 1.5 %base.1 = f32[4,128]{1,0:T(4,128)S(1)} custom-call(f32[4,3456]{1,0:T(4,128)S(1)} %copy-done.13, f32[128,3456]{1,0:T(8,128)S(1)} %bitcast.11), custom_call_target="tpu_custom_call" | custom-call | tf_op jit(solution)/shard_map/base/pallas_call | solution.py:307
  10.4 0.0 collective-permute-done.from_a.refs_2_
  10.4 0.0 copy-start.8
  10.4 0.0 collective-permute-done.1.from_b.refs_3_
  10.4 0.0 copy-start.9
  10.5 7.1 %collective-permute-start.2 = (bf16[4,128,128]{2,1,0:T(8,128)(2,1)S(1)}, bf16[4,128,128]{2,1,0:T(8,128)(2,1)S(1)}, u32[]{:S(2)}, u32[]{:S(2)}) collective-permute-start(bf16[4,128,128]{2,1,0:T(8,128)(2,1)S(1)} %edge.2), channel_id=1, source_target_pairs={{0,1},{1,0},{2,3},{3,2},{4,5},{5,4},{6,7},{7,6},{8,9},{9,8},{10,11... | collective-permute-start | bytes 393224 | tf_op jit(solution)/shard_map/ppermute | solution.py:278
  17.5 1.0 collective-permute-done.2.middle.refs_4_
  18.5 0.0 copy-start.10
  18.5 0.0 copy-done.15
  18.5 0.0 copy-done.12
  18.5 0.0 copy-done.1
  18.5 0.0 copy-done.14
  18.5 2.9 %forward.1 = (bf16[128,2,4,128]{3,2,1,0:T(4,128)(2,1)}, bf16[4,128,128]{2,1,0:T(8,128)(2,1)S(1)}, bf16[4,128,128]{2,1,0:T(8,128)(2,1)S(1)}, f32[32,8,128]{2,1,0:T(8,128)}) custom-call(bf16[4,128,128]{2,1,0:T(8,128)(2,1)S(1)} %get-tuple-element.31.here_a.refs_0_, bf16[4,128,128]{2,1,0:T(8,128)(2,1)S(1)} %get-tuple-element.32.here_b.refs_1_, ...), custom_call_target="tpu_custom_call" | custom-call | tf_op jit(solution)/shard_map/forward/pallas_call | solution.py:307
  21.4 0.0 copy-done.6
  21.4 0.0 copy-done.7
  21.4 0.0 copy-start.2
  21.4 0.7 copy-done.2
  22.1 0.0 copy-start.4
  22.1 0.6 copy-done.4
  22.7 0.0 copy-start.3
  22.7 0.0 copy-start.5
  22.7 8.8 %all-to-all-start = ((f32[32,8,128]{2,1,0:T(8,128)}), f32[32,8,128]{2,1,0:T(8,128)S(1)}, u32[]{:S(2)}, u32[]{:S(2)}) async-start(f32[32,8,128]{2,1,0:T(8,128)} %get-tuple-element.37), calls=%async_computation | async-start | bytes 262144 | tf_op jit(solution)/shard_map/all_to_all | solution.py:303
  31.6 0.0 copy-done.8
  31.6 0.0 copy-done.9
  31.6 0.0 copy-done.10
  31.6 5.0 %gradient.1 = (bf16[128,3456]{1,0:T(8,128)(2,1)}, bf16[128,3456]{1,0:T(8,128)(2,1)}) custom-call(bf16[4,128,128]{2,1,0:T(8,128)(2,1)} %copy-done.6, bf16[4,128,128]{2,1,0:T(8,128)(2,1)} %copy-done.7, bf16[4,128,128]{2,1,0:T(8,128)(2,1)} %copy-done.8, bf16[4,128,128]{2,1,0:T(8,128)(2,1)} %copy-done.9, bf16[4,128,128]{2,1,0:T(8,128)(2,1)} %copy-done.10, ...), custom_call_target="tpu_custom_call" | custom-call | tf_op jit(solution)/shard_map/gradient/pallas_call | solution.py:339
  36.6 4.1 %all-to-all-done.parts = f32[32,8,128]{2,1,0:T(8,128)S(1)} async-done(((f32[32,8,128]{2,1,0:T(8,128)}), f32[32,8,128]{2,1,0:T(8,128)S(1)}, u32[]{:S(2)}, u32[]{:S(2)}) %all-to-all-start) | async-done | bytes 131104 | tf_op jit(solution)/shard_map/all_to_all | solution.py:303
  40.7 0.7 fold.3
  41.4 11.8 %all-to-all-start.1 = ((f32[16,8,128]{2,1,0:T(8,128)}), f32[16,8,128]{2,1,0:T(8,128)S(1)}, u32[]{:S(2)}, u32[]{:S(2)}) async-start(f32[16,8,128]{2,1,0:T(8,128)} %fold.3), calls=%async_computation.1 | async-start | bytes 131072 | tf_op jit(solution)/shard_map/all_to_all | solution.py:303
  53.2 0.0 copy-done.3
  53.2 3.3 %collective-permute-start.3 = (bf16[4,128,128]{2,1,0:T(8,128)(2,1)S(1)}, bf16[4,128,128]{2,1,0:T(8,128)(2,1)S(1)}, u32[]{:S(2)}, u32[]{:S(2)}) collective-permute-start(bf16[4,128,128]{2,1,0:T(8,128)(2,1)S(1)} %copy-done.3), channel_id=1, source_target_pairs={{0,2},{2,0},{4,6},{6,4},{8,10},{10,8},{12,14},{14,12},{1,3},{3,1},... | collective-permute-start | bytes 393224 | tf_op jit(solution)/shard_map/ppermute | solution.py:289
  56.5 0.0 copy-done.5
  56.5 0.7 collective-permute-start.4
  57.2 3.8 %all-to-all-done.1.refs_0_ = f32[16,8,128]{2,1,0:T(8,128)S(1)} async-done(((f32[16,8,128]{2,1,0:T(8,128)}), f32[16,8,128]{2,1,0:T(8,128)S(1)}, u32[]{:S(2)}, u32[]{:S(2)}) %all-to-all-start.1) | async-done | bytes 65568 | tf_op jit(solution)/shard_map/all_to_all | solution.py:303
  61.0 2.4 %project.1 = (f32[4,128]{1,0:T(4,128)}, f32[1,128]{1,0:T(1,128)}, f32[32,4,128]{2,1,0:T(4,128)}) custom-call(f32[16,8,128]{2,1,0:T(8,128)S(1)} %all-to-all-done.1.refs_0_, bf16[128,3456]{1,0:T(8,128)(2,1)} %get-tuple-element.45.refs_1_.refs_2_, bf16[128,3456]{1,0:T(8,128)(2,1)} %get-tuple-element.46.refs_2_.refs_3_), custom_call_target="tpu_custom_call" | custom-call | tf_op jit(solution)/shard_map/project/pallas_call | solution.py:339
  63.5 4.4 %all-to-all-start.2 = ((f32[32,4,128]{2,1,0:T(4,128)}), f32[32,4,128]{2,1,0:T(4,128)S(1)}, u32[]{:S(2)}, u32[]{:S(2)}) async-start(f32[32,4,128]{2,1,0:T(4,128)} %get-tuple-element.47.refs_1_), calls=%async_computation.2 | async-start | bytes 131072 | tf_op jit(solution)/shard_map/all_to_all | solution.py:303
  67.9 3.0 %residual.1 = f32[128,3456]{1,0:T(8,128)} custom-call(f32[4,128]{1,0:T(4,128)} %get-tuple-element.28.refs_0_, f32[32,4,128]{2,1,0:T(4,128)} %get-tuple-element.47.refs_1_, bf16[128,3456]{1,0:T(8,128)(2,1)} %get-tuple-element.45.refs_1_.refs_2_, bf16[128,3456]{1,0:T(8,128)(2,1)} %get-tuple-element.46.refs_2_.refs_3_), custom_call_target="tpu_custom_call" | custom-call | tf_op jit(solution)/shard_map/residual/pallas_call | solution.py:339
  70.9 0.0 collective-permute-done.3.from_a.refs_2_
  70.9 0.0 collective-permute-done.4.from_b.refs_3_
  70.9 4.8 %all-to-all-done.2 = f32[32,4,128]{2,1,0:T(4,128)S(1)} async-done(((f32[32,4,128]{2,1,0:T(4,128)}), f32[32,4,128]{2,1,0:T(4,128)S(1)}, u32[]{:S(2)}, u32[]{:S(2)}) %all-to-all-start.2) | async-done | bytes 65568 | tf_op jit(solution)/shard_map/all_to_all | solution.py:303
  75.7 0.7 fold.4
  76.4 3.9 %all-to-all-start.3 = ((f32[32,8,128]{2,1,0:T(8,128)}), f32[32,8,128]{2,1,0:T(8,128)S(1)}, u32[]{:S(2)}, u32[]{:S(2)}) async-start(f32[32,8,128]{2,1,0:T(8,128)} %fold.4), calls=%async_computation.3 | async-start | bytes 262144 | tf_op jit(solution)/shard_map/all_to_all | solution.py:303
  80.4 2.4 %collective-permute-start.5 = (bf16[4,128,128]{2,1,0:T(8,128)(2,1)S(1)}, bf16[4,128,128]{2,1,0:T(8,128)(2,1)S(1)}, u32[]{:S(2)}, u32[]{:S(2)}) collective-permute-start(bf16[4,128,128]{2,1,0:T(8,128)(2,1)S(1)} %edge.3), channel_id=1, source_target_pairs={{0,1},{1,0},{2,3},{3,2},{4,5},{5,4},{6,7},{7,6},{8,9},{9,8},{10,11... | collective-permute-start | bytes 393224 | tf_op jit(solution)/shard_map/ppermute | solution.py:278
  82.7 1.0 collective-permute-done.5.refs_4_
  83.7 5.8 %all-to-all-done.3.parts = f32[32,8,128]{2,1,0:T(8,128)S(1)} async-done(((f32[32,8,128]{2,1,0:T(8,128)}), f32[32,8,128]{2,1,0:T(8,128)S(1)}, u32[]{:S(2)}, u32[]{:S(2)}) %all-to-all-start.3) | async-done | bytes 131104 | tf_op jit(solution)/shard_map/all_to_all | solution.py:303
  89.5 0.7 fold.5
  90.1 5.4 %all-to-all-start.4 = ((f32[16,8,128]{2,1,0:T(8,128)}), f32[16,8,128]{2,1,0:T(8,128)S(1)}, u32[]{:S(2)}, u32[]{:S(2)}) async-start(f32[16,8,128]{2,1,0:T(8,128)} %fold.5), calls=%async_computation.4 | async-start | bytes 131072 | tf_op jit(solution)/shard_map/all_to_all | solution.py:303
  95.5 3.8 %backward.1 = bf16[128,2,4,128]{3,2,1,0:T(4,128)(2,1)} custom-call(bf16[4,128,128]{2,1,0:T(8,128)(2,1)S(1)} %copy-done.3, bf16[4,128,128]{2,1,0:T(8,128)(2,1)S(1)} %copy-done.5, bf16[4,128,128]{2,1,0:T(8,128)(2,1)S(1)} %collective-permute-done.3.from_a.refs_2_, bf16[4,128,128]{2,1,0:T(8,128)(2,1)S(1)} %collective-permute-done.4.from_b.refs_3_, ...), custom_call_target="tpu_custom_call" | custom-call | tf_op jit(solution)/shard_map/backward/pallas_call | solution.py:339
  99.4 4.0 %all-to-all-done.4 = f32[16,8,128]{2,1,0:T(8,128)S(1)} async-done(((f32[16,8,128]{2,1,0:T(8,128)}), f32[16,8,128]{2,1,0:T(8,128)S(1)}, u32[]{:S(2)}, u32[]{:S(2)}) %all-to-all-start.4) | async-done | bytes 65568 | tf_op jit(solution)/shard_map/all_to_all | solution.py:303
  103.4 0.6 finish.1
  (3 shorter events, 0.1 us)
Async XLA Ops:
  0.6 17.9 %copy-start.15 = (f32[128]{0:T(128)S(1)}, f32[128]{0:T(128)}, u32[]{:S(2)}) copy-start(f32[128]{0:T(128)} %param.9) | copy-start | bytes 1540
  0.6 1.0 copy-start.11
  1.6 16.9 %copy-start.12 = (bf16[1,128,2,4,128]{4,3,2,1,0:T(4,128)(2,1)S(1)}, bf16[1,128,2,4,128]{4,3,2,1,0:T(4,128)(2,1)}, u32[]{:S(2)}) copy-start(bf16[1,128,2,4,128]{4,3,2,1,0:T(4,128)(2,1)} %param.7) | copy-start | bytes 786436
  1.8 19.6 %copy-start.6 = (bf16[4,128,128]{2,1,0:T(8,128)(2,1)}, bf16[4,128,128]{2,1,0:T(8,128)(2,1)S(1)}, u32[]{:S(2)}) copy-start(bf16[4,128,128]{2,1,0:T(8,128)(2,1)S(1)} %get-tuple-element.31.here_a.refs_0_) | copy-start | bytes 393220
  1.8 19.6 %copy-start.7 = (bf16[4,128,128]{2,1,0:T(8,128)(2,1)}, bf16[4,128,128]{2,1,0:T(8,128)(2,1)S(1)}, u32[]{:S(2)}) copy-start(bf16[4,128,128]{2,1,0:T(8,128)(2,1)S(1)} %get-tuple-element.32.here_b.refs_1_) | copy-start | bytes 393220
  1.8 8.5 %collective-permute-start = (bf16[4,128,128]{2,1,0:T(8,128)(2,1)S(1)}, bf16[4,128,128]{2,1,0:T(8,128)(2,1)S(1)}, u32[]{:S(2)}, u32[]{:S(2)}) collective-permute-start(bf16[4,128,128]{2,1,0:T(8,128)(2,1)S(1)} %get-tuple-element.31.here_a.refs_0_), channel_id=1, source_target_pairs={{0,2},{2,0},{4,6},{6,4},{8,10},{10,8},{12,14},{14,12},{1,3},{3,1},... | collective-permute-start | bytes 393224 | tf_op jit(solution)/shard_map/ppermute | solution.py:289
  5.9 4.5 %collective-permute-start.1 = (bf16[4,128,128]{2,1,0:T(8,128)(2,1)S(1)}, bf16[4,128,128]{2,1,0:T(8,128)(2,1)S(1)}, u32[]{:S(2)}, u32[]{:S(2)}) collective-permute-start(bf16[4,128,128]{2,1,0:T(8,128)(2,1)S(1)} %get-tuple-element.32.here_b.refs_1_), channel_id=1, source_target_pairs={{2,4},{4,2},{6,8},{8,6},{10,12},{12,10},{3,5},{5,3},{7,9},{9,7},{1... | collective-permute-start | bytes 393224 | tf_op jit(solution)/shard_map/ppermute | solution.py:289
  6.6 1.5 %copy-start = (f32[1,1,1,128,3456]{4,3,2,1,0:T(8,128)S(1)}, f32[1,1,1,128,3456]{4,3,2,1,0:T(8,128)}, u32[]{:S(2)}) copy-start(f32[1,1,1,128,3456]{4,3,2,1,0:T(8,128)} %param.10) | copy-start | bytes 5308420
  8.0 0.8 copy-start.13
  8.8 9.7 %copy-start.1 = (bf16[27,128,128]{2,1,0:T(8,128)(2,1)S(1)}, bf16[27,128,128]{2,1,0:T(8,128)(2,1)}, u32[]{:S(2)}) copy-start(bf16[27,128,128]{2,1,0:T(8,128)(2,1)} %refs_5_.1) | copy-start | bytes 2654212
  8.8 9.7 %copy-start.14 = (f32[4,3456]{1,0:T(4,128)S(1)}, f32[4,3456]{1,0:T(4,128)}, u32[]{:S(2)}) copy-start(f32[4,3456]{1,0:T(4,128)} %warm.3) | copy-start | bytes 165892
  10.4 21.2 %copy-start.8 = (bf16[4,128,128]{2,1,0:T(8,128)(2,1)}, bf16[4,128,128]{2,1,0:T(8,128)(2,1)S(1)}, u32[]{:S(2)}) copy-start(bf16[4,128,128]{2,1,0:T(8,128)(2,1)S(1)} %collective-permute-done.from_a.refs_2_) | copy-start | bytes 393220
  10.4 21.2 %copy-start.9 = (bf16[4,128,128]{2,1,0:T(8,128)(2,1)}, bf16[4,128,128]{2,1,0:T(8,128)(2,1)S(1)}, u32[]{:S(2)}) copy-start(bf16[4,128,128]{2,1,0:T(8,128)(2,1)S(1)} %collective-permute-done.1.from_b.refs_3_) | copy-start | bytes 393220
  10.5 8.0 %collective-permute-start.2 = (bf16[4,128,128]{2,1,0:T(8,128)(2,1)S(1)}, bf16[4,128,128]{2,1,0:T(8,128)(2,1)S(1)}, u32[]{:S(2)}, u32[]{:S(2)}) collective-permute-start(bf16[4,128,128]{2,1,0:T(8,128)(2,1)S(1)} %edge.2), channel_id=1, source_target_pairs={{0,1},{1,0},{2,3},{3,2},{4,5},{5,4},{6,7},{7,6},{8,9},{9,8},{10,11... | collective-permute-start | bytes 393224 | tf_op jit(solution)/shard_map/ppermute | solution.py:278
  18.5 13.1 %copy-start.10 = (bf16[4,128,128]{2,1,0:T(8,128)(2,1)}, bf16[4,128,128]{2,1,0:T(8,128)(2,1)S(1)}, u32[]{:S(2)}) copy-start(bf16[4,128,128]{2,1,0:T(8,128)(2,1)S(1)} %collective-permute-done.2.middle.refs_4_) | copy-start | bytes 393220
  21.4 0.7 copy-start.2
  22.1 0.6 copy-start.4
  22.7 30.5 %copy-start.3 = (bf16[4,128,128]{2,1,0:T(8,128)(2,1)S(1)}, bf16[4,128,128]{2,1,0:T(8,128)(2,1)}, u32[]{:S(2)}) copy-start(bf16[4,128,128]{2,1,0:T(8,128)(2,1)} %copy-done.2) | copy-start | bytes 393220
  22.7 33.8 %copy-start.5 = (bf16[4,128,128]{2,1,0:T(8,128)(2,1)S(1)}, bf16[4,128,128]{2,1,0:T(8,128)(2,1)}, u32[]{:S(2)}) copy-start(bf16[4,128,128]{2,1,0:T(8,128)(2,1)} %copy-done.4) | copy-start | bytes 393220
  22.7 18.0 %all-to-all-start = ((f32[32,8,128]{2,1,0:T(8,128)}), f32[32,8,128]{2,1,0:T(8,128)S(1)}, u32[]{:S(2)}, u32[]{:S(2)}) async-start(f32[32,8,128]{2,1,0:T(8,128)} %get-tuple-element.37), calls=%async_computation | async-start | bytes 262144 | tf_op jit(solution)/shard_map/all_to_all | solution.py:303
  41.4 19.7 %all-to-all-start.1 = ((f32[16,8,128]{2,1,0:T(8,128)}), f32[16,8,128]{2,1,0:T(8,128)S(1)}, u32[]{:S(2)}, u32[]{:S(2)}) async-start(f32[16,8,128]{2,1,0:T(8,128)} %fold.3), calls=%async_computation.1 | async-start | bytes 131072 | tf_op jit(solution)/shard_map/all_to_all | solution.py:303
  53.2 17.7 %collective-permute-start.3 = (bf16[4,128,128]{2,1,0:T(8,128)(2,1)S(1)}, bf16[4,128,128]{2,1,0:T(8,128)(2,1)S(1)}, u32[]{:S(2)}, u32[]{:S(2)}) collective-permute-start(bf16[4,128,128]{2,1,0:T(8,128)(2,1)S(1)} %copy-done.3), channel_id=1, source_target_pairs={{0,2},{2,0},{4,6},{6,4},{8,10},{10,8},{12,14},{14,12},{1,3},{3,1},... | collective-permute-start | bytes 393224 | tf_op jit(solution)/shard_map/ppermute | solution.py:289
  56.5 14.4 %collective-permute-start.4 = (bf16[4,128,128]{2,1,0:T(8,128)(2,1)S(1)}, bf16[4,128,128]{2,1,0:T(8,128)(2,1)S(1)}, u32[]{:S(2)}, u32[]{:S(2)}) collective-permute-start(bf16[4,128,128]{2,1,0:T(8,128)(2,1)S(1)} %copy-done.5), channel_id=1, source_target_pairs={{2,4},{4,2},{6,8},{8,6},{10,12},{12,10},{3,5},{5,3},{7,9},{9,7},{1... | collective-permute-start | bytes 393224 | tf_op jit(solution)/shard_map/ppermute | solution.py:289
  63.5 12.2 %all-to-all-start.2 = ((f32[32,4,128]{2,1,0:T(4,128)}), f32[32,4,128]{2,1,0:T(4,128)S(1)}, u32[]{:S(2)}, u32[]{:S(2)}) async-start(f32[32,4,128]{2,1,0:T(4,128)} %get-tuple-element.47.refs_1_), calls=%async_computation.2 | async-start | bytes 131072 | tf_op jit(solution)/shard_map/all_to_all | solution.py:303
  76.4 13.1 %all-to-all-start.3 = ((f32[32,8,128]{2,1,0:T(8,128)}), f32[32,8,128]{2,1,0:T(8,128)S(1)}, u32[]{:S(2)}, u32[]{:S(2)}) async-start(f32[32,8,128]{2,1,0:T(8,128)} %fold.4), calls=%async_computation.3 | async-start | bytes 262144 | tf_op jit(solution)/shard_map/all_to_all | solution.py:303
  80.4 3.3 %collective-permute-start.5 = (bf16[4,128,128]{2,1,0:T(8,128)(2,1)S(1)}, bf16[4,128,128]{2,1,0:T(8,128)(2,1)S(1)}, u32[]{:S(2)}, u32[]{:S(2)}) collective-permute-start(bf16[4,128,128]{2,1,0:T(8,128)(2,1)S(1)} %edge.3), channel_id=1, source_target_pairs={{0,1},{1,0},{2,3},{3,2},{4,5},{5,4},{6,7},{7,6},{8,9},{9,8},{10,11... | collective-permute-start | bytes 393224 | tf_op jit(solution)/shard_map/ppermute | solution.py:278
  90.1 13.2 %all-to-all-start.4 = ((f32[16,8,128]{2,1,0:T(8,128)}), f32[16,8,128]{2,1,0:T(8,128)S(1)}, u32[]{:S(2)}, u32[]{:S(2)}) async-start(f32[16,8,128]{2,1,0:T(8,128)} %fold.5), calls=%async_computation.4 | async-start | bytes 131072 | tf_op jit(solution)/shard_map/all_to_all | solution.py:303

commit v10 on v8

--- a/solution.py
+++ b/solution.py
@@ -116,7 +116,7 @@
 def forward_kernel(
     here_a, here_b, from_a, from_b, middle, upstream,
     weights, warm, bias, base,
-    act, grad_a, grad_b, edges, sums, planes,
+    act, grad, edges, sums, planes,
 ):
     across = rows_across(middle, middle[2], middle[3])
     fill_planes(planes, here_a, here_b, from_a, from_b, across)
@@ -159,21 +159,21 @@
     for copy in range(sums.shape[0]):
         sums[copy] = both
     for y in range(CY):
-        grad_a[y] = jnp.where(even, cube[1][y], cube[0][y])
-        grad_b[y] = jnp.where(even, cube[0][y], cube[1][y])
+        grad[0, y] = jnp.where(even, cube[1][y], cube[0][y])
+        grad[1, y] = jnp.where(even, cube[0][y], cube[1][y])
 
 
 def gradient_kernel(wait, block, upper_out, lower_out, planes, upper, lower, sem):
-    here_a, here_b, from_a, from_b, middle, grad_a, grad_b, error = block
+    here_a, here_b, from_a, from_b, middle, grad, error = block
     wait(0, 1, 2, 3, 4)
     across = rows_across(middle, middle[2], middle[3])
     fill_planes(planes, here_a, here_b, from_a, from_b, across)
-    wait(5, 6)
-    even = is_even()
-    side_a = jnp.concatenate([grad_a[y] for y in range(CY)], axis=1)
-    side_b = jnp.concatenate([grad_b[y] for y in range(CY)], axis=1)
+    wait(5)
+    even = is_even()
+    side_a = jnp.concatenate([grad[0, y] for y in range(CY)], axis=1)
+    side_b = jnp.concatenate([grad[1, y] for y in range(CY)], axis=1)
     grads = (jnp.where(even, side_b, side_a), jnp.where(even, side_a, side_b))
-    wait(7)
+    wait(6)
     leaving = []
     for pair in range(9):
         span = pl.ds(pair * GROUP, GROUP)
@@ -258,11 +258,11 @@
 
 
 def backward_kernel(wait, held, out, planes):
-    here_a, here_b, from_a, from_b, middle, weights = held
-    wait(0, 1, 2, 3, 4)
+    grad, from_a, from_b, middle, weights = held
+    wait(0, 1, 2, 3)
     across = rows_across(middle, from_a[CY], from_b[CY])
-    fill_planes(planes, here_a, here_b, from_a, from_b, across)
-    wait(5)
+    fill_planes(planes, grad.at[0], grad.at[1], from_a, from_b, across)
+    wait(4)
     totals = [None] * CX
     for pair in range(9):
         taps = [TAPS - 1 - 3 * pair - c for c in range(3)]
@@ -276,11 +276,11 @@
         out[:, x] = totals[x].astype(BF16).reshape(C, CY, CZ)
 
 
-def pack_kernel(here_a, here_b, middle, to_a, to_b):
+def pack_kernel(grad, middle, to_a, to_b):
     even = is_even()
     for y in range(CY):
-        to_a[y] = here_a[y]
-        to_b[y] = here_b[y]
+        to_a[y] = grad[0, y]
+        to_b[y] = grad[1, y]
     to_a[CY] = jnp.where(even, middle[1], middle[0])
     to_b[CY] = jnp.where(even, middle[0], middle[1])
 
@@ -389,14 +389,13 @@
     from_a, from_b, base = tie((from_a, from_b, base))
     edge = call(edge_kernel, "edge", 2, bf16(PX, C, CZ), (here_a, here_b, from_a, from_b))
     block = (here_a, here_b, from_a, from_b, swap_cores(edge))
-    act, grad_a, grad_b, edges, sums = call(
+    act, grad, edges, sums = call(
         forward_kernel,
         "forward",
         12,
         (
             bf16(C, CX, CY, CZ),
-            bf16(CY, C, CZ),
-            bf16(CY, C, CZ),
+            bf16(CX, CY, C, CZ),
             bf16(CX, C, CZ),
             f32(chips, 2 * RANK, C),
         ),
@@ -409,7 +408,7 @@
         "gradient",
         60,
         (bf16(C, K), bf16(C, K)),
-        (*block, grad_a, grad_b, error),
+        (*block, grad, error),
         [planes, pltpu.VMEM((C, K), BF16), pltpu.VMEM((C, K), BF16), pltpu.SemaphoreType.DMA((18,))],
         HBM,
     )
@@ -435,14 +434,14 @@
     )
     width = padded // columns * RANK
     mine = swap(blocks, BLOCK)
-    mine, new_error, middle, near_a, near_b = tie((mine, new_error, middle, grad_a, grad_b))
+    mine, new_error, middle, grad = tie((mine, new_error, middle, grad))
     mine = swap(fold(mine.reshape(columns, width, C), chips), DP)
     to_a, to_b = call(
         pack_kernel,
         "pack",
         4,
         (bf16(CY + 1, C, CZ), bf16(CY + 1, C, CZ)),
-        (near_a, near_b, middle),
+        (grad, middle),
     )
     g_from_a, g_from_b = exchange_x(to_a, to_b)
     blocks = swap(fold(mine, columns), BLOCK).reshape(padded, RANK, C)
@@ -451,7 +450,7 @@
         "backward",
         40,
         bf16(C, CX, CY, CZ),
-        (near_a, near_b, g_from_a, g_from_b, middle, weights),
+        (grad, g_from_a, g_from_b, middle, weights),
         [planes],
     )
     factor_q = call(

time: 104 us -> 103 us (level)
    unnamed x32 -> x28, local copies, waits for them, and re-layouts: 4.59 us -> 3.98 us
  transfers between devices with their start and end apart: 11 -> 11, of which waited for: 7 -> 7; matrix products, arithmetic and copies ran while one was open for 0% -> 0% of each run, Pallas kernels for 14% -> 13%
where the time goes in v10:
time: 103 us; the launch traced here: 102 us
  starting transfers between devices  49.9 us (48%)
  waiting for transfers between devices  26.3 us (26%)
  Pallas kernels  21.3 us (21%)
  local copies, waits for them, and re-layouts  3.98 us (4%)
    all_to_all x5, starting transfers between devices, swap(): return lax.all_to_all(x, axes, 0, 0, tiled=True)  33.3 us
    all_to_all x5, waiting for transfers between devices, swap(): return lax.all_to_all(x, axes, 0, 0, tiled=True)  24.1 us
    pallas_call x4, Pallas kernels, fetch_and_call(): pl.pallas_call(body, out_shape=shapes, in_specs=[VMEM] * len(near) + [HBM...  14 us
    ppermute x2, starting transfers between devices, swap_cores(): return lax.ppermute(edge, 'sy', [(0, 1), (1, 0)])  9.08 us
    pallas_call x9, Pallas kernels, call(): pl.pallas_call(kernel, out_shape=shapes, in_specs=[VMEM] * len(args), out...  7.34 us
    ppermute x2, starting transfers between devices, exchange_x(): lax.ppermute(to_a, 'sx', pairs_a)  6.17 us
    unnamed x28, local copies, waits for them, and re-layouts  3.98 us
    ppermute x2, waiting for transfers between devices, swap_cores(): return lax.ppermute(edge, 'sy', [(0, 1), (1, 0)])  2.08 us
  transfers between devices with their start and end apart: 11, of which 7 were waited for; matrix products, arithmetic and copies ran while one was open for 0% of the time, Pallas kernels for 13%

profile of v10, /device:TPU:1, one launch (start us, length us, event | category | flops | bytes accessed | tf_op | source)
XLA Modules:
  0.0 102.3 jit_solution(8182955368511641264)
XLA Ops:
  0.6 0.0 copy-start.13
  0.6 0.0 copy-start.9
  0.7 0.9 copy-done.9
  1.6 0.0 copy-start.10
  1.6 0.2 relayout.1
  1.8 0.0 copy-start.4
  1.8 0.0 copy-start.5
  1.8 4.0 %collective-permute-start = (bf16[4,128,128]{2,1,0:T(8,128)(2,1)S(1)}, bf16[4,128,128]{2,1,0:T(8,128)(2,1)S(1)}, u32[]{:S(2)}, u32[]{:S(2)}) collective-permute-start(bf16[4,128,128]{2,1,0:T(8,128)(2,1)S(1)} %get-tuple-element.32.here_a.refs_0_), channel_id=1, source_target_pairs={{0,2},{2,0},{4,6},{6,4},{8,10},{10,8},{12,14},{14,12},{1,3},{3,1},... | collective-permute-start | bytes 393224 | tf_op jit(solution)/shard_map/ppermute | solution.py:300
  5.9 0.7 collective-permute-start.1
  6.6 0.0 copy-start
  6.6 1.5 %copy-done = f32[1,1,1,128,3456]{4,3,2,1,0:T(8,128)S(1)} copy-done((f32[1,1,1,128,3456]{4,3,2,1,0:T(8,128)S(1)}, f32[1,1,1,128,3456]{4,3,2,1,0:T(8,128)}, u32[]{:S(2)}) %copy-start) | copy-done | bytes 1769496
  8.0 0.0 copy-start.11
  8.0 0.8 copy-done.11
  8.8 0.0 copy-start.1
  8.8 0.0 copy-start.12
  8.8 1.5 %base.1 = f32[4,128]{1,0:T(4,128)S(1)} custom-call(f32[4,3456]{1,0:T(4,128)S(1)} %copy-done.11, f32[128,3456]{1,0:T(8,128)S(1)} %bitcast.11), custom_call_target="tpu_custom_call" | custom-call | tf_op jit(solution)/shard_map/base/pallas_call | solution.py:318
  10.4 0.0 collective-permute-done.from_a.refs_2_
  10.4 0.0 copy-start.6
  10.4 0.0 collective-permute-done.1.from_b.refs_3_
  10.4 0.0 copy-start.7
  10.5 7.1 %collective-permute-start.2 = (bf16[4,128,128]{2,1,0:T(8,128)(2,1)S(1)}, bf16[4,128,128]{2,1,0:T(8,128)(2,1)S(1)}, u32[]{:S(2)}, u32[]{:S(2)}) collective-permute-start(bf16[4,128,128]{2,1,0:T(8,128)(2,1)S(1)} %edge.1), channel_id=1, source_target_pairs={{0,1},{1,0},{2,3},{3,2},{4,5},{5,4},{6,7},{7,6},{8,9},{9,8},{10,11... | collective-permute-start | bytes 393224 | tf_op jit(solution)/shard_map/ppermute | solution.py:289
  17.5 1.0 collective-permute-done.2.middle.refs_4_
  18.5 0.0 copy-start.8
  18.5 0.0 copy-done.13
  18.5 0.0 copy-done.10
  18.5 0.0 copy-done.1
  18.5 0.0 copy-done.12
  18.5 2.9 %forward.1 = (bf16[128,2,4,128]{3,2,1,0:T(4,128)(2,1)}, bf16[2,4,128,128]{3,2,1,0:T(8,128)(2,1)S(1)}, bf16[2,128,128]{2,1,0:T(8,128)(2,1)S(1)}, f32[32,8,128]{2,1,0:T(8,128)}) custom-call(bf16[4,128,128]{2,1,0:T(8,128)(2,1)S(1)} %get-tuple-element.32.here_a.refs_0_, bf16[4,128,128]{2,1,0:T(8,128)(2,1)S(1)} %get-tuple-element.33.here_b.refs_1_, ...), custom_call_target="tpu_custom_call" | custom-call | tf_op jit(solution)/shard_map/forward/pallas_call | solution.py:318
  21.4 0.0 copy-done.4
  21.4 0.0 copy-done.5
  21.4 0.0 copy-start.2
  21.4 0.7 copy-done.2
  22.1 8.7 %all-to-all-start = ((f32[32,8,128]{2,1,0:T(8,128)}), f32[32,8,128]{2,1,0:T(8,128)S(1)}, u32[]{:S(2)}, u32[]{:S(2)}) async-start(f32[32,8,128]{2,1,0:T(8,128)} %get-tuple-element.38), calls=%async_computation | async-start | bytes 262144 | tf_op jit(solution)/shard_map/all_to_all | solution.py:314
  30.8 0.0 copy-done.6
  30.8 0.0 copy-done.7
  30.8 0.0 copy-done.8
  30.9 5.0 %gradient.1 = (bf16[128,3456]{1,0:T(8,128)(2,1)}, bf16[128,3456]{1,0:T(8,128)(2,1)}) custom-call(bf16[4,128,128]{2,1,0:T(8,128)(2,1)} %copy-done.4, bf16[4,128,128]{2,1,0:T(8,128)(2,1)} %copy-done.5, bf16[4,128,128]{2,1,0:T(8,128)(2,1)} %copy-done.6, bf16[4,128,128]{2,1,0:T(8,128)(2,1)} %copy-done.7, bf16[4,128,128]{2,1,0:T(8,128)(2,1)} %copy-done.8, ...), custom_call_target="tpu_custom_call" | custom-call | tf_op jit(solution)/shard_map/gradient/pallas_call | solution.py:350
  35.9 4.1 %all-to-all-done.parts = f32[32,8,128]{2,1,0:T(8,128)S(1)} async-done(((f32[32,8,128]{2,1,0:T(8,128)}), f32[32,8,128]{2,1,0:T(8,128)S(1)}, u32[]{:S(2)}, u32[]{:S(2)}) %all-to-all-start) | async-done | bytes 131104 | tf_op jit(solution)/shard_map/all_to_all | solution.py:314
  40.0 0.7 fold.3
  40.7 11.8 %all-to-all-start.1 = ((f32[16,8,128]{2,1,0:T(8,128)}), f32[16,8,128]{2,1,0:T(8,128)S(1)}, u32[]{:S(2)}, u32[]{:S(2)}) async-start(f32[16,8,128]{2,1,0:T(8,128)} %fold.3), calls=%async_computation.1 | async-start | bytes 131072 | tf_op jit(solution)/shard_map/all_to_all | solution.py:314
  52.5 2.0 %collective-permute-start.3 = (bf16[2,128,128]{2,1,0:T(8,128)(2,1)S(1)}, bf16[2,128,128]{2,1,0:T(8,128)(2,1)S(1)}, u32[]{:S(2)}, u32[]{:S(2)}) collective-permute-start(bf16[2,128,128]{2,1,0:T(8,128)(2,1)S(1)} %get-tuple-element.44), channel_id=1, source_target_pairs={{0,1},{1,0},{2,3},{3,2},{4,5},{5,4},{6,7},{7,6},{8,9},{9,8},{10,11... | collective-permute-start | bytes 196616 | tf_op jit(solution)/shard_map/ppermute | solution.py:289
  54.5 1.1 %collective-permute-done.3.middle.refs_3_ = bf16[2,128,128]{2,1,0:T(8,128)(2,1)S(1)} collective-permute-done((bf16[2,128,128]{2,1,0:T(8,128)(2,1)S(1)}, bf16[2,128,128]{2,1,0:T(8,128)(2,1)S(1)}, u32[]{:S(2)}, u32[]{:S(2)}) %collective-permute-start.3) | collective-permute-done | bytes 65568 | tf_op jit(solution)/shard_map/ppermute | solution.py:289
  55.6 4.7 %all-to-all-done.1.refs_0_ = f32[16,8,128]{2,1,0:T(8,128)S(1)} async-done(((f32[16,8,128]{2,1,0:T(8,128)}), f32[16,8,128]{2,1,0:T(8,128)S(1)}, u32[]{:S(2)}, u32[]{:S(2)}) %all-to-all-start.1) | async-done | bytes 65568 | tf_op jit(solution)/shard_map/all_to_all | solution.py:314
  60.3 2.4 %project.1 = (f32[4,128]{1,0:T(4,128)}, f32[1,128]{1,0:T(1,128)}, f32[32,4,128]{2,1,0:T(4,128)}) custom-call(f32[16,8,128]{2,1,0:T(8,128)S(1)} %all-to-all-done.1.refs_0_, bf16[128,3456]{1,0:T(8,128)(2,1)} %get-tuple-element.46.refs_1_.refs_2_, bf16[128,3456]{1,0:T(8,128)(2,1)} %get-tuple-element.47.refs_2_.refs_3_), custom_call_target="tpu_custom_call" | custom-call | tf_op jit(solution)/shard_map/project/pallas_call | solution.py:350
  62.7 3.4 %all-to-all-start.2 = ((f32[32,4,128]{2,1,0:T(4,128)}), f32[32,4,128]{2,1,0:T(4,128)S(1)}, u32[]{:S(2)}, u32[]{:S(2)}) async-start(f32[32,4,128]{2,1,0:T(4,128)} %get-tuple-element.48.refs_1_), calls=%async_computation.2 | async-start | bytes 131072 | tf_op jit(solution)/shard_map/all_to_all | solution.py:314
  66.2 0.0 copy-start.3
  66.2 3.0 %residual.1 = f32[128,3456]{1,0:T(8,128)} custom-call(f32[4,128]{1,0:T(4,128)} %get-tuple-element.29.refs_0_, f32[32,4,128]{2,1,0:T(4,128)} %get-tuple-element.48.refs_1_, bf16[128,3456]{1,0:T(8,128)(2,1)} %get-tuple-element.46.refs_1_.refs_2_, bf16[128,3456]{1,0:T(8,128)(2,1)} %get-tuple-element.47.refs_2_.refs_3_), custom_call_target="tpu_custom_call" | custom-call | tf_op jit(solution)/shard_map/residual/pallas_call | solution.py:350
  69.3 4.8 %all-to-all-done.2 = f32[32,4,128]{2,1,0:T(4,128)S(1)} async-done(((f32[32,4,128]{2,1,0:T(4,128)}), f32[32,4,128]{2,1,0:T(4,128)S(1)}, u32[]{:S(2)}, u32[]{:S(2)}) %all-to-all-start.2) | async-done | bytes 65568 | tf_op jit(solution)/shard_map/all_to_all | solution.py:314
  74.0 0.7 fold.4
  74.7 3.9 %all-to-all-start.3 = ((f32[32,8,128]{2,1,0:T(8,128)}), f32[32,8,128]{2,1,0:T(8,128)S(1)}, u32[]{:S(2)}, u32[]{:S(2)}) async-start(f32[32,8,128]{2,1,0:T(8,128)} %fold.4), calls=%async_computation.3 | async-start | bytes 262144 | tf_op jit(solution)/shard_map/all_to_all | solution.py:314
  78.7 0.0 copy-done.3
  78.7 2.1 %collective-permute-start.4 = (bf16[5,128,128]{2,1,0:T(8,128)(2,1)S(1)}, bf16[5,128,128]{2,1,0:T(8,128)(2,1)S(1)}, u32[]{:S(2)}, u32[]{:S(2)}) collective-permute-start(bf16[5,128,128]{2,1,0:T(8,128)(2,1)S(1)} %get-tuple-element.53), channel_id=1, source_target_pairs={{0,2},{2,0},{4,6},{6,4},{8,10},{10,8},{12,14},{14,12},{1,3},{3,1},... | collective-permute-start | bytes 491528 | tf_op jit(solution)/shard_map/ppermute | solution.py:300
  80.9 0.7 collective-permute-start.5
  81.5 6.3 %all-to-all-done.3.parts = f32[32,8,128]{2,1,0:T(8,128)S(1)} async-done(((f32[32,8,128]{2,1,0:T(8,128)}), f32[32,8,128]{2,1,0:T(8,128)S(1)}, u32[]{:S(2)}, u32[]{:S(2)}) %all-to-all-start.3) | async-done | bytes 131104 | tf_op jit(solution)/shard_map/all_to_all | solution.py:314
  87.8 0.7 fold.5
  88.5 5.4 %all-to-all-start.4 = ((f32[16,8,128]{2,1,0:T(8,128)}), f32[16,8,128]{2,1,0:T(8,128)S(1)}, u32[]{:S(2)}, u32[]{:S(2)}) async-start(f32[16,8,128]{2,1,0:T(8,128)} %fold.5), calls=%async_computation.4 | async-start | bytes 131072 | tf_op jit(solution)/shard_map/all_to_all | solution.py:314
  93.8 0.0 collective-permute-done.4.refs_1_
  93.9 0.0 collective-permute-done.5.refs_2_
  93.9 3.5 %backward.1 = bf16[128,2,4,128]{3,2,1,0:T(4,128)(2,1)} custom-call(bf16[2,4,128,128]{3,2,1,0:T(8,128)(2,1)S(1)} %copy-done.3, bf16[5,128,128]{2,1,0:T(8,128)(2,1)S(1)} %collective-permute-done.4.refs_1_, bf16[5,128,128]{2,1,0:T(8,128)(2,1)S(1)} %collective-permute-done.5.refs_2_, bf16[2,128,128]{2,1,0:T(8,128)(2,1)S(1)} %collective-permute-done.3.middle.refs_3_, ...), custom_call_target="tpu_custom_call" | custom-call | tf_op jit(solution)/shard_map/backward/pallas_call | solution.py:350
  97.4 4.3 %all-to-all-done.4 = f32[16,8,128]{2,1,0:T(8,128)S(1)} async-done(((f32[16,8,128]{2,1,0:T(8,128)}), f32[16,8,128]{2,1,0:T(8,128)S(1)}, u32[]{:S(2)}, u32[]{:S(2)}) %all-to-all-start.4) | async-done | bytes 65568 | tf_op jit(solution)/shard_map/all_to_all | solution.py:314
  101.7 0.6 finish.1
  (2 shorter events, 0.1 us)
Async XLA Ops:
  0.6 17.9 %copy-start.13 = (f32[128]{0:T(128)S(1)}, f32[128]{0:T(128)}, u32[]{:S(2)}) copy-start(f32[128]{0:T(128)} %param.9) | copy-start | bytes 1540
  0.6 1.0 copy-start.9
  1.6 16.9 %copy-start.10 = (bf16[1,128,2,4,128]{4,3,2,1,0:T(4,128)(2,1)S(1)}, bf16[1,128,2,4,128]{4,3,2,1,0:T(4,128)(2,1)}, u32[]{:S(2)}) copy-start(bf16[1,128,2,4,128]{4,3,2,1,0:T(4,128)(2,1)} %param.7) | copy-start | bytes 786436
  1.8 19.6 %copy-start.4 = (bf16[4,128,128]{2,1,0:T(8,128)(2,1)}, bf16[4,128,128]{2,1,0:T(8,128)(2,1)S(1)}, u32[]{:S(2)}) copy-start(bf16[4,128,128]{2,1,0:T(8,128)(2,1)S(1)} %get-tuple-element.32.here_a.refs_0_) | copy-start | bytes 393220
  1.8 19.6 %copy-start.5 = (bf16[4,128,128]{2,1,0:T(8,128)(2,1)}, bf16[4,128,128]{2,1,0:T(8,128)(2,1)S(1)}, u32[]{:S(2)}) copy-start(bf16[4,128,128]{2,1,0:T(8,128)(2,1)S(1)} %get-tuple-element.33.here_b.refs_1_) | copy-start | bytes 393220
  1.8 8.5 %collective-permute-start = (bf16[4,128,128]{2,1,0:T(8,128)(2,1)S(1)}, bf16[4,128,128]{2,1,0:T(8,128)(2,1)S(1)}, u32[]{:S(2)}, u32[]{:S(2)}) collective-permute-start(bf16[4,128,128]{2,1,0:T(8,128)(2,1)S(1)} %get-tuple-element.32.here_a.refs_0_), channel_id=1, source_target_pairs={{0,2},{2,0},{4,6},{6,4},{8,10},{10,8},{12,14},{14,12},{1,3},{3,1},... | collective-permute-start | bytes 393224 | tf_op jit(solution)/shard_map/ppermute | solution.py:300
  5.9 4.5 %collective-permute-start.1 = (bf16[4,128,128]{2,1,0:T(8,128)(2,1)S(1)}, bf16[4,128,128]{2,1,0:T(8,128)(2,1)S(1)}, u32[]{:S(2)}, u32[]{:S(2)}) collective-permute-start(bf16[4,128,128]{2,1,0:T(8,128)(2,1)S(1)} %get-tuple-element.33.here_b.refs_1_), channel_id=1, source_target_pairs={{2,4},{4,2},{6,8},{8,6},{10,12},{12,10},{3,5},{5,3},{7,9},{9,7},{1... | collective-permute-start | bytes 393224 | tf_op jit(solution)/shard_map/ppermute | solution.py:300
  6.6 1.5 %copy-start = (f32[1,1,1,128,3456]{4,3,2,1,0:T(8,128)S(1)}, f32[1,1,1,128,3456]{4,3,2,1,0:T(8,128)}, u32[]{:S(2)}) copy-start(f32[1,1,1,128,3456]{4,3,2,1,0:T(8,128)} %param.10) | copy-start | bytes 5308420
  8.0 0.8 copy-start.11
  8.8 9.7 %copy-start.1 = (bf16[27,128,128]{2,1,0:T(8,128)(2,1)S(1)}, bf16[27,128,128]{2,1,0:T(8,128)(2,1)}, u32[]{:S(2)}) copy-start(bf16[27,128,128]{2,1,0:T(8,128)(2,1)} %refs_4_.1) | copy-start | bytes 2654212
  8.8 9.7 %copy-start.12 = (f32[4,3456]{1,0:T(4,128)S(1)}, f32[4,3456]{1,0:T(4,128)}, u32[]{:S(2)}) copy-start(f32[4,3456]{1,0:T(4,128)} %warm.3) | copy-start | bytes 165892
  10.4 20.5 %copy-start.6 = (bf16[4,128,128]{2,1,0:T(8,128)(2,1)}, bf16[4,128,128]{2,1,0:T(8,128)(2,1)S(1)}, u32[]{:S(2)}) copy-start(bf16[4,128,128]{2,1,0:T(8,128)(2,1)S(1)} %collective-permute-done.from_a.refs_2_) | copy-start | bytes 393220
  10.4 20.4 %copy-start.7 = (bf16[4,128,128]{2,1,0:T(8,128)(2,1)}, bf16[4,128,128]{2,1,0:T(8,128)(2,1)S(1)}, u32[]{:S(2)}) copy-start(bf16[4,128,128]{2,1,0:T(8,128)(2,1)S(1)} %collective-permute-done.1.from_b.refs_3_) | copy-start | bytes 393220
  10.5 8.0 %collective-permute-start.2 = (bf16[4,128,128]{2,1,0:T(8,128)(2,1)S(1)}, bf16[4,128,128]{2,1,0:T(8,128)(2,1)S(1)}, u32[]{:S(2)}, u32[]{:S(2)}) collective-permute-start(bf16[4,128,128]{2,1,0:T(8,128)(2,1)S(1)} %edge.1), channel_id=1, source_target_pairs={{0,1},{1,0},{2,3},{3,2},{4,5},{5,4},{6,7},{7,6},{8,9},{9,8},{10,11... | collective-permute-start | bytes 393224 | tf_op jit(solution)/shard_map/ppermute | solution.py:289
  18.5 12.3 %copy-start.8 = (bf16[4,128,128]{2,1,0:T(8,128)(2,1)}, bf16[4,128,128]{2,1,0:T(8,128)(2,1)S(1)}, u32[]{:S(2)}) copy-start(bf16[4,128,128]{2,1,0:T(8,128)(2,1)S(1)} %collective-permute-done.2.middle.refs_4_) | copy-start | bytes 393220
  21.4 0.7 copy-start.2
  22.1 17.8 %all-to-all-start = ((f32[32,8,128]{2,1,0:T(8,128)}), f32[32,8,128]{2,1,0:T(8,128)S(1)}, u32[]{:S(2)}, u32[]{:S(2)}) async-start(f32[32,8,128]{2,1,0:T(8,128)} %get-tuple-element.38), calls=%async_computation | async-start | bytes 262144 | tf_op jit(solution)/shard_map/all_to_all | solution.py:314
  40.7 19.6 %all-to-all-start.1 = ((f32[16,8,128]{2,1,0:T(8,128)}), f32[16,8,128]{2,1,0:T(8,128)S(1)}, u32[]{:S(2)}, u32[]{:S(2)}) async-start(f32[16,8,128]{2,1,0:T(8,128)} %fold.3), calls=%async_computation.1 | async-start | bytes 131072 | tf_op jit(solution)/shard_map/all_to_all | solution.py:314
  52.5 3.1 %collective-permute-start.3 = (bf16[2,128,128]{2,1,0:T(8,128)(2,1)S(1)}, bf16[2,128,128]{2,1,0:T(8,128)(2,1)S(1)}, u32[]{:S(2)}, u32[]{:S(2)}) collective-permute-start(bf16[2,128,128]{2,1,0:T(8,128)(2,1)S(1)} %get-tuple-element.44), channel_id=1, source_target_pairs={{0,1},{1,0},{2,3},{3,2},{4,5},{5,4},{6,7},{7,6},{8,9},{9,8},{10,11... | collective-permute-start | bytes 196616 | tf_op jit(solution)/shard_map/ppermute | solution.py:289
  62.7 11.3 %all-to-all-start.2 = ((f32[32,4,128]{2,1,0:T(4,128)}), f32[32,4,128]{2,1,0:T(4,128)S(1)}, u32[]{:S(2)}, u32[]{:S(2)}) async-start(f32[32,4,128]{2,1,0:T(4,128)} %get-tuple-element.48.refs_1_), calls=%async_computation.2 | async-start | bytes 131072 | tf_op jit(solution)/shard_map/all_to_all | solution.py:314
  66.2 12.5 %copy-start.3 = (bf16[2,4,128,128]{3,2,1,0:T(8,128)(2,1)S(1)}, bf16[2,4,128,128]{3,2,1,0:T(8,128)(2,1)}, u32[]{:S(2)}) copy-start(bf16[2,4,128,128]{3,2,1,0:T(8,128)(2,1)} %copy-done.2) | copy-start | bytes 786436
  74.7 13.1 %all-to-all-start.3 = ((f32[32,8,128]{2,1,0:T(8,128)}), f32[32,8,128]{2,1,0:T(8,128)S(1)}, u32[]{:S(2)}, u32[]{:S(2)}) async-start(f32[32,8,128]{2,1,0:T(8,128)} %fold.4), calls=%async_computation.3 | async-start | bytes 262144 | tf_op jit(solution)/shard_map/all_to_all | solution.py:314
  78.7 15.1 %collective-permute-start.4 = (bf16[5,128,128]{2,1,0:T(8,128)(2,1)S(1)}, bf16[5,128,128]{2,1,0:T(8,128)(2,1)S(1)}, u32[]{:S(2)}, u32[]{:S(2)}) collective-permute-start(bf16[5,128,128]{2,1,0:T(8,128)(2,1)S(1)} %get-tuple-element.53), channel_id=1, source_target_pairs={{0,2},{2,0},{4,6},{6,4},{8,10},{10,8},{12,14},{14,12},{1,3},{3,1},... | collective-permute-start | bytes 491528 | tf_op jit(solution)/shard_map/ppermute | solution.py:300
  80.9 13.0 %collective-permute-start.5 = (bf16[5,128,128]{2,1,0:T(8,128)(2,1)S(1)}, bf16[5,128,128]{2,1,0:T(8,128)(2,1)S(1)}, u32[]{:S(2)}, u32[]{:S(2)}) collective-permute-start(bf16[5,128,128]{2,1,0:T(8,128)(2,1)S(1)} %get-tuple-element.54), channel_id=1, source_target_pairs={{2,4},{4,2},{6,8},{8,6},{10,12},{12,10},{3,5},{5,3},{7,9},{9,7},{1... | collective-permute-start | bytes 491528 | tf_op jit(solution)/shard_map/ppermute | solution.py:300
  88.5 13.2 %all-to-all-start.4 = ((f32[16,8,128]{2,1,0:T(8,128)}), f32[16,8,128]{2,1,0:T(8,128)S(1)}, u32[]{:S(2)}, u32[]{:S(2)}) async-start(f32[16,8,128]{2,1,0:T(8,128)} %fold.5), calls=%async_computation.4 | async-start | bytes 131072 | tf_op jit(solution)/shard_map/all_to_all | solution.py:314

commit v11 on v10

--- a/solution.py
+++ b/solution.py
@@ -233,11 +233,10 @@
 def residual_kernel(wait, held, out, new_error, sem):
     basis, blocks, upper, lower = held
     wait(0, 1)
-    b1, b2, b3 = pieces(basis[...])
-    left = jnp.concatenate([b1, b2, b3, b1, b2, b1], axis=0).astype(BF16)
-    q = jnp.concatenate([blocks[tap] for tap in range(TAPS)], axis=1)
-    q1, q2, q3 = pieces(q)
-    right = jnp.concatenate([q1, q1, q1, q2, q2, q3], axis=0).astype(BF16)
+    b1, b2, _ = pieces(basis[...])
+    left = jnp.concatenate([b1, b1, b2, jnp.zeros_like(b1)], axis=0).astype(BF16)
+    q1, q2, _ = pieces(jnp.concatenate([blocks[tap] for tap in range(TAPS)], axis=1))
+    right = jnp.concatenate([q1, q2, q1, jnp.zeros_like(q1)], axis=0).astype(BF16)
     wait(2, 3)
     leaving = []
     for pair in range(9):

time: 103 us -> 103 us (level)
  no operation moved by 1% of the time
where the time goes in v11:
time: 103 us; the launch traced here: 102 us
  starting transfers between devices  49.9 us (48%)
  waiting for transfers between devices  26.3 us (26%)
  Pallas kernels  21.3 us (21%)
  local copies, waits for them, and re-layouts  3.98 us (4%)
    all_to_all x5, starting transfers between devices, swap(): return lax.all_to_all(x, axes, 0, 0, tiled=True)  33.3 us
    all_to_all x5, waiting for transfers between devices, swap(): return lax.all_to_all(x, axes, 0, 0, tiled=True)  24.2 us
    pallas_call x4, Pallas kernels, fetch_and_call(): pl.pallas_call(body, out_shape=shapes, in_specs=[VMEM] * len(near) + [HBM...  13.9 us
    ppermute x2, starting transfers between devices, swap_cores(): return lax.ppermute(edge, 'sy', [(0, 1), (1, 0)])  9.08 us
    pallas_call x9, Pallas kernels, call(): pl.pallas_call(kernel, out_shape=shapes, in_specs=[VMEM] * len(args), out...  7.34 us
    ppermute x2, starting transfers between devices, exchange_x(): lax.ppermute(to_a, 'sx', pairs_a)  6.17 us
    unnamed x28, local copies, waits for them, and re-layouts  3.98 us
    ppermute x2, waiting for transfers between devices, swap_cores(): return lax.ppermute(edge, 'sy', [(0, 1), (1, 0)])  2.08 us
  transfers between devices with their start and end apart: 11, of which 7 were waited for; matrix products, arithmetic and copies ran while one was open for 0% of the time, Pallas kernels for 13%

profile of v11, /device:TPU:1, one launch (start us, length us, event | category | flops | bytes accessed | tf_op | source)
XLA Modules:
  0.0 102.3 jit_solution(1518803033089326611)
XLA Ops:
  0.6 0.0 copy-start.13
  0.6 0.0 copy-start.9
  0.7 0.9 copy-done.9
  1.6 0.0 copy-start.10
  1.6 0.2 relayout.1
  1.8 0.0 copy-start.4
  1.8 0.0 copy-start.5
  1.8 4.0 %collective-permute-start = (bf16[4,128,128]{2,1,0:T(8,128)(2,1)S(1)}, bf16[4,128,128]{2,1,0:T(8,128)(2,1)S(1)}, u32[]{:S(2)}, u32[]{:S(2)}) collective-permute-start(bf16[4,128,128]{2,1,0:T(8,128)(2,1)S(1)} %get-tuple-element.32.here_a.refs_0_), channel_id=1, source_target_pairs={{0,2},{2,0},{4,6},{6,4},{8,10},{10,8},{12,14},{14,12},{1,3},{3,1},... | collective-permute-start | bytes 393224 | tf_op jit(solution)/shard_map/ppermute | solution.py:299
  5.9 0.7 collective-permute-start.1
  6.6 0.0 copy-start
  6.6 1.5 %copy-done = f32[1,1,1,128,3456]{4,3,2,1,0:T(8,128)S(1)} copy-done((f32[1,1,1,128,3456]{4,3,2,1,0:T(8,128)S(1)}, f32[1,1,1,128,3456]{4,3,2,1,0:T(8,128)}, u32[]{:S(2)}) %copy-start) | copy-done | bytes 1769496
  8.0 0.0 copy-start.11
  8.0 0.8 copy-done.11
  8.8 0.0 copy-start.1
  8.8 0.0 copy-start.12
  8.8 1.5 %base.1 = f32[4,128]{1,0:T(4,128)S(1)} custom-call(f32[4,3456]{1,0:T(4,128)S(1)} %copy-done.11, f32[128,3456]{1,0:T(8,128)S(1)} %bitcast.11), custom_call_target="tpu_custom_call" | custom-call | tf_op jit(solution)/shard_map/base/pallas_call | solution.py:317
  10.4 0.0 collective-permute-done.from_a.refs_2_
  10.4 0.0 copy-start.6
  10.4 0.0 collective-permute-done.1.from_b.refs_3_
  10.4 0.0 copy-start.7
  10.5 7.1 %collective-permute-start.2 = (bf16[4,128,128]{2,1,0:T(8,128)(2,1)S(1)}, bf16[4,128,128]{2,1,0:T(8,128)(2,1)S(1)}, u32[]{:S(2)}, u32[]{:S(2)}) collective-permute-start(bf16[4,128,128]{2,1,0:T(8,128)(2,1)S(1)} %edge.1), channel_id=1, source_target_pairs={{0,1},{1,0},{2,3},{3,2},{4,5},{5,4},{6,7},{7,6},{8,9},{9,8},{10,11... | collective-permute-start | bytes 393224 | tf_op jit(solution)/shard_map/ppermute | solution.py:288
  17.5 1.0 collective-permute-done.2.middle.refs_4_
  18.5 0.0 copy-start.8
  18.5 0.0 copy-done.13
  18.5 0.0 copy-done.10
  18.5 0.0 copy-done.1
  18.5 0.0 copy-done.12
  18.5 2.9 %forward.1 = (bf16[128,2,4,128]{3,2,1,0:T(4,128)(2,1)}, bf16[2,4,128,128]{3,2,1,0:T(8,128)(2,1)S(1)}, bf16[2,128,128]{2,1,0:T(8,128)(2,1)S(1)}, f32[32,8,128]{2,1,0:T(8,128)}) custom-call(bf16[4,128,128]{2,1,0:T(8,128)(2,1)S(1)} %get-tuple-element.32.here_a.refs_0_, bf16[4,128,128]{2,1,0:T(8,128)(2,1)S(1)} %get-tuple-element.33.here_b.refs_1_, ...), custom_call_target="tpu_custom_call" | custom-call | tf_op jit(solution)/shard_map/forward/pallas_call | solution.py:317
  21.4 0.0 copy-done.4
  21.4 0.0 copy-done.5
  21.4 0.0 copy-start.2
  21.4 0.7 copy-done.2
  22.1 8.7 %all-to-all-start = ((f32[32,8,128]{2,1,0:T(8,128)}), f32[32,8,128]{2,1,0:T(8,128)S(1)}, u32[]{:S(2)}, u32[]{:S(2)}) async-start(f32[32,8,128]{2,1,0:T(8,128)} %get-tuple-element.38), calls=%async_computation | async-start | bytes 262144 | tf_op jit(solution)/shard_map/all_to_all | solution.py:313
  30.8 0.0 copy-done.6
  30.8 0.0 copy-done.7
  30.8 0.0 copy-done.8
  30.9 5.0 %gradient.1 = (bf16[128,3456]{1,0:T(8,128)(2,1)}, bf16[128,3456]{1,0:T(8,128)(2,1)}) custom-call(bf16[4,128,128]{2,1,0:T(8,128)(2,1)} %copy-done.4, bf16[4,128,128]{2,1,0:T(8,128)(2,1)} %copy-done.5, bf16[4,128,128]{2,1,0:T(8,128)(2,1)} %copy-done.6, bf16[4,128,128]{2,1,0:T(8,128)(2,1)} %copy-done.7, bf16[4,128,128]{2,1,0:T(8,128)(2,1)} %copy-done.8, ...), custom_call_target="tpu_custom_call" | custom-call | tf_op jit(solution)/shard_map/gradient/pallas_call | solution.py:349
  35.9 4.1 %all-to-all-done.parts = f32[32,8,128]{2,1,0:T(8,128)S(1)} async-done(((f32[32,8,128]{2,1,0:T(8,128)}), f32[32,8,128]{2,1,0:T(8,128)S(1)}, u32[]{:S(2)}, u32[]{:S(2)}) %all-to-all-start) | async-done | bytes 131104 | tf_op jit(solution)/shard_map/all_to_all | solution.py:313
  40.0 0.7 fold.3
  40.7 11.8 %all-to-all-start.1 = ((f32[16,8,128]{2,1,0:T(8,128)}), f32[16,8,128]{2,1,0:T(8,128)S(1)}, u32[]{:S(2)}, u32[]{:S(2)}) async-start(f32[16,8,128]{2,1,0:T(8,128)} %fold.3), calls=%async_computation.1 | async-start | bytes 131072 | tf_op jit(solution)/shard_map/all_to_all | solution.py:313
  52.5 2.0 %collective-permute-start.3 = (bf16[2,128,128]{2,1,0:T(8,128)(2,1)S(1)}, bf16[2,128,128]{2,1,0:T(8,128)(2,1)S(1)}, u32[]{:S(2)}, u32[]{:S(2)}) collective-permute-start(bf16[2,128,128]{2,1,0:T(8,128)(2,1)S(1)} %get-tuple-element.44), channel_id=1, source_target_pairs={{0,1},{1,0},{2,3},{3,2},{4,5},{5,4},{6,7},{7,6},{8,9},{9,8},{10,11... | collective-permute-start | bytes 196616 | tf_op jit(solution)/shard_map/ppermute | solution.py:288
  54.5 1.1 %collective-permute-done.3.middle.refs_3_ = bf16[2,128,128]{2,1,0:T(8,128)(2,1)S(1)} collective-permute-done((bf16[2,128,128]{2,1,0:T(8,128)(2,1)S(1)}, bf16[2,128,128]{2,1,0:T(8,128)(2,1)S(1)}, u32[]{:S(2)}, u32[]{:S(2)}) %collective-permute-start.3) | collective-permute-done | bytes 65568 | tf_op jit(solution)/shard_map/ppermute | solution.py:288
  55.6 4.7 %all-to-all-done.1.refs_0_ = f32[16,8,128]{2,1,0:T(8,128)S(1)} async-done(((f32[16,8,128]{2,1,0:T(8,128)}), f32[16,8,128]{2,1,0:T(8,128)S(1)}, u32[]{:S(2)}, u32[]{:S(2)}) %all-to-all-start.1) | async-done | bytes 65568 | tf_op jit(solution)/shard_map/all_to_all | solution.py:313
  60.3 2.4 %project.1 = (f32[4,128]{1,0:T(4,128)}, f32[1,128]{1,0:T(1,128)}, f32[32,4,128]{2,1,0:T(4,128)}) custom-call(f32[16,8,128]{2,1,0:T(8,128)S(1)} %all-to-all-done.1.refs_0_, bf16[128,3456]{1,0:T(8,128)(2,1)} %get-tuple-element.46.refs_1_.refs_2_, bf16[128,3456]{1,0:T(8,128)(2,1)} %get-tuple-element.47.refs_2_.refs_3_), custom_call_target="tpu_custom_call" | custom-call | tf_op jit(solution)/shard_map/project/pallas_call | solution.py:349
  62.7 3.4 %all-to-all-start.2 = ((f32[32,4,128]{2,1,0:T(4,128)}), f32[32,4,128]{2,1,0:T(4,128)S(1)}, u32[]{:S(2)}, u32[]{:S(2)}) async-start(f32[32,4,128]{2,1,0:T(4,128)} %get-tuple-element.48.refs_1_), calls=%async_computation.2 | async-start | bytes 131072 | tf_op jit(solution)/shard_map/all_to_all | solution.py:313
  66.2 0.0 copy-start.3
  66.2 3.0 %residual.1 = f32[128,3456]{1,0:T(8,128)} custom-call(f32[4,128]{1,0:T(4,128)} %get-tuple-element.29.refs_0_, f32[32,4,128]{2,1,0:T(4,128)} %get-tuple-element.48.refs_1_, bf16[128,3456]{1,0:T(8,128)(2,1)} %get-tuple-element.46.refs_1_.refs_2_, bf16[128,3456]{1,0:T(8,128)(2,1)} %get-tuple-element.47.refs_2_.refs_3_), custom_call_target="tpu_custom_call" | custom-call | tf_op jit(solution)/shard_map/residual/pallas_call | solution.py:349
  69.2 4.8 %all-to-all-done.2 = f32[32,4,128]{2,1,0:T(4,128)S(1)} async-done(((f32[32,4,128]{2,1,0:T(4,128)}), f32[32,4,128]{2,1,0:T(4,128)S(1)}, u32[]{:S(2)}, u32[]{:S(2)}) %all-to-all-start.2) | async-done | bytes 65568 | tf_op jit(solution)/shard_map/all_to_all | solution.py:313
  74.0 0.7 fold.4
  74.7 3.9 %all-to-all-start.3 = ((f32[32,8,128]{2,1,0:T(8,128)}), f32[32,8,128]{2,1,0:T(8,128)S(1)}, u32[]{:S(2)}, u32[]{:S(2)}) async-start(f32[32,8,128]{2,1,0:T(8,128)} %fold.4), calls=%async_computation.3 | async-start | bytes 262144 | tf_op jit(solution)/shard_map/all_to_all | solution.py:313
  78.7 0.0 copy-done.3
  78.7 2.1 %collective-permute-start.4 = (bf16[5,128,128]{2,1,0:T(8,128)(2,1)S(1)}, bf16[5,128,128]{2,1,0:T(8,128)(2,1)S(1)}, u32[]{:S(2)}, u32[]{:S(2)}) collective-permute-start(bf16[5,128,128]{2,1,0:T(8,128)(2,1)S(1)} %get-tuple-element.53), channel_id=1, source_target_pairs={{0,2},{2,0},{4,6},{6,4},{8,10},{10,8},{12,14},{14,12},{1,3},{3,1},... | collective-permute-start | bytes 491528 | tf_op jit(solution)/shard_map/ppermute | solution.py:299
  80.9 0.7 collective-permute-start.5
  81.5 6.3 %all-to-all-done.3.parts = f32[32,8,128]{2,1,0:T(8,128)S(1)} async-done(((f32[32,8,128]{2,1,0:T(8,128)}), f32[32,8,128]{2,1,0:T(8,128)S(1)}, u32[]{:S(2)}, u32[]{:S(2)}) %all-to-all-start.3) | async-done | bytes 131104 | tf_op jit(solution)/shard_map/all_to_all | solution.py:313
  87.8 0.7 fold.5
  88.5 5.4 %all-to-all-start.4 = ((f32[16,8,128]{2,1,0:T(8,128)}), f32[16,8,128]{2,1,0:T(8,128)S(1)}, u32[]{:S(2)}, u32[]{:S(2)}) async-start(f32[16,8,128]{2,1,0:T(8,128)} %fold.5), calls=%async_computation.4 | async-start | bytes 131072 | tf_op jit(solution)/shard_map/all_to_all | solution.py:313
  93.8 0.0 collective-permute-done.4.refs_1_
  93.9 0.0 collective-permute-done.5.refs_2_
  93.9 3.5 %backward.1 = bf16[128,2,4,128]{3,2,1,0:T(4,128)(2,1)} custom-call(bf16[2,4,128,128]{3,2,1,0:T(8,128)(2,1)S(1)} %copy-done.3, bf16[5,128,128]{2,1,0:T(8,128)(2,1)S(1)} %collective-permute-done.4.refs_1_, bf16[5,128,128]{2,1,0:T(8,128)(2,1)S(1)} %collective-permute-done.5.refs_2_, bf16[2,128,128]{2,1,0:T(8,128)(2,1)S(1)} %collective-permute-done.3.middle.refs_3_, ...), custom_call_target="tpu_custom_call" | custom-call | tf_op jit(solution)/shard_map/backward/pallas_call | solution.py:349
  97.4 4.3 %all-to-all-done.4 = f32[16,8,128]{2,1,0:T(8,128)S(1)} async-done(((f32[16,8,128]{2,1,0:T(8,128)}), f32[16,8,128]{2,1,0:T(8,128)S(1)}, u32[]{:S(2)}, u32[]{:S(2)}) %all-to-all-start.4) | async-done | bytes 65568 | tf_op jit(solution)/shard_map/all_to_all | solution.py:313
  101.7 0.6 finish.1
  (2 shorter events, 0.1 us)
Async XLA Ops:
  0.6 17.9 %copy-start.13 = (f32[128]{0:T(128)S(1)}, f32[128]{0:T(128)}, u32[]{:S(2)}) copy-start(f32[128]{0:T(128)} %param.9) | copy-start | bytes 1540
  0.6 1.0 copy-start.9
  1.6 16.9 %copy-start.10 = (bf16[1,128,2,4,128]{4,3,2,1,0:T(4,128)(2,1)S(1)}, bf16[1,128,2,4,128]{4,3,2,1,0:T(4,128)(2,1)}, u32[]{:S(2)}) copy-start(bf16[1,128,2,4,128]{4,3,2,1,0:T(4,128)(2,1)} %param.7) | copy-start | bytes 786436
  1.8 19.6 %copy-start.4 = (bf16[4,128,128]{2,1,0:T(8,128)(2,1)}, bf16[4,128,128]{2,1,0:T(8,128)(2,1)S(1)}, u32[]{:S(2)}) copy-start(bf16[4,128,128]{2,1,0:T(8,128)(2,1)S(1)} %get-tuple-element.32.here_a.refs_0_) | copy-start | bytes 393220
  1.8 19.6 %copy-start.5 = (bf16[4,128,128]{2,1,0:T(8,128)(2,1)}, bf16[4,128,128]{2,1,0:T(8,128)(2,1)S(1)}, u32[]{:S(2)}) copy-start(bf16[4,128,128]{2,1,0:T(8,128)(2,1)S(1)} %get-tuple-element.33.here_b.refs_1_) | copy-start | bytes 393220
  1.8 8.5 %collective-permute-start = (bf16[4,128,128]{2,1,0:T(8,128)(2,1)S(1)}, bf16[4,128,128]{2,1,0:T(8,128)(2,1)S(1)}, u32[]{:S(2)}, u32[]{:S(2)}) collective-permute-start(bf16[4,128,128]{2,1,0:T(8,128)(2,1)S(1)} %get-tuple-element.32.here_a.refs_0_), channel_id=1, source_target_pairs={{0,2},{2,0},{4,6},{6,4},{8,10},{10,8},{12,14},{14,12},{1,3},{3,1},... | collective-permute-start | bytes 393224 | tf_op jit(solution)/shard_map/ppermute | solution.py:299
  5.9 4.5 %collective-permute-start.1 = (bf16[4,128,128]{2,1,0:T(8,128)(2,1)S(1)}, bf16[4,128,128]{2,1,0:T(8,128)(2,1)S(1)}, u32[]{:S(2)}, u32[]{:S(2)}) collective-permute-start(bf16[4,128,128]{2,1,0:T(8,128)(2,1)S(1)} %get-tuple-element.33.here_b.refs_1_), channel_id=1, source_target_pairs={{2,4},{4,2},{6,8},{8,6},{10,12},{12,10},{3,5},{5,3},{7,9},{9,7},{1... | collective-permute-start | bytes 393224 | tf_op jit(solution)/shard_map/ppermute | solution.py:299
  6.6 1.5 %copy-start = (f32[1,1,1,128,3456]{4,3,2,1,0:T(8,128)S(1)}, f32[1,1,1,128,3456]{4,3,2,1,0:T(8,128)}, u32[]{:S(2)}) copy-start(f32[1,1,1,128,3456]{4,3,2,1,0:T(8,128)} %param.10) | copy-start | bytes 5308420
  8.0 0.8 copy-start.11
  8.8 9.7 %copy-start.1 = (bf16[27,128,128]{2,1,0:T(8,128)(2,1)S(1)}, bf16[27,128,128]{2,1,0:T(8,128)(2,1)}, u32[]{:S(2)}) copy-start(bf16[27,128,128]{2,1,0:T(8,128)(2,1)} %refs_4_.1) | copy-start | bytes 2654212
  8.8 9.7 %copy-start.12 = (f32[4,3456]{1,0:T(4,128)S(1)}, f32[4,3456]{1,0:T(4,128)}, u32[]{:S(2)}) copy-start(f32[4,3456]{1,0:T(4,128)} %warm.3) | copy-start | bytes 165892
  10.4 20.5 %copy-start.6 = (bf16[4,128,128]{2,1,0:T(8,128)(2,1)}, bf16[4,128,128]{2,1,0:T(8,128)(2,1)S(1)}, u32[]{:S(2)}) copy-start(bf16[4,128,128]{2,1,0:T(8,128)(2,1)S(1)} %collective-permute-done.from_a.refs_2_) | copy-start | bytes 393220
  10.4 20.4 %copy-start.7 = (bf16[4,128,128]{2,1,0:T(8,128)(2,1)}, bf16[4,128,128]{2,1,0:T(8,128)(2,1)S(1)}, u32[]{:S(2)}) copy-start(bf16[4,128,128]{2,1,0:T(8,128)(2,1)S(1)} %collective-permute-done.1.from_b.refs_3_) | copy-start | bytes 393220
  10.5 8.0 %collective-permute-start.2 = (bf16[4,128,128]{2,1,0:T(8,128)(2,1)S(1)}, bf16[4,128,128]{2,1,0:T(8,128)(2,1)S(1)}, u32[]{:S(2)}, u32[]{:S(2)}) collective-permute-start(bf16[4,128,128]{2,1,0:T(8,128)(2,1)S(1)} %edge.1), channel_id=1, source_target_pairs={{0,1},{1,0},{2,3},{3,2},{4,5},{5,4},{6,7},{7,6},{8,9},{9,8},{10,11... | collective-permute-start | bytes 393224 | tf_op jit(solution)/shard_map/ppermute | solution.py:288
  18.5 12.3 %copy-start.8 = (bf16[4,128,128]{2,1,0:T(8,128)(2,1)}, bf16[4,128,128]{2,1,0:T(8,128)(2,1)S(1)}, u32[]{:S(2)}) copy-start(bf16[4,128,128]{2,1,0:T(8,128)(2,1)S(1)} %collective-permute-done.2.middle.refs_4_) | copy-start | bytes 393220
  21.4 0.7 copy-start.2
  22.1 17.8 %all-to-all-start = ((f32[32,8,128]{2,1,0:T(8,128)}), f32[32,8,128]{2,1,0:T(8,128)S(1)}, u32[]{:S(2)}, u32[]{:S(2)}) async-start(f32[32,8,128]{2,1,0:T(8,128)} %get-tuple-element.38), calls=%async_computation | async-start | bytes 262144 | tf_op jit(solution)/shard_map/all_to_all | solution.py:313
  40.7 19.6 %all-to-all-start.1 = ((f32[16,8,128]{2,1,0:T(8,128)}), f32[16,8,128]{2,1,0:T(8,128)S(1)}, u32[]{:S(2)}, u32[]{:S(2)}) async-start(f32[16,8,128]{2,1,0:T(8,128)} %fold.3), calls=%async_computation.1 | async-start | bytes 131072 | tf_op jit(solution)/shard_map/all_to_all | solution.py:313
  52.5 3.1 %collective-permute-start.3 = (bf16[2,128,128]{2,1,0:T(8,128)(2,1)S(1)}, bf16[2,128,128]{2,1,0:T(8,128)(2,1)S(1)}, u32[]{:S(2)}, u32[]{:S(2)}) collective-permute-start(bf16[2,128,128]{2,1,0:T(8,128)(2,1)S(1)} %get-tuple-element.44), channel_id=1, source_target_pairs={{0,1},{1,0},{2,3},{3,2},{4,5},{5,4},{6,7},{7,6},{8,9},{9,8},{10,11... | collective-permute-start | bytes 196616 | tf_op jit(solution)/shard_map/ppermute | solution.py:288
  62.7 11.3 %all-to-all-start.2 = ((f32[32,4,128]{2,1,0:T(4,128)}), f32[32,4,128]{2,1,0:T(4,128)S(1)}, u32[]{:S(2)}, u32[]{:S(2)}) async-start(f32[32,4,128]{2,1,0:T(4,128)} %get-tuple-element.48.refs_1_), calls=%async_computation.2 | async-start | bytes 131072 | tf_op jit(solution)/shard_map/all_to_all | solution.py:313
  66.2 12.5 %copy-start.3 = (bf16[2,4,128,128]{3,2,1,0:T(8,128)(2,1)S(1)}, bf16[2,4,128,128]{3,2,1,0:T(8,128)(2,1)}, u32[]{:S(2)}) copy-start(bf16[2,4,128,128]{3,2,1,0:T(8,128)(2,1)} %copy-done.2) | copy-start | bytes 786436
  74.7 13.1 %all-to-all-start.3 = ((f32[32,8,128]{2,1,0:T(8,128)}), f32[32,8,128]{2,1,0:T(8,128)S(1)}, u32[]{:S(2)}, u32[]{:S(2)}) async-start(f32[32,8,128]{2,1,0:T(8,128)} %fold.4), calls=%async_computation.3 | async-start | bytes 262144 | tf_op jit(solution)/shard_map/all_to_all | solution.py:313
  78.7 15.1 %collective-permute-start.4 = (bf16[5,128,128]{2,1,0:T(8,128)(2,1)S(1)}, bf16[5,128,128]{2,1,0:T(8,128)(2,1)S(1)}, u32[]{:S(2)}, u32[]{:S(2)}) collective-permute-start(bf16[5,128,128]{2,1,0:T(8,128)(2,1)S(1)} %get-tuple-element.53), channel_id=1, source_target_pairs={{0,2},{2,0},{4,6},{6,4},{8,10},{10,8},{12,14},{14,12},{1,3},{3,1},... | collective-permute-start | bytes 491528 | tf_op jit(solution)/shard_map/ppermute | solution.py:299
  80.9 13.0 %collective-permute-start.5 = (bf16[5,128,128]{2,1,0:T(8,128)(2,1)S(1)}, bf16[5,128,128]{2,1,0:T(8,128)(2,1)S(1)}, u32[]{:S(2)}, u32[]{:S(2)}) collective-permute-start(bf16[5,128,128]{2,1,0:T(8,128)(2,1)S(1)} %get-tuple-element.54), channel_id=1, source_target_pairs={{2,4},{4,2},{6,8},{8,6},{10,12},{12,10},{3,5},{5,3},{7,9},{9,7},{1... | collective-permute-start | bytes 491528 | tf_op jit(solution)/shard_map/ppermute | solution.py:299
  88.5 13.2 %all-to-all-start.4 = ((f32[16,8,128]{2,1,0:T(8,128)}), f32[16,8,128]{2,1,0:T(8,128)S(1)}, u32[]{:S(2)}, u32[]{:S(2)}) async-start(f32[16,8,128]{2,1,0:T(8,128)} %fold.5), calls=%async_computation.4 | async-start | bytes 131072 | tf_op jit(solution)/shard_map/all_to_all | solution.py:313
